TPU v7x, 32 devices: a whole 2x2x4 slice. The times are simulated.
32 devices in a mesh: expert: 4 (over z), cuts: 2 (over core), dp: 4 (over y, x).
Axes of the slice: x: 2, y: 2, z: 4, core: 2. Of those that a mesh axis runs over, the one named last changes fastest.
Arguments:
- tokens: float32 [4096, 1024], P(('expert', 'dp')), may hold values from -6 to 6
- cotangent: float32 [4096, 1024], P(('expert', 'dp')), may hold values from -1.25 to 1.25
- routes: int32 [4096, 2], P(('expert', 'dp')), may hold values from 0 to 3, all different within a row; in each aligned block of 256 rows (0 to 255, 256 to 511, ...) at most 192 rows name the same one
- combine_index: int32 [4096, 2], P(('expert', 'dp')), may hold values from 0 to 255
- combine_table: float32 [256], replicated, may hold values from 0.1 to 1
- w_in: bfloat16 [4, 1024, 2688], P('expert', None, 'cuts'), may hold values from -0.1875 to 0.1875
- w_out: bfloat16 [4, 2688, 1024], P('expert', 'cuts'), may hold values from -0.125 to 0.125
Outputs:
- layer_out: float32 [4096, 1024], P(('expert', 'dp'))
- d_tokens: float32 [4096, 1024], P(('expert', 'dp'))
- grad_in: float32 [4, 1024, 2688], P('expert', 'dp', 'cuts')
- grad_out: float32 [4, 2688, 1024], P('expert', 'cuts', 'dp')
Inputs may be any that keep to these rules, and one draw needn't show every extreme that they name: `routes`: each row names 2 different experts. Among the rows of one device no expert is named more than 192 times, and in the rows of some device some expert is named exactly 192 times.
All inputs are finite; a program needn't handle non-finite values.
Results may differ from a plain program's by a relative error of at most 0.011.
Values may be sent and summed in bfloat16 or wider, within the bound.
No kernel may reach another device: no remote copies, remote signals or barrier semaphores. Data moves between devices by JAX's collectives and lax.ppermute only.
A program may use at most 128 MiB of HBM per device.

v0:
```python
import jax
import jax.numpy as jnp
from jax import lax
from jax.sharding import PartitionSpec as P


def shards(tokens, cotangent, routes, combine_index, combine_table, w_in, w_out):
    owners = lax.axis_size("expert")
    token_count, feature_width = tokens.shape
    top_count = routes.shape[1]
    pair_count = token_count * top_count
    capacity = max(2, 3 * pair_count // (2 * owners))
    table_size = combine_table.shape[0]
    routes_flat = routes.reshape(pair_count)
    index_flat = combine_index.reshape(pair_count)
    weight = jnp.sum(
        jnp.where(
            index_flat[:, None] == jnp.arange(table_size, dtype=jnp.int32)[None, :],
            combine_table[None, :],
            0.0,
        ),
        axis=1,
    )
    onehot = (routes_flat[:, None] == jnp.arange(owners, dtype=jnp.int32)[None, :]).astype(
        jnp.int32
    )
    before = jnp.cumsum(onehot, axis=0) - onehot
    row_rank = jnp.sum(before * onehot, axis=1)
    slot_index = routes_flat * capacity + row_rank
    source = (
        jnp.full((owners * capacity,), pair_count, jnp.int32)
        .at[slot_index]
        .set(jnp.arange(pair_count, dtype=jnp.int32))
    )
    filled = source < pair_count
    picked = jnp.minimum(source, pair_count - 1)
    token_row = picked // top_count
    outgoing = jnp.where(filled[:, None], tokens[token_row], 0.0).astype(jnp.bfloat16)
    arrived = lax.all_to_all(
        outgoing.reshape(owners, capacity, feature_width),
        "expert",
        split_axis=0,
        concat_axis=0,
        tiled=True,
    )
    arrived = arrived.reshape(owners * capacity, feature_width)
    inner_weight = w_in[0]
    outer_weight = w_out[0]
    activation = jnp.dot(arrived, inner_weight, preferred_element_type=jnp.float32)
    positive = jnp.maximum(activation, 0.0)
    hidden = (positive * positive).astype(jnp.bfloat16)
    partial_value = jnp.dot(hidden, outer_weight, preferred_element_type=jnp.float32)
    scaled = jnp.where(filled, weight[picked], 0.0)
    grad_outgoing = (scaled[:, None] * cotangent[token_row]).astype(jnp.bfloat16)
    grad_arrived = lax.all_to_all(
        grad_outgoing.reshape(owners, capacity, feature_width),
        "expert",
        split_axis=0,
        concat_axis=0,
        tiled=True,
    )
    grad_arrived = grad_arrived.reshape(owners * capacity, feature_width)
    contract_last = (((1,), (1,)), ((), ()))
    contract_first = (((0,), (0,)), ((), ()))
    d_hidden = lax.dot_general(
        grad_arrived, outer_weight, contract_last, preferred_element_type=jnp.float32
    )
    d_act = (d_hidden * 2.0 * positive).astype(jnp.bfloat16)
    back_partial = lax.dot_general(
        d_act, inner_weight, contract_last, preferred_element_type=jnp.float32
    )
    grad_inner = lax.dot_general(arrived, d_act, contract_first, preferred_element_type=jnp.float32)
    grad_outer = lax.dot_general(
        hidden, grad_arrived, contract_first, preferred_element_type=jnp.float32
    )
    shared_rows = lax.psum_scatter(
        partial_value.astype(jnp.bfloat16), "cuts", scatter_dimension=1, tiled=True
    )
    half_width = shared_rows.shape[1]
    returned = lax.all_to_all(
        shared_rows.reshape(owners, capacity, half_width),
        "expert",
        split_axis=0,
        concat_axis=0,
        tiled=True,
    )
    returned = returned.reshape(owners * capacity, half_width)[slot_index].astype(jnp.float32)
    part_out = jnp.sum(
        (weight[:, None] * returned).reshape(token_count, top_count, half_width), axis=1
    )
    layer_out = lax.all_gather(part_out.astype(jnp.bfloat16), "cuts", axis=1, tiled=True).astype(
        part_out.dtype
    )
    back_shared = lax.psum_scatter(
        back_partial.astype(jnp.bfloat16), "cuts", scatter_dimension=1, tiled=True
    )
    back_rows = lax.all_to_all(
        back_shared.reshape(owners, capacity, half_width),
        "expert",
        split_axis=0,
        concat_axis=0,
        tiled=True,
    )
    back_rows = back_rows.reshape(owners * capacity, half_width)[slot_index].astype(jnp.float32)
    part_grad = jnp.sum(back_rows.reshape(token_count, top_count, half_width), axis=1)
    d_tokens = lax.all_gather(part_grad.astype(jnp.bfloat16), "cuts", axis=1, tiled=True).astype(
        part_grad.dtype
    )
    grad_in = lax.psum_scatter(
        grad_inner.astype(jnp.bfloat16), "dp", scatter_dimension=0, tiled=True
    ).astype(jnp.float32)[None]
    grad_out = lax.psum_scatter(
        grad_outer.astype(jnp.bfloat16), "dp", scatter_dimension=1, tiled=True
    ).astype(jnp.float32)[None]
    return (layer_out, d_tokens, grad_in, grad_out)


def solution(mesh):
    in_specs = (
        P(("expert", "dp"), None),
        P(("expert", "dp"), None),
        P(("expert", "dp"), None),
        P(("expert", "dp"), None),
        P(),
        P("expert", None, "cuts"),
        P("expert", "cuts", None),
    )
    out_specs = (
        P(("expert", "dp"), None),
        P(("expert", "dp"), None),
        P("expert", "dp", "cuts"),
        P("expert", "cuts", "dp"),
    )
    return jax.shard_map(shards, mesh=mesh, in_specs=in_specs, out_specs=out_specs, check_vma=False)
```

profile of v0, /device:TPU:0, one launch (start us, length us, event | category | flops | bytes accessed | tf_op | source)
XLA Modules:
  0.0 242.9 jit_solution(4089372872072466537)
XLA Ops:
  11.2 2.4 %scatter_custom_fusion = s32[768]{0:T(1024)S(1)} fusion(s32[512]{0:T(512)S(1)} %bitcast.61, s32[512]{0:T(512)S(1)} %iota.15, s32[]{:T(128)} %constant.14.clone.1), kind=kCustom, calls=%fused_computation.50 | custom fusion | bytes 3076 | tf_op jit(solution)/shard_map/scatter | solution.py:33
  15.5 5.0 %gather_fusion.2 = f32[768]{0:T(1024)S(1)} fusion(f32[512]{0:T(512)S(1)} %select_reduce_fusion, s32[1024]{0:T(1024)S(1)} %get-tuple-element.8), kind=kCustom, calls=%fused_computation.2 | custom fusion | bytes 9216 | tf_op jit(solution)/shard_map/gather | solution.py:53
  20.6 5.8 %gather_fusion = bf16[768,1024]{1,0:T(8,128)(2,1)} fusion(f32[256,1024]{1,0:T(8,128)} %param.7, s32[1024]{0:T(1024)S(1)} %get-tuple-element.9), kind=kCustom, calls=%fused_computation | custom fusion | bytes 3148800 | tf_op jit(solution)/shard_map/gather | solution.py:38
  26.4 2.9 %select_convert_fusion = bf16[4,192,1024]{2,1,0:T(8,128)(2,1)} fusion(bf16[4,192,1024]{2,1,0:T(8,128)(2,1)} %bitcast.58, pred[4,192]{1,0:T(4,128)(4,1)S(1)} %broadcast_in_dim.60), kind=kLoop, calls=%fused_computation.12 | loop fusion | flops 786432 | bytes 3146496 | tf_op jit(solution)/shard_map/convert_element_type | solution.py:38
  29.3 6.3 %all-to-all-start = ((bf16[4,192,1024]{2,1,0:T(8,128)(2,1)}), bf16[4,192,1024]{2,1,0:T(8,128)(2,1)}, u32[]{:S(2)}, u32[]{:S(2)}) async-start(bf16[4,192,1024]{2,1,0:T(8,128)(2,1)} %select_convert_fusion), calls=%async_computation | async-start | bytes 3145728 | tf_op jit(solution)/shard_map/all_to_all | solution.py:39
  35.7 5.9 %gather_fusion.3 = f32[768,1024]{1,0:T(8,128)} fusion(f32[256,1024]{1,0:T(8,128)} %param.8, s32[1024]{0:T(1024)S(1)} %get-tuple-element.9), kind=kCustom, calls=%fused_computation.3 | custom fusion | bytes 6294528 | tf_op jit(solution)/shard_map/gather | solution.py:54
  41.6 3.3 %multiply_convert_fusion.2 = bf16[4,192,1024]{2,1,0:T(8,128)(2,1)} fusion(f32[4,192,1024]{2,1,0:T(8,128)} %bitcast.57, f32[4,192]{1,0:T(4,128)S(1)} %mul.61), kind=kLoop, calls=%fused_computation.11 | loop fusion | flops 1572864 | bytes 4721664 | tf_op jit(solution)/shard_map/convert_element_type | solution.py:54
  44.9 27.8 %all-to-all-done = bf16[4,192,1024]{2,1,0:T(8,128)(2,1)} async-done(((bf16[4,192,1024]{2,1,0:T(8,128)(2,1)}), bf16[4,192,1024]{2,1,0:T(8,128)(2,1)}, u32[]{:S(2)}, u32[]{:S(2)}) %all-to-all-start) | async-done | bytes 1572896 | tf_op jit(solution)/shard_map/all_to_all | solution.py:39
  72.7 4.4 %all-to-all-start.2 = ((bf16[4,192,1024]{2,1,0:T(8,128)(2,1)}), bf16[4,192,1024]{2,1,0:T(8,128)(2,1)}, u32[]{:S(2)}, u32[]{:S(2)}) async-start(bf16[4,192,1024]{2,1,0:T(8,128)(2,1)} %multiply_convert_fusion.2), calls=%async_computation.3 | async-start | bytes 3145728 | tf_op jit(solution)/shard_map/all_to_all | solution.py:55
  77.1 5.7 %convolution_maximum_fusion = f32[768,1344]{0,1:T(8,128)} fusion(bf16[768,1024]{1,0:T(8,128)(2,1)} %bitcast.4, bf16[1,1024,1344]{1,2,0:T(8,128)(2,1)S(1)} %copy-done), kind=kOutput, calls=%fused_computation.8 | convolution fusion | flops 2114961408 | bytes 8454144 | tf_op jit(solution)/shard_map/dot_general | solution.py:49
  82.8 30.8 %all-to-all-done.2 = bf16[4,192,1024]{2,1,0:T(8,128)(2,1)} async-done(((bf16[4,192,1024]{2,1,0:T(8,128)(2,1)}), bf16[4,192,1024]{2,1,0:T(8,128)(2,1)}, u32[]{:S(2)}, u32[]{:S(2)}) %all-to-all-start.2) | async-done | bytes 1572896 | tf_op jit(solution)/shard_map/all_to_all | solution.py:55
  113.6 5.8 %multiply_convert_fusion = bf16[768,1344]{0,1:T(8,128)(2,1)S(1)} fusion(f32[768,1344]{0,1:T(8,128)} %convolution_maximum_fusion, bf16[768,1024]{1,0:T(8,128)(2,1)} %bitcast.10, bf16[1,1344,1024]{2,1,0:T(8,128)(2,1)} %param.13), kind=kOutput, calls=%fused_computation.6 | convolution fusion | flops 2117025792 | bytes 10518528 | tf_op jit(solution)/shard_map/dot_general | solution.py:65
  119.4 1.4 copy-done.2
  120.8 3.8 %fusion.6 = bf16[768,1024]{1,0:T(8,128)(2,1)} fusion(bf16[768,1344]{0,1:T(8,128)(2,1)S(1)} %multiply_convert_fusion, bf16[1,1024,1344]{1,2,0:T(8,128)(2,1)S(1)} %copy-done), kind=kOutput, calls=%fused_computation.19 | convolution fusion | flops 2114715648 | bytes 6389760 | tf_op jit(solution)/shard_map/dot_general | solution.py:69
  124.9 6.8 %fusion.9 = bf16[768,1024]{1,0:T(8,128)(2,1)} fusion(bf16[1,1344,1024]{2,1,0:T(8,128)(2,1)} %param.13, f32[768,1344]{0,1:T(8,128)} %convolution_maximum_fusion), kind=kOutput, calls=%fused_computation.20 | convolution fusion | flops 2116780032 | bytes 8454144 | tf_op jit(solution)/shard_map/dot_general | solution.py:52
  131.8 6.0 %convolution_convert_fusion = bf16[1024,1344]{0,1:T(8,128)(2,1)} fusion(bf16[768,1344]{0,1:T(8,128)(2,1)} %copy-done.2, bf16[768,1024]{1,0:T(8,128)(2,1)} %bitcast.4), kind=kOutput, calls=%fused_computation.9 | convolution fusion | flops 2115305472 | bytes 6389760 | tf_op jit(solution)/shard_map/dot_general | solution.py:72
  137.9 6.6 %convolution_convert_fusion.1 = bf16[1344,1024]{1,0:T(8,128)(2,1)} fusion(bf16[768,1024]{1,0:T(8,128)(2,1)} %bitcast.10, f32[768,1344]{0,1:T(8,128)} %convolution_maximum_fusion), kind=kOutput, calls=%fused_computation.10 | convolution fusion | flops 2117369856 | bytes 8454144 | tf_op jit(solution)/shard_map/dot_general | solution.py:73
  144.5 3.5 %all-to-all-start.3 = ((bf16[4,192,512]{2,1,0:T(8,128)(2,1)}), bf16[4,192,512]{2,1,0:T(8,128)(2,1)S(1)}, u32[]{:S(2)}, u32[]{:S(2)}) async-start(bf16[4,192,512]{2,1,0:T(8,128)(2,1)} %bitcast.60), calls=%async_computation.5 | async-start | bytes 1572864 | tf_op jit(solution)/shard_map/all_to_all | solution.py:97
  148.1 19.6 %all-to-all-done.3 = bf16[4,192,512]{2,1,0:T(8,128)(2,1)S(1)} async-done(((bf16[4,192,512]{2,1,0:T(8,128)(2,1)}), bf16[4,192,512]{2,1,0:T(8,128)(2,1)S(1)}, u32[]{:S(2)}, u32[]{:S(2)}) %all-to-all-start.3) | async-done | bytes 786464 | tf_op jit(solution)/shard_map/all_to_all | solution.py:97
  168.5 3.5 %all-to-all-start.1 = ((bf16[4,192,512]{2,1,0:T(8,128)(2,1)}), bf16[4,192,512]{2,1,0:T(8,128)(2,1)S(1)}, u32[]{:S(2)}, u32[]{:S(2)}) async-start(bf16[4,192,512]{2,1,0:T(8,128)(2,1)} %bitcast.59), calls=%async_computation.2 | async-start | bytes 1572864 | tf_op jit(solution)/shard_map/all_to_all | solution.py:80
  172.8 3.9 %gather_fusion.4 = bf16[512,512]{1,0:T(8,128)(2,1)} fusion(bf16[768,512]{1,0:T(8,128)(2,1)} %bitcast.56, s32[1024]{0:T(1024)S(1)} %pad_clamp_fusion.1), kind=kCustom, calls=%fused_computation.4 | custom fusion | bytes 1050624 | tf_op jit(solution)/shard_map/gather | solution.py:104
  176.7 2.0 gather.28
  178.7 3.1 %reduce_sum.45 = bf16[256,512]{1,0:T(8,128)(2,1)} reduce(bf16[256,2,512]{2,1,0:T(2,128)(2,1)} %gather.28, bf16[]{:T(256)} %constant.37.clone.1), dimensions={1}, to_apply=%region_8.9 | reduce | flops 131072 | bytes 786434 | tf_op jit(solution)/shard_map/reduce_sum | solution.py:105
  181.8 2.4 all_gather.7
  185.2 6.3 %all-to-all-done.1 = bf16[4,192,512]{2,1,0:T(8,128)(2,1)S(1)} async-done(((bf16[4,192,512]{2,1,0:T(8,128)(2,1)}), bf16[4,192,512]{2,1,0:T(8,128)(2,1)S(1)}, u32[]{:S(2)}, u32[]{:S(2)}) %all-to-all-start.1) | async-done | bytes 786464 | tf_op jit(solution)/shard_map/all_to_all | solution.py:80
  191.6 2.6 %gather_fusion.1 = bf16[512,512]{1,0:T(8,128)(2,1)} fusion(bf16[768,512]{1,0:T(8,128)(2,1)S(1)} %bitcast.55, s32[1024]{0:T(1024)S(1)} %pad_clamp_fusion.1), kind=kCustom, calls=%fused_computation.1 | custom fusion | bytes 1050624 | tf_op jit(solution)/shard_map/gather | solution.py:87
  194.2 2.7 %reshape.109 = f32[256,2,512]{2,1,0:T(2,128)} reshape(bf16[512,512]{1,0:T(8,128)(2,1)} %gather_fusion.1) | data formatting | bytes 1572864 | tf_op jit(solution)/shard_map/convert_element_type | solution.py:87
  196.8 2.6 %multiply_reduce_fusion = bf16[256,512]{1,0:T(8,128)(2,1)S(1)} fusion(f32[256,2,512]{2,1,0:T(2,128)} %reshape.109, f32[256,2]{1,0:T(8,128)} %mul.53), kind=kLoop, calls=%fused_computation.21 | loop fusion | flops 393216 | bytes 1312768 | tf_op jit(solution)/shard_map/reduce_sum | solution.py:88
  199.5 2.2 all_gather.6
  202.7 2.3 bitcast_convert_fusion.1
  205.0 29.1 %reduce-scatter.11.cloned.1.call-done = bf16[1344,256]{1,0:T(8,128)(2,1)} async-done(((bf16[1344,1024]{1,0:T(8,128)(2,1)}), bf16[1344,256]{1,0:T(8,128)(2,1)}) %reduce-scatter.11.cloned.1.call-update) | async-done | bytes 688144 | tf_op jit(solution)/shard_map/reduce_scatter | solution.py:112
  234.1 2.3 bitcast_convert_fusion
  (42 shorter events, 10.3 us)
Async XLA Ops:
  7.2 69.9 %copy-start = (bf16[1,1024,1344]{1,2,0:T(8,128)(2,1)S(1)}, bf16[1,1024,1344]{1,2,0:T(8,128)(2,1)}, u32[]{:S(2)}) copy-start(bf16[1,1024,1344]{1,2,0:T(8,128)(2,1)} %param.12) | copy-start | bytes 8257540
  29.3 43.4 %all-to-all-start = ((bf16[4,192,1024]{2,1,0:T(8,128)(2,1)}), bf16[4,192,1024]{2,1,0:T(8,128)(2,1)}, u32[]{:S(2)}, u32[]{:S(2)}) async-start(bf16[4,192,1024]{2,1,0:T(8,128)(2,1)} %select_convert_fusion), calls=%async_computation | async-start | bytes 3145728 | tf_op jit(solution)/shard_map/all_to_all | solution.py:39
  72.7 40.9 %all-to-all-start.2 = ((bf16[4,192,1024]{2,1,0:T(8,128)(2,1)}), bf16[4,192,1024]{2,1,0:T(8,128)(2,1)}, u32[]{:S(2)}, u32[]{:S(2)}) async-start(bf16[4,192,1024]{2,1,0:T(8,128)(2,1)} %multiply_convert_fusion.2), calls=%async_computation.3 | async-start | bytes 3145728 | tf_op jit(solution)/shard_map/all_to_all | solution.py:55
  77.1 67.5 %reduce-scatter.7.cloned.1.call-start = ((), (), s32[]{:S(2)}) async-start(), calls=%async_computation.9 | async-start | bytes 2359296 | tf_op jit(solution)/shard_map/reduce_scatter | solution.py:94
  119.4 1.4 copy-start.2
  124.6 23.4 %reduce-scatter.5.cloned.1.call-start = ((), (), s32[]{:S(2)}) async-start(), calls=%async_computation.8 | async-start | bytes 2359296 | tf_op jit(solution)/shard_map/reduce_scatter | solution.py:76
  131.7 71.0 %reduce-scatter.9.cloned.1.call-start = ((), (), s32[]{:S(2)}) async-start(), calls=%async_computation.10 | async-start | bytes 3440640 | tf_op jit(solution)/shard_map/reduce_scatter | solution.py:109
  137.9 96.2 %reduce-scatter.11.cloned.1.call-start = ((), (), s32[]{:S(2)}) async-start(), calls=%async_computation.11 | async-start | bytes 3440640 | tf_op jit(solution)/shard_map/reduce_scatter | solution.py:112
  144.5 23.1 %all-to-all-start.3 = ((bf16[4,192,512]{2,1,0:T(8,128)(2,1)}), bf16[4,192,512]{2,1,0:T(8,128)(2,1)S(1)}, u32[]{:S(2)}, u32[]{:S(2)}) async-start(bf16[4,192,512]{2,1,0:T(8,128)(2,1)} %bitcast.60), calls=%async_computation.5 | async-start | bytes 1572864 | tf_op jit(solution)/shard_map/all_to_all | solution.py:97
  167.6 0.9 copy-start.1
  168.5 23.1 %all-to-all-start.1 = ((bf16[4,192,512]{2,1,0:T(8,128)(2,1)}), bf16[4,192,512]{2,1,0:T(8,128)(2,1)S(1)}, u32[]{:S(2)}, u32[]{:S(2)}) async-start(bf16[4,192,512]{2,1,0:T(8,128)(2,1)} %bitcast.59), calls=%async_computation.2 | async-start | bytes 1572864 | tf_op jit(solution)/shard_map/all_to_all | solution.py:80
Sparse Core Ops, SparseCore 0:
  124.7 8.1 reduce-scatter.6
  135.3 10.2 reduce-scatter.4
  148.6 41.8 reduce-scatter.8
  193.4 40.6 reduce-scatter.10
where the time goes:
time: 244 us; the launch traced here: 243 us
  waiting for transfers between devices  114 us (47%)
  local copies, waits for them, and re-layouts  36.3 us (15%)
  matrix products  34.8 us (14%)
  other arithmetic  21.7 us (9%)
  starting transfers between devices  18 us (7%)
  between operations  13.9 us (6%)
  blocking collectives  4.56 us (2%)
    all_to_all x1, waiting for transfers between devices, shards(): lax.all_to_all(grad_outgoing.reshape(owners, capacity, feature_width), 'e...  30.8 us
    reduce_scatter x1, waiting for transfers between devices, shards(): lax.psum_scatter(grad_outer.astype(jnp.bfloat16), 'dp', scatter_dimension...  29.1 us
    all_to_all x1, waiting for transfers between devices, shards(): lax.all_to_all(outgoing.reshape(owners, capacity, feature_width), 'expert...  27.8 us
    all_to_all x1, waiting for transfers between devices, shards(): lax.all_to_all(back_shared.reshape(owners, capacity, half_width), 'expert...  19.6 us
    dot_general x1, matrix products, shards(): jnp.dot(hidden, outer_weight, preferred_element_type=jnp.float32)  6.84 us
    dot_general x1, matrix products, shards(): lax.dot_general(hidden, grad_arrived, contract_first, preferred_element_t...  6.56 us
    all_to_all x1, starting transfers between devices, shards(): lax.all_to_all(outgoing.reshape(owners, capacity, feature_width), 'expert...  6.32 us
    all_to_all x1, waiting for transfers between devices, shards(): lax.all_to_all(shared_rows.reshape(owners, capacity, half_width), 'expert...  6.3 us
  transfers between devices with their start and end apart: 8, of which 5 were waited for; matrix products, arithmetic and copies ran while one was open for 23% of the time, Pallas kernels for 0%

commit v1 on v0

v1 whole, which is shorter than its diff:
```python
import functools

import jax
import jax.numpy as jnp
from jax import lax
from jax.experimental import pallas as pl
from jax.experimental.pallas import tpu as pltpu
from jax.sharding import PartitionSpec as P

BF16 = jnp.bfloat16
F32 = jnp.float32
ROW_TILE = 16
COLUMN_TILE = 256
VMEM_BYTES = 56 * 1024 * 1024
MATMUL = (((1,), (0,)), ((), ()))
CONTRACT_LAST = (((1,), (1,)), ((), ()))
CONTRACT_FIRST = (((0,), (0,)), ((), ()))


def mxu(a, b, dims=MATMUL):
    return lax.dot_general(a, b, dims, preferred_element_type=F32)


def shape(rows, columns, dtype=BF16):
    return jax.ShapeDtypeStruct((rows, columns), dtype)


def local(body, outs, operands, flops, name, scratch=()):
    moved = sum(x.size * x.dtype.itemsize for x in (*operands, *outs))
    return pl.pallas_call(
        body,
        out_shape=tuple(outs),
        in_specs=[pl.BlockSpec(memory_space=pltpu.VMEM)] * len(operands),
        out_specs=tuple([pl.BlockSpec(memory_space=pltpu.VMEM)] * len(outs)),
        scratch_shapes=list(scratch),
        compiler_params=pltpu.CompilerParams(vmem_limit_bytes=VMEM_BYTES),
        cost_estimate=pl.CostEstimate(flops=flops, bytes_accessed=moved, transcendentals=0),
        name=name,
    )(*operands)


def window(index, width):
    return pl.ds(pl.multiple_of(index * width, width), width)


def over_columns(width, step):
    full = width // COLUMN_TILE

    def body(i, carry):
        step(window(i, COLUMN_TILE))
        return carry

    lax.fori_loop(0, full, body, 0)
    if width % COLUMN_TILE:
        step(pl.ds(full * COLUMN_TILE, width - full * COLUMN_TILE))


def picks(meta, k, shift, capacity):
    rows = lax.broadcasted_iota(jnp.int32, (meta.shape[0], capacity), 1) + shift * capacity
    return (meta[:, k : k + 1].astype(jnp.int32) == rows).astype(F32).astype(BF16)


def route_body(owners, capacity, routes_ref, index_ref, table_ref, tokens_ref, meta_ref, own_ref, *sends):
    me, core = lax.axis_index("expert"), lax.axis_index("cuts")
    count, top = routes_ref.shape
    width = -(-owners // 128) * 128
    half = tokens_ref.shape[1] // lax.axis_size("cuts")
    routes, index = routes_ref[...], index_ref[...]
    expert_lane = lax.broadcasted_iota(jnp.int32, (count, width), 1)
    named = [routes[:, k : k + 1] == expert_lane for k in range(top)]
    onehot = sum(n.astype(F32) for n in named).astype(BF16)
    earlier = lax.broadcasted_iota(jnp.int32, (count, count), 0) > lax.broadcasted_iota(
        jnp.int32, (count, count), 1
    )
    before = mxu(earlier.astype(F32).astype(BF16), onehot)
    level = lax.broadcasted_iota(jnp.int32, (count, table_ref.shape[1]), 1)
    lane = lax.broadcasted_iota(jnp.int32, meta_ref.shape, 1)
    meta = jnp.zeros(meta_ref.shape, F32)
    for k in range(top):
        rank = jnp.sum(jnp.where(named[k], before, 0.0), axis=1, keepdims=True)
        shift = routes[:, k : k + 1] - me
        shift = jnp.where(shift < 0, shift + owners, shift)
        slot = (shift * capacity).astype(F32) + rank
        weight = jnp.sum(
            jnp.where(index[:, k : k + 1] == level, table_ref[...], 0.0), axis=1, keepdims=True
        )
        meta = jnp.where(lane == k, slot, jnp.where(lane == top + k, weight, meta))
    meta_ref[...] = meta
    wide = tokens_ref[...].astype(BF16)
    narrow = tokens_ref[:, window(core, half)].astype(BF16)
    for shift, ref in enumerate((own_ref, *sends)):
        chosen = sum(picks(meta, k, shift, capacity) for k in range(top))
        ref[...] = mxu(chosen, narrow if shift else wide, CONTRACT_FIRST).astype(BF16)


def weigh_body(top, capacity, meta_ref, cotangent_ref, own_ref, *sends):
    core = lax.axis_index("cuts")
    meta = meta_ref[...]
    half = cotangent_ref.shape[1] // lax.axis_size("cuts")

    def scaled(values):
        return [(meta[:, top + k : top + k + 1] * values).astype(BF16) for k in range(top)]

    wide, narrow = scaled(cotangent_ref[...]), scaled(cotangent_ref[:, window(core, half)])
    for shift, ref in enumerate((own_ref, *sends)):
        rows = narrow if shift else wide
        ref[...] = sum(
            mxu(picks(meta, k, shift, capacity), rows[k], CONTRACT_FIRST) for k in range(top)
        ).astype(BF16)


def assemble(full_ref, own, mine, other):
    core = lax.axis_index("cuts")
    capacity, half = mine[0].shape
    full_ref[:capacity, :] = own[...]
    for i, (a, b) in enumerate(zip(mine, other, strict=True), 1):
        rows = slice(i * capacity, (i + 1) * capacity)
        full_ref[rows, window(core, half)] = a[...]
        full_ref[rows, window(1 - core, half)] = b[...]


def forward_body(remote, own, *refs):
    mine, other = refs[:remote], refs[remote : 2 * remote]
    inner_ref, outer_ref, x_ref, positive_ref, hidden_ref, keep_ref, give_ref = refs[2 * remote :]
    core = lax.axis_index("cuts")
    assemble(x_ref, own, mine, other)

    def activate(columns):
        positive = jnp.maximum(mxu(x_ref[...], inner_ref[:, columns]), 0.0)
        positive_ref[:, columns] = positive.astype(BF16)
        hidden_ref[:, columns] = (positive * positive).astype(BF16)

    over_columns(inner_ref.shape[1], activate)
    to_halves(hidden_ref, outer_ref, MATMUL, keep_ref, give_ref)


def to_halves(rows_ref, weight_ref, dims, keep_ref, give_ref):
    core = lax.axis_index("cuts")
    half = keep_ref.shape[1]
    for owner, ref in ((1 - core, give_ref), (core, keep_ref)):

        def step(i, carry, owner=owner, ref=ref):
            features = window(owner * (half // COLUMN_TILE) + i, COLUMN_TILE)
            weight = weight_ref[:, features] if dims == MATMUL else weight_ref[features, :]
            ref[:, window(i, COLUMN_TILE)] = mxu(rows_ref[...], weight, dims).astype(BF16)
            return carry

        lax.fori_loop(0, half // COLUMN_TILE, step, 0)


def split_body(keep_ref, came_ref, *outs):
    capacity = outs[0].shape[0]
    for i, ref in enumerate(outs):
        rows = slice(i * capacity, (i + 1) * capacity)
        ref[...] = (keep_ref[rows, :].astype(F32) + came_ref[rows, :].astype(F32)).astype(BF16)


def outer_grad_body(remote, own, *refs):
    mine, other = refs[:remote], refs[remote : 2 * remote]
    hidden_ref, g_ref, *outs = refs[2 * remote :]
    me = lax.axis_index("dp")
    assemble(g_ref, own, mine, other)
    groups = len(outs) // 2
    rows = outs[0].shape[0]
    width = outs[0].shape[1]
    for k in reversed(range(groups)):
        block = g_ref[:, window(me ^ k, width)]
        for part in range(2):
            hidden = hidden_ref[:, part * rows : (part + 1) * rows]
            outs[2 * k + part][...] = mxu(hidden, block, CONTRACT_FIRST).astype(BF16)


def backward_body(g_ref, positive_ref, inner_ref, outer_ref, d_act_ref, keep_ref, give_ref):
    def step(columns):
        d_hidden = mxu(g_ref[...], outer_ref[columns, :], CONTRACT_LAST)
        d_act_ref[:, columns] = (d_hidden * 2.0 * positive_ref[:, columns].astype(F32)).astype(BF16)

    over_columns(positive_ref.shape[1], step)
    to_halves(d_act_ref, inner_ref, CONTRACT_LAST, keep_ref, give_ref)


def inner_grad_body(x_ref, d_act_ref, *outs):
    me = lax.axis_index("dp")
    groups = len(outs) // 2
    rows = outs[0].shape[0]
    for k in reversed(range(groups)):
        for part in range(2):
            block = x_ref[:, window((me ^ k) * 2 + part, rows)]
            ref = outs[2 * k + part]

            def step(columns, block=block, ref=ref):
                ref[:, columns] = mxu(block, d_act_ref[:, columns], CONTRACT_FIRST).astype(BF16)

            over_columns(d_act_ref.shape[1], step)


def combine_body(top, weighted, meta_ref, *refs):
    *chunks, wide_ref, narrow_ref = refs
    meta = meta_ref[...]
    capacity = chunks[0].shape[0]
    total = 0.0
    if weighted:
        for k in range(top):
            got = sum(mxu(picks(meta, k, s, capacity), c[...]) for s, c in enumerate(chunks))
            total += meta[:, top + k : top + k + 1] * got
    else:
        for s, c in enumerate(chunks):
            total += mxu(sum(picks(meta, k, s, capacity) for k in range(top)), c[...])
    wide_ref[...] = total
    narrow_ref[...] = total.astype(BF16)


def join_body(mine_ref, other_ref, out_ref):
    core = lax.axis_index("cuts")
    half = mine_ref.shape[1]
    out_ref[:, window(core, half)] = mine_ref[...]
    out_ref[:, window(1 - core, half)] = other_ref[...].astype(F32)


def shifted(x, axis, shift):
    size = lax.axis_size(axis)
    return lax.ppermute(x, axis, [(i, (i + shift) % size) for i in range(size)])


def partner(x, axis, bit):
    return lax.ppermute(x, axis, [(i, i ^ bit) for i in range(lax.axis_size(axis))])


def sum_over_groups(blocks, bits):
    blocks = dict(blocks)
    for at, bit in enumerate(bits):
        came = {r ^ bit: partner(blocks[r], "dp", bit) for r in sorted(blocks, reverse=True) if r & bit}
        last = at == len(bits) - 1
        blocks = {
            r: (blocks[r].astype(F32) + came[r].astype(F32)).astype(F32 if last else BF16) for r in came
        }
    return blocks[0]


def shards(tokens, cotangent, routes, combine_index, combine_table, w_in, w_out):
    owners, groups = lax.axis_size("expert"), lax.axis_size("dp")
    count, features = tokens.shape
    top = routes.shape[1]
    half = features // lax.axis_size("cuts")
    capacity = -(-max(2, 3 * count * top // (2 * owners)) // ROW_TILE) * ROW_TILE
    slots = owners * capacity
    remote = owners - 1
    inner, outer = w_in[0], w_out[0]
    units = inner.shape[1]
    bits = [1 << i for i in range(groups.bit_length() - 1)]

    def exchange(sends):
        mine = [shifted(x, "expert", s) for s, x in enumerate(sends, 1)]
        return mine, [partner(x, "cuts", 1) for x in mine]

    def give_back(keep, give):
        chunks = local(
            split_body, [shape(capacity, half)] * owners, [keep, partner(give, "cuts", 1)], 0, "split"
        )
        return [chunks[0]] + [shifted(x, "expert", -s) for s, x in enumerate(chunks[1:], 1)]

    def combine(chunks, weighted):
        wide, narrow = local(
            functools.partial(combine_body, top, weighted),
            [shape(count, half, F32), shape(count, half)],
            [meta, *chunks],
            2 * count * slots * half,
            "combine",
        )
        (out,) = local(
            join_body, [shape(count, features, F32)], [wide, partner(narrow, "cuts", 1)], 0, "join"
        )
        return out

    meta, own, *sends = local(
        functools.partial(route_body, owners, capacity),
        [shape(count, 128, F32), shape(capacity, features)] + [shape(capacity, half)] * remote,
        [routes, combine_index, combine_table[None, :], tokens],
        2 * count * slots * features,
        "route",
    )
    mine, other = exchange(sends)
    grad_own, *grad_sends = local(
        functools.partial(weigh_body, top, capacity),
        [shape(capacity, features)] + [shape(capacity, half)] * remote,
        [meta, cotangent],
        4 * count * slots * features,
        "weigh",
    )
    grad_mine, grad_other = exchange(grad_sends)
    work = 2 * slots * features * units
    arrived, positive, hidden, keep, give = local(
        functools.partial(forward_body, remote),
        [shape(slots, features), shape(slots, units), shape(slots, units)] + [shape(slots, half)] * 2,
        [own, *mine, *other, inner, outer],
        2 * work,
        "forward",
    )
    returned = give_back(keep, give)
    grad_rows, *outer_parts = local(
        functools.partial(outer_grad_body, remote),
        [shape(slots, features)] + [shape(units // 2, features // groups)] * (2 * groups),
        [grad_own, *grad_mine, *grad_other, hidden],
        work,
        "outer_grad",
    )
    outer_sums = [
        sum_over_groups({r: outer_parts[2 * r + part] for r in range(groups)}, order)
        for part, order in enumerate((bits, bits[::-1]))
    ]
    d_act, grad_keep, grad_give = local(
        backward_body,
        [shape(slots, units)] + [shape(slots, half)] * 2,
        [grad_rows, positive, inner, outer],
        2 * work,
        "backward",
    )
    grad_returned = give_back(grad_keep, grad_give)
    inner_parts = local(
        inner_grad_body,
        [shape(features // groups // 2, units)] * (2 * groups),
        [arrived, d_act],
        work,
        "inner_grad",
    )
    inner_sums = [
        sum_over_groups({r: inner_parts[2 * r + part] for r in range(groups)}, order)
        for part, order in enumerate((bits, bits[::-1]))
    ]
    layer_out = combine(returned, True)
    d_tokens = combine(grad_returned, False)
    grad_in = jnp.concatenate(inner_sums, axis=0)[None]
    grad_out = jnp.concatenate(outer_sums, axis=0)[None]
    return (layer_out, d_tokens, grad_in, grad_out)


def solution(mesh):
    in_specs = (
        P(("expert", "dp"), None),
        P(("expert", "dp"), None),
        P(("expert", "dp"), None),
        P(("expert", "dp"), None),
        P(),
        P("expert", None, "cuts"),
        P("expert", "cuts", None),
    )
    out_specs = (
        P(("expert", "dp"), None),
        P(("expert", "dp"), None),
        P("expert", "dp", "cuts"),
        P("expert", "cuts", "dp"),
    )
    return jax.shard_map(shards, mesh=mesh, in_specs=in_specs, out_specs=out_specs, check_vma=False)
```

time: 244 us -> 201 us (0.82)
  Pallas kernels: 0 us -> 68.9 us
  waiting for transfers between devices: 114 us -> 70.4 us
  matrix products: 34.8 us -> 0 us
  local copies, waits for them, and re-layouts: 36.3 us -> 11.1 us
  starting transfers between devices: 18 us -> 41 us
  other arithmetic: 21.7 us -> 7.78 us
  between operations: 13.9 us -> 0.85 us
  blocking collectives: 4.56 us -> 0 us
    all_to_all x4 -> x0, waiting for transfers between devices: 84.4 us -> none  [the longest x1 30.8 us: shards(): lax.all_to_all(grad_outgoing.reshape(owners, capacity, feature_width), 'e...]
    ppermute x0 -> x34, waiting for transfers between devices: none -> 70.4 us  [the longest x12 36.8 us: shifted(): return lax.ppermute(x, axis, [(i, (i + shift) % size) for i in range(size)])]
    pallas_call x0 -> x12, Pallas kernels: none -> 68.9 us  [local(): pl.pallas_call(body, out_shape=tuple(outs), in_specs=[pl.BlockSpec(memory...]
    ppermute x0 -> x34, starting transfers between devices: none -> 41 us  [the longest x12 23.6 us: shifted(): return lax.ppermute(x, axis, [(i, (i + shift) % size) for i in range(size)])]
    dot_general x6 -> x0, matrix products: 34.8 us -> none  [the longest x1 6.84 us: shards(): jnp.dot(hidden, outer_weight, preferred_element_type=jnp.float32)]
    reduce_scatter x4 -> x0, waiting for transfers between devices: 29.1 us -> none  [the longest x1 29.1 us: shards(): lax.psum_scatter(grad_outer.astype(jnp.bfloat16), 'dp', scatter_dimension...]
    gather x6 -> x0, local copies, waits for them, and re-layouts: 25.2 us -> none  [the longest x2 5.91 us: shards(): back_rows.reshape(owners * capacity, half_width)[slot_index]]
    all_to_all x4 -> x0, starting transfers between devices: 17.7 us -> none  [the longest x1 6.32 us: shards(): lax.all_to_all(outgoing.reshape(owners, capacity, feature_width), 'expert...]
  transfers between devices with their start and end apart: 8 -> 34, of which waited for: 5 -> 12; matrix products, arithmetic and copies ran while one was open for 23% -> 6% of each run, Pallas kernels for 0% -> 14%
where the time goes in v1:
time: 201 us; the launch traced here: 200 us
  waiting for transfers between devices  70.4 us (35%)
  Pallas kernels  68.9 us (34%)
  starting transfers between devices  41 us (20%)
  local copies, waits for them, and re-layouts  11.1 us (6%)
  other arithmetic  7.78 us (4%)
    pallas_call x12, Pallas kernels, local(): pl.pallas_call(body, out_shape=tuple(outs), in_specs=[pl.BlockSpec(memory...  68.9 us
    ppermute x12, waiting for transfers between devices, shifted(): return lax.ppermute(x, axis, [(i, (i + shift) % size) for i in range(size)])  36.8 us
    ppermute x22, waiting for transfers between devices, partner(): lax.ppermute(x, axis, [(i, i ^ bit) for i in range(lax.axis_size(axis))])  33.5 us
    ppermute x12, starting transfers between devices, shifted(): return lax.ppermute(x, axis, [(i, (i + shift) % size) for i in range(size)])  23.6 us
    ppermute x22, starting transfers between devices, partner(): lax.ppermute(x, axis, [(i, i ^ bit) for i in range(lax.axis_size(axis))])  17.4 us
    unnamed x64, local copies, waits for them, and re-layouts  11.1 us
  transfers between devices with their start and end apart: 34, of which 12 were waited for; matrix products, arithmetic and copies ran while one was open for 6% of the time, Pallas kernels for 14%

profile of v1, /device:TPU:0, one launch (start us, length us, event | category | flops | bytes accessed | tf_op | source)
XLA Modules:
  0.0 200.0 jit_solution(17857236364262995341)
XLA Ops:
  3.6 3.5 %route.1 = (f32[256,128]{1,0:T(8,128)}, bf16[192,1024]{1,0:T(8,128)(2,1)}, bf16[192,512]{1,0:T(8,128)(2,1)}, bf16[192,512]{1,0:T(8,128)(2,1)}, bf16[192,512]{1,0:T(8,128)(2,1)}) custom-call(s32[256,2]{1,0:T(8,128)} %copy.11.routes_ref, s32[256,2]{1,0:T(8,128)} %copy.12.index_ref, f32[1,256]{1,0:T(1,128)} %bitcast.11, f32[256,1024]{1,0:T(8,128)} %tokens_ref.1), custom_call_target="tpu_custom_call" | custom-call | flops 402653184 | bytes 2167808 | tf_op jit(solution)/shard_map/route/pallas_call | solution.py:30
  7.0 3.0 %collective-permute-start = (bf16[192,512]{1,0:T(8,128)(2,1)}, bf16[192,512]{1,0:T(8,128)(2,1)S(1)}, u32[]{:S(2)}, u32[]{:S(2)}) collective-permute-start(bf16[192,512]{1,0:T(8,128)(2,1)} %get-tuple-element.52), channel_id=1, source_target_pairs={{0,8},{8,16},{16,24},{24,0},{1,9},{9,17},{17,25},{25,1},{2,10},{10... | collective-permute-start | bytes 589832 | tf_op jit(solution)/shard_map/ppermute | solution.py:222
  10.1 2.6 %collective-permute-start.1 = (bf16[192,512]{1,0:T(8,128)(2,1)}, bf16[192,512]{1,0:T(8,128)(2,1)}, u32[]{:S(2)}, u32[]{:S(2)}) collective-permute-start(bf16[192,512]{1,0:T(8,128)(2,1)} %get-tuple-element.53), channel_id=1, source_target_pairs={{0,16},{8,24},{16,0},{24,8},{1,17},{9,25},{17,1},{25,9},{2,18},{10... | collective-permute-start | bytes 589832 | tf_op jit(solution)/shard_map/ppermute | solution.py:222
  14.0 3.1 %weigh.1 = (bf16[192,1024]{1,0:T(8,128)(2,1)}, bf16[192,512]{1,0:T(8,128)(2,1)}, bf16[192,512]{1,0:T(8,128)(2,1)}, bf16[192,512]{1,0:T(8,128)(2,1)}) custom-call(f32[256,128]{1,0:T(8,128)} %get-tuple-element.50.meta_ref, f32[256,1024]{1,0:T(8,128)} %cotangent_ref.1), custom_call_target="tpu_custom_call" | custom-call | flops 805306368 | bytes 2162688 | tf_op jit(solution)/shard_map/weigh/pallas_call | solution.py:30
  18.2 3.0 %collective-permute-start.13 = (bf16[192,512]{1,0:T(8,128)(2,1)}, bf16[192,512]{1,0:T(8,128)(2,1)S(1)}, u32[]{:S(2)}, u32[]{:S(2)}) collective-permute-start(bf16[192,512]{1,0:T(8,128)(2,1)} %get-tuple-element.66), channel_id=1, source_target_pairs={{0,24},{8,0},{16,8},{24,16},{1,25},{9,1},{17,9},{25,17},{2,26},{10... | collective-permute-start | bytes 589832 | tf_op jit(solution)/shard_map/ppermute | solution.py:222
  21.2 5.6 %collective-permute-done.1.refs_1_ = bf16[192,512]{1,0:T(8,128)(2,1)} collective-permute-done((bf16[192,512]{1,0:T(8,128)(2,1)}, bf16[192,512]{1,0:T(8,128)(2,1)}, u32[]{:S(2)}, u32[]{:S(2)}) %collective-permute-start.1) | collective-permute-done | bytes 196640 | tf_op jit(solution)/shard_map/ppermute | solution.py:222
  27.3 3.6 %collective-permute-done.11.refs_0_ = bf16[192,512]{1,0:T(8,128)(2,1)S(1)} collective-permute-done((bf16[192,512]{1,0:T(8,128)(2,1)}, bf16[192,512]{1,0:T(8,128)(2,1)S(1)}, u32[]{:S(2)}, u32[]{:S(2)}) %collective-permute-start.11) | collective-permute-done | bytes 196640 | tf_op jit(solution)/shard_map/ppermute | solution.py:222
  30.9 2.9 %copy.13 = bf16[1,1024,1344]{2,1,0:T(8,128)(2,1)} copy(bf16[1,1024,1344]{1,2,0:T(8,128)(2,1)S(1)} %copy-done) | data formatting | bytes 5505024 | tf_op args[5]
  33.7 8.9 %collective-permute-done.12.refs_1_ = bf16[192,512]{1,0:T(8,128)(2,1)S(1)} collective-permute-done((bf16[192,512]{1,0:T(8,128)(2,1)}, bf16[192,512]{1,0:T(8,128)(2,1)S(1)}, u32[]{:S(2)}, u32[]{:S(2)}) %collective-permute-start.12) | collective-permute-done | bytes 196640 | tf_op jit(solution)/shard_map/ppermute | solution.py:222
  43.3 12.3 %forward.1 = (bf16[768,1024]{1,0:T(8,128)(2,1)}, bf16[768,1344]{1,0:T(8,128)(2,1)}, bf16[768,1344]{1,0:T(8,128)(2,1)}, bf16[768,512]{1,0:T(8,128)(2,1)}, bf16[768,512]{1,0:T(8,128)(2,1)}) custom-call(bf16[192,1024]{1,0:T(8,128)(2,1)} %get-tuple-element.51.own, bf16[192,512]{1,0:T(8,128)(2,1)} %copy-done.23, bf16[192,512]{1,0:T(8,128)(2,1)} %collective-permute-done.1.refs_1_, ...), custom_call_target="tpu_custom_call" | custom-call | flops 4227858432 | bytes 14352384 | tf_op jit(solution)/shard_map/forward/pallas_call | solution.py:30
  56.4 8.1 %outer_grad.1 = (bf16[768,1024]{1,0:T(8,128)(2,1)}, bf16[672,256]{1,0:T(8,128)(2,1)}, bf16[672,256]{1,0:T(8,128)(2,1)}, bf16[672,256]{1,0:T(8,128)(2,1)}, bf16[6...) custom-call(bf16[192,1024]{1,0:T(8,128)(2,1)} %get-tuple-element.63., ...), custom_call_target="tpu_custom_call" | custom-call | flops 2113929216 | bytes 7962624 | tf_op jit(solution)/shard_map/outer_grad/pallas_call | solution.py:30
  64.5 11.7 %backward.1 = (bf16[768,1344]{1,0:T(8,128)(2,1)}, bf16[768,512]{1,0:T(8,128)(2,1)}, bf16[768,512]{1,0:T(8,128)(2,1)}) custom-call(bf16[768,1024]{1,0:T(8,128)(2,1)} %get-tuple-element.68.g_ref, bf16[768,1344]{1,0:T(8,128)(2,1)} %get-tuple-element.69.positive_ref, bf16[1024,1344]{1,0:T(8,128)(2,1)} %bitcast.8, bf16[1344,1024]{1,0:T(8,128)(2,1)} %bitcast.10), custom_call_target="tpu_custom_call" | custom-call | flops 4227858432 | bytes 12779520 | tf_op jit(solution)/shard_map/backward/pallas_call | solution.py:30
  76.2 15.7 %inner_grad.1 = (bf16[128,1344]{1,0:T(8,128)(2,1)}, bf16[128,1344]{1,0:T(8,128)(2,1)}, bf16[128,1344]{1,0:T(8,128)(2,1)}, bf16[128,1344]{1,0:T(8,128)(2,1)}, bf1...) custom-call(bf16[768,1024]{1,0:T(8,128)(2,1)} %get-tuple-element.78.x, ...), custom_call_target="tpu_custom_call" | custom-call | flops 2113929216 | bytes 6389760 | tf_op jit(solution)/shard_map/inner_grad/pallas_call | solution.py:30
  97.2 6.2 %collective-permute-done.23 = bf16[128,1344]{1,0:T(8,128)(2,1)S(1)} collective-permute-done((bf16[128,1344]{1,0:T(8,128)(2,1)}, bf16[128,1344]{1,0:T(8,128)(2,1)S(1)}, u32[]{:S(2)}, u32[]{:S(2)}) %collective-permute-start.23) | collective-permute-done | bytes 344096 | tf_op jit(solution)/shard_map/ppermute | solution.py:226
  106.0 7.1 %collective-permute-done.26 = bf16[128,1344]{1,0:T(8,128)(2,1)S(1)} collective-permute-done((bf16[128,1344]{1,0:T(8,128)(2,1)}, bf16[128,1344]{1,0:T(8,128)(2,1)S(1)}, u32[]{:S(2)}, u32[]{:S(2)}) %collective-permute-start.26) | collective-permute-done | bytes 344096 | tf_op jit(solution)/shard_map/ppermute | solution.py:226
  115.8 2.4 %collective-permute-done.29 = bf16[672,256]{1,0:T(8,128)(2,1)S(1)} collective-permute-done((bf16[672,256]{1,0:T(8,128)(2,1)S(1)}, bf16[672,256]{1,0:T(8,128)(2,1)S(1)}, u32[]{:S(2)}, u32[]{:S(2)}) %collective-permute-start.29) | collective-permute-done | bytes 344096 | tf_op jit(solution)/shard_map/ppermute | solution.py:226
  121.8 3.6 %collective-permute-done.22 = bf16[128,1344]{1,0:T(8,128)(2,1)S(1)} collective-permute-done((bf16[128,1344]{1,0:T(8,128)(2,1)}, bf16[128,1344]{1,0:T(8,128)(2,1)S(1)}, u32[]{:S(2)}, u32[]{:S(2)}) %collective-permute-start.22) | collective-permute-done | bytes 344096 | tf_op jit(solution)/shard_map/ppermute | solution.py:226
  126.9 2.6 %collective-permute-done.24 = bf16[128,1344]{1,0:T(8,128)(2,1)S(1)} collective-permute-done((bf16[128,1344]{1,0:T(8,128)(2,1)S(1)}, bf16[128,1344]{1,0:T(8,128)(2,1)S(1)}, u32[]{:S(2)}, u32[]{:S(2)}) %collective-permute-start.24) | collective-permute-done | bytes 344096 | tf_op jit(solution)/shard_map/ppermute | solution.py:226
  131.1 11.6 %collective-permute-done.25 = bf16[128,1344]{1,0:T(8,128)(2,1)S(1)} collective-permute-done((bf16[128,1344]{1,0:T(8,128)(2,1)S(1)}, bf16[128,1344]{1,0:T(8,128)(2,1)S(1)}, u32[]{:S(2)}, u32[]{:S(2)}) %collective-permute-start.25) | collective-permute-done | bytes 344096 | tf_op jit(solution)/shard_map/ppermute | solution.py:226
  144.4 1.6 collective-permute-start.33
  147.6 2.4 %split.2 = (bf16[192,512]{1,0:T(8,128)(2,1)}, bf16[192,512]{1,0:T(8,128)(2,1)}, bf16[192,512]{1,0:T(8,128)(2,1)}, bf16[192,512]{1,0:T(8,128)(2,1)}) custom-call(bf16[768,512]{1,0:T(8,128)(2,1)} %get-tuple-element.55.keep_ref, bf16[768,512]{1,0:T(8,128)(2,1)} %copy-done.1), custom_call_target="tpu_custom_call" | custom-call | bytes 2359296 | tf_op jit(solution)/shard_map/split/pallas_call | solution.py:30
  150.0 5.7 %collective-permute-start.7 = (bf16[192,512]{1,0:T(8,128)(2,1)}, bf16[192,512]{1,0:T(8,128)(2,1)S(1)}, u32[]{:S(2)}, u32[]{:S(2)}) collective-permute-start(bf16[192,512]{1,0:T(8,128)(2,1)} %get-tuple-element.58), channel_id=1, source_target_pairs={{0,24},{8,0},{16,8},{24,16},{1,25},{9,1},{17,9},{25,17},{2,26},{10... | collective-permute-start | bytes 589832 | tf_op jit(solution)/shard_map/ppermute | solution.py:222
  156.8 2.5 %collective-permute-start.8 = (bf16[192,512]{1,0:T(8,128)(2,1)S(1)}, bf16[192,512]{1,0:T(8,128)(2,1)S(1)}, u32[]{:S(2)}, u32[]{:S(2)}) collective-permute-start(bf16[192,512]{1,0:T(8,128)(2,1)S(1)} %copy-done.26), channel_id=1, source_target_pairs={{0,16},{8,24},{16,0},{24,8},{1,17},{9,25},{17,1},{25,9},{2,18},{10... | collective-permute-start | bytes 589832 | tf_op jit(solution)/shard_map/ppermute | solution.py:222
  159.3 1.7 collective-permute-start.9
  161.0 2.3 %split.3 = (bf16[192,512]{1,0:T(8,128)(2,1)}, bf16[192,512]{1,0:T(8,128)(2,1)}, bf16[192,512]{1,0:T(8,128)(2,1)}, bf16[192,512]{1,0:T(8,128)(2,1)}) custom-call(bf16[768,512]{1,0:T(8,128)(2,1)} %get-tuple-element.70.keep_ref, bf16[768,512]{1,0:T(8,128)(2,1)} %copy-done.2), custom_call_target="tpu_custom_call" | custom-call | bytes 2359296 | tf_op jit(solution)/shard_map/split/pallas_call | solution.py:30
  163.3 2.1 %collective-permute-start.18 = (bf16[192,512]{1,0:T(8,128)(2,1)}, bf16[192,512]{1,0:T(8,128)(2,1)S(1)}, u32[]{:S(2)}, u32[]{:S(2)}) collective-permute-start(bf16[192,512]{1,0:T(8,128)(2,1)} %get-tuple-element.73), channel_id=1, source_target_pairs={{0,24},{8,0},{16,8},{24,16},{1,25},{9,1},{17,9},{25,17},{2,26},{10... | collective-permute-start | bytes 589832 | tf_op jit(solution)/shard_map/ppermute | solution.py:222
  167.3 15.1 %collective-permute-done.8.refs_2_ = bf16[192,512]{1,0:T(8,128)(2,1)S(1)} collective-permute-done((bf16[192,512]{1,0:T(8,128)(2,1)S(1)}, bf16[192,512]{1,0:T(8,128)(2,1)S(1)}, u32[]{:S(2)}, u32[]{:S(2)}) %collective-permute-start.8) | collective-permute-done | bytes 196640 | tf_op jit(solution)/shard_map/ppermute | solution.py:222
  183.2 2.9 %combine.2 = (f32[256,512]{1,0:T(8,128)}, bf16[256,512]{1,0:T(8,128)(2,1)}) custom-call(f32[256,128]{1,0:T(8,128)} %get-tuple-element.50.meta_ref, bf16[192,512]{1,0:T(8,128)(2,1)} %get-tuple-element.57.refs_0_, bf16[192,512]{1,0:T(8,128)(2,1)} %copy-done.11, bf16[192,512]{1,0:T(8,128)(2,1)} %copy-done.12, bf16[192,512]{1,0:T(8,128)(2,1)} %copy-done.14), custom_call_target="tpu_custom_call" | custom-call | flops 201326592 | bytes 1703936 | tf_op jit(solution)/shard_map/combine/pallas_call | solution.py:30
  186.1 3.6 %collective-permute-done.19.refs_2_ = bf16[192,512]{1,0:T(8,128)(2,1)S(1)} collective-permute-done((bf16[192,512]{1,0:T(8,128)(2,1)}, bf16[192,512]{1,0:T(8,128)(2,1)S(1)}, u32[]{:S(2)}, u32[]{:S(2)}) %collective-permute-start.19) | collective-permute-done | bytes 196640 | tf_op jit(solution)/shard_map/ppermute | solution.py:222
  190.4 2.7 %combine.3 = (f32[256,512]{1,0:T(8,128)}, bf16[256,512]{1,0:T(8,128)(2,1)}) custom-call(f32[256,128]{1,0:T(8,128)} %get-tuple-element.50.meta_ref, bf16[192,512]{1,0:T(8,128)(2,1)} %get-tuple-element.72.refs_0_, bf16[192,512]{1,0:T(8,128)(2,1)} %copy-done.13, bf16[192,512]{1,0:T(8,128)(2,1)} %copy-done.15, bf16[192,512]{1,0:T(8,128)(2,1)} %copy-done.16), custom_call_target="tpu_custom_call" | custom-call | flops 201326592 | bytes 1703936 | tf_op jit(solution)/shard_map/combine/pallas_call | solution.py:30
  195.0 2.2 %join.2 = f32[256,1024]{1,0:T(8,128)} custom-call(f32[256,512]{1,0:T(8,128)} %get-tuple-element.61.mine_ref, bf16[256,512]{1,0:T(8,128)(2,1)} %copy-done.9), custom_call_target="tpu_custom_call" | custom-call | bytes 1835008 | tf_op jit(solution)/shard_map/join/pallas_call | solution.py:30
  197.9 2.2 %join.3 = f32[256,1024]{1,0:T(8,128)} custom-call(f32[256,512]{1,0:T(8,128)} %get-tuple-element.76.mine_ref, bf16[256,512]{1,0:T(8,128)(2,1)} %copy-done.10), custom_call_target="tpu_custom_call" | custom-call | bytes 1835008 | tf_op jit(solution)/shard_map/join/pallas_call | solution.py:30
  (122 shorter events, 34.9 us)
Async XLA Ops:
  7.0 11.1 %collective-permute-start = (bf16[192,512]{1,0:T(8,128)(2,1)}, bf16[192,512]{1,0:T(8,128)(2,1)S(1)}, u32[]{:S(2)}, u32[]{:S(2)}) collective-permute-start(bf16[192,512]{1,0:T(8,128)(2,1)} %get-tuple-element.52), channel_id=1, source_target_pairs={{0,8},{8,16},{16,24},{24,0},{1,9},{9,17},{17,25},{25,1},{2,10},{10... | collective-permute-start | bytes 589832 | tf_op jit(solution)/shard_map/ppermute | solution.py:222
  10.1 16.7 %collective-permute-start.1 = (bf16[192,512]{1,0:T(8,128)(2,1)}, bf16[192,512]{1,0:T(8,128)(2,1)}, u32[]{:S(2)}, u32[]{:S(2)}) collective-permute-start(bf16[192,512]{1,0:T(8,128)(2,1)} %get-tuple-element.53), channel_id=1, source_target_pairs={{0,16},{8,24},{16,0},{24,8},{1,17},{9,25},{17,1},{25,9},{2,18},{10... | collective-permute-start | bytes 589832 | tf_op jit(solution)/shard_map/ppermute | solution.py:222
  12.7 14.1 %collective-permute-start.2 = (bf16[192,512]{1,0:T(8,128)(2,1)}, bf16[192,512]{1,0:T(8,128)(2,1)}, u32[]{:S(2)}, u32[]{:S(2)}) collective-permute-start(bf16[192,512]{1,0:T(8,128)(2,1)} %get-tuple-element.54), channel_id=1, source_target_pairs={{0,24},{8,0},{16,8},{24,16},{1,25},{9,1},{17,9},{25,17},{2,26},{10... | collective-permute-start | bytes 589832 | tf_op jit(solution)/shard_map/ppermute | solution.py:222
  17.1 13.8 %collective-permute-start.11 = (bf16[192,512]{1,0:T(8,128)(2,1)}, bf16[192,512]{1,0:T(8,128)(2,1)S(1)}, u32[]{:S(2)}, u32[]{:S(2)}) collective-permute-start(bf16[192,512]{1,0:T(8,128)(2,1)} %get-tuple-element.64), channel_id=1, source_target_pairs={{0,8},{8,16},{16,24},{24,0},{1,9},{9,17},{17,25},{25,1},{2,10},{10... | collective-permute-start | bytes 589832 | tf_op jit(solution)/shard_map/ppermute | solution.py:222
  17.8 24.9 %collective-permute-start.12 = (bf16[192,512]{1,0:T(8,128)(2,1)}, bf16[192,512]{1,0:T(8,128)(2,1)S(1)}, u32[]{:S(2)}, u32[]{:S(2)}) collective-permute-start(bf16[192,512]{1,0:T(8,128)(2,1)} %get-tuple-element.65), channel_id=1, source_target_pairs={{0,16},{8,24},{16,0},{24,8},{1,17},{9,25},{17,1},{25,9},{2,18},{10... | collective-permute-start | bytes 589832 | tf_op jit(solution)/shard_map/ppermute | solution.py:222
  18.2 24.5 %collective-permute-start.13 = (bf16[192,512]{1,0:T(8,128)(2,1)}, bf16[192,512]{1,0:T(8,128)(2,1)S(1)}, u32[]{:S(2)}, u32[]{:S(2)}) collective-permute-start(bf16[192,512]{1,0:T(8,128)(2,1)} %get-tuple-element.66), channel_id=1, source_target_pairs={{0,24},{8,0},{16,8},{24,16},{1,25},{9,1},{17,9},{25,17},{2,26},{10... | collective-permute-start | bytes 589832 | tf_op jit(solution)/shard_map/ppermute | solution.py:222
  26.7 16.4 %collective-permute-start.3 = (bf16[192,512]{1,0:T(8,128)(2,1)S(1)}, bf16[192,512]{1,0:T(8,128)(2,1)}, u32[]{:S(2)}, u32[]{:S(2)}) collective-permute-start(bf16[192,512]{1,0:T(8,128)(2,1)S(1)} %collective-permute-done.refs_0_), channel_id=1, source_target_pairs={{0,4},{4,0},{1,5},{5,1},{2,6},{6,2},{3,7},{7,3},{8,12},{12,8},{9,1... | collective-permute-start | bytes 589832 | tf_op jit(solution)/shard_map/ppermute | solution.py:226
  26.7 16.5 %collective-permute-start.4 = (bf16[192,512]{1,0:T(8,128)(2,1)}, bf16[192,512]{1,0:T(8,128)(2,1)}, u32[]{:S(2)}, u32[]{:S(2)}) collective-permute-start(bf16[192,512]{1,0:T(8,128)(2,1)} %collective-permute-done.1.refs_1_), channel_id=1, source_target_pairs={{0,4},{4,0},{1,5},{5,1},{2,6},{6,2},{3,7},{7,3},{8,12},{12,8},{9,1... | collective-permute-start | bytes 589832 | tf_op jit(solution)/shard_map/ppermute | solution.py:226
  30.8 12.4 %collective-permute-start.5 = (bf16[192,512]{1,0:T(8,128)(2,1)}, bf16[192,512]{1,0:T(8,128)(2,1)}, u32[]{:S(2)}, u32[]{:S(2)}) collective-permute-start(bf16[192,512]{1,0:T(8,128)(2,1)} %collective-permute-done.2.refs_2_), channel_id=1, source_target_pairs={{0,4},{4,0},{1,5},{5,1},{2,6},{6,2},{3,7},{7,3},{8,12},{12,8},{9,1... | collective-permute-start | bytes 589832 | tf_op jit(solution)/shard_map/ppermute | solution.py:226
  42.6 12.9 %collective-permute-start.14 = (bf16[192,512]{1,0:T(8,128)(2,1)S(1)}, bf16[192,512]{1,0:T(8,128)(2,1)S(1)}, u32[]{:S(2)}, u32[]{:S(2)}) collective-permute-start(bf16[192,512]{1,0:T(8,128)(2,1)S(1)} %collective-permute-done.11.refs_0_), channel_id=1, source_target_pairs={{0,4},{4,0},{1,5},{5,1},{2,6},{6,2},{3,7},{7,3},{8,12},{12,8},{9,1... | collective-permute-start | bytes 589832 | tf_op jit(solution)/shard_map/ppermute | solution.py:226
  42.7 12.9 %collective-permute-start.15 = (bf16[192,512]{1,0:T(8,128)(2,1)S(1)}, bf16[192,512]{1,0:T(8,128)(2,1)S(1)}, u32[]{:S(2)}, u32[]{:S(2)}) collective-permute-start(bf16[192,512]{1,0:T(8,128)(2,1)S(1)} %collective-permute-done.12.refs_1_), channel_id=1, source_target_pairs={{0,4},{4,0},{1,5},{5,1},{2,6},{6,2},{3,7},{7,3},{8,12},{12,8},{9,1... | collective-permute-start | bytes 589832 | tf_op jit(solution)/shard_map/ppermute | solution.py:226
  43.2 12.5 %collective-permute-start.16 = (bf16[192,512]{1,0:T(8,128)(2,1)S(1)}, bf16[192,512]{1,0:T(8,128)(2,1)S(1)}, u32[]{:S(2)}, u32[]{:S(2)}) collective-permute-start(bf16[192,512]{1,0:T(8,128)(2,1)S(1)} %collective-permute-done.13.refs_2_), channel_id=1, source_target_pairs={{0,4},{4,0},{1,5},{5,1},{2,6},{6,2},{3,7},{7,3},{8,12},{12,8},{9,1... | collective-permute-start | bytes 589832 | tf_op jit(solution)/shard_map/ppermute | solution.py:226
  91.9 11.5 %collective-permute-start.23 = (bf16[128,1344]{1,0:T(8,128)(2,1)}, bf16[128,1344]{1,0:T(8,128)(2,1)S(1)}, u32[]{:S(2)}, u32[]{:S(2)}) collective-permute-start(bf16[128,1344]{1,0:T(8,128)(2,1)} %get-tuple-element.83), channel_id=1, source_target_pairs={{0,1},{1,0},{2,3},{3,2},{4,5},{5,4},{6,7},{7,6},{8,9},{9,8},{10,11... | collective-permute-start | bytes 1032200 | tf_op jit(solution)/shard_map/ppermute | solution.py:226
  93.4 50.9 %collective-permute-start.6 = (bf16[768,512]{1,0:T(8,128)(2,1)S(1)}, bf16[768,512]{1,0:T(8,128)(2,1)S(1)}, u32[]{:S(2)}, u32[]{:S(2)}) collective-permute-start(bf16[768,512]{1,0:T(8,128)(2,1)S(1)} %copy-done.17), channel_id=1, source_target_pairs={{0,4},{4,0},{1,5},{5,1},{2,6},{6,2},{3,7},{7,3},{8,12},{12,8},{9,1... | collective-permute-start | bytes 2359304 | tf_op jit(solution)/shard_map/ppermute | solution.py:226
  93.6 56.4 %collective-permute-start.28 = (bf16[672,256]{1,0:T(8,128)(2,1)}, bf16[672,256]{1,0:T(8,128)(2,1)S(1)}, u32[]{:S(2)}, u32[]{:S(2)}) collective-permute-start(bf16[672,256]{1,0:T(8,128)(2,1)} %get-tuple-element.89), channel_id=1, source_target_pairs={{0,1},{1,0},{2,3},{3,2},{4,5},{5,4},{6,7},{7,6},{8,9},{9,8},{10,11... | collective-permute-start | bytes 1032200 | tf_op jit(solution)/shard_map/ppermute | solution.py:226
  94.2 24.0 %collective-permute-start.29 = (bf16[672,256]{1,0:T(8,128)(2,1)S(1)}, bf16[672,256]{1,0:T(8,128)(2,1)S(1)}, u32[]{:S(2)}, u32[]{:S(2)}) collective-permute-start(bf16[672,256]{1,0:T(8,128)(2,1)S(1)} %copy-done.20), channel_id=1, source_target_pairs={{0,1},{1,0},{2,3},{3,2},{4,5},{5,4},{6,7},{7,6},{8,9},{9,8},{10,11... | collective-permute-start | bytes 1032200 | tf_op jit(solution)/shard_map/ppermute | solution.py:226
  95.6 24.8 %collective-permute-start.32 = (bf16[672,256]{1,0:T(8,128)(2,1)S(1)}, bf16[672,256]{1,0:T(8,128)(2,1)S(1)}, u32[]{:S(2)}, u32[]{:S(2)}) collective-permute-start(bf16[672,256]{1,0:T(8,128)(2,1)S(1)} %copy-done.19), channel_id=1, source_target_pairs={{0,2},{1,3},{2,0},{3,1},{4,6},{5,7},{6,4},{7,5},{8,10},{9,11},{10,... | collective-permute-start | bytes 1032200 | tf_op jit(solution)/shard_map/ppermute | solution.py:226
  103.4 9.7 %collective-permute-start.26 = (bf16[128,1344]{1,0:T(8,128)(2,1)}, bf16[128,1344]{1,0:T(8,128)(2,1)S(1)}, u32[]{:S(2)}, u32[]{:S(2)}) collective-permute-start(bf16[128,1344]{1,0:T(8,128)(2,1)} %get-tuple-element.87), channel_id=1, source_target_pairs={{0,2},{1,3},{2,0},{3,1},{4,6},{5,7},{6,4},{7,5},{8,10},{9,11},{10,... | collective-permute-start | bytes 1032200 | tf_op jit(solution)/shard_map/ppermute | solution.py:226
  113.1 12.3 %collective-permute-start.22 = (bf16[128,1344]{1,0:T(8,128)(2,1)}, bf16[128,1344]{1,0:T(8,128)(2,1)S(1)}, u32[]{:S(2)}, u32[]{:S(2)}) collective-permute-start(bf16[128,1344]{1,0:T(8,128)(2,1)} %get-tuple-element.81), channel_id=1, source_target_pairs={{0,1},{1,0},{2,3},{3,2},{4,5},{5,4},{6,7},{7,6},{8,9},{9,8},{10,11... | collective-permute-start | bytes 1032200 | tf_op jit(solution)/shard_map/ppermute | solution.py:226
  118.1 11.3 %collective-permute-start.24 = (bf16[128,1344]{1,0:T(8,128)(2,1)S(1)}, bf16[128,1344]{1,0:T(8,128)(2,1)S(1)}, u32[]{:S(2)}, u32[]{:S(2)}) collective-permute-start(bf16[128,1344]{1,0:T(8,128)(2,1)S(1)} %add_convert_fusion.2), channel_id=1, source_target_pairs={{0,2},{1,3},{2,0},{3,1},{4,6},{5,7},{6,4},{7,5},{8,10},{9,11},{10,... | collective-permute-start | bytes 1032200 | tf_op jit(solution)/shard_map/ppermute | solution.py:226
  120.5 42.9 %collective-permute-start.31 = (bf16[672,256]{1,0:T(8,128)(2,1)}, bf16[672,256]{1,0:T(8,128)(2,1)}, u32[]{:S(2)}, u32[]{:S(2)}) collective-permute-start(bf16[672,256]{1,0:T(8,128)(2,1)} %get-tuple-element.93), channel_id=1, source_target_pairs={{0,2},{1,3},{2,0},{3,1},{4,6},{5,7},{6,4},{7,5},{8,10},{9,11},{10,... | collective-permute-start | bytes 1032200 | tf_op jit(solution)/shard_map/ppermute | solution.py:226
  125.4 17.3 %collective-permute-start.25 = (bf16[128,1344]{1,0:T(8,128)(2,1)S(1)}, bf16[128,1344]{1,0:T(8,128)(2,1)S(1)}, u32[]{:S(2)}, u32[]{:S(2)}) collective-permute-start(bf16[128,1344]{1,0:T(8,128)(2,1)S(1)} %copy-done.18), channel_id=1, source_target_pairs={{0,2},{1,3},{2,0},{3,1},{4,6},{5,7},{6,4},{7,5},{8,10},{9,11},{10,... | collective-permute-start | bytes 1032200 | tf_op jit(solution)/shard_map/ppermute | solution.py:226
  129.5 13.2 %collective-permute-start.27 = (bf16[128,1344]{1,0:T(8,128)(2,1)S(1)}, bf16[128,1344]{1,0:T(8,128)(2,1)S(1)}, u32[]{:S(2)}, u32[]{:S(2)}) collective-permute-start(bf16[128,1344]{1,0:T(8,128)(2,1)S(1)} %add_convert_fusion), channel_id=1, source_target_pairs={{0,1},{1,0},{2,3},{3,2},{4,5},{5,4},{6,7},{7,6},{8,9},{9,8},{10,11... | collective-permute-start | bytes 1032200 | tf_op jit(solution)/shard_map/ppermute | solution.py:226
  142.7 16.5 %collective-permute-start.17 = (bf16[768,512]{1,0:T(8,128)(2,1)}, bf16[768,512]{1,0:T(8,128)(2,1)S(1)}, u32[]{:S(2)}, u32[]{:S(2)}) collective-permute-start(bf16[768,512]{1,0:T(8,128)(2,1)} %get-tuple-element.71), channel_id=1, source_target_pairs={{0,4},{4,0},{1,5},{5,1},{2,6},{6,2},{3,7},{7,3},{8,12},{12,8},{9,1... | collective-permute-start | bytes 2359304 | tf_op jit(solution)/shard_map/ppermute | solution.py:226
  142.7 12.9 %collective-permute-start.30 = (bf16[672,256]{1,0:T(8,128)(2,1)}, bf16[672,256]{1,0:T(8,128)(2,1)}, u32[]{:S(2)}, u32[]{:S(2)}) collective-permute-start(bf16[672,256]{1,0:T(8,128)(2,1)} %add_convert_fusion.6), channel_id=1, source_target_pairs={{0,2},{1,3},{2,0},{3,1},{4,6},{5,7},{6,4},{7,5},{8,10},{9,11},{10,... | collective-permute-start | bytes 1032200 | tf_op jit(solution)/shard_map/ppermute | solution.py:226
  144.4 21.1 %collective-permute-start.33 = (bf16[672,256]{1,0:T(8,128)(2,1)}, bf16[672,256]{1,0:T(8,128)(2,1)}, u32[]{:S(2)}, u32[]{:S(2)}) collective-permute-start(bf16[672,256]{1,0:T(8,128)(2,1)} %add_convert_fusion.4), channel_id=1, source_target_pairs={{0,1},{1,0},{2,3},{3,2},{4,5},{5,4},{6,7},{7,6},{8,9},{9,8},{10,11... | collective-permute-start | bytes 1032200 | tf_op jit(solution)/shard_map/ppermute | solution.py:226
  150.0 15.7 %collective-permute-start.7 = (bf16[192,512]{1,0:T(8,128)(2,1)}, bf16[192,512]{1,0:T(8,128)(2,1)S(1)}, u32[]{:S(2)}, u32[]{:S(2)}) collective-permute-start(bf16[192,512]{1,0:T(8,128)(2,1)} %get-tuple-element.58), channel_id=1, source_target_pairs={{0,24},{8,0},{16,8},{24,16},{1,25},{9,1},{17,9},{25,17},{2,26},{10... | collective-permute-start | bytes 589832 | tf_op jit(solution)/shard_map/ppermute | solution.py:222
  156.8 25.7 %collective-permute-start.8 = (bf16[192,512]{1,0:T(8,128)(2,1)S(1)}, bf16[192,512]{1,0:T(8,128)(2,1)S(1)}, u32[]{:S(2)}, u32[]{:S(2)}) collective-permute-start(bf16[192,512]{1,0:T(8,128)(2,1)S(1)} %copy-done.26), channel_id=1, source_target_pairs={{0,16},{8,24},{16,0},{24,8},{1,17},{9,25},{17,1},{25,9},{2,18},{10... | collective-permute-start | bytes 589832 | tf_op jit(solution)/shard_map/ppermute | solution.py:222
  159.3 23.2 %collective-permute-start.9 = (bf16[192,512]{1,0:T(8,128)(2,1)S(1)}, bf16[192,512]{1,0:T(8,128)(2,1)S(1)}, u32[]{:S(2)}, u32[]{:S(2)}) collective-permute-start(bf16[192,512]{1,0:T(8,128)(2,1)S(1)} %copy-done.25), channel_id=1, source_target_pairs={{0,8},{8,16},{16,24},{24,0},{1,9},{9,17},{17,25},{25,1},{2,10},{10... | collective-permute-start | bytes 589832 | tf_op jit(solution)/shard_map/ppermute | solution.py:222
  163.3 22.8 %collective-permute-start.18 = (bf16[192,512]{1,0:T(8,128)(2,1)}, bf16[192,512]{1,0:T(8,128)(2,1)S(1)}, u32[]{:S(2)}, u32[]{:S(2)}) collective-permute-start(bf16[192,512]{1,0:T(8,128)(2,1)} %get-tuple-element.73), channel_id=1, source_target_pairs={{0,24},{8,0},{16,8},{24,16},{1,25},{9,1},{17,9},{25,17},{2,26},{10... | collective-permute-start | bytes 589832 | tf_op jit(solution)/shard_map/ppermute | solution.py:222
  165.5 24.2 %collective-permute-start.19 = (bf16[192,512]{1,0:T(8,128)(2,1)}, bf16[192,512]{1,0:T(8,128)(2,1)S(1)}, u32[]{:S(2)}, u32[]{:S(2)}) collective-permute-start(bf16[192,512]{1,0:T(8,128)(2,1)} %get-tuple-element.74), channel_id=1, source_target_pairs={{0,16},{8,24},{16,0},{24,8},{1,17},{9,25},{17,1},{25,9},{2,18},{10... | collective-permute-start | bytes 589832 | tf_op jit(solution)/shard_map/ppermute | solution.py:222
  165.6 24.0 %collective-permute-start.20 = (bf16[192,512]{1,0:T(8,128)(2,1)}, bf16[192,512]{1,0:T(8,128)(2,1)S(1)}, u32[]{:S(2)}, u32[]{:S(2)}) collective-permute-start(bf16[192,512]{1,0:T(8,128)(2,1)} %get-tuple-element.75), channel_id=1, source_target_pairs={{0,8},{8,16},{16,24},{24,0},{1,9},{9,17},{17,25},{25,1},{2,10},{10... | collective-permute-start | bytes 589832 | tf_op jit(solution)/shard_map/ppermute | solution.py:222
  (32 other events, 296.6 us)

commit v2 on v1

v2 whole, which is shorter than its diff:
```python
import functools

import jax
import jax.numpy as jnp
from jax import lax
from jax.experimental import pallas as pl
from jax.experimental.pallas import tpu as pltpu
from jax.sharding import PartitionSpec as P

BF16 = jnp.bfloat16
F32 = jnp.float32
ROW_TILE = 16
TILE = 256
VMEM_BYTES = 56 * 1024 * 1024
MATMUL = (((1,), (0,)), ((), ()))
CONTRACT_LAST = (((1,), (1,)), ((), ()))
CONTRACT_FIRST = (((0,), (0,)), ((), ()))


def mxu(a, b, dims=MATMUL):
    return lax.dot_general(a, b, dims, preferred_element_type=F32)


def shape(rows, columns, dtype=BF16):
    return jax.ShapeDtypeStruct((rows, columns), dtype)


def local(body, outs, operands, flops, name, scratch=()):
    moved = sum(x.size * x.dtype.itemsize for x in (*operands, *outs))
    return pl.pallas_call(
        body,
        out_shape=tuple(outs),
        in_specs=[pl.BlockSpec(memory_space=pltpu.VMEM)] * len(operands),
        out_specs=tuple([pl.BlockSpec(memory_space=pltpu.VMEM)] * len(outs)),
        scratch_shapes=list(scratch),
        compiler_params=pltpu.CompilerParams(vmem_limit_bytes=VMEM_BYTES),
        cost_estimate=pl.CostEstimate(flops=flops, bytes_accessed=moved, transcendentals=0),
        name=name,
    )(*operands)


def window(index, width):
    return pl.ds(pl.multiple_of(index * width, width), width)


def over_tiles(width, step):
    full = width // TILE

    def body(i, carry):
        step(window(i, TILE))
        return carry

    lax.fori_loop(0, full, body, 0)
    if width % TILE:
        step(pl.ds(full * TILE, width - full * TILE))


def picks(meta, k, shift, capacity):
    rows = lax.broadcasted_iota(jnp.int32, (meta.shape[0], capacity), 1) + shift * capacity
    return (meta[:, k : k + 1].astype(jnp.int32) == rows).astype(F32).astype(BF16)


def columns_of(table_t):
    count = table_t.shape[1]
    unit = lax.broadcasted_iota(jnp.int32, (count, count), 0) == lax.broadcasted_iota(
        jnp.int32, (count, count), 1
    )
    return mxu(unit.astype(F32).astype(BF16), table_t.astype(F32).astype(BF16), CONTRACT_LAST).astype(jnp.int32)


def route_body(owners, capacity, routes_ref, index_ref, table_ref, tokens_ref, meta_ref, own_ref, *sends):
    me, core = lax.axis_index("expert"), lax.axis_index("cuts")
    top, count = routes_ref.shape
    width = -(-owners // 128) * 128
    half = tokens_ref.shape[1] // lax.axis_size("cuts")
    routes, index = columns_of(routes_ref[...]), columns_of(index_ref[...])
    expert_lane = lax.broadcasted_iota(jnp.int32, (count, width), 1)
    named = [routes[:, k : k + 1] == expert_lane for k in range(top)]
    onehot = sum(n.astype(F32) for n in named).astype(BF16)
    earlier = lax.broadcasted_iota(jnp.int32, (count, count), 0) > lax.broadcasted_iota(
        jnp.int32, (count, count), 1
    )
    before = mxu(earlier.astype(F32).astype(BF16), onehot)
    level = lax.broadcasted_iota(jnp.int32, (count, table_ref.shape[1]), 1)
    lane = lax.broadcasted_iota(jnp.int32, meta_ref.shape, 1)
    meta = jnp.zeros(meta_ref.shape, F32)
    for k in range(top):
        rank = jnp.sum(jnp.where(named[k], before, 0.0), axis=1, keepdims=True)
        shift = routes[:, k : k + 1] - me
        shift = jnp.where(shift < 0, shift + owners, shift)
        slot = (shift * capacity).astype(F32) + rank
        weight = jnp.sum(
            jnp.where(index[:, k : k + 1] == level, table_ref[...], 0.0), axis=1, keepdims=True
        )
        meta = jnp.where(lane == k, slot, jnp.where(lane == top + k, weight, meta))
    meta_ref[...] = meta
    wide = tokens_ref[...].astype(BF16)
    narrow = tokens_ref[:, window(core, half)].astype(BF16)
    for shift, ref in enumerate((own_ref, *sends)):
        chosen = sum(picks(meta, k, shift, capacity) for k in range(top))
        ref[...] = mxu(chosen, narrow if shift else wide, CONTRACT_FIRST).astype(BF16)


def weigh_body(top, capacity, meta_ref, cotangent_ref, own_ref, *sends):
    core = lax.axis_index("cuts")
    meta = meta_ref[...]
    half = cotangent_ref.shape[1] // lax.axis_size("cuts")

    def scaled(values):
        return [(meta[:, top + k : top + k + 1] * values).astype(BF16) for k in range(top)]

    wide, narrow = scaled(cotangent_ref[...]), scaled(cotangent_ref[:, window(core, half)])
    for shift, ref in enumerate((own_ref, *sends)):
        rows = narrow if shift else wide
        ref[...] = sum(
            mxu(picks(meta, k, shift, capacity), rows[k], CONTRACT_FIRST) for k in range(top)
        ).astype(BF16)


def assemble(full_ref, own, mine, other):
    core = lax.axis_index("cuts")
    capacity, half = mine[0].shape
    full_ref[:capacity, :] = own[...]
    for i, (a, b) in enumerate(zip(mine, other, strict=True), 1):
        rows = slice(i * capacity, (i + 1) * capacity)
        full_ref[rows, window(core, half)] = a[...]
        full_ref[rows, window(1 - core, half)] = b[...]


def to_halves(rows_ref, weight_ref, keep_ref, give_ref):
    core = lax.axis_index("cuts")
    half = keep_ref.shape[1]
    for owner, ref in ((1 - core, give_ref), (core, keep_ref)):

        def step(i, carry, owner=owner, ref=ref):
            features = window(owner * (half // TILE) + i, TILE)
            ref[:, window(i, TILE)] = mxu(rows_ref[...], weight_ref[:, features]).astype(BF16)
            return carry

        lax.fori_loop(0, half // TILE, step, 0)


def forward_body(remote, own, *refs):
    mine, other = refs[:remote], refs[remote : 2 * remote]
    inner_ref, outer_ref, x_ref, positive_ref, hidden_ref, keep_ref, give_ref, turned = refs[2 * remote :]
    assemble(x_ref, own, mine, other)

    def activate(units):
        positive = jnp.maximum(mxu(inner_ref[units, :], x_ref[...], CONTRACT_LAST), 0.0)
        positive_ref[units, :] = positive.astype(BF16)
        hidden = (positive * positive).astype(BF16)
        hidden_ref[units, :] = hidden
        turned[:, units] = hidden.T

    over_tiles(inner_ref.shape[0], activate)
    to_halves(turned, outer_ref, keep_ref, give_ref)


def backward_body(g_ref, positive_ref, inner_ref, outer_ref, d_act_ref, keep_ref, give_ref, turned):
    def step(units):
        d_hidden = mxu(outer_ref[units, :], g_ref[...], CONTRACT_LAST)
        d_act = (d_hidden * 2.0 * positive_ref[units, :].astype(F32)).astype(BF16)
        d_act_ref[units, :] = d_act
        turned[:, units] = d_act.T

    over_tiles(outer_ref.shape[0], step)
    to_halves(turned, inner_ref, keep_ref, give_ref)


def split_body(keep_ref, came_ref, *outs):
    capacity = outs[0].shape[0]
    for i, ref in enumerate(outs):
        rows = slice(i * capacity, (i + 1) * capacity)
        ref[...] = (keep_ref[rows, :].astype(F32) + came_ref[rows, :].astype(F32)).astype(BF16)


def gather_body(remote, own, *refs):
    assemble(refs[2 * remote], own, refs[:remote], refs[remote : 2 * remote])


def pieces(keys, units_ref, rows_ref, outs):
    me = lax.axis_index("dp")
    for (block, part), ref in zip(keys, outs, strict=True):
        rows, width = ref.shape
        features = rows_ref[:, window(me ^ block, width)]
        ref[...] = mxu(units_ref[part * rows : (part + 1) * rows, :], features).astype(BF16)


def grad_body(keys, units_ref, rows_ref, *outs):
    pieces(keys, units_ref, rows_ref, outs)


def first_grad_body(keys, remote, own, *refs):
    units_ref, rows_ref, *outs = refs[2 * remote :]
    assemble(rows_ref, own, refs[:remote], refs[remote : 2 * remote])
    pieces(keys, units_ref, rows_ref, outs)


def combine_body(top, weighted, meta_ref, *refs):
    *chunks, wide_ref, narrow_ref = refs
    meta = meta_ref[...]
    capacity = chunks[0].shape[0]
    total = 0.0
    if weighted:
        for k in range(top):
            got = sum(mxu(picks(meta, k, s, capacity), c[...]) for s, c in enumerate(chunks))
            total += meta[:, top + k : top + k + 1] * got
    else:
        for s, c in enumerate(chunks):
            total += mxu(sum(picks(meta, k, s, capacity) for k in range(top)), c[...])
    wide_ref[...] = total
    narrow_ref[...] = total.astype(BF16)


def join_body(mine_ref, other_ref, out_ref):
    core = lax.axis_index("cuts")
    half = mine_ref.shape[1]
    out_ref[:, window(core, half)] = mine_ref[...]
    out_ref[:, window(1 - core, half)] = other_ref[...].astype(F32)


def shifted(x, axis, shift):
    size = lax.axis_size(axis)
    return lax.ppermute(x, axis, [(i, (i + shift) % size) for i in range(size)])


def partner(x, axis, bit):
    return lax.ppermute(x, axis, [(i, i ^ bit) for i in range(lax.axis_size(axis))])


def after(values, *earlier):
    return lax.optimization_barrier((values, earlier))[0]


def halve(blocks, bit, dtype):
    came = {r ^ bit: partner(blocks[r], "dp", bit) for r in sorted(blocks, reverse=True) if r & bit}
    return {r: (blocks[r].astype(F32) + came[r].astype(F32)).astype(dtype) for r in came}


def shards(tokens, cotangent, routes, combine_index, combine_table, w_in, w_out):
    owners, groups = lax.axis_size("expert"), lax.axis_size("dp")
    count, features = tokens.shape
    top = routes.shape[1]
    half = features // lax.axis_size("cuts")
    capacity = -(-max(2, 3 * count * top // (2 * owners)) // ROW_TILE) * ROW_TILE
    slots = owners * capacity
    remote = owners - 1
    inner, outer = w_in[0].T, w_out[0]
    units = outer.shape[0]
    bits = [1 << i for i in range(groups.bit_length() - 1)]
    orders = (bits, bits[::-1])
    piece = shape(units // 2, features // groups)
    keys = [(r, part) for r in reversed(range(groups)) for part in range(2)]
    leaving = [(r, part) for r, part in keys if r & orders[part][0]]
    staying = [key for key in keys if key not in leaving]
    work = 2 * slots * features * units

    def across_cores(chunks):
        return [partner(x, "cuts", 1) for x in chunks]

    def over_experts(chunks, sign):
        return [shifted(x, "expert", sign * s) for s, x in enumerate(chunks, 1)]

    def split(keep, came):
        return local(split_body, [shape(capacity, half)] * owners, [keep, came], 0, "split")

    def combine(chunks, weighted):
        return local(
            functools.partial(combine_body, top, weighted),
            [shape(count, half, F32), shape(count, half)],
            [meta, *chunks],
            2 * count * slots * half,
            "combine",
        )

    def join(wide, came):
        return local(join_body, [shape(count, features, F32)], [wide, came], 0, "join")[0]

    def halved(pieces, step, dtype=BF16):
        out = {}
        for part, order in enumerate(orders):
            mine = {r: x for (r, p), x in pieces.items() if p == part}
            out |= {(r, part): x for r, x in halve(mine, order[step], dtype).items()}
        return out

    meta, own, *sends = local(
        functools.partial(route_body, owners, capacity),
        [shape(count, 128, F32), shape(capacity, features)] + [shape(capacity, half)] * remote,
        [routes.T, combine_index.T, combine_table[None, :], tokens],
        2 * count * slots * features,
        "route",
    )
    mine = over_experts(sends, 1)
    grad_own, *grad_sends = local(
        functools.partial(weigh_body, top, capacity),
        [shape(capacity, features)] + [shape(capacity, half)] * remote,
        [meta, cotangent],
        4 * count * slots * features,
        "weigh",
    )
    grad_mine = over_experts(grad_sends, 1)
    mine = after(mine, grad_sends)
    other = across_cores(mine)
    arrived, positive, hidden, keep, give = local(
        functools.partial(forward_body, remote),
        [shape(slots, features), shape(units, slots), shape(units, slots)] + [shape(slots, half)] * 2,
        [own, *mine, *other, inner, outer],
        2 * work,
        "forward",
        [pltpu.VMEM((slots, units), BF16)],
    )
    grad_mine, hidden, keep, give = after((grad_mine, hidden, keep, give))
    came = partner(give, "cuts", 1)
    grad_other = across_cores(grad_mine)
    grad_rows, *out = local(
        functools.partial(first_grad_body, leaving, remote),
        [shape(slots, features)] + [piece] * len(leaving),
        [grad_own, *grad_mine, *grad_other, hidden],
        work // 2,
        "outer_leaving",
    )
    outer_pieces = dict(zip(leaving, out, strict=True))
    keep, came = after((keep, came), grad_rows)
    chunks = split(keep, came)
    returned = [chunks[0]] + over_experts(chunks[1:], -1)
    hidden, grad_rows = after((hidden, grad_rows), chunks)
    out = local(
        functools.partial(grad_body, staying), [piece] * len(staying), [hidden, grad_rows], work // 2, "outer_staying"
    )
    outer_pieces |= dict(zip(staying, out, strict=True))
    grad_rows, positive = after((grad_rows, positive), out)
    d_act, grad_keep, grad_give = local(
        backward_body,
        [shape(units, slots)] + [shape(slots, half)] * 2,
        [grad_rows, positive, inner, outer],
        2 * work,
        "backward",
        [pltpu.VMEM((slots, units), BF16)],
    )
    outer_pieces = halved(outer_pieces, 0)
    d_act, grad_give, outer_pieces, returned = after((d_act, grad_give, outer_pieces, returned))
    grad_came = partner(grad_give, "cuts", 1)
    out = local(
        functools.partial(grad_body, leaving), [piece] * len(leaving), [d_act, arrived], work // 2, "inner_leaving"
    )
    inner_pieces = dict(zip(leaving, out, strict=True))
    grad_keep, grad_came = after((grad_keep, grad_came), out)
    chunks = split(grad_keep, grad_came)
    grad_returned = [chunks[0]] + over_experts(chunks[1:], -1)
    d_act, arrived = after((d_act, arrived), chunks)
    out = local(
        functools.partial(grad_body, staying), [piece] * len(staying), [d_act, arrived], work // 2, "inner_staying"
    )
    inner_pieces |= dict(zip(staying, out, strict=True))
    returned = after(returned, out)
    wide, narrow = combine(returned, True)
    layer_out = join(wide, partner(narrow, "cuts", 1))
    outer_pieces = halved(outer_pieces, 1, F32)
    inner_pieces = halved(inner_pieces, 0)
    inner_pieces, grad_returned = after((inner_pieces, grad_returned), wide)
    wide, narrow = combine(grad_returned, False)
    d_tokens = join(wide, partner(narrow, "cuts", 1))
    inner_pieces = halved(inner_pieces, 1, F32)
    grad_in, grad_out = (
        jnp.concatenate([p[0, 0], p[0, 1]], axis=0) for p in (inner_pieces, outer_pieces)
    )
    return (layer_out, d_tokens, grad_in.T[None], grad_out[None])


def solution(mesh):
    in_specs = (
        P(("expert", "dp"), None),
        P(("expert", "dp"), None),
        P(("expert", "dp"), None),
        P(("expert", "dp"), None),
        P(),
        P("expert", None, "cuts"),
        P("expert", "cuts", None),
    )
    out_specs = (
        P(("expert", "dp"), None),
        P(("expert", "dp"), None),
        P("expert", "dp", "cuts"),
        P("expert", "cuts", "dp"),
    )
    return jax.shard_map(shards, mesh=mesh, in_specs=in_specs, out_specs=out_specs, check_vma=False)
```

time: 201 us -> 139 us (0.69)
  waiting for transfers between devices: 70.4 us -> 22.8 us
  local copies, waits for them, and re-layouts: 11.1 us -> 3.82 us
  Pallas kernels: 68.9 us -> 62.9 us
    ppermute x22, waiting for transfers between devices: 33.5 us -> 4.51 us  [partner(): lax.ppermute(x, axis, [(i, i ^ bit) for i in range(lax.axis_size(axis))])]
    ppermute x12, waiting for transfers between devices: 36.8 us -> 18.3 us  [shifted(): return lax.ppermute(x, axis, [(i, (i + shift) % size) for i in range(size)])]
    unnamed x64 -> x66, local copies, waits for them, and re-layouts: 11.1 us -> 3.82 us
    pallas_call x12 -> x14, Pallas kernels: 68.9 us -> 62.9 us  [local(): pl.pallas_call(body, out_shape=tuple(outs), in_specs=[pl.BlockSpec(memory...]
    add x4, other arithmetic: 2.58 us -> 0.28 us  [halve(): blocks[r].astype(F32) + came[r].astype(F32)]
    ppermute x22, starting transfers between devices: 17.4 us -> 15.2 us  [partner(): lax.ppermute(x, axis, [(i, i ^ bit) for i in range(lax.axis_size(axis))])]
    convert_element_type x4 -> x8, other arithmetic: 3.94 us -> 4.63 us  [halve(): (blocks[r].astype(F32) + came[r].astype(F32)).astype(dtype)]
  transfers between devices with their start and end apart: 34 -> 34, of which waited for: 12 -> 7; matrix products, arithmetic and copies ran while one was open for 6% -> 4% of each run, Pallas kernels for 14% -> 43%
where the time goes in v2:
time: 139 us
  Pallas kernels  62.9 us (45%)
  starting transfers between devices  40.8 us (29%)
  waiting for transfers between devices  22.8 us (16%)
  other arithmetic  7.25 us (5%)
  local copies, waits for them, and re-layouts  3.82 us (3%)
    pallas_call x14, Pallas kernels, local(): pl.pallas_call(body, out_shape=tuple(outs), in_specs=[pl.BlockSpec(memory...  62.9 us
    ppermute x12, starting transfers between devices, shifted(): return lax.ppermute(x, axis, [(i, (i + shift) % size) for i in range(size)])  25.6 us
    ppermute x12, waiting for transfers between devices, shifted(): return lax.ppermute(x, axis, [(i, (i + shift) % size) for i in range(size)])  18.3 us
    ppermute x22, starting transfers between devices, partner(): lax.ppermute(x, axis, [(i, i ^ bit) for i in range(lax.axis_size(axis))])  15.2 us
    convert_element_type x8, other arithmetic, halve(): (blocks[r].astype(F32) + came[r].astype(F32)).astype(dtype)  4.63 us
    ppermute x22, waiting for transfers between devices, partner(): lax.ppermute(x, axis, [(i, i ^ bit) for i in range(lax.axis_size(axis))])  4.51 us
    unnamed x66, local copies, waits for them, and re-layouts  3.82 us
  transfers between devices with their start and end apart: 34, of which 7 were waited for; matrix products, arithmetic and copies ran while one was open for 4% of the time, Pallas kernels for 43%

profile of v2, /device:TPU:0, one launch (start us, length us, event | category | flops | bytes accessed | tf_op | source)
XLA Modules:
  0.0 138.5 jit_solution(13476645760327337505)
XLA Ops:
  0.6 3.6 %route.1 = (f32[256,128]{1,0:T(8,128)}, bf16[192,1024]{1,0:T(8,128)(2,1)}, bf16[192,512]{1,0:T(8,128)(2,1)}, bf16[192,512]{1,0:T(8,128)(2,1)}, bf16[192,512]{1,0:T(8,128)(2,1)}) custom-call(s32[2,256]{1,0:T(2,128)} %bitcast.17, s32[2,256]{1,0:T(2,128)} %bitcast.18, f32[1,256]{1,0:T(1,128)} %bitcast.19, f32[256,1024]{1,0:T(8,128)} %tokens_ref.1), custom_call_target="tpu_custom_call" | custom-call | flops 402653184 | bytes 2167808 | tf_op jit(solution)/shard_map/route/pallas_call | solution.py:30
  4.2 3.0 %collective-permute-start.3 = (bf16[192,512]{1,0:T(8,128)(2,1)}, bf16[192,512]{1,0:T(8,128)(2,1)S(1)}, u32[]{:S(2)}, u32[]{:S(2)}) collective-permute-start(bf16[192,512]{1,0:T(8,128)(2,1)} %get-tuple-element.96), channel_id=1, source_target_pairs={{0,8},{8,16},{16,24},{24,0},{1,9},{9,17},{17,25},{25,1},{2,10},{10... | collective-permute-start | bytes 589832 | tf_op jit(solution)/shard_map/ppermute | solution.py:224
  7.3 2.6 %collective-permute-start.4 = (bf16[192,512]{1,0:T(8,128)(2,1)}, bf16[192,512]{1,0:T(8,128)(2,1)S(1)}, u32[]{:S(2)}, u32[]{:S(2)}) collective-permute-start(bf16[192,512]{1,0:T(8,128)(2,1)} %get-tuple-element.97), channel_id=1, source_target_pairs={{0,16},{8,24},{16,0},{24,8},{1,17},{9,25},{17,1},{25,9},{2,18},{10... | collective-permute-start | bytes 589832 | tf_op jit(solution)/shard_map/ppermute | solution.py:224
  9.9 1.3 collective-permute-start.5
  11.2 2.9 %weigh.1 = (bf16[192,1024]{1,0:T(8,128)(2,1)}, bf16[192,512]{1,0:T(8,128)(2,1)}, bf16[192,512]{1,0:T(8,128)(2,1)}, bf16[192,512]{1,0:T(8,128)(2,1)}) custom-call(f32[256,128]{1,0:T(8,128)} %get-tuple-element.91.meta_ref, f32[256,1024]{1,0:T(8,128)} %cotangent_ref.1), custom_call_target="tpu_custom_call" | custom-call | flops 805306368 | bytes 2162688 | tf_op jit(solution)/shard_map/weigh/pallas_call | solution.py:30
  15.4 7.6 %collective-permute-done.4.refs_1_ = bf16[192,512]{1,0:T(8,128)(2,1)S(1)} collective-permute-done((bf16[192,512]{1,0:T(8,128)(2,1)}, bf16[192,512]{1,0:T(8,128)(2,1)S(1)}, u32[]{:S(2)}, u32[]{:S(2)}) %collective-permute-start.4) | collective-permute-done | bytes 196640 | tf_op jit(solution)/shard_map/ppermute | solution.py:224
  23.6 4.6 %collective-permute-start = (bf16[192,512]{1,0:T(8,128)(2,1)}, bf16[192,512]{1,0:T(8,128)(2,1)S(1)}, u32[]{:S(2)}, u32[]{:S(2)}) collective-permute-start(bf16[192,512]{1,0:T(8,128)(2,1)} %get-tuple-element.92), channel_id=1, source_target_pairs={{0,8},{8,16},{16,24},{24,0},{1,9},{9,17},{17,25},{25,1},{2,10},{10... | collective-permute-start | bytes 589832 | tf_op jit(solution)/shard_map/ppermute | solution.py:224
  28.2 1.7 %collective-permute-start.1 = (bf16[192,512]{1,0:T(8,128)(2,1)}, bf16[192,512]{1,0:T(8,128)(2,1)S(1)}, u32[]{:S(2)}, u32[]{:S(2)}) collective-permute-start(bf16[192,512]{1,0:T(8,128)(2,1)} %get-tuple-element.93), channel_id=1, source_target_pairs={{0,16},{8,24},{16,0},{24,8},{1,17},{9,25},{17,1},{25,9},{2,18},{10... | collective-permute-start | bytes 589832 | tf_op jit(solution)/shard_map/ppermute | solution.py:224
  31.3 12.9 %forward.1 = (bf16[768,1024]{1,0:T(8,128)(2,1)}, bf16[1344,768]{1,0:T(8,128)(2,1)}, bf16[1344,768]{1,0:T(8,128)(2,1)}, bf16[768,512]{1,0:T(8,128)(2,1)}, bf16[768,512]{1,0:T(8,128)(2,1)}) custom-call(bf16[192,1024]{1,0:T(8,128)(2,1)} %get-tuple-element.95.own, bf16[192,512]{1,0:T(8,128)(2,1)} %copy-done.20, bf16[192,512]{1,0:T(8,128)(2,1)} %copy-done.23, ...), custom_call_target="tpu_custom_call" | custom-call | flops 4227858432 | bytes 14352384 | tf_op jit(solution)/shard_map/forward/pallas_call | solution.py:30
  45.3 1.5 %collective-permute-done.10.refs_4_ = bf16[192,512]{1,0:T(8,128)(2,1)S(1)} collective-permute-done((bf16[192,512]{1,0:T(8,128)(2,1)S(1)}, bf16[192,512]{1,0:T(8,128)(2,1)S(1)}, u32[]{:S(2)}, u32[]{:S(2)}) %collective-permute-start.10) | collective-permute-done | bytes 196640 | tf_op jit(solution)/shard_map/ppermute | solution.py:228
  48.1 4.4 %outer_leaving.1 = (bf16[768,1024]{1,0:T(8,128)(2,1)}, bf16[672,256]{1,0:T(8,128)(2,1)}, bf16[672,256]{1,0:T(8,128)(2,1)}, bf16[672,256]{1,0:T(8,128)(2,1)}, bf16[672,256]{1,0:T(8,128)(2,1)}) custom-call(bf16[192,1024]{1,0:T(8,128)(2,1)} %get-tuple-element.106.own, bf16[192,512]{1,0:T(8,128)(2,1)} %copy-done.16, bf16[192,512]{1,0:T(8,128)(2,1)} %copy-done.17, ...), custom_call_target="tpu_custom_call" | custom-call | flops 1056964608 | bytes 6586368 | tf_op jit(solution)/shard_map/outer_leaving/pallas_call | solution.py:30
  52.5 1.5 %collective-permute-start.16 = (bf16[672,256]{1,0:T(8,128)(2,1)}, bf16[672,256]{1,0:T(8,128)(2,1)S(1)}, u32[]{:S(2)}, u32[]{:S(2)}) collective-permute-start(bf16[672,256]{1,0:T(8,128)(2,1)} %get-tuple-element.133), channel_id=1, source_target_pairs={{0,1},{1,0},{2,3},{3,2},{4,5},{5,4},{6,7},{7,6},{8,9},{9,8},{10,11... | collective-permute-start | bytes 1032200 | tf_op jit(solution)/shard_map/ppermute | solution.py:228
  54.0 1.5 %collective-permute-start.15 = (bf16[672,256]{1,0:T(8,128)(2,1)}, bf16[672,256]{1,0:T(8,128)(2,1)S(1)}, u32[]{:S(2)}, u32[]{:S(2)}) collective-permute-start(bf16[672,256]{1,0:T(8,128)(2,1)} %get-tuple-element.132), channel_id=1, source_target_pairs={{0,2},{1,3},{2,0},{3,1},{4,6},{5,7},{6,4},{7,5},{8,10},{9,11},{10,... | collective-permute-start | bytes 1032200 | tf_op jit(solution)/shard_map/ppermute | solution.py:228
  57.5 2.3 %split.2 = (bf16[192,512]{1,0:T(8,128)(2,1)}, bf16[192,512]{1,0:T(8,128)(2,1)}, bf16[192,512]{1,0:T(8,128)(2,1)}, bf16[192,512]{1,0:T(8,128)(2,1)}) custom-call(bf16[768,512]{1,0:T(8,128)(2,1)} %get-tuple-element.113.keep_ref, bf16[768,512]{1,0:T(8,128)(2,1)} %copy-done), custom_call_target="tpu_custom_call" | custom-call | bytes 2359296 | tf_op jit(solution)/shard_map/split/pallas_call | solution.py:30
  59.8 4.7 %collective-permute-start.17 = (bf16[192,512]{1,0:T(8,128)(2,1)}, bf16[192,512]{1,0:T(8,128)(2,1)S(1)}, u32[]{:S(2)}, u32[]{:S(2)}) collective-permute-start(bf16[192,512]{1,0:T(8,128)(2,1)} %get-tuple-element.116), channel_id=1, source_target_pairs={{0,24},{8,0},{16,8},{24,16},{1,25},{9,1},{17,9},{25,17},{2,26},{10... | collective-permute-start | bytes 589832 | tf_op jit(solution)/shard_map/ppermute | solution.py:224
  64.5 4.2 %outer_staying.1 = (bf16[672,256]{1,0:T(8,128)(2,1)}, bf16[672,256]{1,0:T(8,128)(2,1)}, bf16[672,256]{1,0:T(8,128)(2,1)}, bf16[672,256]{1,0:T(8,128)(2,1)}) custom-call(bf16[1344,768]{1,0:T(8,128)(2,1)} %get-tuple-element.121.refs_6_.units_ref, bf16[768,1024]{1,0:T(8,128)(2,1)} %get-tuple-element.126.rows_ref.g_ref), custom_call_target="tpu_custom_call" | custom-call | flops 1056964608 | bytes 5013504 | tf_op jit(solution)/shard_map/outer_staying/pallas_call | solution.py:30
  72.0 12.1 %backward.1 = (bf16[1344,768]{1,0:T(8,128)(2,1)}, bf16[768,512]{1,0:T(8,128)(2,1)}, bf16[768,512]{1,0:T(8,128)(2,1)}) custom-call(bf16[768,1024]{1,0:T(8,128)(2,1)} %get-tuple-element.126.rows_ref.g_ref, bf16[1344,768]{1,0:T(8,128)(2,1)} %get-tuple-element.127.positive_ref, bf16[1344,1024]{1,0:T(8,128)(2,1)} %bitcast.14, bf16[1344,1024]{1,0:T(8,128)(2,1)} %bitcast.16), custom_call_target="tpu_custom_call" | custom-call | flops 4227858432 | bytes 12779520 | tf_op jit(solution)/shard_map/backward/pallas_call | solution.py:30
  84.4 1.6 %collective-permute-start.32 = (bf16[672,256]{1,0:T(8,128)(2,1)S(1)}, bf16[672,256]{1,0:T(8,128)(2,1)S(1)}, u32[]{:S(2)}, u32[]{:S(2)}) collective-permute-start(bf16[672,256]{1,0:T(8,128)(2,1)S(1)} %add_convert_fusion.4), channel_id=1, source_target_pairs={{0,2},{1,3},{2,0},{3,1},{4,6},{5,7},{6,4},{7,5},{8,10},{9,11},{10,... | collective-permute-start | bytes 1032200 | tf_op jit(solution)/shard_map/ppermute | solution.py:228
  85.9 1.5 %collective-permute-start.33 = (bf16[672,256]{1,0:T(8,128)(2,1)S(1)}, bf16[672,256]{1,0:T(8,128)(2,1)S(1)}, u32[]{:S(2)}, u32[]{:S(2)}) collective-permute-start(bf16[672,256]{1,0:T(8,128)(2,1)S(1)} %add_convert_fusion.5), channel_id=1, source_target_pairs={{0,1},{1,0},{2,3},{3,2},{4,5},{5,4},{6,7},{7,6},{8,9},{9,8},{10,11... | collective-permute-start | bytes 1032200 | tf_op jit(solution)/shard_map/ppermute | solution.py:228
  87.5 4.1 %inner_leaving.1 = (bf16[672,256]{1,0:T(8,128)(2,1)}, bf16[672,256]{1,0:T(8,128)(2,1)}, bf16[672,256]{1,0:T(8,128)(2,1)}, bf16[672,256]{1,0:T(8,128)(2,1)}) custom-call(bf16[1344,768]{1,0:T(8,128)(2,1)} %get-tuple-element.152.units_ref, bf16[768,1024]{1,0:T(8,128)(2,1)} %get-tuple-element.153.rows_ref), custom_call_target="tpu_custom_call" | custom-call | flops 1056964608 | bytes 5013504 | tf_op jit(solution)/shard_map/inner_leaving/pallas_call | solution.py:30
  92.7 2.4 %collective-permute-done.32 = bf16[672,256]{1,0:T(8,128)(2,1)S(1)} collective-permute-done((bf16[672,256]{1,0:T(8,128)(2,1)S(1)}, bf16[672,256]{1,0:T(8,128)(2,1)S(1)}, u32[]{:S(2)}, u32[]{:S(2)}) %collective-permute-start.32) | collective-permute-done | bytes 344096 | tf_op jit(solution)/shard_map/ppermute | solution.py:228
  95.0 1.8 %collective-permute-start.23 = (bf16[672,256]{1,0:T(8,128)(2,1)}, bf16[672,256]{1,0:T(8,128)(2,1)S(1)}, u32[]{:S(2)}, u32[]{:S(2)}) collective-permute-start(bf16[672,256]{1,0:T(8,128)(2,1)} %get-tuple-element.144), channel_id=1, source_target_pairs={{0,2},{1,3},{2,0},{3,1},{4,6},{5,7},{6,4},{7,5},{8,10},{9,11},{10,... | collective-permute-start | bytes 1032200 | tf_op jit(solution)/shard_map/ppermute | solution.py:228
  96.9 1.6 %collective-permute-start.22 = (bf16[672,256]{1,0:T(8,128)(2,1)S(1)}, bf16[672,256]{1,0:T(8,128)(2,1)S(1)}, u32[]{:S(2)}, u32[]{:S(2)}) collective-permute-start(bf16[672,256]{1,0:T(8,128)(2,1)S(1)} %copy-done.14), channel_id=1, source_target_pairs={{0,1},{1,0},{2,3},{3,2},{4,5},{5,4},{6,7},{7,6},{8,9},{9,8},{10,11... | collective-permute-start | bytes 1032200 | tf_op jit(solution)/shard_map/ppermute | solution.py:228
  98.5 2.3 %split.3 = (bf16[192,512]{1,0:T(8,128)(2,1)}, bf16[192,512]{1,0:T(8,128)(2,1)}, bf16[192,512]{1,0:T(8,128)(2,1)}, bf16[192,512]{1,0:T(8,128)(2,1)}) custom-call(bf16[768,512]{1,0:T(8,128)(2,1)} %get-tuple-element.146.keep_ref, bf16[768,512]{1,0:T(8,128)(2,1)} %copy-done.1), custom_call_target="tpu_custom_call" | custom-call | bytes 2359296 | tf_op jit(solution)/shard_map/split/pallas_call | solution.py:30
  100.8 4.2 %inner_staying.1 = (bf16[672,256]{1,0:T(8,128)(2,1)}, bf16[672,256]{1,0:T(8,128)(2,1)}, bf16[672,256]{1,0:T(8,128)(2,1)}, bf16[672,256]{1,0:T(8,128)(2,1)}) custom-call(bf16[1344,768]{1,0:T(8,128)(2,1)} %get-tuple-element.152.units_ref, bf16[768,1024]{1,0:T(8,128)(2,1)} %get-tuple-element.153.rows_ref), custom_call_target="tpu_custom_call" | custom-call | flops 1056964608 | bytes 5013504 | tf_op jit(solution)/shard_map/inner_staying/pallas_call | solution.py:30
  105.0 3.9 %collective-permute-start.26 = (bf16[192,512]{1,0:T(8,128)(2,1)S(1)}, bf16[192,512]{1,0:T(8,128)(2,1)S(1)}, u32[]{:S(2)}, u32[]{:S(2)}) collective-permute-start(bf16[192,512]{1,0:T(8,128)(2,1)S(1)} %copy-done.25), channel_id=1, source_target_pairs={{0,24},{8,0},{16,8},{24,16},{1,25},{9,1},{17,9},{25,17},{2,26},{10... | collective-permute-start | bytes 589832 | tf_op jit(solution)/shard_map/ppermute | solution.py:224
  111.6 1.5 %collective-permute-start.28 = (bf16[192,512]{1,0:T(8,128)(2,1)S(1)}, bf16[192,512]{1,0:T(8,128)(2,1)S(1)}, u32[]{:S(2)}, u32[]{:S(2)}) collective-permute-start(bf16[192,512]{1,0:T(8,128)(2,1)S(1)} %copy-done.19), channel_id=1, source_target_pairs={{0,8},{8,16},{16,24},{24,0},{1,9},{9,17},{17,25},{25,1},{2,10},{10... | collective-permute-start | bytes 589832 | tf_op jit(solution)/shard_map/ppermute | solution.py:224
  113.2 2.9 %combine.2 = (f32[256,512]{1,0:T(8,128)}, bf16[256,512]{1,0:T(8,128)(2,1)}) custom-call(f32[256,128]{1,0:T(8,128)} %get-tuple-element.91.meta_ref, bf16[192,512]{1,0:T(8,128)(2,1)} %get-tuple-element.158.refs_0_, bf16[192,512]{1,0:T(8,128)(2,1)} %copy-done.8, bf16[192,512]{1,0:T(8,128)(2,1)} %copy-done.9, bf16[192,512]{1,0:T(8,128)(2,1)} %copy-done.10), custom_call_target="tpu_custom_call" | custom-call | flops 201326592 | bytes 1703936 | tf_op jit(solution)/shard_map/combine/pallas_call | solution.py:30
  116.2 9.5 %collective-permute-done.27.refs_2_ = bf16[192,512]{1,0:T(8,128)(2,1)S(1)} collective-permute-done((bf16[192,512]{1,0:T(8,128)(2,1)S(1)}, bf16[192,512]{1,0:T(8,128)(2,1)S(1)}, u32[]{:S(2)}, u32[]{:S(2)}) %collective-permute-start.27) | collective-permute-done | bytes 196640 | tf_op jit(solution)/shard_map/ppermute | solution.py:224
  127.5 2.6 %combine.3 = (f32[256,512]{1,0:T(8,128)}, bf16[256,512]{1,0:T(8,128)(2,1)}) custom-call(f32[256,128]{1,0:T(8,128)} %get-tuple-element.91.meta_ref, bf16[192,512]{1,0:T(8,128)(2,1)} %get-tuple-element.164.refs_0_, bf16[192,512]{1,0:T(8,128)(2,1)} %copy-done.11, bf16[192,512]{1,0:T(8,128)(2,1)} %copy-done.12, bf16[192,512]{1,0:T(8,128)(2,1)} %copy-done.13), custom_call_target="tpu_custom_call" | custom-call | flops 201326592 | bytes 1703936 | tf_op jit(solution)/shard_map/combine/pallas_call | solution.py:30
  132.2 2.2 %join.2 = f32[256,1024]{1,0:T(8,128)} custom-call(f32[256,512]{1,0:T(8,128)} %get-tuple-element.162.mine_ref, bf16[256,512]{1,0:T(8,128)(2,1)} %copy-done.6), custom_call_target="tpu_custom_call" | custom-call | bytes 1835008 | tf_op jit(solution)/shard_map/join/pallas_call | solution.py:30
  135.0 2.2 %join.3 = f32[256,1024]{1,0:T(8,128)} custom-call(f32[256,512]{1,0:T(8,128)} %get-tuple-element.168.mine_ref, bf16[256,512]{1,0:T(8,128)(2,1)} %copy-done.7), custom_call_target="tpu_custom_call" | custom-call | bytes 1835008 | tf_op jit(solution)/shard_map/join/pallas_call | solution.py:30
  (130 shorter events, 21.0 us)
Async XLA Ops:
  4.2 11.1 %collective-permute-start.3 = (bf16[192,512]{1,0:T(8,128)(2,1)}, bf16[192,512]{1,0:T(8,128)(2,1)S(1)}, u32[]{:S(2)}, u32[]{:S(2)}) collective-permute-start(bf16[192,512]{1,0:T(8,128)(2,1)} %get-tuple-element.96), channel_id=1, source_target_pairs={{0,8},{8,16},{16,24},{24,0},{1,9},{9,17},{17,25},{25,1},{2,10},{10... | collective-permute-start | bytes 589832 | tf_op jit(solution)/shard_map/ppermute | solution.py:224
  7.3 15.7 %collective-permute-start.4 = (bf16[192,512]{1,0:T(8,128)(2,1)}, bf16[192,512]{1,0:T(8,128)(2,1)S(1)}, u32[]{:S(2)}, u32[]{:S(2)}) collective-permute-start(bf16[192,512]{1,0:T(8,128)(2,1)} %get-tuple-element.97), channel_id=1, source_target_pairs={{0,16},{8,24},{16,0},{24,8},{1,17},{9,25},{17,1},{25,9},{2,18},{10... | collective-permute-start | bytes 589832 | tf_op jit(solution)/shard_map/ppermute | solution.py:224
  9.9 13.1 %collective-permute-start.5 = (bf16[192,512]{1,0:T(8,128)(2,1)}, bf16[192,512]{1,0:T(8,128)(2,1)S(1)}, u32[]{:S(2)}, u32[]{:S(2)}) collective-permute-start(bf16[192,512]{1,0:T(8,128)(2,1)} %get-tuple-element.98), channel_id=1, source_target_pairs={{0,24},{8,0},{16,8},{24,16},{1,25},{9,1},{17,9},{25,17},{2,26},{10... | collective-permute-start | bytes 589832 | tf_op jit(solution)/shard_map/ppermute | solution.py:224
  23.0 6.9 %collective-permute-start.6 = (bf16[192,512]{1,0:T(8,128)(2,1)S(1)}, bf16[192,512]{1,0:T(8,128)(2,1)S(1)}, u32[]{:S(2)}, u32[]{:S(2)}) collective-permute-start(bf16[192,512]{1,0:T(8,128)(2,1)S(1)} %collective-permute-done.3.refs_0_), channel_id=1, source_target_pairs={{0,4},{4,0},{1,5},{5,1},{2,6},{6,2},{3,7},{7,3},{8,12},{12,8},{9,1... | collective-permute-start | bytes 589832 | tf_op jit(solution)/shard_map/ppermute | solution.py:228
  23.0 7.5 %collective-permute-start.7 = (bf16[192,512]{1,0:T(8,128)(2,1)S(1)}, bf16[192,512]{1,0:T(8,128)(2,1)S(1)}, u32[]{:S(2)}, u32[]{:S(2)}) collective-permute-start(bf16[192,512]{1,0:T(8,128)(2,1)S(1)} %collective-permute-done.4.refs_1_), channel_id=1, source_target_pairs={{0,4},{4,0},{1,5},{5,1},{2,6},{6,2},{3,7},{7,3},{8,12},{12,8},{9,1... | collective-permute-start | bytes 589832 | tf_op jit(solution)/shard_map/ppermute | solution.py:228
  23.5 7.0 %collective-permute-start.8 = (bf16[192,512]{1,0:T(8,128)(2,1)S(1)}, bf16[192,512]{1,0:T(8,128)(2,1)S(1)}, u32[]{:S(2)}, u32[]{:S(2)}) collective-permute-start(bf16[192,512]{1,0:T(8,128)(2,1)S(1)} %collective-permute-done.5.refs_2_), channel_id=1, source_target_pairs={{0,4},{4,0},{1,5},{5,1},{2,6},{6,2},{3,7},{7,3},{8,12},{12,8},{9,1... | collective-permute-start | bytes 589832 | tf_op jit(solution)/shard_map/ppermute | solution.py:228
  23.6 20.6 %collective-permute-start = (bf16[192,512]{1,0:T(8,128)(2,1)}, bf16[192,512]{1,0:T(8,128)(2,1)S(1)}, u32[]{:S(2)}, u32[]{:S(2)}) collective-permute-start(bf16[192,512]{1,0:T(8,128)(2,1)} %get-tuple-element.92), channel_id=1, source_target_pairs={{0,8},{8,16},{16,24},{24,0},{1,9},{9,17},{17,25},{25,1},{2,10},{10... | collective-permute-start | bytes 589832 | tf_op jit(solution)/shard_map/ppermute | solution.py:224
  28.2 16.0 %collective-permute-start.1 = (bf16[192,512]{1,0:T(8,128)(2,1)}, bf16[192,512]{1,0:T(8,128)(2,1)S(1)}, u32[]{:S(2)}, u32[]{:S(2)}) collective-permute-start(bf16[192,512]{1,0:T(8,128)(2,1)} %get-tuple-element.93), channel_id=1, source_target_pairs={{0,16},{8,24},{16,0},{24,8},{1,17},{9,25},{17,1},{25,9},{2,18},{10... | collective-permute-start | bytes 589832 | tf_op jit(solution)/shard_map/ppermute | solution.py:224
  29.9 14.3 %collective-permute-start.2 = (bf16[192,512]{1,0:T(8,128)(2,1)}, bf16[192,512]{1,0:T(8,128)(2,1)S(1)}, u32[]{:S(2)}, u32[]{:S(2)}) collective-permute-start(bf16[192,512]{1,0:T(8,128)(2,1)} %get-tuple-element.94), channel_id=1, source_target_pairs={{0,24},{8,0},{16,8},{24,16},{1,25},{9,1},{17,9},{25,17},{2,26},{10... | collective-permute-start | bytes 589832 | tf_op jit(solution)/shard_map/ppermute | solution.py:224
  44.2 12.4 %collective-permute-start.12 = (bf16[768,512]{1,0:T(8,128)(2,1)}, bf16[768,512]{1,0:T(8,128)(2,1)S(1)}, u32[]{:S(2)}, u32[]{:S(2)}) collective-permute-start(bf16[768,512]{1,0:T(8,128)(2,1)} %get-tuple-element.112), channel_id=1, source_target_pairs={{0,4},{4,0},{1,5},{5,1},{2,6},{6,2},{3,7},{7,3},{8,12},{12,8},{9,1... | collective-permute-start | bytes 2359304 | tf_op jit(solution)/shard_map/ppermute | solution.py:228
  44.9 2.5 %collective-permute-start.9 = (bf16[192,512]{1,0:T(8,128)(2,1)S(1)}, bf16[192,512]{1,0:T(8,128)(2,1)S(1)}, u32[]{:S(2)}, u32[]{:S(2)}) collective-permute-start(bf16[192,512]{1,0:T(8,128)(2,1)S(1)} %collective-permute-done.refs_0_), channel_id=1, source_target_pairs={{0,4},{4,0},{1,5},{5,1},{2,6},{6,2},{3,7},{7,3},{8,12},{12,8},{9,1... | collective-permute-start | bytes 589832 | tf_op jit(solution)/shard_map/ppermute | solution.py:228
  52.5 16.1 %collective-permute-start.16 = (bf16[672,256]{1,0:T(8,128)(2,1)}, bf16[672,256]{1,0:T(8,128)(2,1)S(1)}, u32[]{:S(2)}, u32[]{:S(2)}) collective-permute-start(bf16[672,256]{1,0:T(8,128)(2,1)} %get-tuple-element.133), channel_id=1, source_target_pairs={{0,1},{1,0},{2,3},{3,2},{4,5},{5,4},{6,7},{7,6},{8,9},{9,8},{10,11... | collective-permute-start | bytes 1032200 | tf_op jit(solution)/shard_map/ppermute | solution.py:228
  54.0 16.5 %collective-permute-start.15 = (bf16[672,256]{1,0:T(8,128)(2,1)}, bf16[672,256]{1,0:T(8,128)(2,1)S(1)}, u32[]{:S(2)}, u32[]{:S(2)}) collective-permute-start(bf16[672,256]{1,0:T(8,128)(2,1)} %get-tuple-element.132), channel_id=1, source_target_pairs={{0,2},{1,3},{2,0},{3,1},{4,6},{5,7},{6,4},{7,5},{8,10},{9,11},{10,... | collective-permute-start | bytes 1032200 | tf_op jit(solution)/shard_map/ppermute | solution.py:228
  55.5 16.3 %collective-permute-start.14 = (bf16[672,256]{1,0:T(8,128)(2,1)}, bf16[672,256]{1,0:T(8,128)(2,1)S(1)}, u32[]{:S(2)}, u32[]{:S(2)}) collective-permute-start(bf16[672,256]{1,0:T(8,128)(2,1)} %get-tuple-element.131), channel_id=1, source_target_pairs={{0,2},{1,3},{2,0},{3,1},{4,6},{5,7},{6,4},{7,5},{8,10},{9,11},{10,... | collective-permute-start | bytes 1032200 | tf_op jit(solution)/shard_map/ppermute | solution.py:228
  56.0 28.1 %collective-permute-start.13 = (bf16[672,256]{1,0:T(8,128)(2,1)}, bf16[672,256]{1,0:T(8,128)(2,1)S(1)}, u32[]{:S(2)}, u32[]{:S(2)}) collective-permute-start(bf16[672,256]{1,0:T(8,128)(2,1)} %get-tuple-element.130), channel_id=1, source_target_pairs={{0,1},{1,0},{2,3},{3,2},{4,5},{5,4},{6,7},{7,6},{8,9},{9,8},{10,11... | collective-permute-start | bytes 1032200 | tf_op jit(solution)/shard_map/ppermute | solution.py:228
  59.8 24.5 %collective-permute-start.17 = (bf16[192,512]{1,0:T(8,128)(2,1)}, bf16[192,512]{1,0:T(8,128)(2,1)S(1)}, u32[]{:S(2)}, u32[]{:S(2)}) collective-permute-start(bf16[192,512]{1,0:T(8,128)(2,1)} %get-tuple-element.116), channel_id=1, source_target_pairs={{0,24},{8,0},{16,8},{24,16},{1,25},{9,1},{17,9},{25,17},{2,26},{10... | collective-permute-start | bytes 589832 | tf_op jit(solution)/shard_map/ppermute | solution.py:224
  68.6 15.6 %collective-permute-start.18 = (bf16[192,512]{1,0:T(8,128)(2,1)S(1)}, bf16[192,512]{1,0:T(8,128)(2,1)S(1)}, u32[]{:S(2)}, u32[]{:S(2)}) collective-permute-start(bf16[192,512]{1,0:T(8,128)(2,1)S(1)} %copy-done.24), channel_id=1, source_target_pairs={{0,16},{8,24},{16,0},{24,8},{1,17},{9,25},{17,1},{25,9},{2,18},{10... | collective-permute-start | bytes 589832 | tf_op jit(solution)/shard_map/ppermute | solution.py:224
  70.5 13.7 %collective-permute-start.19 = (bf16[192,512]{1,0:T(8,128)(2,1)S(1)}, bf16[192,512]{1,0:T(8,128)(2,1)S(1)}, u32[]{:S(2)}, u32[]{:S(2)}) collective-permute-start(bf16[192,512]{1,0:T(8,128)(2,1)S(1)} %copy-done.21), channel_id=1, source_target_pairs={{0,8},{8,16},{16,24},{24,0},{1,9},{9,17},{17,25},{25,1},{2,10},{10... | collective-permute-start | bytes 589832 | tf_op jit(solution)/shard_map/ppermute | solution.py:224
  84.3 12.6 %collective-permute-start.20 = (bf16[768,512]{1,0:T(8,128)(2,1)}, bf16[768,512]{1,0:T(8,128)(2,1)S(1)}, u32[]{:S(2)}, u32[]{:S(2)}) collective-permute-start(bf16[768,512]{1,0:T(8,128)(2,1)} %get-tuple-element.141), channel_id=1, source_target_pairs={{0,4},{4,0},{1,5},{5,1},{2,6},{6,2},{3,7},{7,3},{8,12},{12,8},{9,1... | collective-permute-start | bytes 2359304 | tf_op jit(solution)/shard_map/ppermute | solution.py:228
  84.4 10.7 %collective-permute-start.32 = (bf16[672,256]{1,0:T(8,128)(2,1)S(1)}, bf16[672,256]{1,0:T(8,128)(2,1)S(1)}, u32[]{:S(2)}, u32[]{:S(2)}) collective-permute-start(bf16[672,256]{1,0:T(8,128)(2,1)S(1)} %add_convert_fusion.4), channel_id=1, source_target_pairs={{0,2},{1,3},{2,0},{3,1},{4,6},{5,7},{6,4},{7,5},{8,10},{9,11},{10,... | collective-permute-start | bytes 1032200 | tf_op jit(solution)/shard_map/ppermute | solution.py:228
  85.9 40.3 %collective-permute-start.33 = (bf16[672,256]{1,0:T(8,128)(2,1)S(1)}, bf16[672,256]{1,0:T(8,128)(2,1)S(1)}, u32[]{:S(2)}, u32[]{:S(2)}) collective-permute-start(bf16[672,256]{1,0:T(8,128)(2,1)S(1)} %add_convert_fusion.5), channel_id=1, source_target_pairs={{0,1},{1,0},{2,3},{3,2},{4,5},{5,4},{6,7},{7,6},{8,9},{9,8},{10,11... | collective-permute-start | bytes 1032200 | tf_op jit(solution)/shard_map/ppermute | solution.py:228
  91.6 13.4 %collective-permute-start.25 = (bf16[672,256]{1,0:T(8,128)(2,1)}, bf16[672,256]{1,0:T(8,128)(2,1)S(1)}, u32[]{:S(2)}, u32[]{:S(2)}) collective-permute-start(bf16[672,256]{1,0:T(8,128)(2,1)} %get-tuple-element.142), channel_id=1, source_target_pairs={{0,1},{1,0},{2,3},{3,2},{4,5},{5,4},{6,7},{7,6},{8,9},{9,8},{10,11... | collective-permute-start | bytes 1032200 | tf_op jit(solution)/shard_map/ppermute | solution.py:228
  92.2 17.8 %collective-permute-start.24 = (bf16[672,256]{1,0:T(8,128)(2,1)}, bf16[672,256]{1,0:T(8,128)(2,1)S(1)}, u32[]{:S(2)}, u32[]{:S(2)}) collective-permute-start(bf16[672,256]{1,0:T(8,128)(2,1)} %get-tuple-element.143), channel_id=1, source_target_pairs={{0,2},{1,3},{2,0},{3,1},{4,6},{5,7},{6,4},{7,5},{8,10},{9,11},{10,... | collective-permute-start | bytes 1032200 | tf_op jit(solution)/shard_map/ppermute | solution.py:228
  95.0 16.6 %collective-permute-start.23 = (bf16[672,256]{1,0:T(8,128)(2,1)}, bf16[672,256]{1,0:T(8,128)(2,1)S(1)}, u32[]{:S(2)}, u32[]{:S(2)}) collective-permute-start(bf16[672,256]{1,0:T(8,128)(2,1)} %get-tuple-element.144), channel_id=1, source_target_pairs={{0,2},{1,3},{2,0},{3,1},{4,6},{5,7},{6,4},{7,5},{8,10},{9,11},{10,... | collective-permute-start | bytes 1032200 | tf_op jit(solution)/shard_map/ppermute | solution.py:228
  96.9 19.2 %collective-permute-start.22 = (bf16[672,256]{1,0:T(8,128)(2,1)S(1)}, bf16[672,256]{1,0:T(8,128)(2,1)S(1)}, u32[]{:S(2)}, u32[]{:S(2)}) collective-permute-start(bf16[672,256]{1,0:T(8,128)(2,1)S(1)} %copy-done.14), channel_id=1, source_target_pairs={{0,1},{1,0},{2,3},{3,2},{4,5},{5,4},{6,7},{7,6},{8,9},{9,8},{10,11... | collective-permute-start | bytes 1032200 | tf_op jit(solution)/shard_map/ppermute | solution.py:228
  105.0 11.2 %collective-permute-start.26 = (bf16[192,512]{1,0:T(8,128)(2,1)S(1)}, bf16[192,512]{1,0:T(8,128)(2,1)S(1)}, u32[]{:S(2)}, u32[]{:S(2)}) collective-permute-start(bf16[192,512]{1,0:T(8,128)(2,1)S(1)} %copy-done.25), channel_id=1, source_target_pairs={{0,24},{8,0},{16,8},{24,16},{1,25},{9,1},{17,9},{25,17},{2,26},{10... | collective-permute-start | bytes 589832 | tf_op jit(solution)/shard_map/ppermute | solution.py:224
  109.9 15.8 %collective-permute-start.27 = (bf16[192,512]{1,0:T(8,128)(2,1)S(1)}, bf16[192,512]{1,0:T(8,128)(2,1)S(1)}, u32[]{:S(2)}, u32[]{:S(2)}) collective-permute-start(bf16[192,512]{1,0:T(8,128)(2,1)S(1)} %copy-done.22), channel_id=1, source_target_pairs={{0,16},{8,24},{16,0},{24,8},{1,17},{9,25},{17,1},{25,9},{2,18},{10... | collective-permute-start | bytes 589832 | tf_op jit(solution)/shard_map/ppermute | solution.py:224
  111.6 14.1 %collective-permute-start.28 = (bf16[192,512]{1,0:T(8,128)(2,1)S(1)}, bf16[192,512]{1,0:T(8,128)(2,1)S(1)}, u32[]{:S(2)}, u32[]{:S(2)}) collective-permute-start(bf16[192,512]{1,0:T(8,128)(2,1)S(1)} %copy-done.19), channel_id=1, source_target_pairs={{0,8},{8,16},{16,24},{24,0},{1,9},{9,17},{17,25},{25,1},{2,10},{10... | collective-permute-start | bytes 589832 | tf_op jit(solution)/shard_map/ppermute | solution.py:224
  125.7 11.5 %collective-permute-start.30 = (bf16[672,256]{1,0:T(8,128)(2,1)S(1)}, bf16[672,256]{1,0:T(8,128)(2,1)S(1)}, u32[]{:S(2)}, u32[]{:S(2)}) collective-permute-start(bf16[672,256]{1,0:T(8,128)(2,1)S(1)} %add_convert_fusion), channel_id=1, source_target_pairs={{0,2},{1,3},{2,0},{3,1},{4,6},{5,7},{6,4},{7,5},{8,10},{9,11},{10,... | collective-permute-start | bytes 1032200 | tf_op jit(solution)/shard_map/ppermute | solution.py:228
  126.4 5.1 %collective-permute-start.21 = (bf16[256,512]{1,0:T(8,128)(2,1)S(1)}, bf16[256,512]{1,0:T(8,128)(2,1)S(1)}, u32[]{:S(2)}, u32[]{:S(2)}) collective-permute-start(bf16[256,512]{1,0:T(8,128)(2,1)S(1)} %copy-done.15), channel_id=1, source_target_pairs={{0,4},{4,0},{1,5},{5,1},{2,6},{6,2},{3,7},{7,3},{8,12},{12,8},{9,1... | collective-permute-start | bytes 786440 | tf_op jit(solution)/shard_map/ppermute | solution.py:228
  126.4 10.8 %collective-permute-start.31 = (bf16[672,256]{1,0:T(8,128)(2,1)S(1)}, bf16[672,256]{1,0:T(8,128)(2,1)S(1)}, u32[]{:S(2)}, u32[]{:S(2)}) collective-permute-start(bf16[672,256]{1,0:T(8,128)(2,1)S(1)} %add_convert_fusion.1), channel_id=1, source_target_pairs={{0,1},{1,0},{2,3},{3,2},{4,5},{5,4},{6,7},{7,6},{8,9},{9,8},{10,11... | collective-permute-start | bytes 1032200 | tf_op jit(solution)/shard_map/ppermute | solution.py:228
  130.1 4.2 %collective-permute-start.29 = (bf16[256,512]{1,0:T(8,128)(2,1)}, bf16[256,512]{1,0:T(8,128)(2,1)S(1)}, u32[]{:S(2)}, u32[]{:S(2)}) collective-permute-start(bf16[256,512]{1,0:T(8,128)(2,1)} %get-tuple-element.169), channel_id=1, source_target_pairs={{0,4},{4,0},{1,5},{5,1},{2,6},{6,2},{3,7},{7,3},{8,12},{12,8},{9,1... | collective-permute-start | bytes 786440 | tf_op jit(solution)/shard_map/ppermute | solution.py:228
  (35 other events, 164.8 us)

commit v3 on v2

--- a/solution.py
+++ b/solution.py
@@ -11,7 +11,8 @@
 F32 = jnp.float32
 ROW_TILE = 16
 TILE = 256
-VMEM_BYTES = 56 * 1024 * 1024
+VMEM_BYTES = 24 * 1024 * 1024
+COST = 64
 MATMUL = (((1,), (0,)), ((), ()))
 CONTRACT_LAST = (((1,), (1,)), ((), ()))
 CONTRACT_FIRST = (((0,), (0,)), ((), ()))
@@ -29,14 +30,14 @@
     moved = sum(x.size * x.dtype.itemsize for x in (*operands, *outs))
     return pl.pallas_call(
         body,
-        out_shape=tuple(outs),
+        out_shape=tuple(pltpu.VMEM(x.shape, x.dtype) for x in outs),
         in_specs=[pl.BlockSpec(memory_space=pltpu.VMEM)] * len(operands),
         out_specs=tuple([pl.BlockSpec(memory_space=pltpu.VMEM)] * len(outs)),
         scratch_shapes=list(scratch),
         compiler_params=pltpu.CompilerParams(vmem_limit_bytes=VMEM_BYTES),
-        cost_estimate=pl.CostEstimate(flops=flops, bytes_accessed=moved, transcendentals=0),
+        cost_estimate=pl.CostEstimate(flops=flops // COST, bytes_accessed=moved // COST, transcendentals=0),
         name=name,
-    )(*operands)
+    )(*[pltpu.with_memory_space_constraint(x, pltpu.VMEM) for x in operands])
 
 
 def window(index, width):
@@ -86,8 +87,7 @@
     meta = jnp.zeros(meta_ref.shape, F32)
     for k in range(top):
         rank = jnp.sum(jnp.where(named[k], before, 0.0), axis=1, keepdims=True)
-        shift = routes[:, k : k + 1] - me
-        shift = jnp.where(shift < 0, shift + owners, shift)
+        shift = routes[:, k : k + 1] ^ me
         slot = (shift * capacity).astype(F32) + rank
         weight = jnp.sum(
             jnp.where(index[:, k : k + 1] == level, table_ref[...], 0.0), axis=1, keepdims=True
@@ -127,44 +127,42 @@
         full_ref[rows, window(1 - core, half)] = b[...]
 
 
-def to_halves(rows_ref, weight_ref, keep_ref, give_ref):
+def hidden_body(remote, own, *refs):
+    mine, other = refs[:remote], refs[remote : 2 * remote]
+    inner_ref, x_ref, positive_ref, hidden_ref = refs[2 * remote :]
+    assemble(x_ref, own, mine, other)
+
+    def step(units):
+        positive = jnp.maximum(mxu(inner_ref[units, :], x_ref[...], CONTRACT_LAST), 0.0)
+        positive_ref[units, :] = positive.astype(BF16)
+        hidden_ref[units, :] = (positive * positive).astype(BF16)
+
+    over_tiles(inner_ref.shape[0], step)
+
+
+def d_act_body(g_ref, positive_ref, outer_ref, d_act_ref):
+    def step(units):
+        d_hidden = mxu(outer_ref[units, :], g_ref[...], CONTRACT_LAST)
+        d_act_ref[units, :] = (d_hidden * 2.0 * positive_ref[units, :].astype(F32)).astype(BF16)
+
+    over_tiles(outer_ref.shape[0], step)
+
+
+def rows_body(units_ref, weight_ref, keep_ref, give_ref, turned):
+    def turn(units):
+        turned[:, units] = units_ref[units, :].T
+
+    over_tiles(units_ref.shape[0], turn)
     core = lax.axis_index("cuts")
     half = keep_ref.shape[1]
     for owner, ref in ((1 - core, give_ref), (core, keep_ref)):
 
         def step(i, carry, owner=owner, ref=ref):
             features = window(owner * (half // TILE) + i, TILE)
-            ref[:, window(i, TILE)] = mxu(rows_ref[...], weight_ref[:, features]).astype(BF16)
+            ref[:, window(i, TILE)] = mxu(turned[...], weight_ref[:, features]).astype(BF16)
             return carry
 
         lax.fori_loop(0, half // TILE, step, 0)
-
-
-def forward_body(remote, own, *refs):
-    mine, other = refs[:remote], refs[remote : 2 * remote]
-    inner_ref, outer_ref, x_ref, positive_ref, hidden_ref, keep_ref, give_ref, turned = refs[2 * remote :]
-    assemble(x_ref, own, mine, other)
-
-    def activate(units):
-        positive = jnp.maximum(mxu(inner_ref[units, :], x_ref[...], CONTRACT_LAST), 0.0)
-        positive_ref[units, :] = positive.astype(BF16)
-        hidden = (positive * positive).astype(BF16)
-        hidden_ref[units, :] = hidden
-        turned[:, units] = hidden.T
-
-    over_tiles(inner_ref.shape[0], activate)
-    to_halves(turned, outer_ref, keep_ref, give_ref)
-
-
-def backward_body(g_ref, positive_ref, inner_ref, outer_ref, d_act_ref, keep_ref, give_ref, turned):
-    def step(units):
-        d_hidden = mxu(outer_ref[units, :], g_ref[...], CONTRACT_LAST)
-        d_act = (d_hidden * 2.0 * positive_ref[units, :].astype(F32)).astype(BF16)
-        d_act_ref[units, :] = d_act
-        turned[:, units] = d_act.T
-
-    over_tiles(outer_ref.shape[0], step)
-    to_halves(turned, inner_ref, keep_ref, give_ref)
 
 
 def split_body(keep_ref, came_ref, *outs):
@@ -180,10 +178,12 @@
 
 def pieces(keys, units_ref, rows_ref, outs):
     me = lax.axis_index("dp")
-    for (block, part), ref in zip(keys, outs, strict=True):
-        rows, width = ref.shape
-        features = rows_ref[:, window(me ^ block, width)]
-        ref[...] = mxu(units_ref[part * rows : (part + 1) * rows, :], features).astype(BF16)
+    for part, (blocks, ref) in enumerate(zip(keys, outs, strict=True)):
+        rows = ref.shape[0] // len(blocks)
+        for i, block in enumerate(blocks):
+            features = rows_ref[:, window(me ^ block, ref.shape[1])]
+            units = units_ref[part * rows : (part + 1) * rows, :]
+            ref[i * rows : (i + 1) * rows, :] = mxu(units, features).astype(BF16)
 
 
 def grad_body(keys, units_ref, rows_ref, *outs):
@@ -219,22 +219,12 @@
     out_ref[:, window(1 - core, half)] = other_ref[...].astype(F32)
 
 
-def shifted(x, axis, shift):
-    size = lax.axis_size(axis)
-    return lax.ppermute(x, axis, [(i, (i + shift) % size) for i in range(size)])
-
-
 def partner(x, axis, bit):
     return lax.ppermute(x, axis, [(i, i ^ bit) for i in range(lax.axis_size(axis))])
 
 
 def after(values, *earlier):
     return lax.optimization_barrier((values, earlier))[0]
-
-
-def halve(blocks, bit, dtype):
-    came = {r ^ bit: partner(blocks[r], "dp", bit) for r in sorted(blocks, reverse=True) if r & bit}
-    return {r: (blocks[r].astype(F32) + came[r].astype(F32)).astype(dtype) for r in came}
 
 
 def shards(tokens, cotangent, routes, combine_index, combine_table, w_in, w_out):
@@ -249,17 +239,22 @@
     units = outer.shape[0]
     bits = [1 << i for i in range(groups.bit_length() - 1)]
     orders = (bits, bits[::-1])
-    piece = shape(units // 2, features // groups)
-    keys = [(r, part) for r in reversed(range(groups)) for part in range(2)]
-    leaving = [(r, part) for r, part in keys if r & orders[part][0]]
-    staying = [key for key in keys if key not in leaving]
+    leaving = [[r for r in range(groups) if r & order[0]] for order in orders]
+    staying = [[r ^ order[0] for r in blocks] for order, blocks in zip(orders, leaving, strict=True)]
+    part_rows = units // 2
+    piece = shape(part_rows * groups // 2, features // groups)
     work = 2 * slots * features * units
 
     def across_cores(chunks):
         return [partner(x, "cuts", 1) for x in chunks]
 
-    def over_experts(chunks, sign):
-        return [shifted(x, "expert", sign * s) for s, x in enumerate(chunks, 1)]
+    def over_experts(chunks):
+        return [partner(x, "expert", s) for s, x in enumerate(chunks, 1)]
+
+    def times_weight(units_rows, weight, name):
+        return local(
+            rows_body, [shape(slots, half)] * 2, [units_rows, weight], work, name, [pltpu.VMEM((slots, units), BF16)]
+        )
 
     def split(keep, came):
         return local(split_body, [shape(capacity, half)] * owners, [keep, came], 0, "split")
@@ -276,12 +271,21 @@
     def join(wide, came):
         return local(join_body, [shape(count, features, F32)], [wide, came], 0, "join")[0]
 
-    def halved(pieces, step, dtype=BF16):
-        out = {}
-        for part, order in enumerate(orders):
-            mine = {r: x for (r, p), x in pieces.items() if p == part}
-            out |= {(r, part): x for r, x in halve(mine, order[step], dtype).items()}
-        return out
+    def grads(keys, units_rows, rows, name):
+        return local(functools.partial(grad_body, keys), [piece] * 2, [units_rows, rows], work // 2, name)
+
+    def added(kept, came, dtype=BF16):
+        return (kept.astype(F32) + came.astype(F32)).astype(dtype)
+
+    def block(stack, i):
+        return stack[i * part_rows : (i + 1) * part_rows]
+
+    def halvings(blocks, order):
+        for bit in order:
+            came = {r ^ bit: partner(blocks[r], "dp", bit) for r in blocks if r & bit}
+            dtype = F32 if bit == order[-1] else BF16
+            blocks = {r: added(blocks[r], came[r], dtype) for r in came}
+        return blocks[0]
 
     meta, own, *sends = local(
         functools.partial(route_body, owners, capacity),
@@ -290,7 +294,7 @@
         2 * count * slots * features,
         "route",
     )
-    mine = over_experts(sends, 1)
+    mine = over_experts(sends)
     grad_own, *grad_sends = local(
         functools.partial(weigh_body, top, capacity),
         [shape(capacity, features)] + [shape(capacity, half)] * remote,
@@ -298,73 +302,75 @@
         4 * count * slots * features,
         "weigh",
     )
-    grad_mine = over_experts(grad_sends, 1)
+    grad_mine = over_experts(grad_sends)
     mine = after(mine, grad_sends)
     other = across_cores(mine)
-    arrived, positive, hidden, keep, give = local(
-        functools.partial(forward_body, remote),
-        [shape(slots, features), shape(units, slots), shape(units, slots)] + [shape(slots, half)] * 2,
-        [own, *mine, *other, inner, outer],
-        2 * work,
-        "forward",
-        [pltpu.VMEM((slots, units), BF16)],
-    )
+    arrived, positive, hidden = local(
+        functools.partial(hidden_body, remote),
+        [shape(slots, features), shape(units, slots), shape(units, slots)],
+        [own, *mine, *other, inner],
+        work,
+        "hidden",
+    )
+    keep, give = times_weight(hidden, outer, "rows")
     grad_mine, hidden, keep, give = after((grad_mine, hidden, keep, give))
     came = partner(give, "cuts", 1)
     grad_other = across_cores(grad_mine)
-    grad_rows, *out = local(
+    grad_rows, *outer_sent = local(
         functools.partial(first_grad_body, leaving, remote),
-        [shape(slots, features)] + [piece] * len(leaving),
+        [shape(slots, features)] + [piece] * 2,
         [grad_own, *grad_mine, *grad_other, hidden],
         work // 2,
         "outer_leaving",
     )
-    outer_pieces = dict(zip(leaving, out, strict=True))
+    outer_came = [partner(x, "dp", order[0]) for x, order in zip(outer_sent, orders, strict=True)]
     keep, came = after((keep, came), grad_rows)
     chunks = split(keep, came)
-    returned = [chunks[0]] + over_experts(chunks[1:], -1)
-    hidden, grad_rows = after((hidden, grad_rows), chunks)
-    out = local(
-        functools.partial(grad_body, staying), [piece] * len(staying), [hidden, grad_rows], work // 2, "outer_staying"
-    )
-    outer_pieces |= dict(zip(staying, out, strict=True))
-    grad_rows, positive = after((grad_rows, positive), out)
-    d_act, grad_keep, grad_give = local(
-        backward_body,
-        [shape(units, slots)] + [shape(slots, half)] * 2,
-        [grad_rows, positive, inner, outer],
-        2 * work,
-        "backward",
-        [pltpu.VMEM((slots, units), BF16)],
-    )
-    outer_pieces = halved(outer_pieces, 0)
-    d_act, grad_give, outer_pieces, returned = after((d_act, grad_give, outer_pieces, returned))
+    returned = [chunks[0]] + over_experts(chunks[1:])
+    grad_rows, positive = after((grad_rows, positive), chunks)
+    (d_act,) = local(
+        d_act_body, [shape(units, slots)], [grad_rows, positive, outer], work, "d_act"
+    )
+    inner_sent = grads(leaving, d_act, arrived, "inner_leaving")
+    hidden, grad_rows = after((hidden, grad_rows), inner_sent)
+    outer_kept = grads(staying, hidden, grad_rows, "outer_staying")
+    d_act_late = after(d_act, outer_kept)
+    grad_keep, grad_give = times_weight(d_act_late, inner, "grad_rows")
+    grad_give, outer_came, outer_kept, returned, d_act, arrived = after(
+        (grad_give, outer_came, outer_kept, returned, d_act, arrived)
+    )
     grad_came = partner(grad_give, "cuts", 1)
-    out = local(
-        functools.partial(grad_body, leaving), [piece] * len(leaving), [d_act, arrived], work // 2, "inner_leaving"
-    )
-    inner_pieces = dict(zip(leaving, out, strict=True))
-    grad_keep, grad_came = after((grad_keep, grad_came), out)
+    inner_kept = grads(staying, d_act, arrived, "inner_staying")
+    outer_own, mixed = [], []
+    for part in range(2):
+        sums = [added(block(outer_kept[part], i), block(outer_came[part], i)) for i in range(groups // 2)]
+        outer_own.append(dict(zip(staying[part], sums, strict=True)))
+    for part in range(2):
+        other = outer_own[1 - part]
+        moving = [other[r] for r in other if r & orders[part][0]]
+        got = partner(jnp.concatenate([*moving, inner_sent[part]], axis=0), "dp", orders[part][0])
+        mixed.append(got)
     chunks = split(grad_keep, grad_came)
-    grad_returned = [chunks[0]] + over_experts(chunks[1:], -1)
-    d_act, arrived = after((d_act, arrived), chunks)
-    out = local(
-        functools.partial(grad_body, staying), [piece] * len(staying), [d_act, arrived], work // 2, "inner_staying"
-    )
-    inner_pieces |= dict(zip(staying, out, strict=True))
-    returned = after(returned, out)
+    grad_returned = [chunks[0]] + over_experts(chunks[1:])
     wide, narrow = combine(returned, True)
     layer_out = join(wide, partner(narrow, "cuts", 1))
-    outer_pieces = halved(outer_pieces, 1, F32)
-    inner_pieces = halved(inner_pieces, 0)
-    inner_pieces, grad_returned = after((inner_pieces, grad_returned), wide)
+    mixed, inner_kept, grad_returned = after((mixed, inner_kept, grad_returned))
+    outer_sums, inner_sums = [], []
+    for part, order in enumerate(orders):
+        bit = orders[1 - part][0]
+        mine = [r for r in outer_own[part] if not r & bit]
+        rest = {r: added(outer_own[part][r], block(mixed[1 - part], i), F32) for i, r in enumerate(mine)}
+        outer_sums.append(halvings(rest, order[2:]) if order[2:] else rest[0])
+        start = len(mine)
+        sums = {
+            r: added(block(inner_kept[part], i), block(mixed[part], start + i)) for i, r in enumerate(staying[part])
+        }
+        inner_sums.append(halvings(sums, order[1:]))
+    grad_out = jnp.concatenate(outer_sums, axis=0)
+    grad_in = jnp.concatenate(inner_sums, axis=0).T
     wide, narrow = combine(grad_returned, False)
     d_tokens = join(wide, partner(narrow, "cuts", 1))
-    inner_pieces = halved(inner_pieces, 1, F32)
-    grad_in, grad_out = (
-        jnp.concatenate([p[0, 0], p[0, 1]], axis=0) for p in (inner_pieces, outer_pieces)
-    )
-    return (layer_out, d_tokens, grad_in.T[None], grad_out[None])
+    return (layer_out, d_tokens, grad_in[None], grad_out[None])
 
 
 def solution(mesh):

time: 139 us -> 115 us (0.83)
  Pallas kernels: 62.9 us -> 25.1 us
  waiting for transfers between devices: 22.8 us -> 42.8 us
  starting transfers between devices: 40.8 us -> 33.2 us
  local copies, waits for them, and re-layouts: 3.82 us -> 8.72 us
  other arithmetic: 7.25 us -> 3.26 us
    ppermute x22 -> x28, waiting for transfers between devices: 4.51 us -> 42.8 us  [partner(): lax.ppermute(x, axis, [(i, i ^ bit) for i in range(lax.axis_size(axis))])]
    pallas_call x14 -> x16, Pallas kernels: 62.9 us -> 25.1 us  [local(): pl.pallas_call(body, out_shape=tuple((pltpu.VMEM(x.shape, x.dtype) for x...]
    ppermute x12 -> x0, starting transfers between devices: 25.6 us -> none  [shifted(): return lax.ppermute(x, axis, [(i, (i + shift) % size) for i in range(size)])]
    ppermute x12 -> x0, waiting for transfers between devices: 18.3 us -> none  [shifted(): return lax.ppermute(x, axis, [(i, (i + shift) % size) for i in range(size)])]
    ppermute x22 -> x28, starting transfers between devices: 15.2 us -> 33.2 us  [partner(): lax.ppermute(x, axis, [(i, i ^ bit) for i in range(lax.axis_size(axis))])]
    unnamed x66 -> x18, local copies, waits for them, and re-layouts: 3.82 us -> 8.72 us
    convert_element_type x8 -> x2, other arithmetic: 4.63 us -> 0.17 us  [added(): return (kept.astype(F32) + came.astype(F32)).astype(dtype)]
  transfers between devices with their start and end apart: 34 -> 28, of which waited for: 7 -> 12; matrix products, arithmetic and copies ran while one was open for 4% -> 3% of each run, Pallas kernels for 43% -> 20%
where the time goes in v3:
time: 115 us; the launch traced here: 114 us
  waiting for transfers between devices  42.8 us (37%)
  starting transfers between devices  33.2 us (29%)
  Pallas kernels  25.1 us (22%)
  local copies, waits for them, and re-layouts  8.72 us (8%)
  other arithmetic  3.26 us (3%)
    ppermute x28, waiting for transfers between devices, partner(): lax.ppermute(x, axis, [(i, i ^ bit) for i in range(lax.axis_size(axis))])  42.8 us
    ppermute x28, starting transfers between devices, partner(): lax.ppermute(x, axis, [(i, i ^ bit) for i in range(lax.axis_size(axis))])  33.2 us
    pallas_call x16, Pallas kernels, local(): pl.pallas_call(body, out_shape=tuple((pltpu.VMEM(x.shape, x.dtype) for x...  25.1 us
    unnamed x18, local copies, waits for them, and re-layouts  8.72 us
    broadcast_in_dim x2, other arithmetic, shards(): return (layer_out, d_tokens, grad_in[None], grad_out[None])  2.33 us
  transfers between devices with their start and end apart: 28, of which 12 were waited for; matrix products, arithmetic and copies ran while one was open for 3% of the time, Pallas kernels for 20%

profile of v3, /device:TPU:0, one launch (start us, length us, event | category | flops | bytes accessed | tf_op | source)
XLA Modules:
  0.0 114.0 jit_solution(8404512450684827508)
XLA Ops:
  3.9 1.6 %route.1 = (f32[256,128]{1,0:T(8,128)S(1)}, bf16[192,1024]{1,0:T(8,128)(2,1)S(1)}, bf16[192,512]{1,0:T(8,128)(2,1)S(1)}, bf16[192,512]{1,0:T(8,128)(2,1)S(1)}, bf16[192,512]{1,0:T(8,128)(2,1)S(1)}) custom-call(s32[2,256]{1,0:T(2,128)S(1)} %bitcast.17, s32[2,256]{1,0:T(2,128)S(1)} %bitcast.18, f32[1,256]{1,0:T(1,128)S(1)} %bitcast.19, f32[256,1024]{1,0:T(8,128)S(1)} %copy-done.3), custom_call_target="tpu_custom_call" | custom-call | flops 6291456 | bytes 33872 | tf_op jit(solution)/shard_map/route/pallas_call | solution.py:31
  5.5 3.1 %collective-permute-start.3 = (bf16[192,512]{1,0:T(8,128)(2,1)S(1)}, bf16[192,512]{1,0:T(8,128)(2,1)S(1)}, u32[]{:S(2)}, u32[]{:S(2)}) collective-permute-start(bf16[192,512]{1,0:T(8,128)(2,1)S(1)} %get-tuple-element.82), channel_id=1, source_target_pairs={{0,8},{8,0},{16,24},{24,16},{1,9},{9,1},{17,25},{25,17},{2,10},{10... | collective-permute-start | bytes 589832 | tf_op jit(solution)/shard_map/ppermute | solution.py:223
  8.6 2.6 %collective-permute-start.4 = (bf16[192,512]{1,0:T(8,128)(2,1)S(1)}, bf16[192,512]{1,0:T(8,128)(2,1)S(1)}, u32[]{:S(2)}, u32[]{:S(2)}) collective-permute-start(bf16[192,512]{1,0:T(8,128)(2,1)S(1)} %get-tuple-element.83), channel_id=1, source_target_pairs={{0,16},{8,24},{16,0},{24,8},{1,17},{9,25},{17,1},{25,9},{2,18},{10... | collective-permute-start | bytes 589832 | tf_op jit(solution)/shard_map/ppermute | solution.py:223
  11.2 1.2 %copy-done.4 = f32[256,1024]{1,0:T(8,128)S(1)} copy-done((f32[256,1024]{1,0:T(8,128)S(1)}, f32[256,1024]{1,0:T(8,128)}, u32[]{:S(2)}) %copy-start.4) | copy-done | bytes 1048600
  13.3 3.6 %collective-permute-done.3.refs_0_ = bf16[192,512]{1,0:T(8,128)(2,1)S(1)} collective-permute-done((bf16[192,512]{1,0:T(8,128)(2,1)S(1)}, bf16[192,512]{1,0:T(8,128)(2,1)S(1)}, u32[]{:S(2)}, u32[]{:S(2)}) %collective-permute-start.3) | collective-permute-done | bytes 196640 | tf_op jit(solution)/shard_map/ppermute | solution.py:223
  16.9 8.8 %collective-permute-done.4.refs_1_ = bf16[192,512]{1,0:T(8,128)(2,1)S(1)} collective-permute-done((bf16[192,512]{1,0:T(8,128)(2,1)S(1)}, bf16[192,512]{1,0:T(8,128)(2,1)S(1)}, u32[]{:S(2)}, u32[]{:S(2)}) %collective-permute-start.4) | collective-permute-done | bytes 196640 | tf_op jit(solution)/shard_map/ppermute | solution.py:223
  26.2 3.4 %collective-permute-start = (bf16[192,512]{1,0:T(8,128)(2,1)S(1)}, bf16[192,512]{1,0:T(8,128)(2,1)S(1)}, u32[]{:S(2)}, u32[]{:S(2)}) collective-permute-start(bf16[192,512]{1,0:T(8,128)(2,1)S(1)} %get-tuple-element.78), channel_id=1, source_target_pairs={{0,8},{8,0},{16,24},{24,16},{1,9},{9,1},{17,25},{25,17},{2,10},{10... | collective-permute-start | bytes 589832 | tf_op jit(solution)/shard_map/ppermute | solution.py:223
  30.6 1.5 %collective-permute-start.2 = (bf16[192,512]{1,0:T(8,128)(2,1)S(1)}, bf16[192,512]{1,0:T(8,128)(2,1)S(1)}, u32[]{:S(2)}, u32[]{:S(2)}) collective-permute-start(bf16[192,512]{1,0:T(8,128)(2,1)S(1)} %get-tuple-element.80), channel_id=1, source_target_pairs={{0,24},{8,16},{16,8},{24,0},{1,25},{9,17},{17,9},{25,1},{2,26},{10... | collective-permute-start | bytes 589832 | tf_op jit(solution)/shard_map/ppermute | solution.py:223
  32.1 1.8 %copy-done.1 = bf16[1,1024,1344]{1,2,0:T(8,128)(2,1)S(1)} copy-done((bf16[1,1024,1344]{1,2,0:T(8,128)(2,1)S(1)}, bf16[1,1024,1344]{1,2,0:T(8,128)(2,1)}, u32[]{:S(2)}) %copy-start.1) | copy-done | bytes 2752536
  33.9 3.9 %hidden.1 = (bf16[768,1024]{1,0:T(8,128)(2,1)S(1)}, bf16[1344,768]{1,0:T(8,128)(2,1)S(1)}, bf16[1344,768]{1,0:T(8,128)(2,1)S(1)}) custom-call(bf16[192,1024]{1,0:T(8,128)(2,1)S(1)} %get-tuple-element.81.own, bf16[192,512]{1,0:T(8,128)(2,1)S(1)} %collective-permute-done.3.refs_0_, bf16[192,512]{1,0:T(8,128)(2,1)S(1)} %collective-permute-done.4.refs_1_, ...), custom_call_target="tpu_custom_call" | custom-call | flops 33030144 | bytes 156672 | tf_op jit(solution)/shard_map/hidden/pallas_call | solution.py:31
  37.8 4.1 %rows.1 = (bf16[768,512]{1,0:T(8,128)(2,1)S(1)}, bf16[768,512]{1,0:T(8,128)(2,1)S(1)}) custom-call(bf16[1344,768]{1,0:T(8,128)(2,1)S(1)} %get-tuple-element.110.units_ref.refs_6_, bf16[1344,1024]{1,0:T(8,128)(2,1)S(1)} %bitcast.13), custom_call_target="tpu_custom_call" | custom-call | flops 33030144 | bytes 99840 | tf_op jit(solution)/shard_map/rows/pallas_call | solution.py:31
  41.9 4.8 %collective-permute-done.1.refs_1_ = bf16[192,512]{1,0:T(8,128)(2,1)S(1)} collective-permute-done((bf16[192,512]{1,0:T(8,128)(2,1)S(1)}, bf16[192,512]{1,0:T(8,128)(2,1)S(1)}, u32[]{:S(2)}, u32[]{:S(2)}) %collective-permute-start.1) | collective-permute-done | bytes 196640 | tf_op jit(solution)/shard_map/ppermute | solution.py:223
  47.7 1.5 %collective-permute-done.9.refs_3_ = bf16[192,512]{1,0:T(8,128)(2,1)S(1)} collective-permute-done((bf16[192,512]{1,0:T(8,128)(2,1)S(1)}, bf16[192,512]{1,0:T(8,128)(2,1)S(1)}, u32[]{:S(2)}, u32[]{:S(2)}) %collective-permute-start.9) | collective-permute-done | bytes 196640 | tf_op jit(solution)/shard_map/ppermute | solution.py:223
  49.8 1.4 %outer_leaving.1 = (bf16[768,1024]{1,0:T(8,128)(2,1)S(1)}, bf16[1344,256]{1,0:T(8,128)(2,1)S(1)}, bf16[1344,256]{1,0:T(8,128)(2,1)S(1)}) custom-call(bf16[192,1024]{1,0:T(8,128)(2,1)S(1)} %get-tuple-element.77.own, bf16[192,512]{1,0:T(8,128)(2,1)S(1)} %collective-permute-done.refs_0_, bf16[192,512]{1,0:T(8,128)(2,1)S(1)} %collective-permute-done.1.refs_1_, ...), custom_call_target="tpu_custom_call" | custom-call | flops 16515072 | bytes 102912 | tf_op jit(solution)/shard_map/outer_leaving/pallas_call | solution.py:31
  51.2 1.6 %collective-permute-start.13 = (bf16[1344,256]{1,0:T(8,128)(2,1)S(1)}, bf16[1344,256]{1,0:T(8,128)(2,1)S(1)}, u32[]{:S(2)}, u32[]{:S(2)}) collective-permute-start(bf16[1344,256]{1,0:T(8,128)(2,1)S(1)} %get-tuple-element.116), channel_id=1, source_target_pairs={{0,1},{1,0},{2,3},{3,2},{4,5},{5,4},{6,7},{7,6},{8,9},{9,8},{10,11... | collective-permute-start | bytes 2064392 | tf_op jit(solution)/shard_map/ppermute | solution.py:223
  52.7 1.5 %collective-permute-start.14 = (bf16[1344,256]{1,0:T(8,128)(2,1)S(1)}, bf16[1344,256]{1,0:T(8,128)(2,1)S(1)}, u32[]{:S(2)}, u32[]{:S(2)}) collective-permute-start(bf16[1344,256]{1,0:T(8,128)(2,1)S(1)} %get-tuple-element.117), channel_id=1, source_target_pairs={{0,2},{1,3},{2,0},{3,1},{4,6},{5,7},{6,4},{7,5},{8,10},{9,11},{10,... | collective-permute-start | bytes 2064392 | tf_op jit(solution)/shard_map/ppermute | solution.py:223
  54.4 4.1 %collective-permute-start.15 = (bf16[192,512]{1,0:T(8,128)(2,1)S(1)}, bf16[192,512]{1,0:T(8,128)(2,1)S(1)}, u32[]{:S(2)}, u32[]{:S(2)}) collective-permute-start(bf16[192,512]{1,0:T(8,128)(2,1)S(1)} %get-tuple-element.102), channel_id=1, source_target_pairs={{0,8},{8,0},{16,24},{24,16},{1,9},{9,1},{17,25},{25,17},{2,10},{10... | collective-permute-start | bytes 589832 | tf_op jit(solution)/shard_map/ppermute | solution.py:223
  59.7 1.4 %collective-permute-start.17 = (bf16[192,512]{1,0:T(8,128)(2,1)S(1)}, bf16[192,512]{1,0:T(8,128)(2,1)S(1)}, u32[]{:S(2)}, u32[]{:S(2)}) collective-permute-start(bf16[192,512]{1,0:T(8,128)(2,1)S(1)} %get-tuple-element.104), channel_id=1, source_target_pairs={{0,24},{8,16},{16,8},{24,0},{1,25},{9,17},{17,9},{25,1},{2,26},{10... | collective-permute-start | bytes 589832 | tf_op jit(solution)/shard_map/ppermute | solution.py:223
  61.1 3.6 %d_act.1.units_ref = bf16[1344,768]{1,0:T(8,128)(2,1)S(1)} custom-call(bf16[768,1024]{1,0:T(8,128)(2,1)S(1)} %get-tuple-element.111.g_ref.rows_ref, bf16[1344,768]{1,0:T(8,128)(2,1)S(1)} %get-tuple-element.106.positive_ref, bf16[1344,1024]{1,0:T(8,128)(2,1)S(1)} %bitcast.14), custom_call_target="tpu_custom_call" | custom-call | flops 33030144 | bytes 132096 | tf_op jit(solution)/shard_map/d_act/pallas_call | solution.py:31
  64.7 1.3 %inner_leaving.1 = (bf16[1344,256]{1,0:T(8,128)(2,1)S(1)}, bf16[1344,256]{1,0:T(8,128)(2,1)S(1)}) custom-call(bf16[1344,768]{1,0:T(8,128)(2,1)S(1)} %d_act.1.units_ref, bf16[768,1024]{1,0:T(8,128)(2,1)S(1)} %get-tuple-element.129.rows_ref), custom_call_target="tpu_custom_call" | custom-call | flops 16515072 | bytes 78336 | tf_op jit(solution)/shard_map/inner_leaving/pallas_call | solution.py:31
  66.0 1.3 %outer_staying.1 = (bf16[1344,256]{1,0:T(8,128)(2,1)S(1)}, bf16[1344,256]{1,0:T(8,128)(2,1)S(1)}) custom-call(bf16[1344,768]{1,0:T(8,128)(2,1)S(1)} %get-tuple-element.110.units_ref.refs_6_, bf16[768,1024]{1,0:T(8,128)(2,1)S(1)} %get-tuple-element.111.g_ref.rows_ref), custom_call_target="tpu_custom_call" | custom-call | flops 16515072 | bytes 78336 | tf_op jit(solution)/shard_map/outer_staying/pallas_call | solution.py:31
  67.8 4.1 %grad_rows.1 = (bf16[768,512]{1,0:T(8,128)(2,1)S(1)}, bf16[768,512]{1,0:T(8,128)(2,1)S(1)}) custom-call(bf16[1344,768]{1,0:T(8,128)(2,1)S(1)} %d_act.1.units_ref, bf16[1344,1024]{1,0:T(8,128)(2,1)S(1)} %bitcast.16), custom_call_target="tpu_custom_call" | custom-call | flops 33030144 | bytes 99840 | tf_op jit(solution)/shard_map/grad_rows/pallas_call | solution.py:31
  71.8 3.9 %collective-permute-done.16.refs_2_ = bf16[192,512]{1,0:T(8,128)(2,1)S(1)} collective-permute-done((bf16[192,512]{1,0:T(8,128)(2,1)S(1)}, bf16[192,512]{1,0:T(8,128)(2,1)S(1)}, u32[]{:S(2)}, u32[]{:S(2)}) %collective-permute-start.16) | collective-permute-done | bytes 196640 | tf_op jit(solution)/shard_map/ppermute | solution.py:223
  79.7 3.1 %collective-permute-start.22 = (bf16[192,512]{1,0:T(8,128)(2,1)S(1)}, bf16[192,512]{1,0:T(8,128)(2,1)S(1)}, u32[]{:S(2)}, u32[]{:S(2)}) collective-permute-start(bf16[192,512]{1,0:T(8,128)(2,1)S(1)} %get-tuple-element.135), channel_id=1, source_target_pairs={{0,8},{8,0},{16,24},{24,16},{1,9},{9,1},{17,25},{25,17},{2,10},{10... | collective-permute-start | bytes 589832 | tf_op jit(solution)/shard_map/ppermute | solution.py:223
  83.9 1.4 %collective-permute-start.24 = (bf16[192,512]{1,0:T(8,128)(2,1)S(1)}, bf16[192,512]{1,0:T(8,128)(2,1)S(1)}, u32[]{:S(2)}, u32[]{:S(2)}) collective-permute-start(bf16[192,512]{1,0:T(8,128)(2,1)S(1)} %get-tuple-element.137), channel_id=1, source_target_pairs={{0,24},{8,16},{16,8},{24,0},{1,25},{9,17},{17,9},{25,1},{2,26},{10... | collective-permute-start | bytes 589832 | tf_op jit(solution)/shard_map/ppermute | solution.py:223
  85.3 1.2 %inner_staying.1 = (bf16[1344,256]{1,0:T(8,128)(2,1)S(1)}, bf16[1344,256]{1,0:T(8,128)(2,1)S(1)}) custom-call(bf16[1344,768]{1,0:T(8,128)(2,1)S(1)} %d_act.1.units_ref, bf16[768,1024]{1,0:T(8,128)(2,1)S(1)} %get-tuple-element.129.rows_ref), custom_call_target="tpu_custom_call" | custom-call | flops 16515072 | bytes 78336 | tf_op jit(solution)/shard_map/inner_staying/pallas_call | solution.py:31
  87.6 4.0 %collective-permute-done.22.refs_1_ = bf16[192,512]{1,0:T(8,128)(2,1)S(1)} collective-permute-done((bf16[192,512]{1,0:T(8,128)(2,1)S(1)}, bf16[192,512]{1,0:T(8,128)(2,1)S(1)}, u32[]{:S(2)}, u32[]{:S(2)}) %collective-permute-start.22) | collective-permute-done | bytes 196640 | tf_op jit(solution)/shard_map/ppermute | solution.py:223
  91.6 8.3 %collective-permute-done.23.refs_2_ = bf16[192,512]{1,0:T(8,128)(2,1)S(1)} collective-permute-done((bf16[192,512]{1,0:T(8,128)(2,1)S(1)}, bf16[192,512]{1,0:T(8,128)(2,1)S(1)}, u32[]{:S(2)}, u32[]{:S(2)}) %collective-permute-start.23) | collective-permute-done | bytes 196640 | tf_op jit(solution)/shard_map/ppermute | solution.py:223
  100.7 1.6 %collective-permute-start.27 = (bf16[672,256]{1,0:T(8,128)(2,1)S(1)}, bf16[672,256]{1,0:T(8,128)(2,1)S(1)}, u32[]{:S(2)}, u32[]{:S(2)}) collective-permute-start(bf16[672,256]{1,0:T(8,128)(2,1)S(1)} %get-tuple-element.149), channel_id=1, source_target_pairs={{0,1},{1,0},{2,3},{3,2},{4,5},{5,4},{6,7},{7,6},{8,9},{9,8},{10,11... | collective-permute-start | bytes 1032200 | tf_op jit(solution)/shard_map/ppermute | solution.py:223
  102.5 1.6 %collective-permute-start.26 = (bf16[672,256]{1,0:T(8,128)(2,1)S(1)}, bf16[672,256]{1,0:T(8,128)(2,1)S(1)}, u32[]{:S(2)}, u32[]{:S(2)}) collective-permute-start(bf16[672,256]{1,0:T(8,128)(2,1)S(1)} %get-tuple-element.151), channel_id=1, source_target_pairs={{0,2},{1,3},{2,0},{3,1},{4,6},{5,7},{6,4},{7,5},{8,10},{9,11},{10,... | collective-permute-start | bytes 1032200 | tf_op jit(solution)/shard_map/ppermute | solution.py:223
  106.3 5.0 %collective-permute-done.27 = bf16[672,256]{1,0:T(8,128)(2,1)S(1)} collective-permute-done((bf16[672,256]{1,0:T(8,128)(2,1)S(1)}, bf16[672,256]{1,0:T(8,128)(2,1)S(1)}, u32[]{:S(2)}, u32[]{:S(2)}) %collective-permute-start.27) | collective-permute-done | bytes 344096 | tf_op jit(solution)/shard_map/ppermute | solution.py:223
  111.4 1.4 %collective-permute-done.26 = bf16[672,256]{1,0:T(8,128)(2,1)S(1)} collective-permute-done((bf16[672,256]{1,0:T(8,128)(2,1)S(1)}, bf16[672,256]{1,0:T(8,128)(2,1)S(1)}, u32[]{:S(2)}, u32[]{:S(2)}) %collective-permute-start.26) | collective-permute-done | bytes 344096 | tf_op jit(solution)/shard_map/ppermute | solution.py:223
  (68 shorter events, 19.8 us)
Async XLA Ops:
  0.6 1.2 %copy-start.3 = (f32[256,1024]{1,0:T(8,128)S(1)}, f32[256,1024]{1,0:T(8,128)}, u32[]{:S(2)}) copy-start(f32[256,1024]{1,0:T(8,128)} %tokens_ref.1) | copy-start | bytes 3145732
  5.5 11.4 %collective-permute-start.3 = (bf16[192,512]{1,0:T(8,128)(2,1)S(1)}, bf16[192,512]{1,0:T(8,128)(2,1)S(1)}, u32[]{:S(2)}, u32[]{:S(2)}) collective-permute-start(bf16[192,512]{1,0:T(8,128)(2,1)S(1)} %get-tuple-element.82), channel_id=1, source_target_pairs={{0,8},{8,0},{16,24},{24,16},{1,9},{9,1},{17,25},{25,17},{2,10},{10... | collective-permute-start | bytes 589832 | tf_op jit(solution)/shard_map/ppermute | solution.py:223
  8.6 17.2 %collective-permute-start.4 = (bf16[192,512]{1,0:T(8,128)(2,1)S(1)}, bf16[192,512]{1,0:T(8,128)(2,1)S(1)}, u32[]{:S(2)}, u32[]{:S(2)}) collective-permute-start(bf16[192,512]{1,0:T(8,128)(2,1)S(1)} %get-tuple-element.83), channel_id=1, source_target_pairs={{0,16},{8,24},{16,0},{24,8},{1,17},{9,25},{17,1},{25,9},{2,18},{10... | collective-permute-start | bytes 589832 | tf_op jit(solution)/shard_map/ppermute | solution.py:223
  11.1 14.6 %collective-permute-start.5 = (bf16[192,512]{1,0:T(8,128)(2,1)S(1)}, bf16[192,512]{1,0:T(8,128)(2,1)S(1)}, u32[]{:S(2)}, u32[]{:S(2)}) collective-permute-start(bf16[192,512]{1,0:T(8,128)(2,1)S(1)} %get-tuple-element.84), channel_id=1, source_target_pairs={{0,24},{8,16},{16,8},{24,0},{1,25},{9,17},{17,9},{25,1},{2,26},{10... | collective-permute-start | bytes 589832 | tf_op jit(solution)/shard_map/ppermute | solution.py:223
  25.7 4.9 %collective-permute-start.6 = (bf16[192,512]{1,0:T(8,128)(2,1)S(1)}, bf16[192,512]{1,0:T(8,128)(2,1)S(1)}, u32[]{:S(2)}, u32[]{:S(2)}) collective-permute-start(bf16[192,512]{1,0:T(8,128)(2,1)S(1)} %collective-permute-done.3.refs_0_), channel_id=1, source_target_pairs={{0,4},{4,0},{1,5},{5,1},{2,6},{6,2},{3,7},{7,3},{8,12},{12,8},{9,1... | collective-permute-start | bytes 589832 | tf_op jit(solution)/shard_map/ppermute | solution.py:223
  25.7 6.3 %collective-permute-start.7 = (bf16[192,512]{1,0:T(8,128)(2,1)S(1)}, bf16[192,512]{1,0:T(8,128)(2,1)S(1)}, u32[]{:S(2)}, u32[]{:S(2)}) collective-permute-start(bf16[192,512]{1,0:T(8,128)(2,1)S(1)} %collective-permute-done.4.refs_1_), channel_id=1, source_target_pairs={{0,4},{4,0},{1,5},{5,1},{2,6},{6,2},{3,7},{7,3},{8,12},{12,8},{9,1... | collective-permute-start | bytes 589832 | tf_op jit(solution)/shard_map/ppermute | solution.py:223
  26.2 5.8 %collective-permute-start.8 = (bf16[192,512]{1,0:T(8,128)(2,1)S(1)}, bf16[192,512]{1,0:T(8,128)(2,1)S(1)}, u32[]{:S(2)}, u32[]{:S(2)}) collective-permute-start(bf16[192,512]{1,0:T(8,128)(2,1)S(1)} %collective-permute-done.5.refs_2_), channel_id=1, source_target_pairs={{0,4},{4,0},{1,5},{5,1},{2,6},{6,2},{3,7},{7,3},{8,12},{12,8},{9,1... | collective-permute-start | bytes 589832 | tf_op jit(solution)/shard_map/ppermute | solution.py:223
  26.2 15.6 %collective-permute-start = (bf16[192,512]{1,0:T(8,128)(2,1)S(1)}, bf16[192,512]{1,0:T(8,128)(2,1)S(1)}, u32[]{:S(2)}, u32[]{:S(2)}) collective-permute-start(bf16[192,512]{1,0:T(8,128)(2,1)S(1)} %get-tuple-element.78), channel_id=1, source_target_pairs={{0,8},{8,0},{16,24},{24,16},{1,9},{9,1},{17,25},{25,17},{2,10},{10... | collective-permute-start | bytes 589832 | tf_op jit(solution)/shard_map/ppermute | solution.py:223
  29.6 17.1 %collective-permute-start.1 = (bf16[192,512]{1,0:T(8,128)(2,1)S(1)}, bf16[192,512]{1,0:T(8,128)(2,1)S(1)}, u32[]{:S(2)}, u32[]{:S(2)}) collective-permute-start(bf16[192,512]{1,0:T(8,128)(2,1)S(1)} %get-tuple-element.79), channel_id=1, source_target_pairs={{0,16},{8,24},{16,0},{24,8},{1,17},{9,25},{17,1},{25,9},{2,18},{10... | collective-permute-start | bytes 589832 | tf_op jit(solution)/shard_map/ppermute | solution.py:223
  30.6 16.1 %collective-permute-start.2 = (bf16[192,512]{1,0:T(8,128)(2,1)S(1)}, bf16[192,512]{1,0:T(8,128)(2,1)S(1)}, u32[]{:S(2)}, u32[]{:S(2)}) collective-permute-start(bf16[192,512]{1,0:T(8,128)(2,1)S(1)} %get-tuple-element.80), channel_id=1, source_target_pairs={{0,24},{8,16},{16,8},{24,0},{1,25},{9,17},{17,9},{25,1},{2,26},{10... | collective-permute-start | bytes 589832 | tf_op jit(solution)/shard_map/ppermute | solution.py:223
  32.1 1.8 %copy-start.1 = (bf16[1,1024,1344]{1,2,0:T(8,128)(2,1)S(1)}, bf16[1,1024,1344]{1,2,0:T(8,128)(2,1)}, u32[]{:S(2)}) copy-start(bf16[1,1024,1344]{1,2,0:T(8,128)(2,1)} %param.12) | copy-start | bytes 8257540
  33.9 3.9 %copy-start = (bf16[1,1344,1024]{2,1,0:T(8,128)(2,1)S(1)}, bf16[1,1344,1024]{2,1,0:T(8,128)(2,1)}, u32[]{:S(2)}) copy-start(bf16[1,1344,1024]{2,1,0:T(8,128)(2,1)} %param.13) | copy-start | bytes 8257540
  46.7 7.6 %collective-permute-start.12 = (bf16[768,512]{1,0:T(8,128)(2,1)S(1)}, bf16[768,512]{1,0:T(8,128)(2,1)S(1)}, u32[]{:S(2)}, u32[]{:S(2)}) collective-permute-start(bf16[768,512]{1,0:T(8,128)(2,1)S(1)} %get-tuple-element.98), channel_id=1, source_target_pairs={{0,4},{4,0},{1,5},{5,1},{2,6},{6,2},{3,7},{7,3},{8,12},{12,8},{9,1... | collective-permute-start | bytes 2359304 | tf_op jit(solution)/shard_map/ppermute | solution.py:223
  46.7 2.6 %collective-permute-start.9 = (bf16[192,512]{1,0:T(8,128)(2,1)S(1)}, bf16[192,512]{1,0:T(8,128)(2,1)S(1)}, u32[]{:S(2)}, u32[]{:S(2)}) collective-permute-start(bf16[192,512]{1,0:T(8,128)(2,1)S(1)} %collective-permute-done.refs_0_), channel_id=1, source_target_pairs={{0,4},{4,0},{1,5},{5,1},{2,6},{6,2},{3,7},{7,3},{8,12},{12,8},{9,1... | collective-permute-start | bytes 589832 | tf_op jit(solution)/shard_map/ppermute | solution.py:223
  47.2 2.3 %collective-permute-start.10 = (bf16[192,512]{1,0:T(8,128)(2,1)S(1)}, bf16[192,512]{1,0:T(8,128)(2,1)S(1)}, u32[]{:S(2)}, u32[]{:S(2)}) collective-permute-start(bf16[192,512]{1,0:T(8,128)(2,1)S(1)} %collective-permute-done.1.refs_1_), channel_id=1, source_target_pairs={{0,4},{4,0},{1,5},{5,1},{2,6},{6,2},{3,7},{7,3},{8,12},{12,8},{9,1... | collective-permute-start | bytes 589832 | tf_op jit(solution)/shard_map/ppermute | solution.py:223
  47.2 2.6 %collective-permute-start.11 = (bf16[192,512]{1,0:T(8,128)(2,1)S(1)}, bf16[192,512]{1,0:T(8,128)(2,1)S(1)}, u32[]{:S(2)}, u32[]{:S(2)}) collective-permute-start(bf16[192,512]{1,0:T(8,128)(2,1)S(1)} %collective-permute-done.2.refs_2_), channel_id=1, source_target_pairs={{0,4},{4,0},{1,5},{5,1},{2,6},{6,2},{3,7},{7,3},{8,12},{12,8},{9,1... | collective-permute-start | bytes 589832 | tf_op jit(solution)/shard_map/ppermute | solution.py:223
  51.2 20.6 %collective-permute-start.13 = (bf16[1344,256]{1,0:T(8,128)(2,1)S(1)}, bf16[1344,256]{1,0:T(8,128)(2,1)S(1)}, u32[]{:S(2)}, u32[]{:S(2)}) collective-permute-start(bf16[1344,256]{1,0:T(8,128)(2,1)S(1)} %get-tuple-element.116), channel_id=1, source_target_pairs={{0,1},{1,0},{2,3},{3,2},{4,5},{5,4},{6,7},{7,6},{8,9},{9,8},{10,11... | collective-permute-start | bytes 2064392 | tf_op jit(solution)/shard_map/ppermute | solution.py:223
  52.7 19.1 %collective-permute-start.14 = (bf16[1344,256]{1,0:T(8,128)(2,1)S(1)}, bf16[1344,256]{1,0:T(8,128)(2,1)S(1)}, u32[]{:S(2)}, u32[]{:S(2)}) collective-permute-start(bf16[1344,256]{1,0:T(8,128)(2,1)S(1)} %get-tuple-element.117), channel_id=1, source_target_pairs={{0,2},{1,3},{2,0},{3,1},{4,6},{5,7},{6,4},{7,5},{8,10},{9,11},{10,... | collective-permute-start | bytes 2064392 | tf_op jit(solution)/shard_map/ppermute | solution.py:223
  54.4 17.4 %collective-permute-start.15 = (bf16[192,512]{1,0:T(8,128)(2,1)S(1)}, bf16[192,512]{1,0:T(8,128)(2,1)S(1)}, u32[]{:S(2)}, u32[]{:S(2)}) collective-permute-start(bf16[192,512]{1,0:T(8,128)(2,1)S(1)} %get-tuple-element.102), channel_id=1, source_target_pairs={{0,8},{8,0},{16,24},{24,16},{1,9},{9,1},{17,25},{25,17},{2,10},{10... | collective-permute-start | bytes 589832 | tf_op jit(solution)/shard_map/ppermute | solution.py:223
  58.6 17.2 %collective-permute-start.16 = (bf16[192,512]{1,0:T(8,128)(2,1)S(1)}, bf16[192,512]{1,0:T(8,128)(2,1)S(1)}, u32[]{:S(2)}, u32[]{:S(2)}) collective-permute-start(bf16[192,512]{1,0:T(8,128)(2,1)S(1)} %get-tuple-element.103), channel_id=1, source_target_pairs={{0,16},{8,24},{16,0},{24,8},{1,17},{9,25},{17,1},{25,9},{2,18},{10... | collective-permute-start | bytes 589832 | tf_op jit(solution)/shard_map/ppermute | solution.py:223
  59.7 16.1 %collective-permute-start.17 = (bf16[192,512]{1,0:T(8,128)(2,1)S(1)}, bf16[192,512]{1,0:T(8,128)(2,1)S(1)}, u32[]{:S(2)}, u32[]{:S(2)}) collective-permute-start(bf16[192,512]{1,0:T(8,128)(2,1)S(1)} %get-tuple-element.104), channel_id=1, source_target_pairs={{0,24},{8,16},{16,8},{24,0},{1,25},{9,17},{17,9},{25,1},{2,26},{10... | collective-permute-start | bytes 589832 | tf_op jit(solution)/shard_map/ppermute | solution.py:223
  66.0 1.8 %copy-start.2 = (bf16[1,1024,1344]{1,2,0:T(8,128)(2,1)S(1)}, bf16[1,1024,1344]{1,2,0:T(8,128)(2,1)}, u32[]{:S(2)}) copy-start(bf16[1,1024,1344]{1,2,0:T(8,128)(2,1)} %param.12) | copy-start | bytes 8257540
  76.1 23.9 %collective-permute-start.20 = (bf16[2016,256]{1,0:T(8,128)(2,1)S(1)}, bf16[2016,256]{1,0:T(8,128)(2,1)S(1)}, u32[]{:S(2)}, u32[]{:S(2)}) collective-permute-start(bf16[2016,256]{1,0:T(8,128)(2,1)S(1)} %pad_maximum_fusion.1), channel_id=1, source_target_pairs={{0,2},{1,3},{2,0},{3,1},{4,6},{5,7},{6,4},{7,5},{8,10},{9,11},{10,... | collective-permute-start | bytes 3096584 | tf_op jit(solution)/shard_map/ppermute | solution.py:223
  76.7 23.3 %collective-permute-start.19 = (bf16[2016,256]{1,0:T(8,128)(2,1)S(1)}, bf16[2016,256]{1,0:T(8,128)(2,1)S(1)}, u32[]{:S(2)}, u32[]{:S(2)}) collective-permute-start(bf16[2016,256]{1,0:T(8,128)(2,1)S(1)} %pad_maximum_fusion), channel_id=1, source_target_pairs={{0,1},{1,0},{2,3},{3,2},{4,5},{5,4},{6,7},{7,6},{8,9},{9,8},{10,11... | collective-permute-start | bytes 3096584 | tf_op jit(solution)/shard_map/ppermute | solution.py:223
  77.2 2.3 %collective-permute-start.21 = (bf16[768,512]{1,0:T(8,128)(2,1)S(1)}, bf16[768,512]{1,0:T(8,128)(2,1)S(1)}, u32[]{:S(2)}, u32[]{:S(2)}) collective-permute-start(bf16[768,512]{1,0:T(8,128)(2,1)S(1)} %get-tuple-element.133), channel_id=1, source_target_pairs={{0,4},{4,0},{1,5},{5,1},{2,6},{6,2},{3,7},{7,3},{8,12},{12,8},{9,1... | collective-permute-start | bytes 2359304 | tf_op jit(solution)/shard_map/ppermute | solution.py:223
  78.0 5.9 %collective-permute-start.18 = (bf16[256,512]{1,0:T(8,128)(2,1)S(1)}, bf16[256,512]{1,0:T(8,128)(2,1)S(1)}, u32[]{:S(2)}, u32[]{:S(2)}) collective-permute-start(bf16[256,512]{1,0:T(8,128)(2,1)S(1)} %get-tuple-element.123), channel_id=1, source_target_pairs={{0,4},{4,0},{1,5},{5,1},{2,6},{6,2},{3,7},{7,3},{8,12},{12,8},{9,1... | collective-permute-start | bytes 786440 | tf_op jit(solution)/shard_map/ppermute | solution.py:223
  79.7 12.0 %collective-permute-start.22 = (bf16[192,512]{1,0:T(8,128)(2,1)S(1)}, bf16[192,512]{1,0:T(8,128)(2,1)S(1)}, u32[]{:S(2)}, u32[]{:S(2)}) collective-permute-start(bf16[192,512]{1,0:T(8,128)(2,1)S(1)} %get-tuple-element.135), channel_id=1, source_target_pairs={{0,8},{8,0},{16,24},{24,16},{1,9},{9,1},{17,25},{25,17},{2,10},{10... | collective-permute-start | bytes 589832 | tf_op jit(solution)/shard_map/ppermute | solution.py:223
  82.8 17.1 %collective-permute-start.23 = (bf16[192,512]{1,0:T(8,128)(2,1)S(1)}, bf16[192,512]{1,0:T(8,128)(2,1)S(1)}, u32[]{:S(2)}, u32[]{:S(2)}) collective-permute-start(bf16[192,512]{1,0:T(8,128)(2,1)S(1)} %get-tuple-element.136), channel_id=1, source_target_pairs={{0,16},{8,24},{16,0},{24,8},{1,17},{9,25},{17,1},{25,9},{2,18},{10... | collective-permute-start | bytes 589832 | tf_op jit(solution)/shard_map/ppermute | solution.py:223
  83.9 16.0 %collective-permute-start.24 = (bf16[192,512]{1,0:T(8,128)(2,1)S(1)}, bf16[192,512]{1,0:T(8,128)(2,1)S(1)}, u32[]{:S(2)}, u32[]{:S(2)}) collective-permute-start(bf16[192,512]{1,0:T(8,128)(2,1)S(1)} %get-tuple-element.137), channel_id=1, source_target_pairs={{0,24},{8,16},{16,8},{24,0},{1,25},{9,17},{17,9},{25,1},{2,26},{10... | collective-permute-start | bytes 589832 | tf_op jit(solution)/shard_map/ppermute | solution.py:223
  100.5 4.8 %collective-permute-start.25 = (bf16[256,512]{1,0:T(8,128)(2,1)S(1)}, bf16[256,512]{1,0:T(8,128)(2,1)S(1)}, u32[]{:S(2)}, u32[]{:S(2)}) collective-permute-start(bf16[256,512]{1,0:T(8,128)(2,1)S(1)} %get-tuple-element.143), channel_id=1, source_target_pairs={{0,4},{4,0},{1,5},{5,1},{2,6},{6,2},{3,7},{7,3},{8,12},{12,8},{9,1... | collective-permute-start | bytes 786440 | tf_op jit(solution)/shard_map/ppermute | solution.py:223
  100.7 10.5 %collective-permute-start.27 = (bf16[672,256]{1,0:T(8,128)(2,1)S(1)}, bf16[672,256]{1,0:T(8,128)(2,1)S(1)}, u32[]{:S(2)}, u32[]{:S(2)}) collective-permute-start(bf16[672,256]{1,0:T(8,128)(2,1)S(1)} %get-tuple-element.149), channel_id=1, source_target_pairs={{0,1},{1,0},{2,3},{3,2},{4,5},{5,4},{6,7},{7,6},{8,9},{9,8},{10,11... | collective-permute-start | bytes 1032200 | tf_op jit(solution)/shard_map/ppermute | solution.py:223
  102.5 10.2 %collective-permute-start.26 = (bf16[672,256]{1,0:T(8,128)(2,1)S(1)}, bf16[672,256]{1,0:T(8,128)(2,1)S(1)}, u32[]{:S(2)}, u32[]{:S(2)}) collective-permute-start(bf16[672,256]{1,0:T(8,128)(2,1)S(1)} %get-tuple-element.151), channel_id=1, source_target_pairs={{0,2},{1,3},{2,0},{3,1},{4,6},{5,7},{6,4},{7,5},{8,10},{9,11},{10,... | collective-permute-start | bytes 1032200 | tf_op jit(solution)/shard_map/ppermute | solution.py:223
  (4 other events, 3.3 us)

commit v4 on v3

--- a/solution.py
+++ b/solution.py
@@ -26,18 +26,18 @@
     return jax.ShapeDtypeStruct((rows, columns), dtype)
 
 
-def local(body, outs, operands, flops, name, scratch=()):
+def local(body, outs, operands, flops, name, scratch=(), space=pltpu.VMEM, gives=pltpu.VMEM):
     moved = sum(x.size * x.dtype.itemsize for x in (*operands, *outs))
     return pl.pallas_call(
         body,
-        out_shape=tuple(pltpu.VMEM(x.shape, x.dtype) for x in outs),
+        out_shape=tuple(gives(x.shape, x.dtype) for x in outs),
         in_specs=[pl.BlockSpec(memory_space=pltpu.VMEM)] * len(operands),
         out_specs=tuple([pl.BlockSpec(memory_space=pltpu.VMEM)] * len(outs)),
         scratch_shapes=list(scratch),
         compiler_params=pltpu.CompilerParams(vmem_limit_bytes=VMEM_BYTES),
         cost_estimate=pl.CostEstimate(flops=flops // COST, bytes_accessed=moved // COST, transcendentals=0),
         name=name,
-    )(*[pltpu.with_memory_space_constraint(x, pltpu.VMEM) for x in operands])
+    )(*[pltpu.with_memory_space_constraint(x, space) for x in operands])
 
 
 def window(index, width):
@@ -219,6 +219,31 @@
     out_ref[:, window(1 - core, half)] = other_ref[...].astype(F32)
 
 
+def added(a, b):
+    return a.astype(F32) + b.astype(F32)
+
+
+def mix_body(kept0, kept1, came0, came1, inner0, inner1, send0, send1, own0, own1):
+    rows = own0.shape[0]
+    for kept, came, own, send, inner in ((kept0, came0, own0, send1, inner1), (kept1, came1, own1, send0, inner0)):
+        own[...] = added(kept[:rows, :], came[:rows, :]).astype(BF16)
+        send[:rows, :] = added(kept[rows:, :], came[rows:, :]).astype(BF16)
+        send[rows:, :] = inner[...]
+
+
+def inner_sum_body(kept0, kept1, mixed0, mixed1, move0, move1, own0, own1):
+    rows = own0.shape[0]
+    for kept, mixed, move, own in ((kept0, mixed0, move0, own0), (kept1, mixed1, move1, own1)):
+        own[...] = added(kept[:rows, :], mixed[rows : 2 * rows, :]).astype(BF16)
+        move[...] = added(kept[rows:, :], mixed[2 * rows :, :]).astype(BF16)
+
+
+def last_sum_body(own0, own1, came0, came1, out_ref):
+    rows = own0.shape[0]
+    out_ref[:rows, :] = added(own0[...], came0[:rows, :])
+    out_ref[rows:, :] = added(own1[...], came1[:rows, :])
+
+
 def partner(x, axis, bit):
     return lax.ppermute(x, axis, [(i, i ^ bit) for i in range(lax.axis_size(axis))])
 
@@ -243,13 +268,16 @@
     staying = [[r ^ order[0] for r in blocks] for order, blocks in zip(orders, leaving, strict=True)]
     part_rows = units // 2
     piece = shape(part_rows * groups // 2, features // groups)
+    quarter = shape(part_rows, features // groups)
+    total = shape(units, features // groups, F32)
     work = 2 * slots * features * units
 
     def across_cores(chunks):
         return [partner(x, "cuts", 1) for x in chunks]
 
     def over_experts(chunks):
-        return [partner(x, "expert", s) for s, x in enumerate(chunks, 1)]
+        got = {s: partner(chunks[s - 1], "expert", s) for s in reversed(range(1, owners))}
+        return [got[s] for s in range(1, owners)]
 
     def times_weight(units_rows, weight, name):
         return local(
@@ -269,23 +297,10 @@
         )
 
     def join(wide, came):
-        return local(join_body, [shape(count, features, F32)], [wide, came], 0, "join")[0]
+        return local(join_body, [shape(count, features, F32)], [wide, came], 0, "join", gives=pltpu.HBM)[0]
 
     def grads(keys, units_rows, rows, name):
         return local(functools.partial(grad_body, keys), [piece] * 2, [units_rows, rows], work // 2, name)
-
-    def added(kept, came, dtype=BF16):
-        return (kept.astype(F32) + came.astype(F32)).astype(dtype)
-
-    def block(stack, i):
-        return stack[i * part_rows : (i + 1) * part_rows]
-
-    def halvings(blocks, order):
-        for bit in order:
-            came = {r ^ bit: partner(blocks[r], "dp", bit) for r in blocks if r & bit}
-            dtype = F32 if bit == order[-1] else BF16
-            blocks = {r: added(blocks[r], came[r], dtype) for r in came}
-        return blocks[0]
 
     meta, own, *sends = local(
         functools.partial(route_body, owners, capacity),
@@ -293,6 +308,7 @@
         [routes.T, combine_index.T, combine_table[None, :], tokens],
         2 * count * slots * features,
         "route",
+        space=pltpu.HBM,
     )
     mine = over_experts(sends)
     grad_own, *grad_sends = local(
@@ -336,40 +352,33 @@
     outer_kept = grads(staying, hidden, grad_rows, "outer_staying")
     d_act_late = after(d_act, outer_kept)
     grad_keep, grad_give = times_weight(d_act_late, inner, "grad_rows")
-    grad_give, outer_came, outer_kept, returned, d_act, arrived = after(
-        (grad_give, outer_came, outer_kept, returned, d_act, arrived)
-    )
+    outer_came = after(outer_came, grad_give)
+    *sends, outer_own0, outer_own1 = local(
+        mix_body,
+        [shape(3 * part_rows, piece.shape[1])] * 2 + [quarter] * 2,
+        [*outer_kept, *outer_came, *inner_sent],
+        0,
+        "mix",
+    )
+    mixed = [partner(x, "dp", order[0]) for x, order in zip(sends, orders, strict=True)]
+    grad_give, returned = after((grad_give, returned))
     grad_came = partner(grad_give, "cuts", 1)
     inner_kept = grads(staying, d_act, arrived, "inner_staying")
-    outer_own, mixed = [], []
-    for part in range(2):
-        sums = [added(block(outer_kept[part], i), block(outer_came[part], i)) for i in range(groups // 2)]
-        outer_own.append(dict(zip(staying[part], sums, strict=True)))
-    for part in range(2):
-        other = outer_own[1 - part]
-        moving = [other[r] for r in other if r & orders[part][0]]
-        got = partner(jnp.concatenate([*moving, inner_sent[part]], axis=0), "dp", orders[part][0])
-        mixed.append(got)
     chunks = split(grad_keep, grad_came)
     grad_returned = [chunks[0]] + over_experts(chunks[1:])
+    move0, move1, inner_own0, inner_own1 = local(
+        inner_sum_body, [quarter] * 4, [*inner_kept, *mixed], 0, "inner_sum"
+    )
+    moved = [partner(x, "dp", order[1]) for x, order in zip((move0, move1), orders, strict=True)]
+    (grad_out,) = local(
+        last_sum_body, [total], [outer_own0, outer_own1, *mixed[::-1]], 0, "outer_last", gives=pltpu.HBM
+    )
+    (grad_in,) = local(last_sum_body, [total], [inner_own0, inner_own1, *moved], 0, "inner_last", gives=pltpu.HBM)
     wide, narrow = combine(returned, True)
     layer_out = join(wide, partner(narrow, "cuts", 1))
-    mixed, inner_kept, grad_returned = after((mixed, inner_kept, grad_returned))
-    outer_sums, inner_sums = [], []
-    for part, order in enumerate(orders):
-        bit = orders[1 - part][0]
-        mine = [r for r in outer_own[part] if not r & bit]
-        rest = {r: added(outer_own[part][r], block(mixed[1 - part], i), F32) for i, r in enumerate(mine)}
-        outer_sums.append(halvings(rest, order[2:]) if order[2:] else rest[0])
-        start = len(mine)
-        sums = {
-            r: added(block(inner_kept[part], i), block(mixed[part], start + i)) for i, r in enumerate(staying[part])
-        }
-        inner_sums.append(halvings(sums, order[1:]))
-    grad_out = jnp.concatenate(outer_sums, axis=0)
-    grad_in = jnp.concatenate(inner_sums, axis=0).T
     wide, narrow = combine(grad_returned, False)
     d_tokens = join(wide, partner(narrow, "cuts", 1))
+    grad_in = grad_in.T
     return (layer_out, d_tokens, grad_in[None], grad_out[None])
 
 

time: 115 us -> 103 us (0.90)
  waiting for transfers between devices: 42.8 us -> 35 us
  Pallas kernels: 25.1 us -> 31.4 us
  local copies, waits for them, and re-layouts: 8.72 us -> 3.51 us
  other arithmetic: 3.26 us -> 0 us
    ppermute x28, waiting for transfers between devices: 42.8 us -> 35 us  [partner(): lax.ppermute(x, axis, [(i, i ^ bit) for i in range(lax.axis_size(axis))])]
    pallas_call x16 -> x20, Pallas kernels: 25.1 us -> 31.4 us  [local(): pl.pallas_call(body, out_shape=tuple((gives(x.shape, x.dtype) for x in ou...]
    unnamed x18 -> x8, local copies, waits for them, and re-layouts: 8.72 us -> 3.51 us
    broadcast_in_dim x2 -> x0, other arithmetic: 2.33 us -> none  [shards(): return (layer_out, d_tokens, grad_in[None], grad_out[None])]
  transfers between devices with their start and end apart: 28 -> 28, of which waited for: 12 -> 13; matrix products, arithmetic and copies ran while one was open for 3% -> 0% of each run, Pallas kernels for 20% -> 27%
where the time goes in v4:
time: 103 us
  waiting for transfers between devices  35 us (34%)
  starting transfers between devices  32.2 us (31%)
  Pallas kernels  31.4 us (30%)
  local copies, waits for them, and re-layouts  3.51 us (3%)
    ppermute x28, waiting for transfers between devices, partner(): lax.ppermute(x, axis, [(i, i ^ bit) for i in range(lax.axis_size(axis))])  35 us
    ppermute x28, starting transfers between devices, partner(): lax.ppermute(x, axis, [(i, i ^ bit) for i in range(lax.axis_size(axis))])  32.2 us
    pallas_call x20, Pallas kernels, local(): pl.pallas_call(body, out_shape=tuple((gives(x.shape, x.dtype) for x in ou...  31.4 us
    unnamed x8, local copies, waits for them, and re-layouts  3.51 us
  transfers between devices with their start and end apart: 28, of which 13 were waited for; matrix products, arithmetic and copies ran while one was open for 0% of the time, Pallas kernels for 27%

profile of v4, /device:TPU:0, one launch (start us, length us, event | category | flops | bytes accessed | tf_op | source)
XLA Modules:
  0.0 102.9 jit_solution(10290997116116594539)
XLA Ops:
  0.6 2.8 %route.1 = (f32[256,128]{1,0:T(8,128)S(1)}, bf16[192,1024]{1,0:T(8,128)(2,1)S(1)}, bf16[192,512]{1,0:T(8,128)(2,1)S(1)}, bf16[192,512]{1,0:T(8,128)(2,1)S(1)}, bf16[192,512]{1,0:T(8,128)(2,1)S(1)}) custom-call(s32[2,256]{1,0:T(2,128)} %bitcast.17, s32[2,256]{1,0:T(2,128)} %bitcast.18, f32[1,256]{1,0:T(1,128)} %bitcast.19, f32[256,1024]{1,0:T(8,128)} %tokens_ref.1), custom_call_target="tpu_custom_call" | custom-call | flops 6291456 | bytes 33872 | tf_op jit(solution)/shard_map/route/pallas_call | solution.py:31
  3.5 3.1 %collective-permute-start.3 = (bf16[192,512]{1,0:T(8,128)(2,1)S(1)}, bf16[192,512]{1,0:T(8,128)(2,1)S(1)}, u32[]{:S(2)}, u32[]{:S(2)}) collective-permute-start(bf16[192,512]{1,0:T(8,128)(2,1)S(1)} %get-tuple-element.78), channel_id=1, source_target_pairs={{0,8},{8,0},{16,24},{24,16},{1,9},{9,1},{17,25},{25,17},{2,10},{10... | collective-permute-start | bytes 589832 | tf_op jit(solution)/shard_map/ppermute | solution.py:248
  6.6 2.6 %collective-permute-start.4 = (bf16[192,512]{1,0:T(8,128)(2,1)S(1)}, bf16[192,512]{1,0:T(8,128)(2,1)S(1)}, u32[]{:S(2)}, u32[]{:S(2)}) collective-permute-start(bf16[192,512]{1,0:T(8,128)(2,1)S(1)} %get-tuple-element.79), channel_id=1, source_target_pairs={{0,16},{8,24},{16,0},{24,8},{1,17},{9,25},{17,1},{25,9},{2,18},{10... | collective-permute-start | bytes 589832 | tf_op jit(solution)/shard_map/ppermute | solution.py:248
  9.1 1.2 %copy-done.3 = f32[256,1024]{1,0:T(8,128)S(1)} copy-done((f32[256,1024]{1,0:T(8,128)S(1)}, f32[256,1024]{1,0:T(8,128)}, u32[]{:S(2)}) %copy-start.3) | copy-done | bytes 1048600
  11.3 3.6 %collective-permute-done.3.refs_0_ = bf16[192,512]{1,0:T(8,128)(2,1)S(1)} collective-permute-done((bf16[192,512]{1,0:T(8,128)(2,1)S(1)}, bf16[192,512]{1,0:T(8,128)(2,1)S(1)}, u32[]{:S(2)}, u32[]{:S(2)}) %collective-permute-start.3) | collective-permute-done | bytes 196640 | tf_op jit(solution)/shard_map/ppermute | solution.py:248
  14.9 8.8 %collective-permute-done.4.refs_1_ = bf16[192,512]{1,0:T(8,128)(2,1)S(1)} collective-permute-done((bf16[192,512]{1,0:T(8,128)(2,1)S(1)}, bf16[192,512]{1,0:T(8,128)(2,1)S(1)}, u32[]{:S(2)}, u32[]{:S(2)}) %collective-permute-start.4) | collective-permute-done | bytes 196640 | tf_op jit(solution)/shard_map/ppermute | solution.py:248
  24.2 3.4 %collective-permute-start = (bf16[192,512]{1,0:T(8,128)(2,1)S(1)}, bf16[192,512]{1,0:T(8,128)(2,1)S(1)}, u32[]{:S(2)}, u32[]{:S(2)}) collective-permute-start(bf16[192,512]{1,0:T(8,128)(2,1)S(1)} %get-tuple-element.74), channel_id=1, source_target_pairs={{0,8},{8,0},{16,24},{24,16},{1,9},{9,1},{17,25},{25,17},{2,10},{10... | collective-permute-start | bytes 589832 | tf_op jit(solution)/shard_map/ppermute | solution.py:248
  28.6 1.5 %collective-permute-start.2 = (bf16[192,512]{1,0:T(8,128)(2,1)S(1)}, bf16[192,512]{1,0:T(8,128)(2,1)S(1)}, u32[]{:S(2)}, u32[]{:S(2)}) collective-permute-start(bf16[192,512]{1,0:T(8,128)(2,1)S(1)} %get-tuple-element.76), channel_id=1, source_target_pairs={{0,24},{8,16},{16,8},{24,0},{1,25},{9,17},{17,9},{25,1},{2,26},{10... | collective-permute-start | bytes 589832 | tf_op jit(solution)/shard_map/ppermute | solution.py:248
  30.1 1.8 %copy-done.1 = bf16[1,1024,1344]{1,2,0:T(8,128)(2,1)S(1)} copy-done((bf16[1,1024,1344]{1,2,0:T(8,128)(2,1)S(1)}, bf16[1,1024,1344]{1,2,0:T(8,128)(2,1)}, u32[]{:S(2)}) %copy-start.1) | copy-done | bytes 2752536
  31.8 3.9 %hidden.1 = (bf16[768,1024]{1,0:T(8,128)(2,1)S(1)}, bf16[1344,768]{1,0:T(8,128)(2,1)S(1)}, bf16[1344,768]{1,0:T(8,128)(2,1)S(1)}) custom-call(bf16[192,1024]{1,0:T(8,128)(2,1)S(1)} %get-tuple-element.77.own, bf16[192,512]{1,0:T(8,128)(2,1)S(1)} %collective-permute-done.3.refs_0_, bf16[192,512]{1,0:T(8,128)(2,1)S(1)} %collective-permute-done.4.refs_1_, ...), custom_call_target="tpu_custom_call" | custom-call | flops 33030144 | bytes 156672 | tf_op jit(solution)/shard_map/hidden/pallas_call | solution.py:31
  35.8 4.1 %rows.1 = (bf16[768,512]{1,0:T(8,128)(2,1)S(1)}, bf16[768,512]{1,0:T(8,128)(2,1)S(1)}) custom-call(bf16[1344,768]{1,0:T(8,128)(2,1)S(1)} %get-tuple-element.106.units_ref.refs_6_, bf16[1344,1024]{1,0:T(8,128)(2,1)S(1)} %bitcast.11), custom_call_target="tpu_custom_call" | custom-call | flops 33030144 | bytes 99840 | tf_op jit(solution)/shard_map/rows/pallas_call | solution.py:31
  39.9 4.8 %collective-permute-done.1.refs_1_ = bf16[192,512]{1,0:T(8,128)(2,1)S(1)} collective-permute-done((bf16[192,512]{1,0:T(8,128)(2,1)S(1)}, bf16[192,512]{1,0:T(8,128)(2,1)S(1)}, u32[]{:S(2)}, u32[]{:S(2)}) %collective-permute-start.1) | collective-permute-done | bytes 196640 | tf_op jit(solution)/shard_map/ppermute | solution.py:248
  46.7 1.4 %outer_leaving.1 = (bf16[768,1024]{1,0:T(8,128)(2,1)S(1)}, bf16[1344,256]{1,0:T(8,128)(2,1)S(1)}, bf16[1344,256]{1,0:T(8,128)(2,1)S(1)}) custom-call(bf16[192,1024]{1,0:T(8,128)(2,1)S(1)} %get-tuple-element.73.own, bf16[192,512]{1,0:T(8,128)(2,1)S(1)} %collective-permute-done.refs_0_, bf16[192,512]{1,0:T(8,128)(2,1)S(1)} %collective-permute-done.1.refs_1_, ...), custom_call_target="tpu_custom_call" | custom-call | flops 16515072 | bytes 102912 | tf_op jit(solution)/shard_map/outer_leaving/pallas_call | solution.py:31
  48.1 1.6 %collective-permute-start.22 = (bf16[1344,256]{1,0:T(8,128)(2,1)S(1)}, bf16[1344,256]{1,0:T(8,128)(2,1)S(1)}, u32[]{:S(2)}, u32[]{:S(2)}) collective-permute-start(bf16[1344,256]{1,0:T(8,128)(2,1)S(1)} %get-tuple-element.128), channel_id=1, source_target_pairs={{0,1},{1,0},{2,3},{3,2},{4,5},{5,4},{6,7},{7,6},{8,9},{9,8},{10,11... | collective-permute-start | bytes 2064392 | tf_op jit(solution)/shard_map/ppermute | solution.py:248
  49.6 1.5 %collective-permute-start.23 = (bf16[1344,256]{1,0:T(8,128)(2,1)S(1)}, bf16[1344,256]{1,0:T(8,128)(2,1)S(1)}, u32[]{:S(2)}, u32[]{:S(2)}) collective-permute-start(bf16[1344,256]{1,0:T(8,128)(2,1)S(1)} %get-tuple-element.129), channel_id=1, source_target_pairs={{0,2},{1,3},{2,0},{3,1},{4,6},{5,7},{6,4},{7,5},{8,10},{9,11},{10,... | collective-permute-start | bytes 2064392 | tf_op jit(solution)/shard_map/ppermute | solution.py:248
  51.3 4.1 %collective-permute-start.13 = (bf16[192,512]{1,0:T(8,128)(2,1)S(1)}, bf16[192,512]{1,0:T(8,128)(2,1)S(1)}, u32[]{:S(2)}, u32[]{:S(2)}) collective-permute-start(bf16[192,512]{1,0:T(8,128)(2,1)S(1)} %get-tuple-element.98), channel_id=1, source_target_pairs={{0,8},{8,0},{16,24},{24,16},{1,9},{9,1},{17,25},{25,17},{2,10},{10... | collective-permute-start | bytes 589832 | tf_op jit(solution)/shard_map/ppermute | solution.py:248
  55.4 1.1 %collective-permute-start.14 = (bf16[192,512]{1,0:T(8,128)(2,1)S(1)}, bf16[192,512]{1,0:T(8,128)(2,1)S(1)}, u32[]{:S(2)}, u32[]{:S(2)}) collective-permute-start(bf16[192,512]{1,0:T(8,128)(2,1)S(1)} %get-tuple-element.99), channel_id=1, source_target_pairs={{0,16},{8,24},{16,0},{24,8},{1,17},{9,25},{17,1},{25,9},{2,18},{10... | collective-permute-start | bytes 589832 | tf_op jit(solution)/shard_map/ppermute | solution.py:248
  56.5 1.4 %collective-permute-start.15 = (bf16[192,512]{1,0:T(8,128)(2,1)S(1)}, bf16[192,512]{1,0:T(8,128)(2,1)S(1)}, u32[]{:S(2)}, u32[]{:S(2)}) collective-permute-start(bf16[192,512]{1,0:T(8,128)(2,1)S(1)} %get-tuple-element.100), channel_id=1, source_target_pairs={{0,24},{8,16},{16,8},{24,0},{1,25},{9,17},{17,9},{25,1},{2,26},{10... | collective-permute-start | bytes 589832 | tf_op jit(solution)/shard_map/ppermute | solution.py:248
  57.9 3.6 %d_act.1.units_ref = bf16[1344,768]{1,0:T(8,128)(2,1)S(1)} custom-call(bf16[768,1024]{1,0:T(8,128)(2,1)S(1)} %get-tuple-element.107.g_ref.rows_ref, bf16[1344,768]{1,0:T(8,128)(2,1)S(1)} %get-tuple-element.102.positive_ref, bf16[1344,1024]{1,0:T(8,128)(2,1)S(1)} %bitcast.12), custom_call_target="tpu_custom_call" | custom-call | flops 33030144 | bytes 132096 | tf_op jit(solution)/shard_map/d_act/pallas_call | solution.py:31
  61.5 1.3 %inner_leaving.1 = (bf16[1344,256]{1,0:T(8,128)(2,1)S(1)}, bf16[1344,256]{1,0:T(8,128)(2,1)S(1)}) custom-call(bf16[1344,768]{1,0:T(8,128)(2,1)S(1)} %d_act.1.units_ref, bf16[768,1024]{1,0:T(8,128)(2,1)S(1)} %get-tuple-element.103.rows_ref), custom_call_target="tpu_custom_call" | custom-call | flops 16515072 | bytes 78336 | tf_op jit(solution)/shard_map/inner_leaving/pallas_call | solution.py:31
  62.8 1.3 %outer_staying.1 = (bf16[1344,256]{1,0:T(8,128)(2,1)S(1)}, bf16[1344,256]{1,0:T(8,128)(2,1)S(1)}) custom-call(bf16[1344,768]{1,0:T(8,128)(2,1)S(1)} %get-tuple-element.106.units_ref.refs_6_, bf16[768,1024]{1,0:T(8,128)(2,1)S(1)} %get-tuple-element.107.g_ref.rows_ref), custom_call_target="tpu_custom_call" | custom-call | flops 16515072 | bytes 78336 | tf_op jit(solution)/shard_map/outer_staying/pallas_call | solution.py:31
  64.6 4.1 %grad_rows.1 = (bf16[768,512]{1,0:T(8,128)(2,1)S(1)}, bf16[768,512]{1,0:T(8,128)(2,1)S(1)}) custom-call(bf16[1344,768]{1,0:T(8,128)(2,1)S(1)} %d_act.1.units_ref, bf16[1344,1024]{1,0:T(8,128)(2,1)S(1)} %bitcast.14), custom_call_target="tpu_custom_call" | custom-call | flops 33030144 | bytes 99840 | tf_op jit(solution)/shard_map/grad_rows/pallas_call | solution.py:31
  70.2 2.4 %collective-permute-done.14.refs_2_ = bf16[192,512]{1,0:T(8,128)(2,1)S(1)} collective-permute-done((bf16[192,512]{1,0:T(8,128)(2,1)S(1)}, bf16[192,512]{1,0:T(8,128)(2,1)S(1)}, u32[]{:S(2)}, u32[]{:S(2)}) %collective-permute-start.14) | collective-permute-done | bytes 196640 | tf_op jit(solution)/shard_map/ppermute | solution.py:248
  72.6 2.3 %collective-permute-done.17.came_ref = bf16[768,512]{1,0:T(8,128)(2,1)S(1)} collective-permute-done((bf16[768,512]{1,0:T(8,128)(2,1)S(1)}, bf16[768,512]{1,0:T(8,128)(2,1)S(1)}, u32[]{:S(2)}, u32[]{:S(2)}) %collective-permute-start.17) | collective-permute-done | bytes 786464 | tf_op jit(solution)/shard_map/ppermute | solution.py:248
  75.1 3.2 %collective-permute-start.18 = (bf16[192,512]{1,0:T(8,128)(2,1)S(1)}, bf16[192,512]{1,0:T(8,128)(2,1)S(1)}, u32[]{:S(2)}, u32[]{:S(2)}) collective-permute-start(bf16[192,512]{1,0:T(8,128)(2,1)S(1)} %get-tuple-element.121), channel_id=1, source_target_pairs={{0,8},{8,0},{16,24},{24,16},{1,9},{9,1},{17,25},{25,17},{2,10},{10... | collective-permute-start | bytes 589832 | tf_op jit(solution)/shard_map/ppermute | solution.py:248
  78.3 1.1 %collective-permute-start.19 = (bf16[192,512]{1,0:T(8,128)(2,1)S(1)}, bf16[192,512]{1,0:T(8,128)(2,1)S(1)}, u32[]{:S(2)}, u32[]{:S(2)}) collective-permute-start(bf16[192,512]{1,0:T(8,128)(2,1)S(1)} %get-tuple-element.122), channel_id=1, source_target_pairs={{0,16},{8,24},{16,0},{24,8},{1,17},{9,25},{17,1},{25,9},{2,18},{10... | collective-permute-start | bytes 589832 | tf_op jit(solution)/shard_map/ppermute | solution.py:248
  79.4 1.4 %collective-permute-start.20 = (bf16[192,512]{1,0:T(8,128)(2,1)S(1)}, bf16[192,512]{1,0:T(8,128)(2,1)S(1)}, u32[]{:S(2)}, u32[]{:S(2)}) collective-permute-start(bf16[192,512]{1,0:T(8,128)(2,1)S(1)} %get-tuple-element.123), channel_id=1, source_target_pairs={{0,24},{8,16},{16,8},{24,0},{1,25},{9,17},{17,9},{25,1},{2,26},{10... | collective-permute-start | bytes 589832 | tf_op jit(solution)/shard_map/ppermute | solution.py:248
  80.8 1.2 %inner_staying.1 = (bf16[1344,256]{1,0:T(8,128)(2,1)S(1)}, bf16[1344,256]{1,0:T(8,128)(2,1)S(1)}) custom-call(bf16[1344,768]{1,0:T(8,128)(2,1)S(1)} %d_act.1.units_ref, bf16[768,1024]{1,0:T(8,128)(2,1)S(1)} %get-tuple-element.103.rows_ref), custom_call_target="tpu_custom_call" | custom-call | flops 16515072 | bytes 78336 | tf_op jit(solution)/shard_map/inner_staying/pallas_call | solution.py:31
  82.1 10.9 %collective-permute-done.24.mixed0.came1 = bf16[2016,256]{1,0:T(8,128)(2,1)S(1)} collective-permute-done((bf16[2016,256]{1,0:T(8,128)(2,1)S(1)}, bf16[2016,256]{1,0:T(8,128)(2,1)S(1)}, u32[]{:S(2)}, u32[]{:S(2)}) %collective-permute-start.24) | collective-permute-done | bytes 1032224 | tf_op jit(solution)/shard_map/ppermute | solution.py:248
  94.1 1.5 %collective-permute-start.27 = (bf16[672,256]{1,0:T(8,128)(2,1)S(1)}, bf16[672,256]{1,0:T(8,128)(2,1)S(1)}, u32[]{:S(2)}, u32[]{:S(2)}) collective-permute-start(bf16[672,256]{1,0:T(8,128)(2,1)S(1)} %get-tuple-element.137), channel_id=1, source_target_pairs={{0,1},{1,0},{2,3},{3,2},{4,5},{5,4},{6,7},{7,6},{8,9},{9,8},{10,11... | collective-permute-start | bytes 1032200 | tf_op jit(solution)/shard_map/ppermute | solution.py:248
  99.0 1.2 %outer_last.1 = f32[1344,256]{1,0:T(8,128)} custom-call(bf16[672,256]{1,0:T(8,128)(2,1)S(1)} %get-tuple-element.138.own0, bf16[672,256]{1,0:T(8,128)(2,1)S(1)} %get-tuple-element.139.own1, bf16[2016,256]{1,0:T(8,128)(2,1)S(1)} %collective-permute-done.25.mixed1.came0, bf16[2016,256]{1,0:T(8,128)(2,1)S(1)} %collective-permute-done.24.mixed0.came1), custom_call_target="tpu_custom_call" | custom-call | bytes 64512 | tf_op jit(solution)/shard_map/outer_last/pallas_call | solution.py:31
  101.7 1.2 %inner_last.1 = f32[1344,256]{1,0:T(8,128)} custom-call(bf16[672,256]{1,0:T(8,128)(2,1)S(1)} %get-tuple-element.134.own0, bf16[672,256]{1,0:T(8,128)(2,1)S(1)} %get-tuple-element.135.own1, bf16[672,256]{1,0:T(8,128)(2,1)S(1)} %collective-permute-done.26.came0, bf16[672,256]{1,0:T(8,128)(2,1)S(1)} %collective-permute-done.27.came1), custom_call_target="tpu_custom_call" | custom-call | bytes 43008 | tf_op jit(solution)/shard_map/inner_last/pallas_call | solution.py:31
  (52 shorter events, 12.9 us)
Async XLA Ops:
  3.5 11.4 %collective-permute-start.3 = (bf16[192,512]{1,0:T(8,128)(2,1)S(1)}, bf16[192,512]{1,0:T(8,128)(2,1)S(1)}, u32[]{:S(2)}, u32[]{:S(2)}) collective-permute-start(bf16[192,512]{1,0:T(8,128)(2,1)S(1)} %get-tuple-element.78), channel_id=1, source_target_pairs={{0,8},{8,0},{16,24},{24,16},{1,9},{9,1},{17,25},{25,17},{2,10},{10... | collective-permute-start | bytes 589832 | tf_op jit(solution)/shard_map/ppermute | solution.py:248
  6.6 17.2 %collective-permute-start.4 = (bf16[192,512]{1,0:T(8,128)(2,1)S(1)}, bf16[192,512]{1,0:T(8,128)(2,1)S(1)}, u32[]{:S(2)}, u32[]{:S(2)}) collective-permute-start(bf16[192,512]{1,0:T(8,128)(2,1)S(1)} %get-tuple-element.79), channel_id=1, source_target_pairs={{0,16},{8,24},{16,0},{24,8},{1,17},{9,25},{17,1},{25,9},{2,18},{10... | collective-permute-start | bytes 589832 | tf_op jit(solution)/shard_map/ppermute | solution.py:248
  9.1 14.6 %collective-permute-start.5 = (bf16[192,512]{1,0:T(8,128)(2,1)S(1)}, bf16[192,512]{1,0:T(8,128)(2,1)S(1)}, u32[]{:S(2)}, u32[]{:S(2)}) collective-permute-start(bf16[192,512]{1,0:T(8,128)(2,1)S(1)} %get-tuple-element.80), channel_id=1, source_target_pairs={{0,24},{8,16},{16,8},{24,0},{1,25},{9,17},{17,9},{25,1},{2,26},{10... | collective-permute-start | bytes 589832 | tf_op jit(solution)/shard_map/ppermute | solution.py:248
  9.1 1.2 %copy-start.3 = (f32[256,1024]{1,0:T(8,128)S(1)}, f32[256,1024]{1,0:T(8,128)}, u32[]{:S(2)}) copy-start(f32[256,1024]{1,0:T(8,128)} %cotangent_ref.1) | copy-start | bytes 3145732
  23.7 4.9 %collective-permute-start.6 = (bf16[192,512]{1,0:T(8,128)(2,1)S(1)}, bf16[192,512]{1,0:T(8,128)(2,1)S(1)}, u32[]{:S(2)}, u32[]{:S(2)}) collective-permute-start(bf16[192,512]{1,0:T(8,128)(2,1)S(1)} %collective-permute-done.3.refs_0_), channel_id=1, source_target_pairs={{0,4},{4,0},{1,5},{5,1},{2,6},{6,2},{3,7},{7,3},{8,12},{12,8},{9,1... | collective-permute-start | bytes 589832 | tf_op jit(solution)/shard_map/ppermute | solution.py:248
  23.7 6.3 %collective-permute-start.7 = (bf16[192,512]{1,0:T(8,128)(2,1)S(1)}, bf16[192,512]{1,0:T(8,128)(2,1)S(1)}, u32[]{:S(2)}, u32[]{:S(2)}) collective-permute-start(bf16[192,512]{1,0:T(8,128)(2,1)S(1)} %collective-permute-done.4.refs_1_), channel_id=1, source_target_pairs={{0,4},{4,0},{1,5},{5,1},{2,6},{6,2},{3,7},{7,3},{8,12},{12,8},{9,1... | collective-permute-start | bytes 589832 | tf_op jit(solution)/shard_map/ppermute | solution.py:248
  24.2 5.8 %collective-permute-start.8 = (bf16[192,512]{1,0:T(8,128)(2,1)S(1)}, bf16[192,512]{1,0:T(8,128)(2,1)S(1)}, u32[]{:S(2)}, u32[]{:S(2)}) collective-permute-start(bf16[192,512]{1,0:T(8,128)(2,1)S(1)} %collective-permute-done.5.refs_2_), channel_id=1, source_target_pairs={{0,4},{4,0},{1,5},{5,1},{2,6},{6,2},{3,7},{7,3},{8,12},{12,8},{9,1... | collective-permute-start | bytes 589832 | tf_op jit(solution)/shard_map/ppermute | solution.py:248
  24.2 15.6 %collective-permute-start = (bf16[192,512]{1,0:T(8,128)(2,1)S(1)}, bf16[192,512]{1,0:T(8,128)(2,1)S(1)}, u32[]{:S(2)}, u32[]{:S(2)}) collective-permute-start(bf16[192,512]{1,0:T(8,128)(2,1)S(1)} %get-tuple-element.74), channel_id=1, source_target_pairs={{0,8},{8,0},{16,24},{24,16},{1,9},{9,1},{17,25},{25,17},{2,10},{10... | collective-permute-start | bytes 589832 | tf_op jit(solution)/shard_map/ppermute | solution.py:248
  27.6 17.1 %collective-permute-start.1 = (bf16[192,512]{1,0:T(8,128)(2,1)S(1)}, bf16[192,512]{1,0:T(8,128)(2,1)S(1)}, u32[]{:S(2)}, u32[]{:S(2)}) collective-permute-start(bf16[192,512]{1,0:T(8,128)(2,1)S(1)} %get-tuple-element.75), channel_id=1, source_target_pairs={{0,16},{8,24},{16,0},{24,8},{1,17},{9,25},{17,1},{25,9},{2,18},{10... | collective-permute-start | bytes 589832 | tf_op jit(solution)/shard_map/ppermute | solution.py:248
  28.6 16.1 %collective-permute-start.2 = (bf16[192,512]{1,0:T(8,128)(2,1)S(1)}, bf16[192,512]{1,0:T(8,128)(2,1)S(1)}, u32[]{:S(2)}, u32[]{:S(2)}) collective-permute-start(bf16[192,512]{1,0:T(8,128)(2,1)S(1)} %get-tuple-element.76), channel_id=1, source_target_pairs={{0,24},{8,16},{16,8},{24,0},{1,25},{9,17},{17,9},{25,1},{2,26},{10... | collective-permute-start | bytes 589832 | tf_op jit(solution)/shard_map/ppermute | solution.py:248
  30.1 1.8 %copy-start.1 = (bf16[1,1024,1344]{1,2,0:T(8,128)(2,1)S(1)}, bf16[1,1024,1344]{1,2,0:T(8,128)(2,1)}, u32[]{:S(2)}) copy-start(bf16[1,1024,1344]{1,2,0:T(8,128)(2,1)} %param.12) | copy-start | bytes 8257540
  31.8 3.9 %copy-start = (bf16[1,1344,1024]{2,1,0:T(8,128)(2,1)S(1)}, bf16[1,1344,1024]{2,1,0:T(8,128)(2,1)}, u32[]{:S(2)}) copy-start(bf16[1,1344,1024]{2,1,0:T(8,128)(2,1)} %param.13) | copy-start | bytes 8257540
  44.7 1.4 %collective-permute-start.9 = (bf16[192,512]{1,0:T(8,128)(2,1)S(1)}, bf16[192,512]{1,0:T(8,128)(2,1)S(1)}, u32[]{:S(2)}, u32[]{:S(2)}) collective-permute-start(bf16[192,512]{1,0:T(8,128)(2,1)S(1)} %collective-permute-done.refs_0_), channel_id=1, source_target_pairs={{0,4},{4,0},{1,5},{5,1},{2,6},{6,2},{3,7},{7,3},{8,12},{12,8},{9,1... | collective-permute-start | bytes 589832 | tf_op jit(solution)/shard_map/ppermute | solution.py:248
  44.7 1.7 %collective-permute-start.10 = (bf16[192,512]{1,0:T(8,128)(2,1)S(1)}, bf16[192,512]{1,0:T(8,128)(2,1)S(1)}, u32[]{:S(2)}, u32[]{:S(2)}) collective-permute-start(bf16[192,512]{1,0:T(8,128)(2,1)S(1)} %collective-permute-done.1.refs_1_), channel_id=1, source_target_pairs={{0,4},{4,0},{1,5},{5,1},{2,6},{6,2},{3,7},{7,3},{8,12},{12,8},{9,1... | collective-permute-start | bytes 589832 | tf_op jit(solution)/shard_map/ppermute | solution.py:248
  45.2 1.5 %collective-permute-start.11 = (bf16[192,512]{1,0:T(8,128)(2,1)S(1)}, bf16[192,512]{1,0:T(8,128)(2,1)S(1)}, u32[]{:S(2)}, u32[]{:S(2)}) collective-permute-start(bf16[192,512]{1,0:T(8,128)(2,1)S(1)} %collective-permute-done.2.refs_2_), channel_id=1, source_target_pairs={{0,4},{4,0},{1,5},{5,1},{2,6},{6,2},{3,7},{7,3},{8,12},{12,8},{9,1... | collective-permute-start | bytes 589832 | tf_op jit(solution)/shard_map/ppermute | solution.py:248
  45.2 5.9 %collective-permute-start.12 = (bf16[768,512]{1,0:T(8,128)(2,1)S(1)}, bf16[768,512]{1,0:T(8,128)(2,1)S(1)}, u32[]{:S(2)}, u32[]{:S(2)}) collective-permute-start(bf16[768,512]{1,0:T(8,128)(2,1)S(1)} %get-tuple-element.94), channel_id=1, source_target_pairs={{0,4},{4,0},{1,5},{5,1},{2,6},{6,2},{3,7},{7,3},{8,12},{12,8},{9,1... | collective-permute-start | bytes 2359304 | tf_op jit(solution)/shard_map/ppermute | solution.py:248
  48.1 20.6 %collective-permute-start.22 = (bf16[1344,256]{1,0:T(8,128)(2,1)S(1)}, bf16[1344,256]{1,0:T(8,128)(2,1)S(1)}, u32[]{:S(2)}, u32[]{:S(2)}) collective-permute-start(bf16[1344,256]{1,0:T(8,128)(2,1)S(1)} %get-tuple-element.128), channel_id=1, source_target_pairs={{0,1},{1,0},{2,3},{3,2},{4,5},{5,4},{6,7},{7,6},{8,9},{9,8},{10,11... | collective-permute-start | bytes 2064392 | tf_op jit(solution)/shard_map/ppermute | solution.py:248
  49.6 19.1 %collective-permute-start.23 = (bf16[1344,256]{1,0:T(8,128)(2,1)S(1)}, bf16[1344,256]{1,0:T(8,128)(2,1)S(1)}, u32[]{:S(2)}, u32[]{:S(2)}) collective-permute-start(bf16[1344,256]{1,0:T(8,128)(2,1)S(1)} %get-tuple-element.129), channel_id=1, source_target_pairs={{0,2},{1,3},{2,0},{3,1},{4,6},{5,7},{6,4},{7,5},{8,10},{9,11},{10,... | collective-permute-start | bytes 2064392 | tf_op jit(solution)/shard_map/ppermute | solution.py:248
  51.3 18.9 %collective-permute-start.13 = (bf16[192,512]{1,0:T(8,128)(2,1)S(1)}, bf16[192,512]{1,0:T(8,128)(2,1)S(1)}, u32[]{:S(2)}, u32[]{:S(2)}) collective-permute-start(bf16[192,512]{1,0:T(8,128)(2,1)S(1)} %get-tuple-element.98), channel_id=1, source_target_pairs={{0,8},{8,0},{16,24},{24,16},{1,9},{9,1},{17,25},{25,17},{2,10},{10... | collective-permute-start | bytes 589832 | tf_op jit(solution)/shard_map/ppermute | solution.py:248
  55.4 17.2 %collective-permute-start.14 = (bf16[192,512]{1,0:T(8,128)(2,1)S(1)}, bf16[192,512]{1,0:T(8,128)(2,1)S(1)}, u32[]{:S(2)}, u32[]{:S(2)}) collective-permute-start(bf16[192,512]{1,0:T(8,128)(2,1)S(1)} %get-tuple-element.99), channel_id=1, source_target_pairs={{0,16},{8,24},{16,0},{24,8},{1,17},{9,25},{17,1},{25,9},{2,18},{10... | collective-permute-start | bytes 589832 | tf_op jit(solution)/shard_map/ppermute | solution.py:248
  56.5 16.1 %collective-permute-start.15 = (bf16[192,512]{1,0:T(8,128)(2,1)S(1)}, bf16[192,512]{1,0:T(8,128)(2,1)S(1)}, u32[]{:S(2)}, u32[]{:S(2)}) collective-permute-start(bf16[192,512]{1,0:T(8,128)(2,1)S(1)} %get-tuple-element.100), channel_id=1, source_target_pairs={{0,24},{8,16},{16,8},{24,0},{1,25},{9,17},{17,9},{25,1},{2,26},{10... | collective-permute-start | bytes 589832 | tf_op jit(solution)/shard_map/ppermute | solution.py:248
  62.8 1.8 %copy-start.2 = (bf16[1,1024,1344]{1,2,0:T(8,128)(2,1)S(1)}, bf16[1,1024,1344]{1,2,0:T(8,128)(2,1)}, u32[]{:S(2)}) copy-start(bf16[1,1024,1344]{1,2,0:T(8,128)(2,1)} %param.12) | copy-start | bytes 8257540
  69.1 23.9 %collective-permute-start.24 = (bf16[2016,256]{1,0:T(8,128)(2,1)S(1)}, bf16[2016,256]{1,0:T(8,128)(2,1)S(1)}, u32[]{:S(2)}, u32[]{:S(2)}) collective-permute-start(bf16[2016,256]{1,0:T(8,128)(2,1)S(1)} %get-tuple-element.132), channel_id=1, source_target_pairs={{0,1},{1,0},{2,3},{3,2},{4,5},{5,4},{6,7},{7,6},{8,9},{9,8},{10,11... | collective-permute-start | bytes 3096584 | tf_op jit(solution)/shard_map/ppermute | solution.py:248
  69.7 23.6 %collective-permute-start.25 = (bf16[2016,256]{1,0:T(8,128)(2,1)S(1)}, bf16[2016,256]{1,0:T(8,128)(2,1)S(1)}, u32[]{:S(2)}, u32[]{:S(2)}) collective-permute-start(bf16[2016,256]{1,0:T(8,128)(2,1)S(1)} %get-tuple-element.133), channel_id=1, source_target_pairs={{0,2},{1,3},{2,0},{3,1},{4,6},{5,7},{6,4},{7,5},{8,10},{9,11},{10,... | collective-permute-start | bytes 3096584 | tf_op jit(solution)/shard_map/ppermute | solution.py:248
  72.6 2.3 %collective-permute-start.17 = (bf16[768,512]{1,0:T(8,128)(2,1)S(1)}, bf16[768,512]{1,0:T(8,128)(2,1)S(1)}, u32[]{:S(2)}, u32[]{:S(2)}) collective-permute-start(bf16[768,512]{1,0:T(8,128)(2,1)S(1)} %get-tuple-element.119), channel_id=1, source_target_pairs={{0,4},{4,0},{1,5},{5,1},{2,6},{6,2},{3,7},{7,3},{8,12},{12,8},{9,1... | collective-permute-start | bytes 2359304 | tf_op jit(solution)/shard_map/ppermute | solution.py:248
  75.1 21.3 %collective-permute-start.18 = (bf16[192,512]{1,0:T(8,128)(2,1)S(1)}, bf16[192,512]{1,0:T(8,128)(2,1)S(1)}, u32[]{:S(2)}, u32[]{:S(2)}) collective-permute-start(bf16[192,512]{1,0:T(8,128)(2,1)S(1)} %get-tuple-element.121), channel_id=1, source_target_pairs={{0,8},{8,0},{16,24},{24,16},{1,9},{9,1},{17,25},{25,17},{2,10},{10... | collective-permute-start | bytes 589832 | tf_op jit(solution)/shard_map/ppermute | solution.py:248
  78.3 18.1 %collective-permute-start.19 = (bf16[192,512]{1,0:T(8,128)(2,1)S(1)}, bf16[192,512]{1,0:T(8,128)(2,1)S(1)}, u32[]{:S(2)}, u32[]{:S(2)}) collective-permute-start(bf16[192,512]{1,0:T(8,128)(2,1)S(1)} %get-tuple-element.122), channel_id=1, source_target_pairs={{0,16},{8,24},{16,0},{24,8},{1,17},{9,25},{17,1},{25,9},{2,18},{10... | collective-permute-start | bytes 589832 | tf_op jit(solution)/shard_map/ppermute | solution.py:248
  79.4 17.0 %collective-permute-start.20 = (bf16[192,512]{1,0:T(8,128)(2,1)S(1)}, bf16[192,512]{1,0:T(8,128)(2,1)S(1)}, u32[]{:S(2)}, u32[]{:S(2)}) collective-permute-start(bf16[192,512]{1,0:T(8,128)(2,1)S(1)} %get-tuple-element.123), channel_id=1, source_target_pairs={{0,24},{8,16},{16,8},{24,0},{1,25},{9,17},{17,9},{25,1},{2,26},{10... | collective-permute-start | bytes 589832 | tf_op jit(solution)/shard_map/ppermute | solution.py:248
  93.5 8.0 %collective-permute-start.26 = (bf16[672,256]{1,0:T(8,128)(2,1)S(1)}, bf16[672,256]{1,0:T(8,128)(2,1)S(1)}, u32[]{:S(2)}, u32[]{:S(2)}) collective-permute-start(bf16[672,256]{1,0:T(8,128)(2,1)S(1)} %get-tuple-element.136), channel_id=1, source_target_pairs={{0,2},{1,3},{2,0},{3,1},{4,6},{5,7},{6,4},{7,5},{8,10},{9,11},{10,... | collective-permute-start | bytes 1032200 | tf_op jit(solution)/shard_map/ppermute | solution.py:248
  94.1 7.6 %collective-permute-start.27 = (bf16[672,256]{1,0:T(8,128)(2,1)S(1)}, bf16[672,256]{1,0:T(8,128)(2,1)S(1)}, u32[]{:S(2)}, u32[]{:S(2)}) collective-permute-start(bf16[672,256]{1,0:T(8,128)(2,1)S(1)} %get-tuple-element.137), channel_id=1, source_target_pairs={{0,1},{1,0},{2,3},{3,2},{4,5},{5,4},{6,7},{7,6},{8,9},{9,8},{10,11... | collective-permute-start | bytes 1032200 | tf_op jit(solution)/shard_map/ppermute | solution.py:248
  96.4 1.6 %collective-permute-start.16 = (bf16[256,512]{1,0:T(8,128)(2,1)S(1)}, bf16[256,512]{1,0:T(8,128)(2,1)S(1)}, u32[]{:S(2)}, u32[]{:S(2)}) collective-permute-start(bf16[256,512]{1,0:T(8,128)(2,1)S(1)} %get-tuple-element.117), channel_id=1, source_target_pairs={{0,4},{4,0},{1,5},{5,1},{2,6},{6,2},{3,7},{7,3},{8,12},{12,8},{9,1... | collective-permute-start | bytes 786440 | tf_op jit(solution)/shard_map/ppermute | solution.py:248
  97.0 3.3 %collective-permute-start.21 = (bf16[256,512]{1,0:T(8,128)(2,1)S(1)}, bf16[256,512]{1,0:T(8,128)(2,1)S(1)}, u32[]{:S(2)}, u32[]{:S(2)}) collective-permute-start(bf16[256,512]{1,0:T(8,128)(2,1)S(1)} %get-tuple-element.125), channel_id=1, source_target_pairs={{0,4},{4,0},{1,5},{5,1},{2,6},{6,2},{3,7},{7,3},{8,12},{12,8},{9,1... | collective-permute-start | bytes 786440 | tf_op jit(solution)/shard_map/ppermute | solution.py:248

commit v5 on v4

--- a/solution.py
+++ b/solution.py
@@ -56,55 +56,70 @@
         step(pl.ds(full * TILE, width - full * TILE))
 
 
+def tiles(units, rows):
+    for part in range(2):
+        for i in range(0, rows, TILE):
+            yield pl.ds(part * (units // 2), units // 2), pl.ds(i, min(TILE, rows - i))
+
+
 def picks(meta, k, shift, capacity):
     rows = lax.broadcasted_iota(jnp.int32, (meta.shape[0], capacity), 1) + shift * capacity
     return (meta[:, k : k + 1].astype(jnp.int32) == rows).astype(F32).astype(BF16)
 
 
+def ones(mask):
+    return mask.astype(F32).astype(BF16)
+
+
 def columns_of(table_t):
     count = table_t.shape[1]
-    unit = lax.broadcasted_iota(jnp.int32, (count, count), 0) == lax.broadcasted_iota(
-        jnp.int32, (count, count), 1
-    )
-    return mxu(unit.astype(F32).astype(BF16), table_t.astype(F32).astype(BF16), CONTRACT_LAST).astype(jnp.int32)
-
-
-def route_body(owners, capacity, routes_ref, index_ref, table_ref, tokens_ref, meta_ref, own_ref, *sends):
+    down, along = (lax.broadcasted_iota(jnp.int32, (count, count), i) for i in range(2))
+    return mxu(ones(down == along), table_t.astype(F32).astype(BF16), CONTRACT_LAST).astype(jnp.int32)
+
+
+def route_body(owners, capacity, routes_ref, tokens_ref, own_ref, *sends):
+    me, core = lax.axis_index("expert"), lax.axis_index("cuts")
+    top, count = routes_ref.shape
+    half = tokens_ref.shape[1] // lax.axis_size("cuts")
+    routes = routes_ref[...]
+    expert = lax.broadcasted_iota(jnp.int32, (-(-owners // ROW_TILE) * ROW_TILE, count), 0)
+    named = [routes[k : k + 1, :] == expert for k in range(top)]
+    down, along = (lax.broadcasted_iota(jnp.int32, (count, count), i) for i in range(2))
+    before = mxu(ones(sum(n.astype(F32) for n in named) > 0.0), ones(down < along))
+    slots = [
+        (routes[k : k + 1, :] ^ me) * capacity
+        + jnp.sum(jnp.where(named[k], before, 0.0), axis=0, keepdims=True).astype(jnp.int32)
+        for k in range(top)
+    ]
+    wide = tokens_ref[...].astype(BF16)
+    narrow = tokens_ref[:, window(core, half)].astype(BF16)
+    row = lax.broadcasted_iota(jnp.int32, (capacity, count), 0)
+    for shift, ref in reversed(list(enumerate((own_ref, *sends)))):
+        chosen = ones(sum((slot == row + shift * capacity).astype(F32) for slot in slots) > 0.0)
+        ref[...] = mxu(chosen, narrow if shift else wide).astype(BF16)
+
+
+def weigh_body(owners, capacity, routes_ref, index_ref, table_ref, cotangent_ref, meta_ref, own_ref, *sends):
     me, core = lax.axis_index("expert"), lax.axis_index("cuts")
     top, count = routes_ref.shape
     width = -(-owners // 128) * 128
-    half = tokens_ref.shape[1] // lax.axis_size("cuts")
+    half = cotangent_ref.shape[1] // lax.axis_size("cuts")
     routes, index = columns_of(routes_ref[...]), columns_of(index_ref[...])
     expert_lane = lax.broadcasted_iota(jnp.int32, (count, width), 1)
     named = [routes[:, k : k + 1] == expert_lane for k in range(top)]
-    onehot = sum(n.astype(F32) for n in named).astype(BF16)
-    earlier = lax.broadcasted_iota(jnp.int32, (count, count), 0) > lax.broadcasted_iota(
-        jnp.int32, (count, count), 1
-    )
-    before = mxu(earlier.astype(F32).astype(BF16), onehot)
+    down, along = (lax.broadcasted_iota(jnp.int32, (count, count), i) for i in range(2))
+    before = mxu(ones(down > along), ones(sum(n.astype(F32) for n in named) > 0.0))
     level = lax.broadcasted_iota(jnp.int32, (count, table_ref.shape[1]), 1)
     lane = lax.broadcasted_iota(jnp.int32, meta_ref.shape, 1)
     meta = jnp.zeros(meta_ref.shape, F32)
     for k in range(top):
         rank = jnp.sum(jnp.where(named[k], before, 0.0), axis=1, keepdims=True)
-        shift = routes[:, k : k + 1] ^ me
-        slot = (shift * capacity).astype(F32) + rank
+        slot = ((routes[:, k : k + 1] ^ me) * capacity).astype(F32) + rank
         weight = jnp.sum(
             jnp.where(index[:, k : k + 1] == level, table_ref[...], 0.0), axis=1, keepdims=True
         )
         meta = jnp.where(lane == k, slot, jnp.where(lane == top + k, weight, meta))
     meta_ref[...] = meta
-    wide = tokens_ref[...].astype(BF16)
-    narrow = tokens_ref[:, window(core, half)].astype(BF16)
-    for shift, ref in enumerate((own_ref, *sends)):
-        chosen = sum(picks(meta, k, shift, capacity) for k in range(top))
-        ref[...] = mxu(chosen, narrow if shift else wide, CONTRACT_FIRST).astype(BF16)
-
-
-def weigh_body(top, capacity, meta_ref, cotangent_ref, own_ref, *sends):
-    core = lax.axis_index("cuts")
-    meta = meta_ref[...]
-    half = cotangent_ref.shape[1] // lax.axis_size("cuts")
 
     def scaled(values):
         return [(meta[:, top + k : top + k + 1] * values).astype(BF16) for k in range(top)]
@@ -132,37 +147,35 @@
     inner_ref, x_ref, positive_ref, hidden_ref = refs[2 * remote :]
     assemble(x_ref, own, mine, other)
 
-    def step(units):
-        positive = jnp.maximum(mxu(inner_ref[units, :], x_ref[...], CONTRACT_LAST), 0.0)
-        positive_ref[units, :] = positive.astype(BF16)
-        hidden_ref[units, :] = (positive * positive).astype(BF16)
-
-    over_tiles(inner_ref.shape[0], step)
+    for units, rows in tiles(inner_ref.shape[0], x_ref.shape[0]):
+        positive = jnp.maximum(mxu(inner_ref[units, :], x_ref[rows, :], CONTRACT_LAST), 0.0)
+        positive_ref[units, rows] = positive.astype(BF16)
+        hidden_ref[units, rows] = (positive * positive).astype(BF16)
 
 
 def d_act_body(g_ref, positive_ref, outer_ref, d_act_ref):
-    def step(units):
-        d_hidden = mxu(outer_ref[units, :], g_ref[...], CONTRACT_LAST)
-        d_act_ref[units, :] = (d_hidden * 2.0 * positive_ref[units, :].astype(F32)).astype(BF16)
-
-    over_tiles(outer_ref.shape[0], step)
-
-
-def rows_body(units_ref, weight_ref, keep_ref, give_ref, turned):
+    for units, rows in tiles(outer_ref.shape[0], g_ref.shape[0]):
+        d_hidden = mxu(outer_ref[units, :], g_ref[rows, :], CONTRACT_LAST)
+        d_act_ref[units, rows] = (d_hidden * 2.0 * positive_ref[units, rows].astype(F32)).astype(BF16)
+
+
+def features_of(owner, rows_ref, weight_ref, out_ref):
+    half = out_ref.shape[1]
+    for i in range(half // TILE):
+        features = window(owner * (half // TILE) + i, TILE)
+        out_ref[:, i * TILE : (i + 1) * TILE] = mxu(rows_ref[...], weight_ref[:, features]).astype(BF16)
+
+
+def give_body(units_ref, weight_ref, turned_ref, give_ref):
     def turn(units):
-        turned[:, units] = units_ref[units, :].T
+        turned_ref[:, units] = units_ref[units, :].T
 
     over_tiles(units_ref.shape[0], turn)
-    core = lax.axis_index("cuts")
-    half = keep_ref.shape[1]
-    for owner, ref in ((1 - core, give_ref), (core, keep_ref)):
-
-        def step(i, carry, owner=owner, ref=ref):
-            features = window(owner * (half // TILE) + i, TILE)
-            ref[:, window(i, TILE)] = mxu(turned[...], weight_ref[:, features]).astype(BF16)
-            return carry
-
-        lax.fori_loop(0, half // TILE, step, 0)
+    features_of(1 - lax.axis_index("cuts"), turned_ref, weight_ref, give_ref)
+
+
+def keep_body(turned_ref, weight_ref, keep_ref):
+    features_of(lax.axis_index("cuts"), turned_ref, weight_ref, keep_ref)
 
 
 def split_body(keep_ref, came_ref, *outs):
@@ -212,11 +225,12 @@
     narrow_ref[...] = total.astype(BF16)
 
 
-def join_body(mine_ref, other_ref, out_ref):
+def join_body(*refs):
     core = lax.axis_index("cuts")
-    half = mine_ref.shape[1]
-    out_ref[:, window(core, half)] = mine_ref[...]
-    out_ref[:, window(1 - core, half)] = other_ref[...].astype(F32)
+    for mine_ref, other_ref, out_ref in (refs[::2], refs[1::2]):
+        half = mine_ref.shape[1]
+        out_ref[:, window(core, half)] = mine_ref[...]
+        out_ref[:, window(1 - core, half)] = other_ref[...].astype(F32)
 
 
 def added(a, b):
@@ -279,10 +293,13 @@
         got = {s: partner(chunks[s - 1], "expert", s) for s in reversed(range(1, owners))}
         return [got[s] for s in range(1, owners)]
 
-    def times_weight(units_rows, weight, name):
+    def given(units_rows, weight, name):
         return local(
-            rows_body, [shape(slots, half)] * 2, [units_rows, weight], work, name, [pltpu.VMEM((slots, units), BF16)]
+            give_body, [shape(slots, units), shape(slots, half)], [units_rows, weight], work // 2, name + "_give"
         )
+
+    def kept(turned, weight, name):
+        return local(keep_body, [shape(slots, half)], [turned, weight], work // 2, name + "_keep")[0]
 
     def split(keep, came):
         return local(split_body, [shape(capacity, half)] * owners, [keep, came], 0, "split")
@@ -296,30 +313,29 @@
             "combine",
         )
 
-    def join(wide, came):
-        return local(join_body, [shape(count, features, F32)], [wide, came], 0, "join", gives=pltpu.HBM)[0]
-
     def grads(keys, units_rows, rows, name):
         return local(functools.partial(grad_body, keys), [piece] * 2, [units_rows, rows], work // 2, name)
 
-    meta, own, *sends = local(
+    own, *sends = local(
         functools.partial(route_body, owners, capacity),
-        [shape(count, 128, F32), shape(capacity, features)] + [shape(capacity, half)] * remote,
-        [routes.T, combine_index.T, combine_table[None, :], tokens],
+        [shape(capacity, features)] + [shape(capacity, half)] * remote,
+        [routes.T, tokens],
         2 * count * slots * features,
         "route",
         space=pltpu.HBM,
     )
     mine = over_experts(sends)
-    grad_own, *grad_sends = local(
-        functools.partial(weigh_body, top, capacity),
-        [shape(capacity, features)] + [shape(capacity, half)] * remote,
-        [meta, cotangent],
+    meta, grad_own, *grad_sends = local(
+        functools.partial(weigh_body, owners, capacity),
+        [shape(count, 128, F32), shape(capacity, features)] + [shape(capacity, half)] * remote,
+        [routes.T, combine_index.T, combine_table[None, :], cotangent],
         4 * count * slots * features,
         "weigh",
+        space=pltpu.HBM,
     )
     grad_mine = over_experts(grad_sends)
-    mine = after(mine, grad_sends)
+    mine, nearest = after((mine, grad_mine[0]), grad_sends)
+    grad_mine = [nearest, *grad_mine[1:]]
     other = across_cores(mine)
     arrived, positive, hidden = local(
         functools.partial(hidden_body, remote),
@@ -328,7 +344,8 @@
         work,
         "hidden",
     )
-    keep, give = times_weight(hidden, outer, "rows")
+    turned, give = given(hidden, outer, "rows")
+    keep = kept(turned, outer, "rows")
     grad_mine, hidden, keep, give = after((grad_mine, hidden, keep, give))
     came = partner(give, "cuts", 1)
     grad_other = across_cores(grad_mine)
@@ -351,8 +368,8 @@
     hidden, grad_rows = after((hidden, grad_rows), inner_sent)
     outer_kept = grads(staying, hidden, grad_rows, "outer_staying")
     d_act_late = after(d_act, outer_kept)
-    grad_keep, grad_give = times_weight(d_act_late, inner, "grad_rows")
-    outer_came = after(outer_came, grad_give)
+    turned, grad_give = given(d_act_late, inner, "grad_rows")
+    grad_keep = kept(turned, inner, "grad_rows")
     *sends, outer_own0, outer_own1 = local(
         mix_body,
         [shape(3 * part_rows, piece.shape[1])] * 2 + [quarter] * 2,
@@ -366,6 +383,8 @@
     inner_kept = grads(staying, d_act, arrived, "inner_staying")
     chunks = split(grad_keep, grad_came)
     grad_returned = [chunks[0]] + over_experts(chunks[1:])
+    wide, narrow = combine(returned, True)
+    mixed = after(mixed, wide)
     move0, move1, inner_own0, inner_own1 = local(
         inner_sum_body, [quarter] * 4, [*inner_kept, *mixed], 0, "inner_sum"
     )
@@ -374,10 +393,17 @@
         last_sum_body, [total], [outer_own0, outer_own1, *mixed[::-1]], 0, "outer_last", gives=pltpu.HBM
     )
     (grad_in,) = local(last_sum_body, [total], [inner_own0, inner_own1, *moved], 0, "inner_last", gives=pltpu.HBM)
-    wide, narrow = combine(returned, True)
-    layer_out = join(wide, partner(narrow, "cuts", 1))
-    wide, narrow = combine(grad_returned, False)
-    d_tokens = join(wide, partner(narrow, "cuts", 1))
+    came = partner(narrow, "cuts", 1)
+    grad_returned = after(grad_returned, grad_out)
+    grad_wide, narrow = combine(grad_returned, False)
+    layer_out, d_tokens = local(
+        join_body,
+        [shape(count, features, F32)] * 2,
+        [wide, grad_wide, came, partner(narrow, "cuts", 1)],
+        0,
+        "join",
+        gives=pltpu.HBM,
+    )
     grad_in = grad_in.T
     return (layer_out, d_tokens, grad_in[None], grad_out[None])
 

time: 103 us -> 101 us (0.981); the launches traced: 103 us -> 99.4 us
  starting transfers between devices: 32.2 us -> 35.1 us
  Pallas kernels: 31.4 us -> 28.6 us
  waiting for transfers between devices: 35 us -> 33.1 us
  local copies, waits for them, and re-layouts: 3.51 us -> 1.78 us
    ppermute x28, starting transfers between devices: 32.2 us -> 35.1 us  [partner(): lax.ppermute(x, axis, [(i, i ^ bit) for i in range(lax.axis_size(axis))])]
    pallas_call x20 -> x21, Pallas kernels: 31.4 us -> 28.6 us  [local(): pl.pallas_call(body, out_shape=tuple((gives(x.shape, x.dtype) for x in ou...]
    ppermute x28, waiting for transfers between devices: 35 us -> 33.1 us  [partner(): lax.ppermute(x, axis, [(i, i ^ bit) for i in range(lax.axis_size(axis))])]
    unnamed x8 -> x6, local copies, waits for them, and re-layouts: 3.51 us -> 1.78 us
  transfers between devices with their start and end apart: 28 -> 28, of which waited for: 13 -> 17; matrix products, arithmetic and copies ran while one was open for 0% -> 0% of each run, Pallas kernels for 27% -> 26%
where the time goes in v5:
time: 101 us; the launch traced here: 99.4 us
  starting transfers between devices  35.1 us (35%)
  waiting for transfers between devices  33.1 us (33%)
  Pallas kernels  28.6 us (28%)
  local copies, waits for them, and re-layouts  1.78 us (2%)
    ppermute x28, starting transfers between devices, partner(): lax.ppermute(x, axis, [(i, i ^ bit) for i in range(lax.axis_size(axis))])  35.1 us
    ppermute x28, waiting for transfers between devices, partner(): lax.ppermute(x, axis, [(i, i ^ bit) for i in range(lax.axis_size(axis))])  33.1 us
    pallas_call x21, Pallas kernels, local(): pl.pallas_call(body, out_shape=tuple((gives(x.shape, x.dtype) for x in ou...  28.6 us
  transfers between devices with their start and end apart: 28, of which 17 were waited for; matrix products, arithmetic and copies ran while one was open for 0% of the time, Pallas kernels for 26%

profile of v5, /device:TPU:0, one launch (start us, length us, event | category | flops | bytes accessed | tf_op | source)
XLA Modules:
  0.0 99.4 jit_solution(18061532517824322978)
XLA Ops:
  0.6 1.8 %route.1 = (bf16[192,1024]{1,0:T(8,128)(2,1)S(1)}, bf16[192,512]{1,0:T(8,128)(2,1)S(1)}, bf16[192,512]{1,0:T(8,128)(2,1)S(1)}, bf16[192,512]{1,0:T(8,128)(2,1)S(1)}) custom-call(s32[2,256]{1,0:T(2,128)} %bitcast.19, f32[256,1024]{1,0:T(8,128)} %tokens_ref.1), custom_call_target="tpu_custom_call" | custom-call | flops 6291456 | bytes 31776 | tf_op jit(solution)/shard_map/route/pallas_call | solution.py:31
  2.5 3.1 %collective-permute-start = (bf16[192,512]{1,0:T(8,128)(2,1)S(1)}, bf16[192,512]{1,0:T(8,128)(2,1)S(1)}, u32[]{:S(2)}, u32[]{:S(2)}) collective-permute-start(bf16[192,512]{1,0:T(8,128)(2,1)S(1)} %get-tuple-element.81), channel_id=1, source_target_pairs={{0,8},{8,0},{16,24},{24,16},{1,9},{9,1},{17,25},{25,17},{2,10},{10... | collective-permute-start | bytes 589832 | tf_op jit(solution)/shard_map/ppermute | solution.py:262
  5.6 2.6 %collective-permute-start.1 = (bf16[192,512]{1,0:T(8,128)(2,1)S(1)}, bf16[192,512]{1,0:T(8,128)(2,1)S(1)}, u32[]{:S(2)}, u32[]{:S(2)}) collective-permute-start(bf16[192,512]{1,0:T(8,128)(2,1)S(1)} %get-tuple-element.82), channel_id=1, source_target_pairs={{0,16},{8,24},{16,0},{24,8},{1,17},{9,25},{17,1},{25,9},{2,18},{10... | collective-permute-start | bytes 589832 | tf_op jit(solution)/shard_map/ppermute | solution.py:262
  8.2 3.2 %weigh.1 = (f32[256,128]{1,0:T(8,128)S(1)}, bf16[192,1024]{1,0:T(8,128)(2,1)S(1)}, bf16[192,512]{1,0:T(8,128)(2,1)S(1)}, bf16[192,512]{1,0:T(8,128)(2,1)S(1)}, bf16[192,512]{1,0:T(8,128)(2,1)S(1)}) custom-call(s32[2,256]{1,0:T(2,128)} %bitcast.20, s32[2,256]{1,0:T(2,128)} %bitcast.21, f32[1,256]{1,0:T(1,128)} %bitcast.22, f32[256,1024]{1,0:T(8,128)} %cotangent_ref.1), custom_call_target="tpu_custom_call" | custom-call | flops 12582912 | bytes 33872 | tf_op jit(solution)/shard_map/weigh/pallas_call | solution.py:31
  12.3 2.0 %collective-permute-done.refs_0_ = bf16[192,512]{1,0:T(8,128)(2,1)S(1)} collective-permute-done((bf16[192,512]{1,0:T(8,128)(2,1)S(1)}, bf16[192,512]{1,0:T(8,128)(2,1)S(1)}, u32[]{:S(2)}, u32[]{:S(2)}) %collective-permute-start) | collective-permute-done | bytes 196640 | tf_op jit(solution)/shard_map/ppermute | solution.py:262
  14.3 8.5 %collective-permute-done.1.refs_1_ = bf16[192,512]{1,0:T(8,128)(2,1)S(1)} collective-permute-done((bf16[192,512]{1,0:T(8,128)(2,1)S(1)}, bf16[192,512]{1,0:T(8,128)(2,1)S(1)}, u32[]{:S(2)}, u32[]{:S(2)}) %collective-permute-start.1) | collective-permute-done | bytes 196640 | tf_op jit(solution)/shard_map/ppermute | solution.py:262
  23.6 4.0 %collective-permute-start.4 = (bf16[192,512]{1,0:T(8,128)(2,1)S(1)}, bf16[192,512]{1,0:T(8,128)(2,1)S(1)}, u32[]{:S(2)}, u32[]{:S(2)}) collective-permute-start(bf16[192,512]{1,0:T(8,128)(2,1)S(1)} %get-tuple-element.85), channel_id=1, source_target_pairs={{0,16},{8,24},{16,0},{24,8},{1,17},{9,25},{17,1},{25,9},{2,18},{10... | collective-permute-start | bytes 589832 | tf_op jit(solution)/shard_map/ppermute | solution.py:262
  27.7 1.3 %collective-permute-start.5 = (bf16[192,512]{1,0:T(8,128)(2,1)S(1)}, bf16[192,512]{1,0:T(8,128)(2,1)S(1)}, u32[]{:S(2)}, u32[]{:S(2)}) collective-permute-start(bf16[192,512]{1,0:T(8,128)(2,1)S(1)} %get-tuple-element.86), channel_id=1, source_target_pairs={{0,24},{8,16},{16,8},{24,0},{1,25},{9,17},{17,9},{25,1},{2,26},{10... | collective-permute-start | bytes 589832 | tf_op jit(solution)/shard_map/ppermute | solution.py:262
  29.0 1.8 %copy-done.1 = bf16[1,1024,1344]{1,2,0:T(8,128)(2,1)S(1)} copy-done((bf16[1,1024,1344]{1,2,0:T(8,128)(2,1)S(1)}, bf16[1,1024,1344]{1,2,0:T(8,128)(2,1)}, u32[]{:S(2)}) %copy-start.1) | copy-done | bytes 2752536
  30.8 2.4 %hidden.1 = (bf16[768,1024]{1,0:T(8,128)(2,1)S(1)}, bf16[1344,768]{1,0:T(8,128)(2,1)S(1)}, bf16[1344,768]{1,0:T(8,128)(2,1)S(1)}) custom-call(bf16[192,1024]{1,0:T(8,128)(2,1)S(1)} %get-tuple-element.88.own, bf16[192,512]{1,0:T(8,128)(2,1)S(1)} %collective-permute-done.refs_0_, bf16[192,512]{1,0:T(8,128)(2,1)S(1)} %collective-permute-done.1.refs_1_, ...), custom_call_target="tpu_custom_call" | custom-call | flops 33030144 | bytes 156672 | tf_op jit(solution)/shard_map/hidden/pallas_call | solution.py:31
  33.2 2.4 %rows_give.1 = (bf16[768,1344]{1,0:T(8,128)(2,1)S(1)}, bf16[768,512]{1,0:T(8,128)(2,1)S(1)}) custom-call(bf16[1344,768]{1,0:T(8,128)(2,1)S(1)} %get-tuple-element.114.units_ref.refs_6_, bf16[1344,1024]{1,0:T(8,128)(2,1)S(1)} %bitcast.11), custom_call_target="tpu_custom_call" | custom-call | flops 16515072 | bytes 119808 | tf_op jit(solution)/shard_map/rows_give/pallas_call | solution.py:31
  35.5 1.4 %rows_keep.1.keep_ref = bf16[768,512]{1,0:T(8,128)(2,1)S(1)} custom-call(bf16[768,1344]{1,0:T(8,128)(2,1)S(1)} %get-tuple-element.93.turned_ref, bf16[1344,1024]{1,0:T(8,128)(2,1)S(1)} %bitcast.12), custom_call_target="tpu_custom_call" | custom-call | flops 16515072 | bytes 87552 | tf_op jit(solution)/shard_map/rows_keep/pallas_call | solution.py:31
  37.0 4.9 %collective-permute-done.4.refs_1_ = bf16[192,512]{1,0:T(8,128)(2,1)S(1)} collective-permute-done((bf16[192,512]{1,0:T(8,128)(2,1)S(1)}, bf16[192,512]{1,0:T(8,128)(2,1)S(1)}, u32[]{:S(2)}, u32[]{:S(2)}) %collective-permute-start.4) | collective-permute-done | bytes 196640 | tf_op jit(solution)/shard_map/ppermute | solution.py:262
  43.8 1.4 %outer_leaving.1 = (bf16[768,1024]{1,0:T(8,128)(2,1)S(1)}, bf16[1344,256]{1,0:T(8,128)(2,1)S(1)}, bf16[1344,256]{1,0:T(8,128)(2,1)S(1)}) custom-call(bf16[192,1024]{1,0:T(8,128)(2,1)S(1)} %get-tuple-element.80.own, bf16[192,512]{1,0:T(8,128)(2,1)S(1)} %collective-permute-done.3.refs_0_, bf16[192,512]{1,0:T(8,128)(2,1)S(1)} %collective-permute-done.4.refs_1_, ...), custom_call_target="tpu_custom_call" | custom-call | flops 16515072 | bytes 102912 | tf_op jit(solution)/shard_map/outer_leaving/pallas_call | solution.py:31
  45.2 1.5 %collective-permute-start.20 = (bf16[1344,256]{1,0:T(8,128)(2,1)S(1)}, bf16[1344,256]{1,0:T(8,128)(2,1)S(1)}, u32[]{:S(2)}, u32[]{:S(2)}) collective-permute-start(bf16[1344,256]{1,0:T(8,128)(2,1)S(1)} %get-tuple-element.131), channel_id=1, source_target_pairs={{0,1},{1,0},{2,3},{3,2},{4,5},{5,4},{6,7},{7,6},{8,9},{9,8},{10,11... | collective-permute-start | bytes 2064392 | tf_op jit(solution)/shard_map/ppermute | solution.py:262
  46.8 1.5 %collective-permute-start.21 = (bf16[1344,256]{1,0:T(8,128)(2,1)S(1)}, bf16[1344,256]{1,0:T(8,128)(2,1)S(1)}, u32[]{:S(2)}, u32[]{:S(2)}) collective-permute-start(bf16[1344,256]{1,0:T(8,128)(2,1)S(1)} %get-tuple-element.132), channel_id=1, source_target_pairs={{0,2},{1,3},{2,0},{3,1},{4,6},{5,7},{6,4},{7,5},{8,10},{9,11},{10,... | collective-permute-start | bytes 2064392 | tf_op jit(solution)/shard_map/ppermute | solution.py:262
  48.5 4.7 %collective-permute-start.13 = (bf16[192,512]{1,0:T(8,128)(2,1)S(1)}, bf16[192,512]{1,0:T(8,128)(2,1)S(1)}, u32[]{:S(2)}, u32[]{:S(2)}) collective-permute-start(bf16[192,512]{1,0:T(8,128)(2,1)S(1)} %get-tuple-element.106), channel_id=1, source_target_pairs={{0,8},{8,0},{16,24},{24,16},{1,9},{9,1},{17,25},{25,17},{2,10},{10... | collective-permute-start | bytes 589832 | tf_op jit(solution)/shard_map/ppermute | solution.py:262
  54.1 1.4 %collective-permute-start.15 = (bf16[192,512]{1,0:T(8,128)(2,1)S(1)}, bf16[192,512]{1,0:T(8,128)(2,1)S(1)}, u32[]{:S(2)}, u32[]{:S(2)}) collective-permute-start(bf16[192,512]{1,0:T(8,128)(2,1)S(1)} %get-tuple-element.108), channel_id=1, source_target_pairs={{0,24},{8,16},{16,8},{24,0},{1,25},{9,17},{17,9},{25,1},{2,26},{10... | collective-permute-start | bytes 589832 | tf_op jit(solution)/shard_map/ppermute | solution.py:262
  55.6 2.3 %d_act.1.units_ref = bf16[1344,768]{1,0:T(8,128)(2,1)S(1)} custom-call(bf16[768,1024]{1,0:T(8,128)(2,1)S(1)} %get-tuple-element.115.g_ref.rows_ref, bf16[1344,768]{1,0:T(8,128)(2,1)S(1)} %get-tuple-element.110.positive_ref, bf16[1344,1024]{1,0:T(8,128)(2,1)S(1)} %bitcast.13), custom_call_target="tpu_custom_call" | custom-call | flops 33030144 | bytes 132096 | tf_op jit(solution)/shard_map/d_act/pallas_call | solution.py:31
  57.9 1.3 %inner_leaving.1 = (bf16[1344,256]{1,0:T(8,128)(2,1)S(1)}, bf16[1344,256]{1,0:T(8,128)(2,1)S(1)}) custom-call(bf16[1344,768]{1,0:T(8,128)(2,1)S(1)} %d_act.1.units_ref, bf16[768,1024]{1,0:T(8,128)(2,1)S(1)} %get-tuple-element.111.rows_ref), custom_call_target="tpu_custom_call" | custom-call | flops 16515072 | bytes 78336 | tf_op jit(solution)/shard_map/inner_leaving/pallas_call | solution.py:31
  59.2 1.3 %outer_staying.1 = (bf16[1344,256]{1,0:T(8,128)(2,1)S(1)}, bf16[1344,256]{1,0:T(8,128)(2,1)S(1)}) custom-call(bf16[1344,768]{1,0:T(8,128)(2,1)S(1)} %get-tuple-element.114.units_ref.refs_6_, bf16[768,1024]{1,0:T(8,128)(2,1)S(1)} %get-tuple-element.115.g_ref.rows_ref), custom_call_target="tpu_custom_call" | custom-call | flops 16515072 | bytes 78336 | tf_op jit(solution)/shard_map/outer_staying/pallas_call | solution.py:31
  60.5 2.4 %collective-permute-done.20.came0 = bf16[1344,256]{1,0:T(8,128)(2,1)S(1)} collective-permute-done((bf16[1344,256]{1,0:T(8,128)(2,1)S(1)}, bf16[1344,256]{1,0:T(8,128)(2,1)S(1)}, u32[]{:S(2)}, u32[]{:S(2)}) %collective-permute-start.20) | collective-permute-done | bytes 688160 | tf_op jit(solution)/shard_map/ppermute | solution.py:262
  65.0 1.5 %collective-permute-start.23 = (bf16[2016,256]{1,0:T(8,128)(2,1)S(1)}, bf16[2016,256]{1,0:T(8,128)(2,1)S(1)}, u32[]{:S(2)}, u32[]{:S(2)}) collective-permute-start(bf16[2016,256]{1,0:T(8,128)(2,1)S(1)} %get-tuple-element.136), channel_id=1, source_target_pairs={{0,2},{1,3},{2,0},{3,1},{4,6},{5,7},{6,4},{7,5},{8,10},{9,11},{10,... | collective-permute-start | bytes 3096584 | tf_op jit(solution)/shard_map/ppermute | solution.py:262
  66.5 2.4 %grad_rows_give.1 = (bf16[768,1344]{1,0:T(8,128)(2,1)S(1)}, bf16[768,512]{1,0:T(8,128)(2,1)S(1)}) custom-call(bf16[1344,768]{1,0:T(8,128)(2,1)S(1)} %d_act.1.units_ref, bf16[1344,1024]{1,0:T(8,128)(2,1)S(1)} %bitcast.15), custom_call_target="tpu_custom_call" | custom-call | flops 16515072 | bytes 119808 | tf_op jit(solution)/shard_map/grad_rows_give/pallas_call | solution.py:31
  68.9 1.3 %collective-permute-done.14.refs_2_ = bf16[192,512]{1,0:T(8,128)(2,1)S(1)} collective-permute-done((bf16[192,512]{1,0:T(8,128)(2,1)S(1)}, bf16[192,512]{1,0:T(8,128)(2,1)S(1)}, u32[]{:S(2)}, u32[]{:S(2)}) %collective-permute-start.14) | collective-permute-done | bytes 196640 | tf_op jit(solution)/shard_map/ppermute | solution.py:262
  70.3 1.4 %grad_rows_keep.1.keep_ref = bf16[768,512]{1,0:T(8,128)(2,1)S(1)} custom-call(bf16[768,1344]{1,0:T(8,128)(2,1)S(1)} %get-tuple-element.125.turned_ref, bf16[1344,1024]{1,0:T(8,128)(2,1)S(1)} %bitcast.16), custom_call_target="tpu_custom_call" | custom-call | flops 16515072 | bytes 87552 | tf_op jit(solution)/shard_map/grad_rows_keep/pallas_call | solution.py:31
  72.8 3.4 %collective-permute-start.17 = (bf16[192,512]{1,0:T(8,128)(2,1)S(1)}, bf16[192,512]{1,0:T(8,128)(2,1)S(1)}, u32[]{:S(2)}, u32[]{:S(2)}) collective-permute-start(bf16[192,512]{1,0:T(8,128)(2,1)S(1)} %get-tuple-element.128), channel_id=1, source_target_pairs={{0,8},{8,0},{16,24},{24,16},{1,9},{9,1},{17,25},{25,17},{2,10},{10... | collective-permute-start | bytes 589832 | tf_op jit(solution)/shard_map/ppermute | solution.py:262
  77.1 1.4 %collective-permute-start.19 = (bf16[192,512]{1,0:T(8,128)(2,1)S(1)}, bf16[192,512]{1,0:T(8,128)(2,1)S(1)}, u32[]{:S(2)}, u32[]{:S(2)}) collective-permute-start(bf16[192,512]{1,0:T(8,128)(2,1)S(1)} %get-tuple-element.130), channel_id=1, source_target_pairs={{0,24},{8,16},{16,8},{24,0},{1,25},{9,17},{17,9},{25,1},{2,26},{10... | collective-permute-start | bytes 589832 | tf_op jit(solution)/shard_map/ppermute | solution.py:262
  80.6 7.7 %collective-permute-done.22.came1.mixed0 = bf16[2016,256]{1,0:T(8,128)(2,1)S(1)} collective-permute-done((bf16[2016,256]{1,0:T(8,128)(2,1)S(1)}, bf16[2016,256]{1,0:T(8,128)(2,1)S(1)}, u32[]{:S(2)}, u32[]{:S(2)}) %collective-permute-start.22) | collective-permute-done | bytes 1032224 | tf_op jit(solution)/shard_map/ppermute | solution.py:262
  88.9 1.6 %collective-permute-start.26 = (bf16[672,256]{1,0:T(8,128)(2,1)S(1)}, bf16[672,256]{1,0:T(8,128)(2,1)S(1)}, u32[]{:S(2)}, u32[]{:S(2)}) collective-permute-start(bf16[672,256]{1,0:T(8,128)(2,1)S(1)} %get-tuple-element.152), channel_id=1, source_target_pairs={{0,2},{1,3},{2,0},{3,1},{4,6},{5,7},{6,4},{7,5},{8,10},{9,11},{10,... | collective-permute-start | bytes 1032200 | tf_op jit(solution)/shard_map/ppermute | solution.py:262
  90.5 1.4 %collective-permute-start.27 = (bf16[672,256]{1,0:T(8,128)(2,1)S(1)}, bf16[672,256]{1,0:T(8,128)(2,1)S(1)}, u32[]{:S(2)}, u32[]{:S(2)}) collective-permute-start(bf16[672,256]{1,0:T(8,128)(2,1)S(1)} %get-tuple-element.153), channel_id=1, source_target_pairs={{0,1},{1,0},{2,3},{3,2},{4,5},{5,4},{6,7},{7,6},{8,9},{9,8},{10,11... | collective-permute-start | bytes 1032200 | tf_op jit(solution)/shard_map/ppermute | solution.py:262
  95.4 1.5 %join.1 = (f32[256,1024]{1,0:T(8,128)}, f32[256,1024]{1,0:T(8,128)}) custom-call(f32[256,512]{1,0:T(8,128)S(1)} %get-tuple-element.124.refs_0_, f32[256,512]{1,0:T(8,128)S(1)} %get-tuple-element.143.refs_1_, bf16[256,512]{1,0:T(8,128)(2,1)S(1)} %collective-permute-done.24.refs_2_, bf16[256,512]{1,0:T(8,128)(2,1)S(1)} %collective-permute-done.25.refs_3_), custom_call_target="tpu_custom_call" | custom-call | bytes 57344 | tf_op jit(solution)/shard_map/join/pallas_call | solution.py:31
  (51 shorter events, 17.8 us)
Async XLA Ops:
  2.5 11.8 %collective-permute-start = (bf16[192,512]{1,0:T(8,128)(2,1)S(1)}, bf16[192,512]{1,0:T(8,128)(2,1)S(1)}, u32[]{:S(2)}, u32[]{:S(2)}) collective-permute-start(bf16[192,512]{1,0:T(8,128)(2,1)S(1)} %get-tuple-element.81), channel_id=1, source_target_pairs={{0,8},{8,0},{16,24},{24,16},{1,9},{9,1},{17,25},{25,17},{2,10},{10... | collective-permute-start | bytes 589832 | tf_op jit(solution)/shard_map/ppermute | solution.py:262
  5.6 17.2 %collective-permute-start.1 = (bf16[192,512]{1,0:T(8,128)(2,1)S(1)}, bf16[192,512]{1,0:T(8,128)(2,1)S(1)}, u32[]{:S(2)}, u32[]{:S(2)}) collective-permute-start(bf16[192,512]{1,0:T(8,128)(2,1)S(1)} %get-tuple-element.82), channel_id=1, source_target_pairs={{0,16},{8,24},{16,0},{24,8},{1,17},{9,25},{17,1},{25,9},{2,18},{10... | collective-permute-start | bytes 589832 | tf_op jit(solution)/shard_map/ppermute | solution.py:262
  8.2 14.6 %collective-permute-start.2 = (bf16[192,512]{1,0:T(8,128)(2,1)S(1)}, bf16[192,512]{1,0:T(8,128)(2,1)S(1)}, u32[]{:S(2)}, u32[]{:S(2)}) collective-permute-start(bf16[192,512]{1,0:T(8,128)(2,1)S(1)} %get-tuple-element.83), channel_id=1, source_target_pairs={{0,24},{8,16},{16,8},{24,0},{1,25},{9,17},{17,9},{25,1},{2,26},{10... | collective-permute-start | bytes 589832 | tf_op jit(solution)/shard_map/ppermute | solution.py:262
  11.3 11.8 %collective-permute-start.3 = (bf16[192,512]{1,0:T(8,128)(2,1)S(1)}, bf16[192,512]{1,0:T(8,128)(2,1)S(1)}, u32[]{:S(2)}, u32[]{:S(2)}) collective-permute-start(bf16[192,512]{1,0:T(8,128)(2,1)S(1)} %get-tuple-element.84), channel_id=1, source_target_pairs={{0,8},{8,0},{16,24},{24,16},{1,9},{9,1},{17,25},{25,17},{2,10},{10... | collective-permute-start | bytes 589832 | tf_op jit(solution)/shard_map/ppermute | solution.py:262
  23.1 5.9 %collective-permute-start.6 = (bf16[192,512]{1,0:T(8,128)(2,1)S(1)}, bf16[192,512]{1,0:T(8,128)(2,1)S(1)}, u32[]{:S(2)}, u32[]{:S(2)}) collective-permute-start(bf16[192,512]{1,0:T(8,128)(2,1)S(1)} %collective-permute-done.refs_0_), channel_id=1, source_target_pairs={{0,4},{4,0},{1,5},{5,1},{2,6},{6,2},{3,7},{7,3},{8,12},{12,8},{9,1... | collective-permute-start | bytes 589832 | tf_op jit(solution)/shard_map/ppermute | solution.py:262
  23.1 5.9 %collective-permute-start.7 = (bf16[192,512]{1,0:T(8,128)(2,1)S(1)}, bf16[192,512]{1,0:T(8,128)(2,1)S(1)}, u32[]{:S(2)}, u32[]{:S(2)}) collective-permute-start(bf16[192,512]{1,0:T(8,128)(2,1)S(1)} %collective-permute-done.1.refs_1_), channel_id=1, source_target_pairs={{0,4},{4,0},{1,5},{5,1},{2,6},{6,2},{3,7},{7,3},{8,12},{12,8},{9,1... | collective-permute-start | bytes 589832 | tf_op jit(solution)/shard_map/ppermute | solution.py:262
  23.6 5.4 %collective-permute-start.8 = (bf16[192,512]{1,0:T(8,128)(2,1)S(1)}, bf16[192,512]{1,0:T(8,128)(2,1)S(1)}, u32[]{:S(2)}, u32[]{:S(2)}) collective-permute-start(bf16[192,512]{1,0:T(8,128)(2,1)S(1)} %collective-permute-done.2.refs_2_), channel_id=1, source_target_pairs={{0,4},{4,0},{1,5},{5,1},{2,6},{6,2},{3,7},{7,3},{8,12},{12,8},{9,1... | collective-permute-start | bytes 589832 | tf_op jit(solution)/shard_map/ppermute | solution.py:262
  23.6 18.2 %collective-permute-start.4 = (bf16[192,512]{1,0:T(8,128)(2,1)S(1)}, bf16[192,512]{1,0:T(8,128)(2,1)S(1)}, u32[]{:S(2)}, u32[]{:S(2)}) collective-permute-start(bf16[192,512]{1,0:T(8,128)(2,1)S(1)} %get-tuple-element.85), channel_id=1, source_target_pairs={{0,16},{8,24},{16,0},{24,8},{1,17},{9,25},{17,1},{25,9},{2,18},{10... | collective-permute-start | bytes 589832 | tf_op jit(solution)/shard_map/ppermute | solution.py:262
  27.7 14.2 %collective-permute-start.5 = (bf16[192,512]{1,0:T(8,128)(2,1)S(1)}, bf16[192,512]{1,0:T(8,128)(2,1)S(1)}, u32[]{:S(2)}, u32[]{:S(2)}) collective-permute-start(bf16[192,512]{1,0:T(8,128)(2,1)S(1)} %get-tuple-element.86), channel_id=1, source_target_pairs={{0,24},{8,16},{16,8},{24,0},{1,25},{9,17},{17,9},{25,1},{2,26},{10... | collective-permute-start | bytes 589832 | tf_op jit(solution)/shard_map/ppermute | solution.py:262
  29.0 1.8 %copy-start.1 = (bf16[1,1024,1344]{1,2,0:T(8,128)(2,1)S(1)}, bf16[1,1024,1344]{1,2,0:T(8,128)(2,1)}, u32[]{:S(2)}) copy-start(bf16[1,1024,1344]{1,2,0:T(8,128)(2,1)} %param.12) | copy-start | bytes 8257540
  30.8 2.4 %copy-start = (bf16[1,1344,1024]{2,1,0:T(8,128)(2,1)S(1)}, bf16[1,1344,1024]{2,1,0:T(8,128)(2,1)}, u32[]{:S(2)}) copy-start(bf16[1,1344,1024]{2,1,0:T(8,128)(2,1)} %param.13) | copy-start | bytes 8257540
  41.8 1.4 %collective-permute-start.9 = (bf16[192,512]{1,0:T(8,128)(2,1)S(1)}, bf16[192,512]{1,0:T(8,128)(2,1)S(1)}, u32[]{:S(2)}, u32[]{:S(2)}) collective-permute-start(bf16[192,512]{1,0:T(8,128)(2,1)S(1)} %collective-permute-done.3.refs_0_), channel_id=1, source_target_pairs={{0,4},{4,0},{1,5},{5,1},{2,6},{6,2},{3,7},{7,3},{8,12},{12,8},{9,1... | collective-permute-start | bytes 589832 | tf_op jit(solution)/shard_map/ppermute | solution.py:262
  41.8 1.7 %collective-permute-start.10 = (bf16[192,512]{1,0:T(8,128)(2,1)S(1)}, bf16[192,512]{1,0:T(8,128)(2,1)S(1)}, u32[]{:S(2)}, u32[]{:S(2)}) collective-permute-start(bf16[192,512]{1,0:T(8,128)(2,1)S(1)} %collective-permute-done.4.refs_1_), channel_id=1, source_target_pairs={{0,4},{4,0},{1,5},{5,1},{2,6},{6,2},{3,7},{7,3},{8,12},{12,8},{9,1... | collective-permute-start | bytes 589832 | tf_op jit(solution)/shard_map/ppermute | solution.py:262
  42.3 1.5 %collective-permute-start.11 = (bf16[192,512]{1,0:T(8,128)(2,1)S(1)}, bf16[192,512]{1,0:T(8,128)(2,1)S(1)}, u32[]{:S(2)}, u32[]{:S(2)}) collective-permute-start(bf16[192,512]{1,0:T(8,128)(2,1)S(1)} %collective-permute-done.5.refs_2_), channel_id=1, source_target_pairs={{0,4},{4,0},{1,5},{5,1},{2,6},{6,2},{3,7},{7,3},{8,12},{12,8},{9,1... | collective-permute-start | bytes 589832 | tf_op jit(solution)/shard_map/ppermute | solution.py:262
  42.3 5.9 %collective-permute-start.12 = (bf16[768,512]{1,0:T(8,128)(2,1)S(1)}, bf16[768,512]{1,0:T(8,128)(2,1)S(1)}, u32[]{:S(2)}, u32[]{:S(2)}) collective-permute-start(bf16[768,512]{1,0:T(8,128)(2,1)S(1)} %get-tuple-element.102), channel_id=1, source_target_pairs={{0,4},{4,0},{1,5},{5,1},{2,6},{6,2},{3,7},{7,3},{8,12},{12,8},{9,1... | collective-permute-start | bytes 2359304 | tf_op jit(solution)/shard_map/ppermute | solution.py:262
  45.2 17.6 %collective-permute-start.20 = (bf16[1344,256]{1,0:T(8,128)(2,1)S(1)}, bf16[1344,256]{1,0:T(8,128)(2,1)S(1)}, u32[]{:S(2)}, u32[]{:S(2)}) collective-permute-start(bf16[1344,256]{1,0:T(8,128)(2,1)S(1)} %get-tuple-element.131), channel_id=1, source_target_pairs={{0,1},{1,0},{2,3},{3,2},{4,5},{5,4},{6,7},{7,6},{8,9},{9,8},{10,11... | collective-permute-start | bytes 2064392 | tf_op jit(solution)/shard_map/ppermute | solution.py:262
  46.8 17.3 %collective-permute-start.21 = (bf16[1344,256]{1,0:T(8,128)(2,1)S(1)}, bf16[1344,256]{1,0:T(8,128)(2,1)S(1)}, u32[]{:S(2)}, u32[]{:S(2)}) collective-permute-start(bf16[1344,256]{1,0:T(8,128)(2,1)S(1)} %get-tuple-element.132), channel_id=1, source_target_pairs={{0,2},{1,3},{2,0},{3,1},{4,6},{5,7},{6,4},{7,5},{8,10},{9,11},{10,... | collective-permute-start | bytes 2064392 | tf_op jit(solution)/shard_map/ppermute | solution.py:262
  48.5 20.5 %collective-permute-start.13 = (bf16[192,512]{1,0:T(8,128)(2,1)S(1)}, bf16[192,512]{1,0:T(8,128)(2,1)S(1)}, u32[]{:S(2)}, u32[]{:S(2)}) collective-permute-start(bf16[192,512]{1,0:T(8,128)(2,1)S(1)} %get-tuple-element.106), channel_id=1, source_target_pairs={{0,8},{8,0},{16,24},{24,16},{1,9},{9,1},{17,25},{25,17},{2,10},{10... | collective-permute-start | bytes 589832 | tf_op jit(solution)/shard_map/ppermute | solution.py:262
  53.1 17.2 %collective-permute-start.14 = (bf16[192,512]{1,0:T(8,128)(2,1)S(1)}, bf16[192,512]{1,0:T(8,128)(2,1)S(1)}, u32[]{:S(2)}, u32[]{:S(2)}) collective-permute-start(bf16[192,512]{1,0:T(8,128)(2,1)S(1)} %get-tuple-element.107), channel_id=1, source_target_pairs={{0,16},{8,24},{16,0},{24,8},{1,17},{9,25},{17,1},{25,9},{2,18},{10... | collective-permute-start | bytes 589832 | tf_op jit(solution)/shard_map/ppermute | solution.py:262
  54.1 16.2 %collective-permute-start.15 = (bf16[192,512]{1,0:T(8,128)(2,1)S(1)}, bf16[192,512]{1,0:T(8,128)(2,1)S(1)}, u32[]{:S(2)}, u32[]{:S(2)}) collective-permute-start(bf16[192,512]{1,0:T(8,128)(2,1)S(1)} %get-tuple-element.108), channel_id=1, source_target_pairs={{0,24},{8,16},{16,8},{24,0},{1,25},{9,17},{17,9},{25,1},{2,26},{10... | collective-permute-start | bytes 589832 | tf_op jit(solution)/shard_map/ppermute | solution.py:262
  64.0 2.5 %copy-start.2 = (bf16[1,1024,1344]{1,2,0:T(8,128)(2,1)S(1)}, bf16[1,1024,1344]{1,2,0:T(8,128)(2,1)}, u32[]{:S(2)}) copy-start(bf16[1,1024,1344]{1,2,0:T(8,128)(2,1)} %param.12) | copy-start | bytes 8257540
  64.4 23.9 %collective-permute-start.22 = (bf16[2016,256]{1,0:T(8,128)(2,1)S(1)}, bf16[2016,256]{1,0:T(8,128)(2,1)S(1)}, u32[]{:S(2)}, u32[]{:S(2)}) collective-permute-start(bf16[2016,256]{1,0:T(8,128)(2,1)S(1)} %get-tuple-element.135), channel_id=1, source_target_pairs={{0,1},{1,0},{2,3},{3,2},{4,5},{5,4},{6,7},{7,6},{8,9},{9,8},{10,11... | collective-permute-start | bytes 3096584 | tf_op jit(solution)/shard_map/ppermute | solution.py:262
  65.0 23.6 %collective-permute-start.23 = (bf16[2016,256]{1,0:T(8,128)(2,1)S(1)}, bf16[2016,256]{1,0:T(8,128)(2,1)S(1)}, u32[]{:S(2)}, u32[]{:S(2)}) collective-permute-start(bf16[2016,256]{1,0:T(8,128)(2,1)S(1)} %get-tuple-element.136), channel_id=1, source_target_pairs={{0,2},{1,3},{2,0},{3,1},{4,6},{5,7},{6,4},{7,5},{8,10},{9,11},{10,... | collective-permute-start | bytes 3096584 | tf_op jit(solution)/shard_map/ppermute | solution.py:262
  70.3 2.3 %collective-permute-start.16 = (bf16[768,512]{1,0:T(8,128)(2,1)S(1)}, bf16[768,512]{1,0:T(8,128)(2,1)S(1)}, u32[]{:S(2)}, u32[]{:S(2)}) collective-permute-start(bf16[768,512]{1,0:T(8,128)(2,1)S(1)} %get-tuple-element.126), channel_id=1, source_target_pairs={{0,4},{4,0},{1,5},{5,1},{2,6},{6,2},{3,7},{7,3},{8,12},{12,8},{9,1... | collective-permute-start | bytes 2359304 | tf_op jit(solution)/shard_map/ppermute | solution.py:262
  72.8 20.4 %collective-permute-start.17 = (bf16[192,512]{1,0:T(8,128)(2,1)S(1)}, bf16[192,512]{1,0:T(8,128)(2,1)S(1)}, u32[]{:S(2)}, u32[]{:S(2)}) collective-permute-start(bf16[192,512]{1,0:T(8,128)(2,1)S(1)} %get-tuple-element.128), channel_id=1, source_target_pairs={{0,8},{8,0},{16,24},{24,16},{1,9},{9,1},{17,25},{25,17},{2,10},{10... | collective-permute-start | bytes 589832 | tf_op jit(solution)/shard_map/ppermute | solution.py:262
  76.2 17.1 %collective-permute-start.18 = (bf16[192,512]{1,0:T(8,128)(2,1)S(1)}, bf16[192,512]{1,0:T(8,128)(2,1)S(1)}, u32[]{:S(2)}, u32[]{:S(2)}) collective-permute-start(bf16[192,512]{1,0:T(8,128)(2,1)S(1)} %get-tuple-element.129), channel_id=1, source_target_pairs={{0,16},{8,24},{16,0},{24,8},{1,17},{9,25},{17,1},{25,9},{2,18},{10... | collective-permute-start | bytes 589832 | tf_op jit(solution)/shard_map/ppermute | solution.py:262
  77.1 16.1 %collective-permute-start.19 = (bf16[192,512]{1,0:T(8,128)(2,1)S(1)}, bf16[192,512]{1,0:T(8,128)(2,1)S(1)}, u32[]{:S(2)}, u32[]{:S(2)}) collective-permute-start(bf16[192,512]{1,0:T(8,128)(2,1)S(1)} %get-tuple-element.130), channel_id=1, source_target_pairs={{0,24},{8,16},{16,8},{24,0},{1,25},{9,17},{17,9},{25,1},{2,26},{10... | collective-permute-start | bytes 589832 | tf_op jit(solution)/shard_map/ppermute | solution.py:262
  88.9 8.0 %collective-permute-start.26 = (bf16[672,256]{1,0:T(8,128)(2,1)S(1)}, bf16[672,256]{1,0:T(8,128)(2,1)S(1)}, u32[]{:S(2)}, u32[]{:S(2)}) collective-permute-start(bf16[672,256]{1,0:T(8,128)(2,1)S(1)} %get-tuple-element.152), channel_id=1, source_target_pairs={{0,2},{1,3},{2,0},{3,1},{4,6},{5,7},{6,4},{7,5},{8,10},{9,11},{10,... | collective-permute-start | bytes 1032200 | tf_op jit(solution)/shard_map/ppermute | solution.py:262
  90.5 7.6 %collective-permute-start.27 = (bf16[672,256]{1,0:T(8,128)(2,1)S(1)}, bf16[672,256]{1,0:T(8,128)(2,1)S(1)}, u32[]{:S(2)}, u32[]{:S(2)}) collective-permute-start(bf16[672,256]{1,0:T(8,128)(2,1)S(1)} %get-tuple-element.153), channel_id=1, source_target_pairs={{0,1},{1,0},{2,3},{3,2},{4,5},{5,4},{6,7},{7,6},{8,9},{9,8},{10,11... | collective-permute-start | bytes 1032200 | tf_op jit(solution)/shard_map/ppermute | solution.py:262
  93.1 1.5 %collective-permute-start.24 = (bf16[256,512]{1,0:T(8,128)(2,1)S(1)}, bf16[256,512]{1,0:T(8,128)(2,1)S(1)}, u32[]{:S(2)}, u32[]{:S(2)}) collective-permute-start(bf16[256,512]{1,0:T(8,128)(2,1)S(1)} %get-tuple-element.144), channel_id=1, source_target_pairs={{0,4},{4,0},{1,5},{5,1},{2,6},{6,2},{3,7},{7,3},{8,12},{12,8},{9,1... | collective-permute-start | bytes 786440 | tf_op jit(solution)/shard_map/ppermute | solution.py:262
  93.8 1.6 %collective-permute-start.25 = (bf16[256,512]{1,0:T(8,128)(2,1)S(1)}, bf16[256,512]{1,0:T(8,128)(2,1)S(1)}, u32[]{:S(2)}, u32[]{:S(2)}) collective-permute-start(bf16[256,512]{1,0:T(8,128)(2,1)S(1)} %get-tuple-element.145), channel_id=1, source_target_pairs={{0,4},{4,0},{1,5},{5,1},{2,6},{6,2},{3,7},{7,3},{8,12},{12,8},{9,1... | collective-permute-start | bytes 786440 | tf_op jit(solution)/shard_map/ppermute | solution.py:262

commit v6 on v5

--- a/solution.py
+++ b/solution.py
@@ -77,26 +77,50 @@
     return mxu(ones(down == along), table_t.astype(F32).astype(BF16), CONTRACT_LAST).astype(jnp.int32)
 
 
-def route_body(owners, capacity, routes_ref, tokens_ref, own_ref, *sends):
+def ranks(routes, owners):
+    count = routes[0].shape[1]
+    expert = lax.broadcasted_iota(jnp.int32, (-(-owners // ROW_TILE) * ROW_TILE, count), 0)
+    named = [route == expert for route in routes]
+    down, along = (lax.broadcasted_iota(jnp.int32, (count, count), i) for i in range(2))
+    before = mxu(ones(sum(n.astype(F32) for n in named) > 0.0), ones(down < along))
+    return [jnp.sum(jnp.where(n, before, 0.0), axis=0, keepdims=True).astype(jnp.int32) for n in named]
+
+
+def rows_for(expert, routes, rank, tokens, capacity):
+    row = lax.broadcasted_iota(jnp.int32, (capacity, tokens.shape[0]), 0)
+    chosen = sum((route == expert).astype(F32) * (r == row).astype(F32) for route, r in zip(routes, rank, strict=True))
+    return mxu(chosen.astype(BF16), tokens).astype(BF16)
+
+
+def route_body(owners, relayed, routes_ref, tokens_ref, own_ref, *sends):
     me, core = lax.axis_index("expert"), lax.axis_index("cuts")
     top, count = routes_ref.shape
     half = tokens_ref.shape[1] // lax.axis_size("cuts")
-    routes = routes_ref[...]
-    expert = lax.broadcasted_iota(jnp.int32, (-(-owners // ROW_TILE) * ROW_TILE, count), 0)
-    named = [routes[k : k + 1, :] == expert for k in range(top)]
-    down, along = (lax.broadcasted_iota(jnp.int32, (count, count), i) for i in range(2))
-    before = mxu(ones(sum(n.astype(F32) for n in named) > 0.0), ones(down < along))
-    slots = [
-        (routes[k : k + 1, :] ^ me) * capacity
-        + jnp.sum(jnp.where(named[k], before, 0.0), axis=0, keepdims=True).astype(jnp.int32)
-        for k in range(top)
-    ]
-    wide = tokens_ref[...].astype(BF16)
+    routes = [routes_ref[k : k + 1, :] for k in range(top)]
+    rank = ranks(routes, owners)
     narrow = tokens_ref[:, window(core, half)].astype(BF16)
-    row = lax.broadcasted_iota(jnp.int32, (capacity, count), 0)
-    for shift, ref in reversed(list(enumerate((own_ref, *sends)))):
-        chosen = ones(sum((slot == row + shift * capacity).astype(F32) for slot in slots) > 0.0)
-        ref[...] = mxu(chosen, narrow if shift else wide).astype(BF16)
+    if relayed:
+        *sends, all_ref = sends
+        line = lax.broadcasted_iota(jnp.int32, (ROW_TILE, count), 0)
+        all_ref[:count, :] = narrow
+        all_ref[count:, :] = jnp.zeros((ROW_TILE, half), BF16)
+        all_ref[count:, :count] = sum(
+            jnp.where(line == k, route, 0).astype(F32) for k, route in enumerate(routes)
+        ).astype(BF16)
+    for shift, ref in reversed(list(enumerate(sends, 1))):
+        ref[...] = rows_for(me ^ shift, routes, rank, narrow, ref.shape[0])
+    own_ref[...] = rows_for(me, routes, rank, tokens_ref[...].astype(BF16), own_ref.shape[0])
+
+
+def pick_body(owners, top, all_ref, mine_ref, relay_ref):
+    me = lax.axis_index("expert")
+    count = all_ref.shape[0] - ROW_TILE
+    lines = all_ref[count:, :count].astype(F32).astype(jnp.int32)
+    routes = [lines[k : k + 1, :] for k in range(top)]
+    rank = ranks(routes, owners)
+    tokens = all_ref[:count, :]
+    relay_ref[...] = rows_for(me ^ 1, routes, rank, tokens, relay_ref.shape[0])
+    mine_ref[...] = rows_for(me, routes, rank, tokens, mine_ref.shape[0])
 
 
 def weigh_body(owners, capacity, routes_ref, index_ref, table_ref, cotangent_ref, meta_ref, own_ref, *sends):
@@ -132,20 +156,20 @@
         ).astype(BF16)
 
 
-def assemble(full_ref, own, mine, other):
+def assemble(full_ref, whole, mine=(), other=()):
     core = lax.axis_index("cuts")
-    capacity, half = mine[0].shape
-    full_ref[:capacity, :] = own[...]
-    for i, (a, b) in enumerate(zip(mine, other, strict=True), 1):
+    capacity = whole[0].shape[0]
+    for i, chunk in enumerate(whole):
+        full_ref[i * capacity : (i + 1) * capacity, :] = chunk[...]
+    for i, (a, b) in enumerate(zip(mine, other, strict=True), len(whole)):
         rows = slice(i * capacity, (i + 1) * capacity)
-        full_ref[rows, window(core, half)] = a[...]
-        full_ref[rows, window(1 - core, half)] = b[...]
-
-
-def hidden_body(remote, own, *refs):
-    mine, other = refs[:remote], refs[remote : 2 * remote]
-    inner_ref, x_ref, positive_ref, hidden_ref = refs[2 * remote :]
-    assemble(x_ref, own, mine, other)
+        full_ref[rows, window(core, a.shape[1])] = a[...]
+        full_ref[rows, window(1 - core, a.shape[1])] = b[...]
+
+
+def hidden_body(owners, *refs):
+    inner_ref, x_ref, positive_ref, hidden_ref = refs[owners:]
+    assemble(x_ref, refs[:owners])
 
     for units, rows in tiles(inner_ref.shape[0], x_ref.shape[0]):
         positive = jnp.maximum(mxu(inner_ref[units, :], x_ref[rows, :], CONTRACT_LAST), 0.0)
@@ -203,9 +227,10 @@
     pieces(keys, units_ref, rows_ref, outs)
 
 
-def first_grad_body(keys, remote, own, *refs):
-    units_ref, rows_ref, *outs = refs[2 * remote :]
-    assemble(rows_ref, own, refs[:remote], refs[remote : 2 * remote])
+def first_grad_body(keys, halves, *refs):
+    chunks, (units_ref, rows_ref), outs = refs[: -len(keys) - 2], refs[-len(keys) - 2 : -len(keys)], refs[-len(keys) :]
+    whole = len(chunks) - 2 * halves
+    assemble(rows_ref, chunks[:whole], chunks[whole : whole + halves], chunks[whole + halves :])
     pieces(keys, units_ref, rows_ref, outs)
 
 
@@ -289,9 +314,11 @@
     def across_cores(chunks):
         return [partner(x, "cuts", 1) for x in chunks]
 
-    def over_experts(chunks):
-        got = {s: partner(chunks[s - 1], "expert", s) for s in reversed(range(1, owners))}
-        return [got[s] for s in range(1, owners)]
+    def joined(chunks):
+        return [lax.all_gather(x, "cuts", axis=1, tiled=True) for x in chunks]
+
+    def over_experts(chunks, first=1):
+        return [partner(x, "expert", s) for s, x in enumerate(chunks, first)]
 
     def given(units_rows, weight, name):
         return local(
@@ -316,15 +343,19 @@
     def grads(keys, units_rows, rows, name):
         return local(functools.partial(grad_body, keys), [piece] * 2, [units_rows, rows], work // 2, name)
 
+    relayed = owners % 4 == 0 and count + ROW_TILE < 2 * capacity and count <= half
+    pairs = range(2, owners, 2) if relayed else ()
+    chunk = shape(capacity, half)
     own, *sends = local(
-        functools.partial(route_body, owners, capacity),
-        [shape(capacity, features)] + [shape(capacity, half)] * remote,
+        functools.partial(route_body, owners, relayed),
+        [shape(capacity, features)] + ([chunk, shape(count + ROW_TILE, half)] if relayed else [chunk] * remote),
         [routes.T, tokens],
         2 * count * slots * features,
         "route",
         space=pltpu.HBM,
     )
-    mine = over_experts(sends)
+    dense = [partner(sends[-1], "expert", s) for s in pairs]
+    mine = over_experts(sends[:1] if relayed else sends)
     meta, grad_own, *grad_sends = local(
         functools.partial(weigh_body, owners, capacity),
         [shape(count, 128, F32), shape(capacity, features)] + [shape(capacity, half)] * remote,
@@ -333,26 +364,36 @@
         "weigh",
         space=pltpu.HBM,
     )
-    grad_mine = over_experts(grad_sends)
-    mine, nearest = after((mine, grad_mine[0]), grad_sends)
-    grad_mine = [nearest, *grad_mine[1:]]
-    other = across_cores(mine)
+    nearest = [] if relayed else over_experts(grad_sends[:1])
+    mine, dense, nearest, grad_sends = after((mine, dense, nearest, grad_sends))
+    relays = []
+    for came in dense:
+        picked, relay = local(
+            functools.partial(pick_body, owners, top), [chunk] * 2, [came], 4 * count * capacity * half, "pick"
+        )
+        mine += [picked, partner(relay, "expert", 1)]
+        relays.append(relay)
+    grad_first, *farther = after(grad_sends, relays)
+    if relayed:
+        nearest = [partner(grad_first, "expert", 1)]
+    grad_mine = nearest + over_experts(farther, 2)
+    grad_whole = [grad_own]
     arrived, positive, hidden = local(
-        functools.partial(hidden_body, remote),
+        functools.partial(hidden_body, owners),
         [shape(slots, features), shape(units, slots), shape(units, slots)],
-        [own, *mine, *other, inner],
+        [own, *joined(mine), inner],
         work,
         "hidden",
     )
     turned, give = given(hidden, outer, "rows")
     keep = kept(turned, outer, "rows")
-    grad_mine, hidden, keep, give = after((grad_mine, hidden, keep, give))
+    grad_mine, grad_whole, hidden, give = after((grad_mine, grad_whole, hidden, give))
     came = partner(give, "cuts", 1)
     grad_other = across_cores(grad_mine)
     grad_rows, *outer_sent = local(
-        functools.partial(first_grad_body, leaving, remote),
+        functools.partial(first_grad_body, leaving, len(grad_mine)),
         [shape(slots, features)] + [piece] * 2,
-        [grad_own, *grad_mine, *grad_other, hidden],
+        [*grad_whole, *grad_mine, *grad_other, hidden],
         work // 2,
         "outer_leaving",
     )

time: 101 us -> 98.8 us (0.978); the launches traced: 99.4 us -> 98.6 us
  blocking collectives: 0 us -> 6.41 us
  starting transfers between devices: 35.1 us -> 31.8 us
  waiting for transfers between devices: 33.1 us -> 30.7 us
  local copies, waits for them, and re-layouts: 1.78 us -> 0.01 us
    all_gather x0 -> x3, blocking collectives: none -> 6.41 us  [joined(): return [lax.all_gather(x, 'cuts', axis=1, tiled=True) for x in chunks]]
    ppermute x28 -> x25, starting transfers between devices: 35.1 us -> 31.8 us  [partner(): lax.ppermute(x, axis, [(i, i ^ bit) for i in range(lax.axis_size(axis))])]
    ppermute x28 -> x25, waiting for transfers between devices: 33.1 us -> 30.7 us  [partner(): lax.ppermute(x, axis, [(i, i ^ bit) for i in range(lax.axis_size(axis))])]
    unnamed x6 -> x4, local copies, waits for them, and re-layouts: 1.78 us -> 0.01 us
    pallas_call x21 -> x22, Pallas kernels: 28.6 us -> 28.8 us  [local(): pl.pallas_call(body, out_shape=tuple((gives(x.shape, x.dtype) for x in ou...]
  transfers between devices with their start and end apart: 28 -> 25, of which waited for: 17 -> 16; matrix products, arithmetic and copies ran while one was open for 0% -> 0% of each run, Pallas kernels for 26% -> 26%
where the time goes in v6:
time: 98.8 us; the launch traced here: 98.6 us
  starting transfers between devices  31.8 us (32%)
  waiting for transfers between devices  30.7 us (31%)
  Pallas kernels  28.8 us (29%)
  blocking collectives  6.41 us (6%)
    ppermute x25, starting transfers between devices, partner(): lax.ppermute(x, axis, [(i, i ^ bit) for i in range(lax.axis_size(axis))])  31.8 us
    ppermute x25, waiting for transfers between devices, partner(): lax.ppermute(x, axis, [(i, i ^ bit) for i in range(lax.axis_size(axis))])  30.7 us
    pallas_call x22, Pallas kernels, local(): pl.pallas_call(body, out_shape=tuple((gives(x.shape, x.dtype) for x in ou...  28.8 us
    all_gather x3, blocking collectives, joined(): return [lax.all_gather(x, 'cuts', axis=1, tiled=True) for x in chunks]  6.41 us
  transfers between devices with their start and end apart: 25, of which 16 were waited for; matrix products, arithmetic and copies ran while one was open for 0% of the time, Pallas kernels for 26%

profile of v6, /device:TPU:0, one launch (start us, length us, event | category | flops | bytes accessed | tf_op | source)
XLA Modules:
  0.0 98.6 jit_solution(14441547314037957814)
XLA Ops:
  0.6 1.9 %route.1 = (bf16[192,1024]{1,0:T(8,128)(2,1)S(1)}, bf16[192,512]{1,0:T(8,128)(2,1)S(1)}, bf16[272,512]{1,0:T(8,128)(2,1)S(1)}) custom-call(s32[2,256]{1,0:T(2,128)} %bitcast.19, f32[256,1024]{1,0:T(8,128)} %tokens_ref.1), custom_call_target="tpu_custom_call" | custom-call | flops 6291456 | bytes 29984 | tf_op jit(solution)/shard_map/route/pallas_call | solution.py:31
  2.5 4.1 %collective-permute-start.1 = (bf16[272,512]{1,0:T(8,128)(2,1)S(1)}, bf16[272,512]{1,0:T(8,128)(2,1)S(1)}, u32[]{:S(2)}, u32[]{:S(2)}) collective-permute-start(bf16[272,512]{1,0:T(8,128)(2,1)S(1)} %get-tuple-element.86), channel_id=1, source_target_pairs={{0,16},{8,24},{16,0},{24,8},{1,17},{9,25},{17,1},{25,9},{2,18},{10... | collective-permute-start | bytes 835592 | tf_op jit(solution)/shard_map/ppermute | solution.py:287
  6.6 1.6 %collective-permute-start = (bf16[192,512]{1,0:T(8,128)(2,1)S(1)}, bf16[192,512]{1,0:T(8,128)(2,1)S(1)}, u32[]{:S(2)}, u32[]{:S(2)}) collective-permute-start(bf16[192,512]{1,0:T(8,128)(2,1)S(1)} %get-tuple-element.85), channel_id=1, source_target_pairs={{0,8},{8,0},{16,24},{24,16},{1,9},{9,1},{17,25},{25,17},{2,10},{10... | collective-permute-start | bytes 589832 | tf_op jit(solution)/shard_map/ppermute | solution.py:287
  8.2 3.2 %weigh.1 = (f32[256,128]{1,0:T(8,128)S(1)}, bf16[192,1024]{1,0:T(8,128)(2,1)S(1)}, bf16[192,512]{1,0:T(8,128)(2,1)S(1)}, bf16[192,512]{1,0:T(8,128)(2,1)S(1)}, bf16[192,512]{1,0:T(8,128)(2,1)S(1)}) custom-call(s32[2,256]{1,0:T(2,128)} %bitcast.20, s32[2,256]{1,0:T(2,128)} %bitcast.21, f32[1,256]{1,0:T(1,128)} %bitcast.22, f32[256,1024]{1,0:T(8,128)} %cotangent_ref.1), custom_call_target="tpu_custom_call" | custom-call | flops 12582912 | bytes 33872 | tf_op jit(solution)/shard_map/weigh/pallas_call | solution.py:31
  11.4 5.4 %collective-permute-done = bf16[192,512]{1,0:T(8,128)(2,1)S(1)} collective-permute-done((bf16[192,512]{1,0:T(8,128)(2,1)S(1)}, bf16[192,512]{1,0:T(8,128)(2,1)S(1)}, u32[]{:S(2)}, u32[]{:S(2)}) %collective-permute-start) | collective-permute-done | bytes 196640 | tf_op jit(solution)/shard_map/ppermute | solution.py:287
  16.8 2.5 %collective-permute-done.1.all_ref = bf16[272,512]{1,0:T(8,128)(2,1)S(1)} collective-permute-done((bf16[272,512]{1,0:T(8,128)(2,1)S(1)}, bf16[272,512]{1,0:T(8,128)(2,1)S(1)}, u32[]{:S(2)}, u32[]{:S(2)}) %collective-permute-start.1) | collective-permute-done | bytes 278560 | tf_op jit(solution)/shard_map/ppermute | solution.py:287
  21.8 2.2 %collective-permute-start.3 = (bf16[192,512]{1,0:T(8,128)(2,1)S(1)}, bf16[192,512]{1,0:T(8,128)(2,1)S(1)}, u32[]{:S(2)}, u32[]{:S(2)}) collective-permute-start(bf16[192,512]{1,0:T(8,128)(2,1)S(1)} %get-tuple-element.96), channel_id=1, source_target_pairs={{0,16},{8,24},{16,0},{24,8},{1,17},{9,25},{17,1},{25,9},{2,18},{10... | collective-permute-start | bytes 589832 | tf_op jit(solution)/shard_map/ppermute | solution.py:287
  23.9 1.4 %collective-permute-start.4 = (bf16[192,512]{1,0:T(8,128)(2,1)S(1)}, bf16[192,512]{1,0:T(8,128)(2,1)S(1)}, u32[]{:S(2)}, u32[]{:S(2)}) collective-permute-start(bf16[192,512]{1,0:T(8,128)(2,1)S(1)} %get-tuple-element.97), channel_id=1, source_target_pairs={{0,24},{8,16},{16,8},{24,0},{1,25},{9,17},{17,9},{25,1},{2,26},{10... | collective-permute-start | bytes 589832 | tf_op jit(solution)/shard_map/ppermute | solution.py:287
  25.3 2.1 %all_gather.9.refs_1_ = bf16[192,1024]{1,0:T(8,128)(2,1)S(1)} all-gather(bf16[192,512]{1,0:T(8,128)(2,1)S(1)} %collective-permute-done), channel_id=1, replica_groups=mesh['expert'=4,'cuts'=2,'dp'=4] {'cuts'}, dimensions={1}, use_global_device_ids=true | all-gather | bytes 589824 | tf_op jit(solution)/shard_map/all_gather | solution.py:318
  27.4 2.1 %all_gather.10.refs_2_ = bf16[192,1024]{1,0:T(8,128)(2,1)S(1)} all-gather(bf16[192,512]{1,0:T(8,128)(2,1)S(1)} %get-tuple-element.101), channel_id=1, replica_groups=mesh['expert'=4,'cuts'=2,'dp'=4] {'cuts'}, dimensions={1}, use_global_device_ids=true | all-gather | bytes 589824 | tf_op jit(solution)/shard_map/all_gather | solution.py:318
  29.5 2.3 %collective-permute-done.5 = bf16[192,512]{1,0:T(8,128)(2,1)S(1)} collective-permute-done((bf16[192,512]{1,0:T(8,128)(2,1)S(1)}, bf16[192,512]{1,0:T(8,128)(2,1)S(1)}, u32[]{:S(2)}, u32[]{:S(2)}) %collective-permute-start.5) | collective-permute-done | bytes 196640 | tf_op jit(solution)/shard_map/ppermute | solution.py:287
  31.8 2.3 %all_gather.11.refs_3_ = bf16[192,1024]{1,0:T(8,128)(2,1)S(1)} all-gather(bf16[192,512]{1,0:T(8,128)(2,1)S(1)} %collective-permute-done.5), channel_id=1, replica_groups=mesh['expert'=4,'cuts'=2,'dp'=4] {'cuts'}, dimensions={1}, use_global_device_ids=true | all-gather | bytes 589824 | tf_op jit(solution)/shard_map/all_gather | solution.py:318
  34.1 2.4 %hidden.1 = (bf16[768,1024]{1,0:T(8,128)(2,1)S(1)}, bf16[1344,768]{1,0:T(8,128)(2,1)S(1)}, bf16[1344,768]{1,0:T(8,128)(2,1)S(1)}) custom-call(bf16[192,1024]{1,0:T(8,128)(2,1)S(1)} %get-tuple-element.99.refs_0_, bf16[192,1024]{1,0:T(8,128)(2,1)S(1)} %all_gather.9.refs_1_, bf16[192,1024]{1,0:T(8,128)(2,1)S(1)} %all_gather.10.refs_2_, ...), custom_call_target="tpu_custom_call" | custom-call | flops 33030144 | bytes 156672 | tf_op jit(solution)/shard_map/hidden/pallas_call | solution.py:31
  36.4 2.2 %rows_give.1 = (bf16[768,1344]{1,0:T(8,128)(2,1)S(1)}, bf16[768,512]{1,0:T(8,128)(2,1)S(1)}) custom-call(bf16[1344,768]{1,0:T(8,128)(2,1)S(1)} %get-tuple-element.124.units_ref.refs_7_, bf16[1344,1024]{1,0:T(8,128)(2,1)S(1)} %bitcast.11), custom_call_target="tpu_custom_call" | custom-call | flops 16515072 | bytes 119808 | tf_op jit(solution)/shard_map/rows_give/pallas_call | solution.py:31
  38.6 2.5 %collective-permute-done.4.refs_3_ = bf16[192,512]{1,0:T(8,128)(2,1)S(1)} collective-permute-done((bf16[192,512]{1,0:T(8,128)(2,1)S(1)}, bf16[192,512]{1,0:T(8,128)(2,1)S(1)}, u32[]{:S(2)}, u32[]{:S(2)}) %collective-permute-start.4) | collective-permute-done | bytes 196640 | tf_op jit(solution)/shard_map/ppermute | solution.py:287
  44.5 1.6 %collective-permute-start.17 = (bf16[1344,256]{1,0:T(8,128)(2,1)S(1)}, bf16[1344,256]{1,0:T(8,128)(2,1)S(1)}, u32[]{:S(2)}, u32[]{:S(2)}) collective-permute-start(bf16[1344,256]{1,0:T(8,128)(2,1)S(1)} %get-tuple-element.141), channel_id=1, source_target_pairs={{0,1},{1,0},{2,3},{3,2},{4,5},{5,4},{6,7},{7,6},{8,9},{9,8},{10,11... | collective-permute-start | bytes 2064392 | tf_op jit(solution)/shard_map/ppermute | solution.py:287
  46.0 1.5 %collective-permute-start.18 = (bf16[1344,256]{1,0:T(8,128)(2,1)S(1)}, bf16[1344,256]{1,0:T(8,128)(2,1)S(1)}, u32[]{:S(2)}, u32[]{:S(2)}) collective-permute-start(bf16[1344,256]{1,0:T(8,128)(2,1)S(1)} %get-tuple-element.142), channel_id=1, source_target_pairs={{0,2},{1,3},{2,0},{3,1},{4,6},{5,7},{6,4},{7,5},{8,10},{9,11},{10,... | collective-permute-start | bytes 2064392 | tf_op jit(solution)/shard_map/ppermute | solution.py:287
  47.6 1.4 %rows_keep.1.keep_ref = bf16[768,512]{1,0:T(8,128)(2,1)S(1)} custom-call(bf16[768,1344]{1,0:T(8,128)(2,1)S(1)} %get-tuple-element.111.turned_ref, bf16[1344,1024]{1,0:T(8,128)(2,1)S(1)} %bitcast.12), custom_call_target="tpu_custom_call" | custom-call | flops 16515072 | bytes 87552 | tf_op jit(solution)/shard_map/rows_keep/pallas_call | solution.py:31
  50.5 2.0 %collective-permute-start.11 = (bf16[192,512]{1,0:T(8,128)(2,1)S(1)}, bf16[192,512]{1,0:T(8,128)(2,1)S(1)}, u32[]{:S(2)}, u32[]{:S(2)}) collective-permute-start(bf16[192,512]{1,0:T(8,128)(2,1)S(1)} %get-tuple-element.117), channel_id=1, source_target_pairs={{0,16},{8,24},{16,0},{24,8},{1,17},{9,25},{17,1},{25,9},{2,18},{10... | collective-permute-start | bytes 589832 | tf_op jit(solution)/shard_map/ppermute | solution.py:287
  52.5 1.4 %collective-permute-start.12 = (bf16[192,512]{1,0:T(8,128)(2,1)S(1)}, bf16[192,512]{1,0:T(8,128)(2,1)S(1)}, u32[]{:S(2)}, u32[]{:S(2)}) collective-permute-start(bf16[192,512]{1,0:T(8,128)(2,1)S(1)} %get-tuple-element.118), channel_id=1, source_target_pairs={{0,24},{8,16},{16,8},{24,0},{1,25},{9,17},{17,9},{25,1},{2,26},{10... | collective-permute-start | bytes 589832 | tf_op jit(solution)/shard_map/ppermute | solution.py:287
  53.9 2.3 %d_act.1.units_ref = bf16[1344,768]{1,0:T(8,128)(2,1)S(1)} custom-call(bf16[768,1024]{1,0:T(8,128)(2,1)S(1)} %get-tuple-element.125.g_ref.rows_ref, bf16[1344,768]{1,0:T(8,128)(2,1)S(1)} %get-tuple-element.120.positive_ref, bf16[1344,1024]{1,0:T(8,128)(2,1)S(1)} %bitcast.13), custom_call_target="tpu_custom_call" | custom-call | flops 33030144 | bytes 132096 | tf_op jit(solution)/shard_map/d_act/pallas_call | solution.py:31
  58.8 3.4 %collective-permute-done.17.came0 = bf16[1344,256]{1,0:T(8,128)(2,1)S(1)} collective-permute-done((bf16[1344,256]{1,0:T(8,128)(2,1)S(1)}, bf16[1344,256]{1,0:T(8,128)(2,1)S(1)}, u32[]{:S(2)}, u32[]{:S(2)}) %collective-permute-start.17) | collective-permute-done | bytes 688160 | tf_op jit(solution)/shard_map/ppermute | solution.py:287
  64.3 1.5 %collective-permute-start.20 = (bf16[2016,256]{1,0:T(8,128)(2,1)S(1)}, bf16[2016,256]{1,0:T(8,128)(2,1)S(1)}, u32[]{:S(2)}, u32[]{:S(2)}) collective-permute-start(bf16[2016,256]{1,0:T(8,128)(2,1)S(1)} %get-tuple-element.146), channel_id=1, source_target_pairs={{0,2},{1,3},{2,0},{3,1},{4,6},{5,7},{6,4},{7,5},{8,10},{9,11},{10,... | collective-permute-start | bytes 3096584 | tf_op jit(solution)/shard_map/ppermute | solution.py:287
  65.8 2.4 %grad_rows_give.1 = (bf16[768,1344]{1,0:T(8,128)(2,1)S(1)}, bf16[768,512]{1,0:T(8,128)(2,1)S(1)}) custom-call(bf16[1344,768]{1,0:T(8,128)(2,1)S(1)} %d_act.1.units_ref, bf16[1344,1024]{1,0:T(8,128)(2,1)S(1)} %bitcast.15), custom_call_target="tpu_custom_call" | custom-call | flops 16515072 | bytes 119808 | tf_op jit(solution)/shard_map/grad_rows_give/pallas_call | solution.py:31
  68.3 1.4 %grad_rows_keep.1.keep_ref = bf16[768,512]{1,0:T(8,128)(2,1)S(1)} custom-call(bf16[768,1344]{1,0:T(8,128)(2,1)S(1)} %get-tuple-element.135.turned_ref, bf16[1344,1024]{1,0:T(8,128)(2,1)S(1)} %bitcast.16), custom_call_target="tpu_custom_call" | custom-call | flops 16515072 | bytes 87552 | tf_op jit(solution)/shard_map/grad_rows_keep/pallas_call | solution.py:31
  70.8 2.6 %collective-permute-start.14 = (bf16[192,512]{1,0:T(8,128)(2,1)S(1)}, bf16[192,512]{1,0:T(8,128)(2,1)S(1)}, u32[]{:S(2)}, u32[]{:S(2)}) collective-permute-start(bf16[192,512]{1,0:T(8,128)(2,1)S(1)} %get-tuple-element.138), channel_id=1, source_target_pairs={{0,8},{8,0},{16,24},{24,16},{1,9},{9,1},{17,25},{25,17},{2,10},{10... | collective-permute-start | bytes 589832 | tf_op jit(solution)/shard_map/ppermute | solution.py:287
  73.4 2.0 %collective-permute-start.15 = (bf16[192,512]{1,0:T(8,128)(2,1)S(1)}, bf16[192,512]{1,0:T(8,128)(2,1)S(1)}, u32[]{:S(2)}, u32[]{:S(2)}) collective-permute-start(bf16[192,512]{1,0:T(8,128)(2,1)S(1)} %get-tuple-element.139), channel_id=1, source_target_pairs={{0,16},{8,24},{16,0},{24,8},{1,17},{9,25},{17,1},{25,9},{2,18},{10... | collective-permute-start | bytes 589832 | tf_op jit(solution)/shard_map/ppermute | solution.py:287
  75.3 1.4 %collective-permute-start.16 = (bf16[192,512]{1,0:T(8,128)(2,1)S(1)}, bf16[192,512]{1,0:T(8,128)(2,1)S(1)}, u32[]{:S(2)}, u32[]{:S(2)}) collective-permute-start(bf16[192,512]{1,0:T(8,128)(2,1)S(1)} %get-tuple-element.140), channel_id=1, source_target_pairs={{0,24},{8,16},{16,8},{24,0},{1,25},{9,17},{17,9},{25,1},{2,26},{10... | collective-permute-start | bytes 589832 | tf_op jit(solution)/shard_map/ppermute | solution.py:287
  78.7 8.8 %collective-permute-done.19.came1.mixed0 = bf16[2016,256]{1,0:T(8,128)(2,1)S(1)} collective-permute-done((bf16[2016,256]{1,0:T(8,128)(2,1)S(1)}, bf16[2016,256]{1,0:T(8,128)(2,1)S(1)}, u32[]{:S(2)}, u32[]{:S(2)}) %collective-permute-start.19) | collective-permute-done | bytes 1032224 | tf_op jit(solution)/shard_map/ppermute | solution.py:287
  88.2 1.6 %collective-permute-start.23 = (bf16[672,256]{1,0:T(8,128)(2,1)S(1)}, bf16[672,256]{1,0:T(8,128)(2,1)S(1)}, u32[]{:S(2)}, u32[]{:S(2)}) collective-permute-start(bf16[672,256]{1,0:T(8,128)(2,1)S(1)} %get-tuple-element.162), channel_id=1, source_target_pairs={{0,2},{1,3},{2,0},{3,1},{4,6},{5,7},{6,4},{7,5},{8,10},{9,11},{10,... | collective-permute-start | bytes 1032200 | tf_op jit(solution)/shard_map/ppermute | solution.py:287
  89.8 1.4 %collective-permute-start.24 = (bf16[672,256]{1,0:T(8,128)(2,1)S(1)}, bf16[672,256]{1,0:T(8,128)(2,1)S(1)}, u32[]{:S(2)}, u32[]{:S(2)}) collective-permute-start(bf16[672,256]{1,0:T(8,128)(2,1)S(1)} %get-tuple-element.163), channel_id=1, source_target_pairs={{0,1},{1,0},{2,3},{3,2},{4,5},{5,4},{6,7},{7,6},{8,9},{9,8},{10,11... | collective-permute-start | bytes 1032200 | tf_op jit(solution)/shard_map/ppermute | solution.py:287
  94.7 1.5 %join.1 = (f32[256,1024]{1,0:T(8,128)}, f32[256,1024]{1,0:T(8,128)}) custom-call(f32[256,512]{1,0:T(8,128)S(1)} %get-tuple-element.134.refs_0_, f32[256,512]{1,0:T(8,128)S(1)} %get-tuple-element.153.refs_1_, bf16[256,512]{1,0:T(8,128)(2,1)S(1)} %collective-permute-done.21.refs_2_, bf16[256,512]{1,0:T(8,128)(2,1)S(1)} %collective-permute-done.22.refs_3_), custom_call_target="tpu_custom_call" | custom-call | bytes 57344 | tf_op jit(solution)/shard_map/join/pallas_call | solution.py:31
  (47 shorter events, 21.8 us)
Async XLA Ops:
  0.6 33.4 %copy-start.1 = (bf16[1,1024,1344]{1,2,0:T(8,128)(2,1)S(1)}, bf16[1,1024,1344]{1,2,0:T(8,128)(2,1)}, u32[]{:S(2)}) copy-start(bf16[1,1024,1344]{1,2,0:T(8,128)(2,1)} %param.12) | copy-start | bytes 8257540
  2.5 16.7 %collective-permute-start.1 = (bf16[272,512]{1,0:T(8,128)(2,1)S(1)}, bf16[272,512]{1,0:T(8,128)(2,1)S(1)}, u32[]{:S(2)}, u32[]{:S(2)}) collective-permute-start(bf16[272,512]{1,0:T(8,128)(2,1)S(1)} %get-tuple-element.86), channel_id=1, source_target_pairs={{0,16},{8,24},{16,0},{24,8},{1,17},{9,25},{17,1},{25,9},{2,18},{10... | collective-permute-start | bytes 835592 | tf_op jit(solution)/shard_map/ppermute | solution.py:287
  6.6 10.2 %collective-permute-start = (bf16[192,512]{1,0:T(8,128)(2,1)S(1)}, bf16[192,512]{1,0:T(8,128)(2,1)S(1)}, u32[]{:S(2)}, u32[]{:S(2)}) collective-permute-start(bf16[192,512]{1,0:T(8,128)(2,1)S(1)} %get-tuple-element.85), channel_id=1, source_target_pairs={{0,8},{8,0},{16,24},{24,16},{1,9},{9,1},{17,25},{25,17},{2,10},{10... | collective-permute-start | bytes 589832 | tf_op jit(solution)/shard_map/ppermute | solution.py:287
  19.7 12.1 %collective-permute-start.5 = (bf16[192,512]{1,0:T(8,128)(2,1)S(1)}, bf16[192,512]{1,0:T(8,128)(2,1)S(1)}, u32[]{:S(2)}, u32[]{:S(2)}) collective-permute-start(bf16[192,512]{1,0:T(8,128)(2,1)S(1)} %get-tuple-element.94), channel_id=1, source_target_pairs={{0,8},{8,0},{16,24},{24,16},{1,9},{9,1},{17,25},{25,17},{2,10},{10... | collective-permute-start | bytes 589832 | tf_op jit(solution)/shard_map/ppermute | solution.py:287
  20.5 18.1 %collective-permute-start.2 = (bf16[192,512]{1,0:T(8,128)(2,1)S(1)}, bf16[192,512]{1,0:T(8,128)(2,1)S(1)}, u32[]{:S(2)}, u32[]{:S(2)}) collective-permute-start(bf16[192,512]{1,0:T(8,128)(2,1)S(1)} %get-tuple-element.95), channel_id=1, source_target_pairs={{0,8},{8,0},{16,24},{24,16},{1,9},{9,1},{17,25},{25,17},{2,10},{10... | collective-permute-start | bytes 589832 | tf_op jit(solution)/shard_map/ppermute | solution.py:287
  21.8 16.9 %collective-permute-start.3 = (bf16[192,512]{1,0:T(8,128)(2,1)S(1)}, bf16[192,512]{1,0:T(8,128)(2,1)S(1)}, u32[]{:S(2)}, u32[]{:S(2)}) collective-permute-start(bf16[192,512]{1,0:T(8,128)(2,1)S(1)} %get-tuple-element.96), channel_id=1, source_target_pairs={{0,16},{8,24},{16,0},{24,8},{1,17},{9,25},{17,1},{25,9},{2,18},{10... | collective-permute-start | bytes 589832 | tf_op jit(solution)/shard_map/ppermute | solution.py:287
  23.9 17.2 %collective-permute-start.4 = (bf16[192,512]{1,0:T(8,128)(2,1)S(1)}, bf16[192,512]{1,0:T(8,128)(2,1)S(1)}, u32[]{:S(2)}, u32[]{:S(2)}) collective-permute-start(bf16[192,512]{1,0:T(8,128)(2,1)S(1)} %get-tuple-element.97), channel_id=1, source_target_pairs={{0,24},{8,16},{16,8},{24,0},{1,25},{9,17},{17,9},{25,1},{2,26},{10... | collective-permute-start | bytes 589832 | tf_op jit(solution)/shard_map/ppermute | solution.py:287
  34.1 2.4 %copy-start = (bf16[1,1344,1024]{2,1,0:T(8,128)(2,1)S(1)}, bf16[1,1344,1024]{2,1,0:T(8,128)(2,1)}, u32[]{:S(2)}) copy-start(bf16[1,1344,1024]{2,1,0:T(8,128)(2,1)} %param.13) | copy-start | bytes 8257540
  41.1 1.4 %collective-permute-start.6 = (bf16[192,512]{1,0:T(8,128)(2,1)S(1)}, bf16[192,512]{1,0:T(8,128)(2,1)S(1)}, u32[]{:S(2)}, u32[]{:S(2)}) collective-permute-start(bf16[192,512]{1,0:T(8,128)(2,1)S(1)} %collective-permute-done.2.refs_1_), channel_id=1, source_target_pairs={{0,4},{4,0},{1,5},{5,1},{2,6},{6,2},{3,7},{7,3},{8,12},{12,8},{9,1... | collective-permute-start | bytes 589832 | tf_op jit(solution)/shard_map/ppermute | solution.py:287
  41.1 1.7 %collective-permute-start.7 = (bf16[192,512]{1,0:T(8,128)(2,1)S(1)}, bf16[192,512]{1,0:T(8,128)(2,1)S(1)}, u32[]{:S(2)}, u32[]{:S(2)}) collective-permute-start(bf16[192,512]{1,0:T(8,128)(2,1)S(1)} %collective-permute-done.3.refs_2_), channel_id=1, source_target_pairs={{0,4},{4,0},{1,5},{5,1},{2,6},{6,2},{3,7},{7,3},{8,12},{12,8},{9,1... | collective-permute-start | bytes 589832 | tf_op jit(solution)/shard_map/ppermute | solution.py:287
  41.6 1.5 %collective-permute-start.8 = (bf16[192,512]{1,0:T(8,128)(2,1)S(1)}, bf16[192,512]{1,0:T(8,128)(2,1)S(1)}, u32[]{:S(2)}, u32[]{:S(2)}) collective-permute-start(bf16[192,512]{1,0:T(8,128)(2,1)S(1)} %collective-permute-done.4.refs_3_), channel_id=1, source_target_pairs={{0,4},{4,0},{1,5},{5,1},{2,6},{6,2},{3,7},{7,3},{8,12},{12,8},{9,1... | collective-permute-start | bytes 589832 | tf_op jit(solution)/shard_map/ppermute | solution.py:287
  41.6 7.3 %collective-permute-start.9 = (bf16[768,512]{1,0:T(8,128)(2,1)S(1)}, bf16[768,512]{1,0:T(8,128)(2,1)S(1)}, u32[]{:S(2)}, u32[]{:S(2)}) collective-permute-start(bf16[768,512]{1,0:T(8,128)(2,1)S(1)} %get-tuple-element.112), channel_id=1, source_target_pairs={{0,4},{4,0},{1,5},{5,1},{2,6},{6,2},{3,7},{7,3},{8,12},{12,8},{9,1... | collective-permute-start | bytes 2359304 | tf_op jit(solution)/shard_map/ppermute | solution.py:287
  44.5 17.6 %collective-permute-start.17 = (bf16[1344,256]{1,0:T(8,128)(2,1)S(1)}, bf16[1344,256]{1,0:T(8,128)(2,1)S(1)}, u32[]{:S(2)}, u32[]{:S(2)}) collective-permute-start(bf16[1344,256]{1,0:T(8,128)(2,1)S(1)} %get-tuple-element.141), channel_id=1, source_target_pairs={{0,1},{1,0},{2,3},{3,2},{4,5},{5,4},{6,7},{7,6},{8,9},{9,8},{10,11... | collective-permute-start | bytes 2064392 | tf_op jit(solution)/shard_map/ppermute | solution.py:287
  46.0 17.3 %collective-permute-start.18 = (bf16[1344,256]{1,0:T(8,128)(2,1)S(1)}, bf16[1344,256]{1,0:T(8,128)(2,1)S(1)}, u32[]{:S(2)}, u32[]{:S(2)}) collective-permute-start(bf16[1344,256]{1,0:T(8,128)(2,1)S(1)} %get-tuple-element.142), channel_id=1, source_target_pairs={{0,2},{1,3},{2,0},{3,1},{4,6},{5,7},{6,4},{7,5},{8,10},{9,11},{10,... | collective-permute-start | bytes 2064392 | tf_op jit(solution)/shard_map/ppermute | solution.py:287
  49.2 19.1 %collective-permute-start.10 = (bf16[192,512]{1,0:T(8,128)(2,1)S(1)}, bf16[192,512]{1,0:T(8,128)(2,1)S(1)}, u32[]{:S(2)}, u32[]{:S(2)}) collective-permute-start(bf16[192,512]{1,0:T(8,128)(2,1)S(1)} %get-tuple-element.116), channel_id=1, source_target_pairs={{0,8},{8,0},{16,24},{24,16},{1,9},{9,1},{17,25},{25,17},{2,10},{10... | collective-permute-start | bytes 589832 | tf_op jit(solution)/shard_map/ppermute | solution.py:287
  50.5 17.7 %collective-permute-start.11 = (bf16[192,512]{1,0:T(8,128)(2,1)S(1)}, bf16[192,512]{1,0:T(8,128)(2,1)S(1)}, u32[]{:S(2)}, u32[]{:S(2)}) collective-permute-start(bf16[192,512]{1,0:T(8,128)(2,1)S(1)} %get-tuple-element.117), channel_id=1, source_target_pairs={{0,16},{8,24},{16,0},{24,8},{1,17},{9,25},{17,1},{25,9},{2,18},{10... | collective-permute-start | bytes 589832 | tf_op jit(solution)/shard_map/ppermute | solution.py:287
  52.5 15.7 %collective-permute-start.12 = (bf16[192,512]{1,0:T(8,128)(2,1)S(1)}, bf16[192,512]{1,0:T(8,128)(2,1)S(1)}, u32[]{:S(2)}, u32[]{:S(2)}) collective-permute-start(bf16[192,512]{1,0:T(8,128)(2,1)S(1)} %get-tuple-element.118), channel_id=1, source_target_pairs={{0,24},{8,16},{16,8},{24,0},{1,25},{9,17},{17,9},{25,1},{2,26},{10... | collective-permute-start | bytes 589832 | tf_op jit(solution)/shard_map/ppermute | solution.py:287
  63.7 23.9 %collective-permute-start.19 = (bf16[2016,256]{1,0:T(8,128)(2,1)S(1)}, bf16[2016,256]{1,0:T(8,128)(2,1)S(1)}, u32[]{:S(2)}, u32[]{:S(2)}) collective-permute-start(bf16[2016,256]{1,0:T(8,128)(2,1)S(1)} %get-tuple-element.145), channel_id=1, source_target_pairs={{0,1},{1,0},{2,3},{3,2},{4,5},{5,4},{6,7},{7,6},{8,9},{9,8},{10,11... | collective-permute-start | bytes 3096584 | tf_op jit(solution)/shard_map/ppermute | solution.py:287
  64.3 23.6 %collective-permute-start.20 = (bf16[2016,256]{1,0:T(8,128)(2,1)S(1)}, bf16[2016,256]{1,0:T(8,128)(2,1)S(1)}, u32[]{:S(2)}, u32[]{:S(2)}) collective-permute-start(bf16[2016,256]{1,0:T(8,128)(2,1)S(1)} %get-tuple-element.146), channel_id=1, source_target_pairs={{0,2},{1,3},{2,0},{3,1},{4,6},{5,7},{6,4},{7,5},{8,10},{9,11},{10,... | collective-permute-start | bytes 3096584 | tf_op jit(solution)/shard_map/ppermute | solution.py:287
  68.2 2.4 %collective-permute-start.13 = (bf16[768,512]{1,0:T(8,128)(2,1)S(1)}, bf16[768,512]{1,0:T(8,128)(2,1)S(1)}, u32[]{:S(2)}, u32[]{:S(2)}) collective-permute-start(bf16[768,512]{1,0:T(8,128)(2,1)S(1)} %get-tuple-element.136), channel_id=1, source_target_pairs={{0,4},{4,0},{1,5},{5,1},{2,6},{6,2},{3,7},{7,3},{8,12},{12,8},{9,1... | collective-permute-start | bytes 2359304 | tf_op jit(solution)/shard_map/ppermute | solution.py:287
  70.8 21.6 %collective-permute-start.14 = (bf16[192,512]{1,0:T(8,128)(2,1)S(1)}, bf16[192,512]{1,0:T(8,128)(2,1)S(1)}, u32[]{:S(2)}, u32[]{:S(2)}) collective-permute-start(bf16[192,512]{1,0:T(8,128)(2,1)S(1)} %get-tuple-element.138), channel_id=1, source_target_pairs={{0,8},{8,0},{16,24},{24,16},{1,9},{9,1},{17,25},{25,17},{2,10},{10... | collective-permute-start | bytes 589832 | tf_op jit(solution)/shard_map/ppermute | solution.py:287
  73.4 19.0 %collective-permute-start.15 = (bf16[192,512]{1,0:T(8,128)(2,1)S(1)}, bf16[192,512]{1,0:T(8,128)(2,1)S(1)}, u32[]{:S(2)}, u32[]{:S(2)}) collective-permute-start(bf16[192,512]{1,0:T(8,128)(2,1)S(1)} %get-tuple-element.139), channel_id=1, source_target_pairs={{0,16},{8,24},{16,0},{24,8},{1,17},{9,25},{17,1},{25,9},{2,18},{10... | collective-permute-start | bytes 589832 | tf_op jit(solution)/shard_map/ppermute | solution.py:287
  75.3 17.1 %collective-permute-start.16 = (bf16[192,512]{1,0:T(8,128)(2,1)S(1)}, bf16[192,512]{1,0:T(8,128)(2,1)S(1)}, u32[]{:S(2)}, u32[]{:S(2)}) collective-permute-start(bf16[192,512]{1,0:T(8,128)(2,1)S(1)} %get-tuple-element.140), channel_id=1, source_target_pairs={{0,24},{8,16},{16,8},{24,0},{1,25},{9,17},{17,9},{25,1},{2,26},{10... | collective-permute-start | bytes 589832 | tf_op jit(solution)/shard_map/ppermute | solution.py:287
  88.2 8.0 %collective-permute-start.23 = (bf16[672,256]{1,0:T(8,128)(2,1)S(1)}, bf16[672,256]{1,0:T(8,128)(2,1)S(1)}, u32[]{:S(2)}, u32[]{:S(2)}) collective-permute-start(bf16[672,256]{1,0:T(8,128)(2,1)S(1)} %get-tuple-element.162), channel_id=1, source_target_pairs={{0,2},{1,3},{2,0},{3,1},{4,6},{5,7},{6,4},{7,5},{8,10},{9,11},{10,... | collective-permute-start | bytes 1032200 | tf_op jit(solution)/shard_map/ppermute | solution.py:287
  89.8 7.6 %collective-permute-start.24 = (bf16[672,256]{1,0:T(8,128)(2,1)S(1)}, bf16[672,256]{1,0:T(8,128)(2,1)S(1)}, u32[]{:S(2)}, u32[]{:S(2)}) collective-permute-start(bf16[672,256]{1,0:T(8,128)(2,1)S(1)} %get-tuple-element.163), channel_id=1, source_target_pairs={{0,1},{1,0},{2,3},{3,2},{4,5},{5,4},{6,7},{7,6},{8,9},{9,8},{10,11... | collective-permute-start | bytes 1032200 | tf_op jit(solution)/shard_map/ppermute | solution.py:287
  92.4 1.5 %collective-permute-start.21 = (bf16[256,512]{1,0:T(8,128)(2,1)S(1)}, bf16[256,512]{1,0:T(8,128)(2,1)S(1)}, u32[]{:S(2)}, u32[]{:S(2)}) collective-permute-start(bf16[256,512]{1,0:T(8,128)(2,1)S(1)} %get-tuple-element.154), channel_id=1, source_target_pairs={{0,4},{4,0},{1,5},{5,1},{2,6},{6,2},{3,7},{7,3},{8,12},{12,8},{9,1... | collective-permute-start | bytes 786440 | tf_op jit(solution)/shard_map/ppermute | solution.py:287
  92.9 1.7 %collective-permute-start.22 = (bf16[256,512]{1,0:T(8,128)(2,1)S(1)}, bf16[256,512]{1,0:T(8,128)(2,1)S(1)}, u32[]{:S(2)}, u32[]{:S(2)}) collective-permute-start(bf16[256,512]{1,0:T(8,128)(2,1)S(1)} %get-tuple-element.155), channel_id=1, source_target_pairs={{0,4},{4,0},{1,5},{5,1},{2,6},{6,2},{3,7},{7,3},{8,12},{12,8},{9,1... | collective-permute-start | bytes 786440 | tf_op jit(solution)/shard_map/ppermute | solution.py:287

commit v7 on v6

--- a/solution.py
+++ b/solution.py
@@ -92,21 +92,23 @@
     return mxu(chosen.astype(BF16), tokens).astype(BF16)
 
 
-def route_body(owners, relayed, routes_ref, tokens_ref, own_ref, *sends):
+def all_body(routes_ref, tokens_ref, all_ref):
+    top, count = routes_ref.shape
+    half = all_ref.shape[1]
+    line = lax.broadcasted_iota(jnp.int32, (ROW_TILE, count), 0)
+    lines = sum(jnp.where(line == k, routes_ref[k : k + 1, :], 0) for k in range(top))
+    all_ref[:count, :] = tokens_ref[:, window(lax.axis_index("cuts"), half)].astype(BF16)
+    all_ref[count:, :] = jnp.zeros((ROW_TILE, half), BF16)
+    all_ref[count:, :count] = lines.astype(F32).astype(BF16)
+
+
+def route_body(owners, routes_ref, tokens_ref, own_ref, *sends):
     me, core = lax.axis_index("expert"), lax.axis_index("cuts")
     top, count = routes_ref.shape
     half = tokens_ref.shape[1] // lax.axis_size("cuts")
     routes = [routes_ref[k : k + 1, :] for k in range(top)]
     rank = ranks(routes, owners)
     narrow = tokens_ref[:, window(core, half)].astype(BF16)
-    if relayed:
-        *sends, all_ref = sends
-        line = lax.broadcasted_iota(jnp.int32, (ROW_TILE, count), 0)
-        all_ref[:count, :] = narrow
-        all_ref[count:, :] = jnp.zeros((ROW_TILE, half), BF16)
-        all_ref[count:, :count] = sum(
-            jnp.where(line == k, route, 0).astype(F32) for k, route in enumerate(routes)
-        ).astype(BF16)
     for shift, ref in reversed(list(enumerate(sends, 1))):
         ref[...] = rows_for(me ^ shift, routes, rank, narrow, ref.shape[0])
     own_ref[...] = rows_for(me, routes, rank, tokens_ref[...].astype(BF16), own_ref.shape[0])
@@ -320,6 +322,12 @@
     def over_experts(chunks, first=1):
         return [partner(x, "expert", s) for s, x in enumerate(chunks, first)]
 
+    def far_first(chunks):
+        return chunks[1:] + chunks[:1]
+
+    def near_first(chunks):
+        return chunks[-1:] + chunks[:-1]
+
     def given(units_rows, weight, name):
         return local(
             give_body, [shape(slots, units), shape(slots, half)], [units_rows, weight], work // 2, name + "_give"
@@ -346,16 +354,20 @@
     relayed = owners % 4 == 0 and count + ROW_TILE < 2 * capacity and count <= half
     pairs = range(2, owners, 2) if relayed else ()
     chunk = shape(capacity, half)
+    if relayed:
+        (everything,) = local(
+            all_body, [shape(count + ROW_TILE, half)], [routes.T, tokens], 0, "all_tokens", space=pltpu.HBM
+        )
     own, *sends = local(
-        functools.partial(route_body, owners, relayed),
-        [shape(capacity, features)] + ([chunk, shape(count + ROW_TILE, half)] if relayed else [chunk] * remote),
+        functools.partial(route_body, owners),
+        [shape(capacity, features)] + [chunk] * (1 if relayed else remote),
         [routes.T, tokens],
         2 * count * slots * features,
         "route",
         space=pltpu.HBM,
     )
-    dense = [partner(sends[-1], "expert", s) for s in pairs]
-    mine = over_experts(sends[:1] if relayed else sends)
+    dense = [partner(everything, "expert", s) for s in pairs]
+    mine = over_experts(sends)
     meta, grad_own, *grad_sends = local(
         functools.partial(weigh_body, owners, capacity),
         [shape(count, 128, F32), shape(capacity, features)] + [shape(capacity, half)] * remote,
@@ -387,7 +399,8 @@
     )
     turned, give = given(hidden, outer, "rows")
     keep = kept(turned, outer, "rows")
-    grad_mine, grad_whole, hidden, give = after((grad_mine, grad_whole, hidden, give))
+    grad_mine, grad_whole, hidden, give = after((far_first(grad_mine), grad_whole, hidden, give))
+    grad_mine = near_first(grad_mine)
     came = partner(give, "cuts", 1)
     grad_other = across_cores(grad_mine)
     grad_rows, *outer_sent = local(

time: 98.8 us -> 96 us (0.972)
  waiting for transfers between devices: 30.7 us -> 26.9 us
  Pallas kernels: 28.8 us -> 30 us
    ppermute x25, waiting for transfers between devices: 30.7 us -> 26.9 us  [partner(): lax.ppermute(x, axis, [(i, i ^ bit) for i in range(lax.axis_size(axis))])]
    pallas_call x22 -> x23, Pallas kernels: 28.8 us -> 30 us  [local(): pl.pallas_call(body, out_shape=tuple((gives(x.shape, x.dtype) for x in ou...]
  transfers between devices with their start and end apart: 25 -> 25, of which waited for: 16 -> 17; matrix products, arithmetic and copies ran while one was open for 0% -> 0% of each run, Pallas kernels for 26% -> 28%
where the time goes in v7:
time: 96 us; the launch traced here: 95.4 us
  starting transfers between devices  31.3 us (33%)
  Pallas kernels  30 us (31%)
  waiting for transfers between devices  26.9 us (28%)
  blocking collectives  6.41 us (7%)
    ppermute x25, starting transfers between devices, partner(): lax.ppermute(x, axis, [(i, i ^ bit) for i in range(lax.axis_size(axis))])  31.3 us
    pallas_call x23, Pallas kernels, local(): pl.pallas_call(body, out_shape=tuple((gives(x.shape, x.dtype) for x in ou...  30 us
    ppermute x25, waiting for transfers between devices, partner(): lax.ppermute(x, axis, [(i, i ^ bit) for i in range(lax.axis_size(axis))])  26.9 us
    all_gather x3, blocking collectives, joined(): return [lax.all_gather(x, 'cuts', axis=1, tiled=True) for x in chunks]  6.41 us
  transfers between devices with their start and end apart: 25, of which 17 were waited for; matrix products, arithmetic and copies ran while one was open for 0% of the time, Pallas kernels for 28%

profile of v7, /device:TPU:0, one launch (start us, length us, event | category | flops | bytes accessed | tf_op | source)
XLA Modules:
  0.0 95.4 jit_solution(4510546533690523550)
XLA Ops:
  0.6 1.3 %all_tokens.1 = bf16[272,512]{1,0:T(8,128)(2,1)S(1)} custom-call(s32[2,256]{1,0:T(2,128)} %bitcast.19, f32[256,1024]{1,0:T(8,128)} %tokens_ref.3), custom_call_target="tpu_custom_call" | custom-call | bytes 20768 | tf_op jit(solution)/shard_map/all_tokens/pallas_call | solution.py:31
  1.9 4.1 %collective-permute-start.1 = (bf16[272,512]{1,0:T(8,128)(2,1)S(1)}, bf16[272,512]{1,0:T(8,128)(2,1)S(1)}, u32[]{:S(2)}, u32[]{:S(2)}) collective-permute-start(bf16[272,512]{1,0:T(8,128)(2,1)S(1)} %all_tokens.1), channel_id=1, source_target_pairs={{0,16},{8,24},{16,0},{24,8},{1,17},{9,25},{17,1},{25,9},{2,18},{10... | collective-permute-start | bytes 835592 | tf_op jit(solution)/shard_map/ppermute | solution.py:289
  6.0 1.7 %route.1 = (bf16[192,1024]{1,0:T(8,128)(2,1)S(1)}, bf16[192,512]{1,0:T(8,128)(2,1)S(1)}) custom-call(s32[2,256]{1,0:T(2,128)} %bitcast.20, f32[256,1024]{1,0:T(8,128)} %tokens_ref.3), custom_call_target="tpu_custom_call" | custom-call | flops 6291456 | bytes 25632 | tf_op jit(solution)/shard_map/route/pallas_call | solution.py:31
  7.8 1.6 %collective-permute-start = (bf16[192,512]{1,0:T(8,128)(2,1)S(1)}, bf16[192,512]{1,0:T(8,128)(2,1)S(1)}, u32[]{:S(2)}, u32[]{:S(2)}) collective-permute-start(bf16[192,512]{1,0:T(8,128)(2,1)S(1)} %get-tuple-element.84), channel_id=1, source_target_pairs={{0,8},{8,0},{16,24},{24,16},{1,9},{9,1},{17,25},{25,17},{2,10},{10... | collective-permute-start | bytes 589832 | tf_op jit(solution)/shard_map/ppermute | solution.py:289
  9.4 3.2 %weigh.1 = (f32[256,128]{1,0:T(8,128)S(1)}, bf16[192,1024]{1,0:T(8,128)(2,1)S(1)}, bf16[192,512]{1,0:T(8,128)(2,1)S(1)}, bf16[192,512]{1,0:T(8,128)(2,1)S(1)}, bf16[192,512]{1,0:T(8,128)(2,1)S(1)}) custom-call(s32[2,256]{1,0:T(2,128)} %bitcast.21, s32[2,256]{1,0:T(2,128)} %bitcast.22, f32[1,256]{1,0:T(1,128)} %bitcast.23, f32[256,1024]{1,0:T(8,128)} %cotangent_ref.1), custom_call_target="tpu_custom_call" | custom-call | flops 12582912 | bytes 33872 | tf_op jit(solution)/shard_map/weigh/pallas_call | solution.py:31
  12.6 6.4 %collective-permute-done = bf16[192,512]{1,0:T(8,128)(2,1)S(1)} collective-permute-done((bf16[192,512]{1,0:T(8,128)(2,1)S(1)}, bf16[192,512]{1,0:T(8,128)(2,1)S(1)}, u32[]{:S(2)}, u32[]{:S(2)}) %collective-permute-start) | collective-permute-done | bytes 196640 | tf_op jit(solution)/shard_map/ppermute | solution.py:289
  19.9 3.4 %collective-permute-start.2 = (bf16[192,512]{1,0:T(8,128)(2,1)S(1)}, bf16[192,512]{1,0:T(8,128)(2,1)S(1)}, u32[]{:S(2)}, u32[]{:S(2)}) collective-permute-start(bf16[192,512]{1,0:T(8,128)(2,1)S(1)} %get-tuple-element.93), channel_id=1, source_target_pairs={{0,16},{8,24},{16,0},{24,8},{1,17},{9,25},{17,1},{25,9},{2,18},{10... | collective-permute-start | bytes 589832 | tf_op jit(solution)/shard_map/ppermute | solution.py:289
  23.9 2.1 %all_gather.9.refs_1_ = bf16[192,1024]{1,0:T(8,128)(2,1)S(1)} all-gather(bf16[192,512]{1,0:T(8,128)(2,1)S(1)} %collective-permute-done), channel_id=1, replica_groups=mesh['expert'=4,'cuts'=2,'dp'=4] {'cuts'}, dimensions={1}, use_global_device_ids=true | all-gather | bytes 589824 | tf_op jit(solution)/shard_map/all_gather | solution.py:320
  26.0 2.1 %all_gather.10.refs_2_ = bf16[192,1024]{1,0:T(8,128)(2,1)S(1)} all-gather(bf16[192,512]{1,0:T(8,128)(2,1)S(1)} %get-tuple-element.99), channel_id=1, replica_groups=mesh['expert'=4,'cuts'=2,'dp'=4] {'cuts'}, dimensions={1}, use_global_device_ids=true | all-gather | bytes 589824 | tf_op jit(solution)/shard_map/all_gather | solution.py:320
  28.0 2.1 %collective-permute-done.5 = bf16[192,512]{1,0:T(8,128)(2,1)S(1)} collective-permute-done((bf16[192,512]{1,0:T(8,128)(2,1)S(1)}, bf16[192,512]{1,0:T(8,128)(2,1)S(1)}, u32[]{:S(2)}, u32[]{:S(2)}) %collective-permute-start.5) | collective-permute-done | bytes 196640 | tf_op jit(solution)/shard_map/ppermute | solution.py:289
  30.2 2.3 %all_gather.11.refs_3_ = bf16[192,1024]{1,0:T(8,128)(2,1)S(1)} all-gather(bf16[192,512]{1,0:T(8,128)(2,1)S(1)} %collective-permute-done.5), channel_id=1, replica_groups=mesh['expert'=4,'cuts'=2,'dp'=4] {'cuts'}, dimensions={1}, use_global_device_ids=true | all-gather | bytes 589824 | tf_op jit(solution)/shard_map/all_gather | solution.py:320
  32.4 2.3 %hidden.1 = (bf16[768,1024]{1,0:T(8,128)(2,1)S(1)}, bf16[1344,768]{1,0:T(8,128)(2,1)S(1)}, bf16[1344,768]{1,0:T(8,128)(2,1)S(1)}) custom-call(bf16[192,1024]{1,0:T(8,128)(2,1)S(1)} %get-tuple-element.97.refs_0_, bf16[192,1024]{1,0:T(8,128)(2,1)S(1)} %all_gather.9.refs_1_, bf16[192,1024]{1,0:T(8,128)(2,1)S(1)} %all_gather.10.refs_2_, ...), custom_call_target="tpu_custom_call" | custom-call | flops 33030144 | bytes 156672 | tf_op jit(solution)/shard_map/hidden/pallas_call | solution.py:31
  34.8 2.2 %rows_give.1 = (bf16[768,1344]{1,0:T(8,128)(2,1)S(1)}, bf16[768,512]{1,0:T(8,128)(2,1)S(1)}) custom-call(bf16[1344,768]{1,0:T(8,128)(2,1)S(1)} %get-tuple-element.122.units_ref.refs_7_, bf16[1344,1024]{1,0:T(8,128)(2,1)S(1)} %bitcast.11), custom_call_target="tpu_custom_call" | custom-call | flops 16515072 | bytes 119808 | tf_op jit(solution)/shard_map/rows_give/pallas_call | solution.py:31
  39.9 1.4 %outer_leaving.1 = (bf16[768,1024]{1,0:T(8,128)(2,1)S(1)}, bf16[1344,256]{1,0:T(8,128)(2,1)S(1)}, bf16[1344,256]{1,0:T(8,128)(2,1)S(1)}) custom-call(bf16[192,1024]{1,0:T(8,128)(2,1)S(1)} %get-tuple-element.102.refs_0_, bf16[192,512]{1,0:T(8,128)(2,1)S(1)} %collective-permute-done.4.refs_1_, bf16[192,512]{1,0:T(8,128)(2,1)S(1)} %collective-permute-done.2.refs_2_, ...), custom_call_target="tpu_custom_call" | custom-call | flops 16515072 | bytes 102912 | tf_op jit(solution)/shard_map/outer_leaving/pallas_call | solution.py:31
  41.3 1.5 %collective-permute-start.17 = (bf16[1344,256]{1,0:T(8,128)(2,1)S(1)}, bf16[1344,256]{1,0:T(8,128)(2,1)S(1)}, u32[]{:S(2)}, u32[]{:S(2)}) collective-permute-start(bf16[1344,256]{1,0:T(8,128)(2,1)S(1)} %get-tuple-element.139), channel_id=1, source_target_pairs={{0,1},{1,0},{2,3},{3,2},{4,5},{5,4},{6,7},{7,6},{8,9},{9,8},{10,11... | collective-permute-start | bytes 2064392 | tf_op jit(solution)/shard_map/ppermute | solution.py:289
  42.8 1.5 %collective-permute-start.18 = (bf16[1344,256]{1,0:T(8,128)(2,1)S(1)}, bf16[1344,256]{1,0:T(8,128)(2,1)S(1)}, u32[]{:S(2)}, u32[]{:S(2)}) collective-permute-start(bf16[1344,256]{1,0:T(8,128)(2,1)S(1)} %get-tuple-element.140), channel_id=1, source_target_pairs={{0,2},{1,3},{2,0},{3,1},{4,6},{5,7},{6,4},{7,5},{8,10},{9,11},{10,... | collective-permute-start | bytes 2064392 | tf_op jit(solution)/shard_map/ppermute | solution.py:289
  44.3 1.4 %rows_keep.1.keep_ref = bf16[768,512]{1,0:T(8,128)(2,1)S(1)} custom-call(bf16[768,1344]{1,0:T(8,128)(2,1)S(1)} %get-tuple-element.109.turned_ref, bf16[1344,1024]{1,0:T(8,128)(2,1)S(1)} %bitcast.12), custom_call_target="tpu_custom_call" | custom-call | flops 16515072 | bytes 87552 | tf_op jit(solution)/shard_map/rows_keep/pallas_call | solution.py:31
  45.9 3.6 %collective-permute-start.10 = (bf16[192,512]{1,0:T(8,128)(2,1)S(1)}, bf16[192,512]{1,0:T(8,128)(2,1)S(1)}, u32[]{:S(2)}, u32[]{:S(2)}) collective-permute-start(bf16[192,512]{1,0:T(8,128)(2,1)S(1)} %get-tuple-element.114), channel_id=1, source_target_pairs={{0,8},{8,0},{16,24},{24,16},{1,9},{9,1},{17,25},{25,17},{2,10},{10... | collective-permute-start | bytes 589832 | tf_op jit(solution)/shard_map/ppermute | solution.py:289
  49.4 1.4 %collective-permute-start.11 = (bf16[192,512]{1,0:T(8,128)(2,1)S(1)}, bf16[192,512]{1,0:T(8,128)(2,1)S(1)}, u32[]{:S(2)}, u32[]{:S(2)}) collective-permute-start(bf16[192,512]{1,0:T(8,128)(2,1)S(1)} %get-tuple-element.115), channel_id=1, source_target_pairs={{0,16},{8,24},{16,0},{24,8},{1,17},{9,25},{17,1},{25,9},{2,18},{10... | collective-permute-start | bytes 589832 | tf_op jit(solution)/shard_map/ppermute | solution.py:289
  51.9 2.3 %d_act.1.units_ref = bf16[1344,768]{1,0:T(8,128)(2,1)S(1)} custom-call(bf16[768,1024]{1,0:T(8,128)(2,1)S(1)} %get-tuple-element.123.g_ref.rows_ref, bf16[1344,768]{1,0:T(8,128)(2,1)S(1)} %get-tuple-element.118.positive_ref, bf16[1344,1024]{1,0:T(8,128)(2,1)S(1)} %bitcast.13), custom_call_target="tpu_custom_call" | custom-call | flops 33030144 | bytes 132096 | tf_op jit(solution)/shard_map/d_act/pallas_call | solution.py:31
  54.2 1.3 %inner_leaving.1 = (bf16[1344,256]{1,0:T(8,128)(2,1)S(1)}, bf16[1344,256]{1,0:T(8,128)(2,1)S(1)}) custom-call(bf16[1344,768]{1,0:T(8,128)(2,1)S(1)} %d_act.1.units_ref, bf16[768,1024]{1,0:T(8,128)(2,1)S(1)} %get-tuple-element.119.rows_ref), custom_call_target="tpu_custom_call" | custom-call | flops 16515072 | bytes 78336 | tf_op jit(solution)/shard_map/inner_leaving/pallas_call | solution.py:31
  56.8 2.1 %collective-permute-done.17.came0 = bf16[1344,256]{1,0:T(8,128)(2,1)S(1)} collective-permute-done((bf16[1344,256]{1,0:T(8,128)(2,1)S(1)}, bf16[1344,256]{1,0:T(8,128)(2,1)S(1)}, u32[]{:S(2)}, u32[]{:S(2)}) %collective-permute-start.17) | collective-permute-done | bytes 688160 | tf_op jit(solution)/shard_map/ppermute | solution.py:289
  61.1 1.4 %collective-permute-start.20 = (bf16[2016,256]{1,0:T(8,128)(2,1)S(1)}, bf16[2016,256]{1,0:T(8,128)(2,1)S(1)}, u32[]{:S(2)}, u32[]{:S(2)}) collective-permute-start(bf16[2016,256]{1,0:T(8,128)(2,1)S(1)} %get-tuple-element.144), channel_id=1, source_target_pairs={{0,2},{1,3},{2,0},{3,1},{4,6},{5,7},{6,4},{7,5},{8,10},{9,11},{10,... | collective-permute-start | bytes 3096584 | tf_op jit(solution)/shard_map/ppermute | solution.py:289
  62.5 2.4 %grad_rows_give.1 = (bf16[768,1344]{1,0:T(8,128)(2,1)S(1)}, bf16[768,512]{1,0:T(8,128)(2,1)S(1)}) custom-call(bf16[1344,768]{1,0:T(8,128)(2,1)S(1)} %d_act.1.units_ref, bf16[1344,1024]{1,0:T(8,128)(2,1)S(1)} %bitcast.15), custom_call_target="tpu_custom_call" | custom-call | flops 16515072 | bytes 119808 | tf_op jit(solution)/shard_map/grad_rows_give/pallas_call | solution.py:31
  65.0 1.7 %collective-permute-done.11.refs_2_ = bf16[192,512]{1,0:T(8,128)(2,1)S(1)} collective-permute-done((bf16[192,512]{1,0:T(8,128)(2,1)S(1)}, bf16[192,512]{1,0:T(8,128)(2,1)S(1)}, u32[]{:S(2)}, u32[]{:S(2)}) %collective-permute-start.11) | collective-permute-done | bytes 196640 | tf_op jit(solution)/shard_map/ppermute | solution.py:289
  66.6 1.4 %grad_rows_keep.1.keep_ref = bf16[768,512]{1,0:T(8,128)(2,1)S(1)} custom-call(bf16[768,1344]{1,0:T(8,128)(2,1)S(1)} %get-tuple-element.133.turned_ref, bf16[1344,1024]{1,0:T(8,128)(2,1)S(1)} %bitcast.16), custom_call_target="tpu_custom_call" | custom-call | flops 16515072 | bytes 87552 | tf_op jit(solution)/shard_map/grad_rows_keep/pallas_call | solution.py:31
  69.1 3.2 %collective-permute-start.14 = (bf16[192,512]{1,0:T(8,128)(2,1)S(1)}, bf16[192,512]{1,0:T(8,128)(2,1)S(1)}, u32[]{:S(2)}, u32[]{:S(2)}) collective-permute-start(bf16[192,512]{1,0:T(8,128)(2,1)S(1)} %get-tuple-element.136), channel_id=1, source_target_pairs={{0,8},{8,0},{16,24},{24,16},{1,9},{9,1},{17,25},{25,17},{2,10},{10... | collective-permute-start | bytes 589832 | tf_op jit(solution)/shard_map/ppermute | solution.py:289
  73.4 1.4 %collective-permute-start.16 = (bf16[192,512]{1,0:T(8,128)(2,1)S(1)}, bf16[192,512]{1,0:T(8,128)(2,1)S(1)}, u32[]{:S(2)}, u32[]{:S(2)}) collective-permute-start(bf16[192,512]{1,0:T(8,128)(2,1)S(1)} %get-tuple-element.138), channel_id=1, source_target_pairs={{0,24},{8,16},{16,8},{24,0},{1,25},{9,17},{17,9},{25,1},{2,26},{10... | collective-permute-start | bytes 589832 | tf_op jit(solution)/shard_map/ppermute | solution.py:289
  76.8 7.5 %collective-permute-done.19.came1.mixed0 = bf16[2016,256]{1,0:T(8,128)(2,1)S(1)} collective-permute-done((bf16[2016,256]{1,0:T(8,128)(2,1)S(1)}, bf16[2016,256]{1,0:T(8,128)(2,1)S(1)}, u32[]{:S(2)}, u32[]{:S(2)}) %collective-permute-start.19) | collective-permute-done | bytes 1032224 | tf_op jit(solution)/shard_map/ppermute | solution.py:289
  84.9 1.6 %collective-permute-start.23 = (bf16[672,256]{1,0:T(8,128)(2,1)S(1)}, bf16[672,256]{1,0:T(8,128)(2,1)S(1)}, u32[]{:S(2)}, u32[]{:S(2)}) collective-permute-start(bf16[672,256]{1,0:T(8,128)(2,1)S(1)} %get-tuple-element.160), channel_id=1, source_target_pairs={{0,2},{1,3},{2,0},{3,1},{4,6},{5,7},{6,4},{7,5},{8,10},{9,11},{10,... | collective-permute-start | bytes 1032200 | tf_op jit(solution)/shard_map/ppermute | solution.py:289
  86.5 1.4 %collective-permute-start.24 = (bf16[672,256]{1,0:T(8,128)(2,1)S(1)}, bf16[672,256]{1,0:T(8,128)(2,1)S(1)}, u32[]{:S(2)}, u32[]{:S(2)}) collective-permute-start(bf16[672,256]{1,0:T(8,128)(2,1)S(1)} %get-tuple-element.161), channel_id=1, source_target_pairs={{0,1},{1,0},{2,3},{3,2},{4,5},{5,4},{6,7},{7,6},{8,9},{9,8},{10,11... | collective-permute-start | bytes 1032200 | tf_op jit(solution)/shard_map/ppermute | solution.py:289
  91.6 1.5 %join.1 = (f32[256,1024]{1,0:T(8,128)}, f32[256,1024]{1,0:T(8,128)}) custom-call(f32[256,512]{1,0:T(8,128)S(1)} %get-tuple-element.132.refs_0_, f32[256,512]{1,0:T(8,128)S(1)} %get-tuple-element.151.refs_1_, bf16[256,512]{1,0:T(8,128)(2,1)S(1)} %collective-permute-done.21.refs_2_, bf16[256,512]{1,0:T(8,128)(2,1)S(1)} %collective-permute-done.22.refs_3_), custom_call_target="tpu_custom_call" | custom-call | bytes 57344 | tf_op jit(solution)/shard_map/join/pallas_call | solution.py:31
  (48 shorter events, 19.8 us)
Async XLA Ops:
  1.9 30.5 %copy-start.1 = (bf16[1,1024,1344]{1,2,0:T(8,128)(2,1)S(1)}, bf16[1,1024,1344]{1,2,0:T(8,128)(2,1)}, u32[]{:S(2)}) copy-start(bf16[1,1024,1344]{1,2,0:T(8,128)(2,1)} %param.12) | copy-start | bytes 8257540
  1.9 17.1 %collective-permute-start.1 = (bf16[272,512]{1,0:T(8,128)(2,1)S(1)}, bf16[272,512]{1,0:T(8,128)(2,1)S(1)}, u32[]{:S(2)}, u32[]{:S(2)}) collective-permute-start(bf16[272,512]{1,0:T(8,128)(2,1)S(1)} %all_tokens.1), channel_id=1, source_target_pairs={{0,16},{8,24},{16,0},{24,8},{1,17},{9,25},{17,1},{25,9},{2,18},{10... | collective-permute-start | bytes 835592 | tf_op jit(solution)/shard_map/ppermute | solution.py:289
  7.8 11.2 %collective-permute-start = (bf16[192,512]{1,0:T(8,128)(2,1)S(1)}, bf16[192,512]{1,0:T(8,128)(2,1)S(1)}, u32[]{:S(2)}, u32[]{:S(2)}) collective-permute-start(bf16[192,512]{1,0:T(8,128)(2,1)S(1)} %get-tuple-element.84), channel_id=1, source_target_pairs={{0,8},{8,0},{16,24},{24,16},{1,9},{9,1},{17,25},{25,17},{2,10},{10... | collective-permute-start | bytes 589832 | tf_op jit(solution)/shard_map/ppermute | solution.py:289
  19.4 10.8 %collective-permute-start.5 = (bf16[192,512]{1,0:T(8,128)(2,1)S(1)}, bf16[192,512]{1,0:T(8,128)(2,1)S(1)}, u32[]{:S(2)}, u32[]{:S(2)}) collective-permute-start(bf16[192,512]{1,0:T(8,128)(2,1)S(1)} %get-tuple-element.92), channel_id=1, source_target_pairs={{0,8},{8,0},{16,24},{24,16},{1,9},{9,1},{17,25},{25,17},{2,10},{10... | collective-permute-start | bytes 589832 | tf_op jit(solution)/shard_map/ppermute | solution.py:289
  19.9 17.6 %collective-permute-start.2 = (bf16[192,512]{1,0:T(8,128)(2,1)S(1)}, bf16[192,512]{1,0:T(8,128)(2,1)S(1)}, u32[]{:S(2)}, u32[]{:S(2)}) collective-permute-start(bf16[192,512]{1,0:T(8,128)(2,1)S(1)} %get-tuple-element.93), channel_id=1, source_target_pairs={{0,16},{8,24},{16,0},{24,8},{1,17},{9,25},{17,1},{25,9},{2,18},{10... | collective-permute-start | bytes 589832 | tf_op jit(solution)/shard_map/ppermute | solution.py:289
  23.2 14.3 %collective-permute-start.3 = (bf16[192,512]{1,0:T(8,128)(2,1)S(1)}, bf16[192,512]{1,0:T(8,128)(2,1)S(1)}, u32[]{:S(2)}, u32[]{:S(2)}) collective-permute-start(bf16[192,512]{1,0:T(8,128)(2,1)S(1)} %get-tuple-element.94), channel_id=1, source_target_pairs={{0,24},{8,16},{16,8},{24,0},{1,25},{9,17},{17,9},{25,1},{2,26},{10... | collective-permute-start | bytes 589832 | tf_op jit(solution)/shard_map/ppermute | solution.py:289
  23.9 14.0 %collective-permute-start.4 = (bf16[192,512]{1,0:T(8,128)(2,1)S(1)}, bf16[192,512]{1,0:T(8,128)(2,1)S(1)}, u32[]{:S(2)}, u32[]{:S(2)}) collective-permute-start(bf16[192,512]{1,0:T(8,128)(2,1)S(1)} %get-tuple-element.95), channel_id=1, source_target_pairs={{0,8},{8,0},{16,24},{24,16},{1,9},{9,1},{17,25},{25,17},{2,10},{10... | collective-permute-start | bytes 589832 | tf_op jit(solution)/shard_map/ppermute | solution.py:289
  32.4 2.4 %copy-start = (bf16[1,1344,1024]{2,1,0:T(8,128)(2,1)S(1)}, bf16[1,1344,1024]{2,1,0:T(8,128)(2,1)}, u32[]{:S(2)}) copy-start(bf16[1,1344,1024]{2,1,0:T(8,128)(2,1)} %param.13) | copy-start | bytes 8257540
  37.9 1.4 %collective-permute-start.6 = (bf16[192,512]{1,0:T(8,128)(2,1)S(1)}, bf16[192,512]{1,0:T(8,128)(2,1)S(1)}, u32[]{:S(2)}, u32[]{:S(2)}) collective-permute-start(bf16[192,512]{1,0:T(8,128)(2,1)S(1)} %collective-permute-done.4.refs_1_), channel_id=1, source_target_pairs={{0,4},{4,0},{1,5},{5,1},{2,6},{6,2},{3,7},{7,3},{8,12},{12,8},{9,1... | collective-permute-start | bytes 589832 | tf_op jit(solution)/shard_map/ppermute | solution.py:289
  37.9 1.7 %collective-permute-start.7 = (bf16[192,512]{1,0:T(8,128)(2,1)S(1)}, bf16[192,512]{1,0:T(8,128)(2,1)S(1)}, u32[]{:S(2)}, u32[]{:S(2)}) collective-permute-start(bf16[192,512]{1,0:T(8,128)(2,1)S(1)} %collective-permute-done.2.refs_2_), channel_id=1, source_target_pairs={{0,4},{4,0},{1,5},{5,1},{2,6},{6,2},{3,7},{7,3},{8,12},{12,8},{9,1... | collective-permute-start | bytes 589832 | tf_op jit(solution)/shard_map/ppermute | solution.py:289
  38.4 1.5 %collective-permute-start.8 = (bf16[192,512]{1,0:T(8,128)(2,1)S(1)}, bf16[192,512]{1,0:T(8,128)(2,1)S(1)}, u32[]{:S(2)}, u32[]{:S(2)}) collective-permute-start(bf16[192,512]{1,0:T(8,128)(2,1)S(1)} %collective-permute-done.3.refs_3_), channel_id=1, source_target_pairs={{0,4},{4,0},{1,5},{5,1},{2,6},{6,2},{3,7},{7,3},{8,12},{12,8},{9,1... | collective-permute-start | bytes 589832 | tf_op jit(solution)/shard_map/ppermute | solution.py:289
  38.4 7.3 %collective-permute-start.9 = (bf16[768,512]{1,0:T(8,128)(2,1)S(1)}, bf16[768,512]{1,0:T(8,128)(2,1)S(1)}, u32[]{:S(2)}, u32[]{:S(2)}) collective-permute-start(bf16[768,512]{1,0:T(8,128)(2,1)S(1)} %get-tuple-element.110), channel_id=1, source_target_pairs={{0,4},{4,0},{1,5},{5,1},{2,6},{6,2},{3,7},{7,3},{8,12},{12,8},{9,1... | collective-permute-start | bytes 2359304 | tf_op jit(solution)/shard_map/ppermute | solution.py:289
  41.3 17.6 %collective-permute-start.17 = (bf16[1344,256]{1,0:T(8,128)(2,1)S(1)}, bf16[1344,256]{1,0:T(8,128)(2,1)S(1)}, u32[]{:S(2)}, u32[]{:S(2)}) collective-permute-start(bf16[1344,256]{1,0:T(8,128)(2,1)S(1)} %get-tuple-element.139), channel_id=1, source_target_pairs={{0,1},{1,0},{2,3},{3,2},{4,5},{5,4},{6,7},{7,6},{8,9},{9,8},{10,11... | collective-permute-start | bytes 2064392 | tf_op jit(solution)/shard_map/ppermute | solution.py:289
  42.8 17.3 %collective-permute-start.18 = (bf16[1344,256]{1,0:T(8,128)(2,1)S(1)}, bf16[1344,256]{1,0:T(8,128)(2,1)S(1)}, u32[]{:S(2)}, u32[]{:S(2)}) collective-permute-start(bf16[1344,256]{1,0:T(8,128)(2,1)S(1)} %get-tuple-element.140), channel_id=1, source_target_pairs={{0,2},{1,3},{2,0},{3,1},{4,6},{5,7},{6,4},{7,5},{8,10},{9,11},{10,... | collective-permute-start | bytes 2064392 | tf_op jit(solution)/shard_map/ppermute | solution.py:289
  45.9 19.1 %collective-permute-start.10 = (bf16[192,512]{1,0:T(8,128)(2,1)S(1)}, bf16[192,512]{1,0:T(8,128)(2,1)S(1)}, u32[]{:S(2)}, u32[]{:S(2)}) collective-permute-start(bf16[192,512]{1,0:T(8,128)(2,1)S(1)} %get-tuple-element.114), channel_id=1, source_target_pairs={{0,8},{8,0},{16,24},{24,16},{1,9},{9,1},{17,25},{25,17},{2,10},{10... | collective-permute-start | bytes 589832 | tf_op jit(solution)/shard_map/ppermute | solution.py:289
  49.4 17.2 %collective-permute-start.11 = (bf16[192,512]{1,0:T(8,128)(2,1)S(1)}, bf16[192,512]{1,0:T(8,128)(2,1)S(1)}, u32[]{:S(2)}, u32[]{:S(2)}) collective-permute-start(bf16[192,512]{1,0:T(8,128)(2,1)S(1)} %get-tuple-element.115), channel_id=1, source_target_pairs={{0,16},{8,24},{16,0},{24,8},{1,17},{9,25},{17,1},{25,9},{2,18},{10... | collective-permute-start | bytes 589832 | tf_op jit(solution)/shard_map/ppermute | solution.py:289
  50.8 15.8 %collective-permute-start.12 = (bf16[192,512]{1,0:T(8,128)(2,1)S(1)}, bf16[192,512]{1,0:T(8,128)(2,1)S(1)}, u32[]{:S(2)}, u32[]{:S(2)}) collective-permute-start(bf16[192,512]{1,0:T(8,128)(2,1)S(1)} %get-tuple-element.116), channel_id=1, source_target_pairs={{0,24},{8,16},{16,8},{24,0},{1,25},{9,17},{17,9},{25,1},{2,26},{10... | collective-permute-start | bytes 589832 | tf_op jit(solution)/shard_map/ppermute | solution.py:289
  60.4 23.9 %collective-permute-start.19 = (bf16[2016,256]{1,0:T(8,128)(2,1)S(1)}, bf16[2016,256]{1,0:T(8,128)(2,1)S(1)}, u32[]{:S(2)}, u32[]{:S(2)}) collective-permute-start(bf16[2016,256]{1,0:T(8,128)(2,1)S(1)} %get-tuple-element.143), channel_id=1, source_target_pairs={{0,1},{1,0},{2,3},{3,2},{4,5},{5,4},{6,7},{7,6},{8,9},{9,8},{10,11... | collective-permute-start | bytes 3096584 | tf_op jit(solution)/shard_map/ppermute | solution.py:289
  61.1 23.5 %collective-permute-start.20 = (bf16[2016,256]{1,0:T(8,128)(2,1)S(1)}, bf16[2016,256]{1,0:T(8,128)(2,1)S(1)}, u32[]{:S(2)}, u32[]{:S(2)}) collective-permute-start(bf16[2016,256]{1,0:T(8,128)(2,1)S(1)} %get-tuple-element.144), channel_id=1, source_target_pairs={{0,2},{1,3},{2,0},{3,1},{4,6},{5,7},{6,4},{7,5},{8,10},{9,11},{10,... | collective-permute-start | bytes 3096584 | tf_op jit(solution)/shard_map/ppermute | solution.py:289
  66.6 2.3 %collective-permute-start.13 = (bf16[768,512]{1,0:T(8,128)(2,1)S(1)}, bf16[768,512]{1,0:T(8,128)(2,1)S(1)}, u32[]{:S(2)}, u32[]{:S(2)}) collective-permute-start(bf16[768,512]{1,0:T(8,128)(2,1)S(1)} %get-tuple-element.134), channel_id=1, source_target_pairs={{0,4},{4,0},{1,5},{5,1},{2,6},{6,2},{3,7},{7,3},{8,12},{12,8},{9,1... | collective-permute-start | bytes 2359304 | tf_op jit(solution)/shard_map/ppermute | solution.py:289
  69.1 20.1 %collective-permute-start.14 = (bf16[192,512]{1,0:T(8,128)(2,1)S(1)}, bf16[192,512]{1,0:T(8,128)(2,1)S(1)}, u32[]{:S(2)}, u32[]{:S(2)}) collective-permute-start(bf16[192,512]{1,0:T(8,128)(2,1)S(1)} %get-tuple-element.136), channel_id=1, source_target_pairs={{0,8},{8,0},{16,24},{24,16},{1,9},{9,1},{17,25},{25,17},{2,10},{10... | collective-permute-start | bytes 589832 | tf_op jit(solution)/shard_map/ppermute | solution.py:289
  72.3 17.1 %collective-permute-start.15 = (bf16[192,512]{1,0:T(8,128)(2,1)S(1)}, bf16[192,512]{1,0:T(8,128)(2,1)S(1)}, u32[]{:S(2)}, u32[]{:S(2)}) collective-permute-start(bf16[192,512]{1,0:T(8,128)(2,1)S(1)} %get-tuple-element.137), channel_id=1, source_target_pairs={{0,16},{8,24},{16,0},{24,8},{1,17},{9,25},{17,1},{25,9},{2,18},{10... | collective-permute-start | bytes 589832 | tf_op jit(solution)/shard_map/ppermute | solution.py:289
  73.4 16.1 %collective-permute-start.16 = (bf16[192,512]{1,0:T(8,128)(2,1)S(1)}, bf16[192,512]{1,0:T(8,128)(2,1)S(1)}, u32[]{:S(2)}, u32[]{:S(2)}) collective-permute-start(bf16[192,512]{1,0:T(8,128)(2,1)S(1)} %get-tuple-element.138), channel_id=1, source_target_pairs={{0,24},{8,16},{16,8},{24,0},{1,25},{9,17},{17,9},{25,1},{2,26},{10... | collective-permute-start | bytes 589832 | tf_op jit(solution)/shard_map/ppermute | solution.py:289
  84.9 8.1 %collective-permute-start.23 = (bf16[672,256]{1,0:T(8,128)(2,1)S(1)}, bf16[672,256]{1,0:T(8,128)(2,1)S(1)}, u32[]{:S(2)}, u32[]{:S(2)}) collective-permute-start(bf16[672,256]{1,0:T(8,128)(2,1)S(1)} %get-tuple-element.160), channel_id=1, source_target_pairs={{0,2},{1,3},{2,0},{3,1},{4,6},{5,7},{6,4},{7,5},{8,10},{9,11},{10,... | collective-permute-start | bytes 1032200 | tf_op jit(solution)/shard_map/ppermute | solution.py:289
  86.5 7.6 %collective-permute-start.24 = (bf16[672,256]{1,0:T(8,128)(2,1)S(1)}, bf16[672,256]{1,0:T(8,128)(2,1)S(1)}, u32[]{:S(2)}, u32[]{:S(2)}) collective-permute-start(bf16[672,256]{1,0:T(8,128)(2,1)S(1)} %get-tuple-element.161), channel_id=1, source_target_pairs={{0,1},{1,0},{2,3},{3,2},{4,5},{5,4},{6,7},{7,6},{8,9},{9,8},{10,11... | collective-permute-start | bytes 1032200 | tf_op jit(solution)/shard_map/ppermute | solution.py:289
  89.2 1.5 %collective-permute-start.21 = (bf16[256,512]{1,0:T(8,128)(2,1)S(1)}, bf16[256,512]{1,0:T(8,128)(2,1)S(1)}, u32[]{:S(2)}, u32[]{:S(2)}) collective-permute-start(bf16[256,512]{1,0:T(8,128)(2,1)S(1)} %get-tuple-element.152), channel_id=1, source_target_pairs={{0,4},{4,0},{1,5},{5,1},{2,6},{6,2},{3,7},{7,3},{8,12},{12,8},{9,1... | collective-permute-start | bytes 786440 | tf_op jit(solution)/shard_map/ppermute | solution.py:289
  90.0 1.6 %collective-permute-start.22 = (bf16[256,512]{1,0:T(8,128)(2,1)S(1)}, bf16[256,512]{1,0:T(8,128)(2,1)S(1)}, u32[]{:S(2)}, u32[]{:S(2)}) collective-permute-start(bf16[256,512]{1,0:T(8,128)(2,1)S(1)} %get-tuple-element.153), channel_id=1, source_target_pairs={{0,4},{4,0},{1,5},{5,1},{2,6},{6,2},{3,7},{7,3},{8,12},{12,8},{9,1... | collective-permute-start | bytes 786440 | tf_op jit(solution)/shard_map/ppermute | solution.py:289

commit v8 on v7

--- a/solution.py
+++ b/solution.py
@@ -264,25 +264,44 @@
     return a.astype(F32) + b.astype(F32)
 
 
-def mix_body(kept0, kept1, came0, came1, inner0, inner1, send0, send1, own0, own1):
-    rows = own0.shape[0]
-    for kept, came, own, send, inner in ((kept0, came0, own0, send1, inner1), (kept1, came1, own1, send0, inner0)):
-        own[...] = added(kept[:rows, :], came[:rows, :]).astype(BF16)
-        send[:rows, :] = added(kept[rows:, :], came[rows:, :]).astype(BF16)
-        send[rows:, :] = inner[...]
-
-
-def inner_sum_body(kept0, kept1, mixed0, mixed1, move0, move1, own0, own1):
-    rows = own0.shape[0]
-    for kept, mixed, move, own in ((kept0, mixed0, move0, own0), (kept1, mixed1, move1, own1)):
-        own[...] = added(kept[:rows, :], mixed[rows : 2 * rows, :]).astype(BF16)
-        move[...] = added(kept[rows:, :], mixed[2 * rows :, :]).astype(BF16)
+def mix_body(kept, came, inner, send, own):
+    rows = own.shape[0]
+    own[...] = added(kept[:rows, :], came[:rows, :]).astype(BF16)
+    send[:rows, :] = added(kept[rows:, :], came[rows:, :]).astype(BF16)
+    send[rows:, :] = inner[...]
+
+
+def inner_sum_body(kept, mixed, move, own):
+    rows = own.shape[0]
+    own[...] = added(kept[:rows, :], mixed[rows : 2 * rows, :]).astype(BF16)
+    move[...] = added(kept[rows:, :], mixed[2 * rows :, :]).astype(BF16)
 
 
 def last_sum_body(own0, own1, came0, came1, out_ref):
     rows = own0.shape[0]
     out_ref[:rows, :] = added(own0[...], came0[:rows, :])
     out_ref[rows:, :] = added(own1[...], came1[:rows, :])
+
+
+def part_sum_body(own, came, *refs):
+    refs[-1][...] = added(own[...], came[...])
+
+
+def part_sum(part, own, came, total, filled=()):
+    whole = pl.BlockSpec(memory_space=pltpu.VMEM)
+    return pl.pallas_call(
+        part_sum_body,
+        grid=(1,),
+        out_shape=(pltpu.HBM(total.shape, total.dtype),),
+        in_specs=[whole] * 2 + [pl.BlockSpec(memory_space=pl.ANY)] * len(filled),
+        out_specs=(pl.BlockSpec(own.shape, lambda i: (part, 0)),),
+        input_output_aliases={2: 0} if filled else {},
+        compiler_params=pltpu.CompilerParams(vmem_limit_bytes=VMEM_BYTES),
+        name="inner_last",
+    )(
+        *[pltpu.with_memory_space_constraint(x, pltpu.VMEM) for x in (own, came)],
+        *[pltpu.with_memory_space_constraint(x, pltpu.HBM) for x in filled],
+    )
 
 
 def partner(x, axis, bit):
@@ -424,31 +443,41 @@
     d_act_late = after(d_act, outer_kept)
     turned, grad_give = given(d_act_late, inner, "grad_rows")
     grad_keep = kept(turned, inner, "grad_rows")
-    *sends, outer_own0, outer_own1 = local(
-        mix_body,
-        [shape(3 * part_rows, piece.shape[1])] * 2 + [quarter] * 2,
-        [*outer_kept, *outer_came, *inner_sent],
-        0,
-        "mix",
-    )
-    mixed = [partner(x, "dp", order[0]) for x, order in zip(sends, orders, strict=True)]
-    grad_give, returned = after((grad_give, returned))
+    sends, outer_own = zip(
+        *[
+            local(
+                mix_body,
+                [shape(3 * part_rows, piece.shape[1]), quarter],
+                [outer_kept[part], outer_came[part], inner_sent[1 - part]],
+                0,
+                "mix",
+            )
+            for part in range(2)
+        ],
+        strict=True,
+    )
+    mixed = [partner(x, "dp", order[0]) for x, order in zip(sends[::-1], orders, strict=True)]
+    grad_give, back = after((grad_give, far_first(returned[1:])))
+    returned = returned[:1] + near_first(back)
     grad_came = partner(grad_give, "cuts", 1)
     inner_kept = grads(staying, d_act, arrived, "inner_staying")
     chunks = split(grad_keep, grad_came)
     grad_returned = [chunks[0]] + over_experts(chunks[1:])
     wide, narrow = combine(returned, True)
-    mixed = after(mixed, wide)
-    move0, move1, inner_own0, inner_own1 = local(
-        inner_sum_body, [quarter] * 4, [*inner_kept, *mixed], 0, "inner_sum"
-    )
-    moved = [partner(x, "dp", order[1]) for x, order in zip((move0, move1), orders, strict=True)]
+    mixed = [after(x, wide) for x in mixed]
+    moving, inner_own = zip(
+        *[local(inner_sum_body, [quarter] * 2, list(x), 0, "inner_sum") for x in zip(inner_kept, mixed, strict=True)],
+        strict=True,
+    )
+    moved = [partner(x, "dp", order[1]) for x, order in zip(moving, orders, strict=True)]
     (grad_out,) = local(
-        last_sum_body, [total], [outer_own0, outer_own1, *mixed[::-1]], 0, "outer_last", gives=pltpu.HBM
-    )
-    (grad_in,) = local(last_sum_body, [total], [inner_own0, inner_own1, *moved], 0, "inner_last", gives=pltpu.HBM)
+        last_sum_body, [total], [*outer_own, *mixed[::-1]], 0, "outer_last", gives=pltpu.HBM
+    )
+    filled = part_sum(0, inner_own[0], moved[0], total)
+    (grad_in,) = part_sum(1, inner_own[1], moved[1], total, filled)
     came = partner(narrow, "cuts", 1)
-    grad_returned = after(grad_returned, grad_out)
+    back = after(far_first(grad_returned[1:]), grad_out)
+    grad_returned = grad_returned[:1] + near_first(back)
     grad_wide, narrow = combine(grad_returned, False)
     layer_out, d_tokens = local(
         join_body,

time: 96 us -> 95 us (0.990)
  waiting for transfers between devices: 26.9 us -> 24.3 us
    ppermute x25, waiting for transfers between devices: 26.9 us -> 24.3 us  [partner(): lax.ppermute(x, axis, [(i, i ^ bit) for i in range(lax.axis_size(axis))])]
    pallas_call x0 -> x2, Pallas kernels: none -> 1.83 us  [part_sum(): pl.pallas_call(part_sum_body, grid=(1,), out_shape=(pltpu.HBM(total.shape...]
    pallas_call x23 -> x24, Pallas kernels: 30 us -> 28.7 us  [local(): pl.pallas_call(body, out_shape=tuple((gives(x.shape, x.dtype) for x in ou...]
  transfers between devices with their start and end apart: 25 -> 25, of which waited for: 17 -> 16; matrix products, arithmetic and copies ran while one was open for 0% -> 0% of each run, Pallas kernels for 28% -> 30%
where the time goes in v8:
time: 95 us; the launch traced here: 94.3 us
  starting transfers between devices  32.2 us (34%)
  Pallas kernels  30.6 us (32%)
  waiting for transfers between devices  24.3 us (26%)
  blocking collectives  6.41 us (7%)
    ppermute x25, starting transfers between devices, partner(): lax.ppermute(x, axis, [(i, i ^ bit) for i in range(lax.axis_size(axis))])  32.2 us
    pallas_call x24, Pallas kernels, local(): pl.pallas_call(body, out_shape=tuple((gives(x.shape, x.dtype) for x in ou...  28.7 us
    ppermute x25, waiting for transfers between devices, partner(): lax.ppermute(x, axis, [(i, i ^ bit) for i in range(lax.axis_size(axis))])  24.3 us
    all_gather x3, blocking collectives, joined(): return [lax.all_gather(x, 'cuts', axis=1, tiled=True) for x in chunks]  6.41 us
  transfers between devices with their start and end apart: 25, of which 16 were waited for; matrix products, arithmetic and copies ran while one was open for 0% of the time, Pallas kernels for 30%

profile of v8, /device:TPU:0, one launch (start us, length us, event | category | flops | bytes accessed | tf_op | source)
XLA Modules:
  0.0 94.3 jit_solution(12016290266870961817)
XLA Ops:
  0.6 1.3 %all_tokens.1 = bf16[272,512]{1,0:T(8,128)(2,1)S(1)} custom-call(s32[2,256]{1,0:T(2,128)} %bitcast.19, f32[256,1024]{1,0:T(8,128)} %tokens_ref.3), custom_call_target="tpu_custom_call" | custom-call | bytes 20768 | tf_op jit(solution)/shard_map/all_tokens/pallas_call | solution.py:31
  1.9 4.1 %collective-permute-start.1 = (bf16[272,512]{1,0:T(8,128)(2,1)S(1)}, bf16[272,512]{1,0:T(8,128)(2,1)S(1)}, u32[]{:S(2)}, u32[]{:S(2)}) collective-permute-start(bf16[272,512]{1,0:T(8,128)(2,1)S(1)} %all_tokens.1), channel_id=1, source_target_pairs={{0,16},{8,24},{16,0},{24,8},{1,17},{9,25},{17,1},{25,9},{2,18},{10... | collective-permute-start | bytes 835592 | tf_op jit(solution)/shard_map/ppermute | solution.py:308
  6.0 1.7 %route.1 = (bf16[192,1024]{1,0:T(8,128)(2,1)S(1)}, bf16[192,512]{1,0:T(8,128)(2,1)S(1)}) custom-call(s32[2,256]{1,0:T(2,128)} %bitcast.20, f32[256,1024]{1,0:T(8,128)} %tokens_ref.3), custom_call_target="tpu_custom_call" | custom-call | flops 6291456 | bytes 25632 | tf_op jit(solution)/shard_map/route/pallas_call | solution.py:31
  7.8 1.6 %collective-permute-start = (bf16[192,512]{1,0:T(8,128)(2,1)S(1)}, bf16[192,512]{1,0:T(8,128)(2,1)S(1)}, u32[]{:S(2)}, u32[]{:S(2)}) collective-permute-start(bf16[192,512]{1,0:T(8,128)(2,1)S(1)} %get-tuple-element.83), channel_id=1, source_target_pairs={{0,8},{8,0},{16,24},{24,16},{1,9},{9,1},{17,25},{25,17},{2,10},{10... | collective-permute-start | bytes 589832 | tf_op jit(solution)/shard_map/ppermute | solution.py:308
  9.4 3.2 %weigh.1 = (f32[256,128]{1,0:T(8,128)S(1)}, bf16[192,1024]{1,0:T(8,128)(2,1)S(1)}, bf16[192,512]{1,0:T(8,128)(2,1)S(1)}, bf16[192,512]{1,0:T(8,128)(2,1)S(1)}, bf16[192,512]{1,0:T(8,128)(2,1)S(1)}) custom-call(s32[2,256]{1,0:T(2,128)} %bitcast.21, s32[2,256]{1,0:T(2,128)} %bitcast.22, f32[1,256]{1,0:T(1,128)} %bitcast.23, f32[256,1024]{1,0:T(8,128)} %cotangent_ref.1), custom_call_target="tpu_custom_call" | custom-call | flops 12582912 | bytes 33872 | tf_op jit(solution)/shard_map/weigh/pallas_call | solution.py:31
  12.6 6.4 %collective-permute-done = bf16[192,512]{1,0:T(8,128)(2,1)S(1)} collective-permute-done((bf16[192,512]{1,0:T(8,128)(2,1)S(1)}, bf16[192,512]{1,0:T(8,128)(2,1)S(1)}, u32[]{:S(2)}, u32[]{:S(2)}) %collective-permute-start) | collective-permute-done | bytes 196640 | tf_op jit(solution)/shard_map/ppermute | solution.py:308
  19.9 3.4 %collective-permute-start.3 = (bf16[192,512]{1,0:T(8,128)(2,1)S(1)}, bf16[192,512]{1,0:T(8,128)(2,1)S(1)}, u32[]{:S(2)}, u32[]{:S(2)}) collective-permute-start(bf16[192,512]{1,0:T(8,128)(2,1)S(1)} %get-tuple-element.96), channel_id=1, source_target_pairs={{0,16},{8,24},{16,0},{24,8},{1,17},{9,25},{17,1},{25,9},{2,18},{10... | collective-permute-start | bytes 589832 | tf_op jit(solution)/shard_map/ppermute | solution.py:308
  23.9 2.1 %all_gather.9.refs_1_ = bf16[192,1024]{1,0:T(8,128)(2,1)S(1)} all-gather(bf16[192,512]{1,0:T(8,128)(2,1)S(1)} %collective-permute-done), channel_id=1, replica_groups=mesh['expert'=4,'cuts'=2,'dp'=4] {'cuts'}, dimensions={1}, use_global_device_ids=true | all-gather | bytes 589824 | tf_op jit(solution)/shard_map/all_gather | solution.py:339
  26.0 2.1 %all_gather.10.refs_2_ = bf16[192,1024]{1,0:T(8,128)(2,1)S(1)} all-gather(bf16[192,512]{1,0:T(8,128)(2,1)S(1)} %get-tuple-element.89), channel_id=1, replica_groups=mesh['expert'=4,'cuts'=2,'dp'=4] {'cuts'}, dimensions={1}, use_global_device_ids=true | all-gather | bytes 589824 | tf_op jit(solution)/shard_map/all_gather | solution.py:339
  28.0 2.1 %collective-permute-done.2 = bf16[192,512]{1,0:T(8,128)(2,1)S(1)} collective-permute-done((bf16[192,512]{1,0:T(8,128)(2,1)S(1)}, bf16[192,512]{1,0:T(8,128)(2,1)S(1)}, u32[]{:S(2)}, u32[]{:S(2)}) %collective-permute-start.2) | collective-permute-done | bytes 196640 | tf_op jit(solution)/shard_map/ppermute | solution.py:308
  30.2 2.3 %all_gather.11.refs_3_ = bf16[192,1024]{1,0:T(8,128)(2,1)S(1)} all-gather(bf16[192,512]{1,0:T(8,128)(2,1)S(1)} %collective-permute-done.2), channel_id=1, replica_groups=mesh['expert'=4,'cuts'=2,'dp'=4] {'cuts'}, dimensions={1}, use_global_device_ids=true | all-gather | bytes 589824 | tf_op jit(solution)/shard_map/all_gather | solution.py:339
  32.4 2.3 %hidden.1 = (bf16[768,1024]{1,0:T(8,128)(2,1)S(1)}, bf16[1344,768]{1,0:T(8,128)(2,1)S(1)}, bf16[1344,768]{1,0:T(8,128)(2,1)S(1)}) custom-call(bf16[192,1024]{1,0:T(8,128)(2,1)S(1)} %get-tuple-element.82.refs_0_, bf16[192,1024]{1,0:T(8,128)(2,1)S(1)} %all_gather.9.refs_1_, bf16[192,1024]{1,0:T(8,128)(2,1)S(1)} %all_gather.10.refs_2_, ...), custom_call_target="tpu_custom_call" | custom-call | flops 33030144 | bytes 156672 | tf_op jit(solution)/shard_map/hidden/pallas_call | solution.py:31
  34.8 2.2 %rows_give.1 = (bf16[768,1344]{1,0:T(8,128)(2,1)S(1)}, bf16[768,512]{1,0:T(8,128)(2,1)S(1)}) custom-call(bf16[1344,768]{1,0:T(8,128)(2,1)S(1)} %get-tuple-element.120.units_ref.refs_7_, bf16[1344,1024]{1,0:T(8,128)(2,1)S(1)} %bitcast.11), custom_call_target="tpu_custom_call" | custom-call | flops 16515072 | bytes 119808 | tf_op jit(solution)/shard_map/rows_give/pallas_call | solution.py:31
  39.9 1.4 %outer_leaving.1 = (bf16[768,1024]{1,0:T(8,128)(2,1)S(1)}, bf16[1344,256]{1,0:T(8,128)(2,1)S(1)}, bf16[1344,256]{1,0:T(8,128)(2,1)S(1)}) custom-call(bf16[192,1024]{1,0:T(8,128)(2,1)S(1)} %get-tuple-element.102.refs_0_, bf16[192,512]{1,0:T(8,128)(2,1)S(1)} %collective-permute-done.5.refs_1_, bf16[192,512]{1,0:T(8,128)(2,1)S(1)} %collective-permute-done.3.refs_2_, ...), custom_call_target="tpu_custom_call" | custom-call | flops 16515072 | bytes 102912 | tf_op jit(solution)/shard_map/outer_leaving/pallas_call | solution.py:31
  41.3 1.5 %collective-permute-start.18 = (bf16[1344,256]{1,0:T(8,128)(2,1)S(1)}, bf16[1344,256]{1,0:T(8,128)(2,1)S(1)}, u32[]{:S(2)}, u32[]{:S(2)}) collective-permute-start(bf16[1344,256]{1,0:T(8,128)(2,1)S(1)} %get-tuple-element.138), channel_id=1, source_target_pairs={{0,2},{1,3},{2,0},{3,1},{4,6},{5,7},{6,4},{7,5},{8,10},{9,11},{10,... | collective-permute-start | bytes 2064392 | tf_op jit(solution)/shard_map/ppermute | solution.py:308
  42.8 1.5 %collective-permute-start.17 = (bf16[1344,256]{1,0:T(8,128)(2,1)S(1)}, bf16[1344,256]{1,0:T(8,128)(2,1)S(1)}, u32[]{:S(2)}, u32[]{:S(2)}) collective-permute-start(bf16[1344,256]{1,0:T(8,128)(2,1)S(1)} %get-tuple-element.136), channel_id=1, source_target_pairs={{0,1},{1,0},{2,3},{3,2},{4,5},{5,4},{6,7},{7,6},{8,9},{9,8},{10,11... | collective-permute-start | bytes 2064392 | tf_op jit(solution)/shard_map/ppermute | solution.py:308
  44.3 1.4 %rows_keep.1.keep_ref = bf16[768,512]{1,0:T(8,128)(2,1)S(1)} custom-call(bf16[768,1344]{1,0:T(8,128)(2,1)S(1)} %get-tuple-element.92.turned_ref, bf16[1344,1024]{1,0:T(8,128)(2,1)S(1)} %bitcast.12), custom_call_target="tpu_custom_call" | custom-call | flops 16515072 | bytes 87552 | tf_op jit(solution)/shard_map/rows_keep/pallas_call | solution.py:31
  45.9 3.6 %collective-permute-start.12 = (bf16[192,512]{1,0:T(8,128)(2,1)S(1)}, bf16[192,512]{1,0:T(8,128)(2,1)S(1)}, u32[]{:S(2)}, u32[]{:S(2)}) collective-permute-start(bf16[192,512]{1,0:T(8,128)(2,1)S(1)} %get-tuple-element.112), channel_id=1, source_target_pairs={{0,8},{8,0},{16,24},{24,16},{1,9},{9,1},{17,25},{25,17},{2,10},{10... | collective-permute-start | bytes 589832 | tf_op jit(solution)/shard_map/ppermute | solution.py:308
  49.4 1.4 %collective-permute-start.10 = (bf16[192,512]{1,0:T(8,128)(2,1)S(1)}, bf16[192,512]{1,0:T(8,128)(2,1)S(1)}, u32[]{:S(2)}, u32[]{:S(2)}) collective-permute-start(bf16[192,512]{1,0:T(8,128)(2,1)S(1)} %get-tuple-element.113), channel_id=1, source_target_pairs={{0,16},{8,24},{16,0},{24,8},{1,17},{9,25},{17,1},{25,9},{2,18},{10... | collective-permute-start | bytes 589832 | tf_op jit(solution)/shard_map/ppermute | solution.py:308
  51.9 2.3 %d_act.1.units_ref = bf16[1344,768]{1,0:T(8,128)(2,1)S(1)} custom-call(bf16[768,1024]{1,0:T(8,128)(2,1)S(1)} %get-tuple-element.121.g_ref.rows_ref, bf16[1344,768]{1,0:T(8,128)(2,1)S(1)} %get-tuple-element.116.positive_ref, bf16[1344,1024]{1,0:T(8,128)(2,1)S(1)} %bitcast.13), custom_call_target="tpu_custom_call" | custom-call | flops 33030144 | bytes 132096 | tf_op jit(solution)/shard_map/d_act/pallas_call | solution.py:31
  56.8 2.1 %collective-permute-done.18.came = bf16[1344,256]{1,0:T(8,128)(2,1)S(1)} collective-permute-done((bf16[1344,256]{1,0:T(8,128)(2,1)S(1)}, bf16[1344,256]{1,0:T(8,128)(2,1)S(1)}, u32[]{:S(2)}, u32[]{:S(2)}) %collective-permute-start.18) | collective-permute-done | bytes 688160 | tf_op jit(solution)/shard_map/ppermute | solution.py:308
  59.1 1.5 %collective-permute-start.20 = (bf16[2016,256]{1,0:T(8,128)(2,1)S(1)}, bf16[2016,256]{1,0:T(8,128)(2,1)S(1)}, u32[]{:S(2)}, u32[]{:S(2)}) collective-permute-start(bf16[2016,256]{1,0:T(8,128)(2,1)S(1)} %get-tuple-element.142), channel_id=1, source_target_pairs={{0,1},{1,0},{2,3},{3,2},{4,5},{5,4},{6,7},{7,6},{8,9},{9,8},{10,11... | collective-permute-start | bytes 3096584 | tf_op jit(solution)/shard_map/ppermute | solution.py:308
  60.8 1.6 %collective-permute-start.19 = (bf16[2016,256]{1,0:T(8,128)(2,1)S(1)}, bf16[2016,256]{1,0:T(8,128)(2,1)S(1)}, u32[]{:S(2)}, u32[]{:S(2)}) collective-permute-start(bf16[2016,256]{1,0:T(8,128)(2,1)S(1)} %get-tuple-element.140), channel_id=1, source_target_pairs={{0,2},{1,3},{2,0},{3,1},{4,6},{5,7},{6,4},{7,5},{8,10},{9,11},{10,... | collective-permute-start | bytes 3096584 | tf_op jit(solution)/shard_map/ppermute | solution.py:308
  62.4 2.4 %grad_rows_give.1 = (bf16[768,1344]{1,0:T(8,128)(2,1)S(1)}, bf16[768,512]{1,0:T(8,128)(2,1)S(1)}) custom-call(bf16[1344,768]{1,0:T(8,128)(2,1)S(1)} %d_act.1.units_ref, bf16[1344,1024]{1,0:T(8,128)(2,1)S(1)} %bitcast.15), custom_call_target="tpu_custom_call" | custom-call | flops 16515072 | bytes 119808 | tf_op jit(solution)/shard_map/grad_rows_give/pallas_call | solution.py:31
  64.8 1.8 %collective-permute-done.10.refs_2_ = bf16[192,512]{1,0:T(8,128)(2,1)S(1)} collective-permute-done((bf16[192,512]{1,0:T(8,128)(2,1)S(1)}, bf16[192,512]{1,0:T(8,128)(2,1)S(1)}, u32[]{:S(2)}, u32[]{:S(2)}) %collective-permute-start.10) | collective-permute-done | bytes 196640 | tf_op jit(solution)/shard_map/ppermute | solution.py:308
  66.6 1.4 %grad_rows_keep.1.keep_ref = bf16[768,512]{1,0:T(8,128)(2,1)S(1)} custom-call(bf16[768,1344]{1,0:T(8,128)(2,1)S(1)} %get-tuple-element.130.turned_ref, bf16[1344,1024]{1,0:T(8,128)(2,1)S(1)} %bitcast.16), custom_call_target="tpu_custom_call" | custom-call | flops 16515072 | bytes 87552 | tf_op jit(solution)/shard_map/grad_rows_keep/pallas_call | solution.py:31
  69.1 4.2 %collective-permute-start.14 = (bf16[192,512]{1,0:T(8,128)(2,1)S(1)}, bf16[192,512]{1,0:T(8,128)(2,1)S(1)}, u32[]{:S(2)}, u32[]{:S(2)}) collective-permute-start(bf16[192,512]{1,0:T(8,128)(2,1)S(1)} %get-tuple-element.133), channel_id=1, source_target_pairs={{0,16},{8,24},{16,0},{24,8},{1,17},{9,25},{17,1},{25,9},{2,18},{10... | collective-permute-start | bytes 589832 | tf_op jit(solution)/shard_map/ppermute | solution.py:308
  73.3 1.4 %collective-permute-start.15 = (bf16[192,512]{1,0:T(8,128)(2,1)S(1)}, bf16[192,512]{1,0:T(8,128)(2,1)S(1)}, u32[]{:S(2)}, u32[]{:S(2)}) collective-permute-start(bf16[192,512]{1,0:T(8,128)(2,1)S(1)} %get-tuple-element.134), channel_id=1, source_target_pairs={{0,24},{8,16},{16,8},{24,0},{1,25},{9,17},{17,9},{25,1},{2,26},{10... | collective-permute-start | bytes 589832 | tf_op jit(solution)/shard_map/ppermute | solution.py:308
  76.7 6.6 %collective-permute-done.20.came1.mixed = bf16[2016,256]{1,0:T(8,128)(2,1)S(1)} collective-permute-done((bf16[2016,256]{1,0:T(8,128)(2,1)S(1)}, bf16[2016,256]{1,0:T(8,128)(2,1)S(1)}, u32[]{:S(2)}, u32[]{:S(2)}) %collective-permute-start.20) | collective-permute-done | bytes 1032224 | tf_op jit(solution)/shard_map/ppermute | solution.py:308
  83.5 1.5 %collective-permute-start.24 = (bf16[672,256]{1,0:T(8,128)(2,1)S(1)}, bf16[672,256]{1,0:T(8,128)(2,1)S(1)}, u32[]{:S(2)}, u32[]{:S(2)}) collective-permute-start(bf16[672,256]{1,0:T(8,128)(2,1)S(1)} %get-tuple-element.157), channel_id=1, source_target_pairs={{0,2},{1,3},{2,0},{3,1},{4,6},{5,7},{6,4},{7,5},{8,10},{9,11},{10,... | collective-permute-start | bytes 1032200 | tf_op jit(solution)/shard_map/ppermute | solution.py:308
  85.1 1.6 %collective-permute-start.23 = (bf16[672,256]{1,0:T(8,128)(2,1)S(1)}, bf16[672,256]{1,0:T(8,128)(2,1)S(1)}, u32[]{:S(2)}, u32[]{:S(2)}) collective-permute-start(bf16[672,256]{1,0:T(8,128)(2,1)S(1)} %get-tuple-element.154), channel_id=1, source_target_pairs={{0,1},{1,0},{2,3},{3,2},{4,5},{5,4},{6,7},{7,6},{8,9},{9,8},{10,11... | collective-permute-start | bytes 1032200 | tf_op jit(solution)/shard_map/ppermute | solution.py:308
  90.4 1.5 %join.1 = (f32[256,1024]{1,0:T(8,128)}, f32[256,1024]{1,0:T(8,128)}) custom-call(f32[256,512]{1,0:T(8,128)S(1)} %get-tuple-element.129.refs_0_, f32[256,512]{1,0:T(8,128)S(1)} %get-tuple-element.147.refs_1_, bf16[256,512]{1,0:T(8,128)(2,1)S(1)} %collective-permute-done.21.refs_2_, bf16[256,512]{1,0:T(8,128)(2,1)S(1)} %collective-permute-done.22.refs_3_), custom_call_target="tpu_custom_call" | custom-call | bytes 57344 | tf_op jit(solution)/shard_map/join/pallas_call | solution.py:31
  (51 shorter events, 18.1 us)
Async XLA Ops:
  1.9 30.5 %copy-start.1 = (bf16[1,1024,1344]{1,2,0:T(8,128)(2,1)S(1)}, bf16[1,1024,1344]{1,2,0:T(8,128)(2,1)}, u32[]{:S(2)}) copy-start(bf16[1,1024,1344]{1,2,0:T(8,128)(2,1)} %param.12) | copy-start | bytes 8257540
  1.9 17.1 %collective-permute-start.1 = (bf16[272,512]{1,0:T(8,128)(2,1)S(1)}, bf16[272,512]{1,0:T(8,128)(2,1)S(1)}, u32[]{:S(2)}, u32[]{:S(2)}) collective-permute-start(bf16[272,512]{1,0:T(8,128)(2,1)S(1)} %all_tokens.1), channel_id=1, source_target_pairs={{0,16},{8,24},{16,0},{24,8},{1,17},{9,25},{17,1},{25,9},{2,18},{10... | collective-permute-start | bytes 835592 | tf_op jit(solution)/shard_map/ppermute | solution.py:308
  7.8 11.2 %collective-permute-start = (bf16[192,512]{1,0:T(8,128)(2,1)S(1)}, bf16[192,512]{1,0:T(8,128)(2,1)S(1)}, u32[]{:S(2)}, u32[]{:S(2)}) collective-permute-start(bf16[192,512]{1,0:T(8,128)(2,1)S(1)} %get-tuple-element.83), channel_id=1, source_target_pairs={{0,8},{8,0},{16,24},{24,16},{1,9},{9,1},{17,25},{25,17},{2,10},{10... | collective-permute-start | bytes 589832 | tf_op jit(solution)/shard_map/ppermute | solution.py:308
  19.4 10.8 %collective-permute-start.2 = (bf16[192,512]{1,0:T(8,128)(2,1)S(1)}, bf16[192,512]{1,0:T(8,128)(2,1)S(1)}, u32[]{:S(2)}, u32[]{:S(2)}) collective-permute-start(bf16[192,512]{1,0:T(8,128)(2,1)S(1)} %get-tuple-element.90), channel_id=1, source_target_pairs={{0,8},{8,0},{16,24},{24,16},{1,9},{9,1},{17,25},{25,17},{2,10},{10... | collective-permute-start | bytes 589832 | tf_op jit(solution)/shard_map/ppermute | solution.py:308
  19.9 17.6 %collective-permute-start.3 = (bf16[192,512]{1,0:T(8,128)(2,1)S(1)}, bf16[192,512]{1,0:T(8,128)(2,1)S(1)}, u32[]{:S(2)}, u32[]{:S(2)}) collective-permute-start(bf16[192,512]{1,0:T(8,128)(2,1)S(1)} %get-tuple-element.96), channel_id=1, source_target_pairs={{0,16},{8,24},{16,0},{24,8},{1,17},{9,25},{17,1},{25,9},{2,18},{10... | collective-permute-start | bytes 589832 | tf_op jit(solution)/shard_map/ppermute | solution.py:308
  23.2 14.3 %collective-permute-start.4 = (bf16[192,512]{1,0:T(8,128)(2,1)S(1)}, bf16[192,512]{1,0:T(8,128)(2,1)S(1)}, u32[]{:S(2)}, u32[]{:S(2)}) collective-permute-start(bf16[192,512]{1,0:T(8,128)(2,1)S(1)} %get-tuple-element.97), channel_id=1, source_target_pairs={{0,24},{8,16},{16,8},{24,0},{1,25},{9,17},{17,9},{25,1},{2,26},{10... | collective-permute-start | bytes 589832 | tf_op jit(solution)/shard_map/ppermute | solution.py:308
  23.9 14.0 %collective-permute-start.5 = (bf16[192,512]{1,0:T(8,128)(2,1)S(1)}, bf16[192,512]{1,0:T(8,128)(2,1)S(1)}, u32[]{:S(2)}, u32[]{:S(2)}) collective-permute-start(bf16[192,512]{1,0:T(8,128)(2,1)S(1)} %get-tuple-element.98), channel_id=1, source_target_pairs={{0,8},{8,0},{16,24},{24,16},{1,9},{9,1},{17,25},{25,17},{2,10},{10... | collective-permute-start | bytes 589832 | tf_op jit(solution)/shard_map/ppermute | solution.py:308
  32.4 2.4 %copy-start = (bf16[1,1344,1024]{2,1,0:T(8,128)(2,1)S(1)}, bf16[1,1344,1024]{2,1,0:T(8,128)(2,1)}, u32[]{:S(2)}) copy-start(bf16[1,1344,1024]{2,1,0:T(8,128)(2,1)} %param.13) | copy-start | bytes 8257540
  37.9 1.4 %collective-permute-start.7 = (bf16[192,512]{1,0:T(8,128)(2,1)S(1)}, bf16[192,512]{1,0:T(8,128)(2,1)S(1)}, u32[]{:S(2)}, u32[]{:S(2)}) collective-permute-start(bf16[192,512]{1,0:T(8,128)(2,1)S(1)} %collective-permute-done.5.refs_1_), channel_id=1, source_target_pairs={{0,4},{4,0},{1,5},{5,1},{2,6},{6,2},{3,7},{7,3},{8,12},{12,8},{9,1... | collective-permute-start | bytes 589832 | tf_op jit(solution)/shard_map/ppermute | solution.py:308
  37.9 1.7 %collective-permute-start.8 = (bf16[192,512]{1,0:T(8,128)(2,1)S(1)}, bf16[192,512]{1,0:T(8,128)(2,1)S(1)}, u32[]{:S(2)}, u32[]{:S(2)}) collective-permute-start(bf16[192,512]{1,0:T(8,128)(2,1)S(1)} %collective-permute-done.3.refs_2_), channel_id=1, source_target_pairs={{0,4},{4,0},{1,5},{5,1},{2,6},{6,2},{3,7},{7,3},{8,12},{12,8},{9,1... | collective-permute-start | bytes 589832 | tf_op jit(solution)/shard_map/ppermute | solution.py:308
  38.4 1.5 %collective-permute-start.9 = (bf16[192,512]{1,0:T(8,128)(2,1)S(1)}, bf16[192,512]{1,0:T(8,128)(2,1)S(1)}, u32[]{:S(2)}, u32[]{:S(2)}) collective-permute-start(bf16[192,512]{1,0:T(8,128)(2,1)S(1)} %collective-permute-done.4.refs_3_), channel_id=1, source_target_pairs={{0,4},{4,0},{1,5},{5,1},{2,6},{6,2},{3,7},{7,3},{8,12},{12,8},{9,1... | collective-permute-start | bytes 589832 | tf_op jit(solution)/shard_map/ppermute | solution.py:308
  38.4 7.3 %collective-permute-start.6 = (bf16[768,512]{1,0:T(8,128)(2,1)S(1)}, bf16[768,512]{1,0:T(8,128)(2,1)S(1)}, u32[]{:S(2)}, u32[]{:S(2)}) collective-permute-start(bf16[768,512]{1,0:T(8,128)(2,1)S(1)} %get-tuple-element.101), channel_id=1, source_target_pairs={{0,4},{4,0},{1,5},{5,1},{2,6},{6,2},{3,7},{7,3},{8,12},{12,8},{9,1... | collective-permute-start | bytes 2359304 | tf_op jit(solution)/shard_map/ppermute | solution.py:308
  41.3 17.6 %collective-permute-start.18 = (bf16[1344,256]{1,0:T(8,128)(2,1)S(1)}, bf16[1344,256]{1,0:T(8,128)(2,1)S(1)}, u32[]{:S(2)}, u32[]{:S(2)}) collective-permute-start(bf16[1344,256]{1,0:T(8,128)(2,1)S(1)} %get-tuple-element.138), channel_id=1, source_target_pairs={{0,2},{1,3},{2,0},{3,1},{4,6},{5,7},{6,4},{7,5},{8,10},{9,11},{10,... | collective-permute-start | bytes 2064392 | tf_op jit(solution)/shard_map/ppermute | solution.py:308
  42.8 17.8 %collective-permute-start.17 = (bf16[1344,256]{1,0:T(8,128)(2,1)S(1)}, bf16[1344,256]{1,0:T(8,128)(2,1)S(1)}, u32[]{:S(2)}, u32[]{:S(2)}) collective-permute-start(bf16[1344,256]{1,0:T(8,128)(2,1)S(1)} %get-tuple-element.136), channel_id=1, source_target_pairs={{0,1},{1,0},{2,3},{3,2},{4,5},{5,4},{6,7},{7,6},{8,9},{9,8},{10,11... | collective-permute-start | bytes 2064392 | tf_op jit(solution)/shard_map/ppermute | solution.py:308
  45.9 18.9 %collective-permute-start.12 = (bf16[192,512]{1,0:T(8,128)(2,1)S(1)}, bf16[192,512]{1,0:T(8,128)(2,1)S(1)}, u32[]{:S(2)}, u32[]{:S(2)}) collective-permute-start(bf16[192,512]{1,0:T(8,128)(2,1)S(1)} %get-tuple-element.112), channel_id=1, source_target_pairs={{0,8},{8,0},{16,24},{24,16},{1,9},{9,1},{17,25},{25,17},{2,10},{10... | collective-permute-start | bytes 589832 | tf_op jit(solution)/shard_map/ppermute | solution.py:308
  49.4 17.2 %collective-permute-start.10 = (bf16[192,512]{1,0:T(8,128)(2,1)S(1)}, bf16[192,512]{1,0:T(8,128)(2,1)S(1)}, u32[]{:S(2)}, u32[]{:S(2)}) collective-permute-start(bf16[192,512]{1,0:T(8,128)(2,1)S(1)} %get-tuple-element.113), channel_id=1, source_target_pairs={{0,16},{8,24},{16,0},{24,8},{1,17},{9,25},{17,1},{25,9},{2,18},{10... | collective-permute-start | bytes 589832 | tf_op jit(solution)/shard_map/ppermute | solution.py:308
  50.8 15.8 %collective-permute-start.11 = (bf16[192,512]{1,0:T(8,128)(2,1)S(1)}, bf16[192,512]{1,0:T(8,128)(2,1)S(1)}, u32[]{:S(2)}, u32[]{:S(2)}) collective-permute-start(bf16[192,512]{1,0:T(8,128)(2,1)S(1)} %get-tuple-element.114), channel_id=1, source_target_pairs={{0,24},{8,16},{16,8},{24,0},{1,25},{9,17},{17,9},{25,1},{2,26},{10... | collective-permute-start | bytes 589832 | tf_op jit(solution)/shard_map/ppermute | solution.py:308
  59.1 24.2 %collective-permute-start.20 = (bf16[2016,256]{1,0:T(8,128)(2,1)S(1)}, bf16[2016,256]{1,0:T(8,128)(2,1)S(1)}, u32[]{:S(2)}, u32[]{:S(2)}) collective-permute-start(bf16[2016,256]{1,0:T(8,128)(2,1)S(1)} %get-tuple-element.142), channel_id=1, source_target_pairs={{0,1},{1,0},{2,3},{3,2},{4,5},{5,4},{6,7},{7,6},{8,9},{9,8},{10,11... | collective-permute-start | bytes 3096584 | tf_op jit(solution)/shard_map/ppermute | solution.py:308
  60.8 24.2 %collective-permute-start.19 = (bf16[2016,256]{1,0:T(8,128)(2,1)S(1)}, bf16[2016,256]{1,0:T(8,128)(2,1)S(1)}, u32[]{:S(2)}, u32[]{:S(2)}) collective-permute-start(bf16[2016,256]{1,0:T(8,128)(2,1)S(1)} %get-tuple-element.140), channel_id=1, source_target_pairs={{0,2},{1,3},{2,0},{3,1},{4,6},{5,7},{6,4},{7,5},{8,10},{9,11},{10,... | collective-permute-start | bytes 3096584 | tf_op jit(solution)/shard_map/ppermute | solution.py:308
  66.6 2.3 %collective-permute-start.13 = (bf16[768,512]{1,0:T(8,128)(2,1)S(1)}, bf16[768,512]{1,0:T(8,128)(2,1)S(1)}, u32[]{:S(2)}, u32[]{:S(2)}) collective-permute-start(bf16[768,512]{1,0:T(8,128)(2,1)S(1)} %get-tuple-element.131), channel_id=1, source_target_pairs={{0,4},{4,0},{1,5},{5,1},{2,6},{6,2},{3,7},{7,3},{8,12},{12,8},{9,1... | collective-permute-start | bytes 2359304 | tf_op jit(solution)/shard_map/ppermute | solution.py:308
  69.1 18.8 %collective-permute-start.14 = (bf16[192,512]{1,0:T(8,128)(2,1)S(1)}, bf16[192,512]{1,0:T(8,128)(2,1)S(1)}, u32[]{:S(2)}, u32[]{:S(2)}) collective-permute-start(bf16[192,512]{1,0:T(8,128)(2,1)S(1)} %get-tuple-element.133), channel_id=1, source_target_pairs={{0,16},{8,24},{16,0},{24,8},{1,17},{9,25},{17,1},{25,9},{2,18},{10... | collective-permute-start | bytes 589832 | tf_op jit(solution)/shard_map/ppermute | solution.py:308
  73.3 14.6 %collective-permute-start.15 = (bf16[192,512]{1,0:T(8,128)(2,1)S(1)}, bf16[192,512]{1,0:T(8,128)(2,1)S(1)}, u32[]{:S(2)}, u32[]{:S(2)}) collective-permute-start(bf16[192,512]{1,0:T(8,128)(2,1)S(1)} %get-tuple-element.134), channel_id=1, source_target_pairs={{0,24},{8,16},{16,8},{24,0},{1,25},{9,17},{17,9},{25,1},{2,26},{10... | collective-permute-start | bytes 589832 | tf_op jit(solution)/shard_map/ppermute | solution.py:308
  74.7 13.6 %collective-permute-start.16 = (bf16[192,512]{1,0:T(8,128)(2,1)S(1)}, bf16[192,512]{1,0:T(8,128)(2,1)S(1)}, u32[]{:S(2)}, u32[]{:S(2)}) collective-permute-start(bf16[192,512]{1,0:T(8,128)(2,1)S(1)} %get-tuple-element.135), channel_id=1, source_target_pairs={{0,8},{8,0},{16,24},{24,16},{1,9},{9,1},{17,25},{25,17},{2,10},{10... | collective-permute-start | bytes 589832 | tf_op jit(solution)/shard_map/ppermute | solution.py:308
  83.5 8.6 %collective-permute-start.24 = (bf16[672,256]{1,0:T(8,128)(2,1)S(1)}, bf16[672,256]{1,0:T(8,128)(2,1)S(1)}, u32[]{:S(2)}, u32[]{:S(2)}) collective-permute-start(bf16[672,256]{1,0:T(8,128)(2,1)S(1)} %get-tuple-element.157), channel_id=1, source_target_pairs={{0,2},{1,3},{2,0},{3,1},{4,6},{5,7},{6,4},{7,5},{8,10},{9,11},{10,... | collective-permute-start | bytes 1032200 | tf_op jit(solution)/shard_map/ppermute | solution.py:308
  85.1 8.2 %collective-permute-start.23 = (bf16[672,256]{1,0:T(8,128)(2,1)S(1)}, bf16[672,256]{1,0:T(8,128)(2,1)S(1)}, u32[]{:S(2)}, u32[]{:S(2)}) collective-permute-start(bf16[672,256]{1,0:T(8,128)(2,1)S(1)} %get-tuple-element.154), channel_id=1, source_target_pairs={{0,1},{1,0},{2,3},{3,2},{4,5},{5,4},{6,7},{7,6},{8,9},{9,8},{10,11... | collective-permute-start | bytes 1032200 | tf_op jit(solution)/shard_map/ppermute | solution.py:308
  87.9 1.5 %collective-permute-start.21 = (bf16[256,512]{1,0:T(8,128)(2,1)S(1)}, bf16[256,512]{1,0:T(8,128)(2,1)S(1)}, u32[]{:S(2)}, u32[]{:S(2)}) collective-permute-start(bf16[256,512]{1,0:T(8,128)(2,1)S(1)} %get-tuple-element.148), channel_id=1, source_target_pairs={{0,4},{4,0},{1,5},{5,1},{2,6},{6,2},{3,7},{7,3},{8,12},{12,8},{9,1... | collective-permute-start | bytes 786440 | tf_op jit(solution)/shard_map/ppermute | solution.py:308
  88.8 1.6 %collective-permute-start.22 = (bf16[256,512]{1,0:T(8,128)(2,1)S(1)}, bf16[256,512]{1,0:T(8,128)(2,1)S(1)}, u32[]{:S(2)}, u32[]{:S(2)}) collective-permute-start(bf16[256,512]{1,0:T(8,128)(2,1)S(1)} %get-tuple-element.149), channel_id=1, source_target_pairs={{0,4},{4,0},{1,5},{5,1},{2,6},{6,2},{3,7},{7,3},{8,12},{12,8},{9,1... | collective-permute-start | bytes 786440 | tf_op jit(solution)/shard_map/ppermute | solution.py:308

commit v9 on v8

--- a/solution.py
+++ b/solution.py
@@ -92,14 +92,11 @@
     return mxu(chosen.astype(BF16), tokens).astype(BF16)
 
 
-def all_body(routes_ref, tokens_ref, all_ref):
-    top, count = routes_ref.shape
-    half = all_ref.shape[1]
-    line = lax.broadcasted_iota(jnp.int32, (ROW_TILE, count), 0)
-    lines = sum(jnp.where(line == k, routes_ref[k : k + 1, :], 0) for k in range(top))
-    all_ref[:count, :] = tokens_ref[:, window(lax.axis_index("cuts"), half)].astype(BF16)
-    all_ref[count:, :] = jnp.zeros((ROW_TILE, half), BF16)
-    all_ref[count:, :count] = lines.astype(F32).astype(BF16)
+def all_body(routes_ref, tokens_ref, all_ref, lines_ref):
+    line = lax.broadcasted_iota(jnp.int32, lines_ref.shape, 0)
+    lines = sum(jnp.where(line == k, routes_ref[k : k + 1, :], 0) for k in range(routes_ref.shape[0]))
+    lines_ref[...] = lines.astype(F32).astype(BF16)
+    all_ref[...] = tokens_ref[:, window(lax.axis_index("cuts"), all_ref.shape[1])].astype(BF16)
 
 
 def route_body(owners, routes_ref, tokens_ref, own_ref, *sends):
@@ -114,13 +111,12 @@
     own_ref[...] = rows_for(me, routes, rank, tokens_ref[...].astype(BF16), own_ref.shape[0])
 
 
-def pick_body(owners, top, all_ref, mine_ref, relay_ref):
+def pick_body(owners, top, all_ref, lines_ref, mine_ref, relay_ref):
     me = lax.axis_index("expert")
-    count = all_ref.shape[0] - ROW_TILE
-    lines = all_ref[count:, :count].astype(F32).astype(jnp.int32)
+    lines = lines_ref[...].astype(F32).astype(jnp.int32)
     routes = [lines[k : k + 1, :] for k in range(top)]
     rank = ranks(routes, owners)
-    tokens = all_ref[:count, :]
+    tokens = all_ref[...]
     relay_ref[...] = rows_for(me ^ 1, routes, rank, tokens, relay_ref.shape[0])
     mine_ref[...] = rows_for(me, routes, rank, tokens, mine_ref.shape[0])
 
@@ -374,8 +370,8 @@
     pairs = range(2, owners, 2) if relayed else ()
     chunk = shape(capacity, half)
     if relayed:
-        (everything,) = local(
-            all_body, [shape(count + ROW_TILE, half)], [routes.T, tokens], 0, "all_tokens", space=pltpu.HBM
+        everything, lines = local(
+            all_body, [shape(count, half), shape(ROW_TILE, count)], [routes.T, tokens], 0, "all_tokens", space=pltpu.HBM
         )
     own, *sends = local(
         functools.partial(route_body, owners),
@@ -387,6 +383,7 @@
     )
     dense = [partner(everything, "expert", s) for s in pairs]
     mine = over_experts(sends)
+    lines = [partner(lines, "expert", s) for s in pairs]
     meta, grad_own, *grad_sends = local(
         functools.partial(weigh_body, owners, capacity),
         [shape(count, 128, F32), shape(capacity, features)] + [shape(capacity, half)] * remote,
@@ -396,11 +393,11 @@
         space=pltpu.HBM,
     )
     nearest = [] if relayed else over_experts(grad_sends[:1])
-    mine, dense, nearest, grad_sends = after((mine, dense, nearest, grad_sends))
+    mine, dense, lines, nearest, grad_sends = after((mine, dense, lines, nearest, grad_sends))
     relays = []
-    for came in dense:
+    for came, named in zip(dense, lines, strict=True):
         picked, relay = local(
-            functools.partial(pick_body, owners, top), [chunk] * 2, [came], 4 * count * capacity * half, "pick"
+            functools.partial(pick_body, owners, top), [chunk] * 2, [came, named], 4 * count * capacity * half, "pick"
         )
         mine += [picked, partner(relay, "expert", 1)]
         relays.append(relay)

time: 95 us -> 94.6 us (level)
  waiting for transfers between devices: 24.3 us -> 23.3 us
    ppermute x25 -> x26, waiting for transfers between devices: 24.3 us -> 23.3 us  [partner(): lax.ppermute(x, axis, [(i, i ^ bit) for i in range(lax.axis_size(axis))])]
    ppermute x25 -> x26, starting transfers between devices: 32.2 us -> 33 us  [partner(): lax.ppermute(x, axis, [(i, i ^ bit) for i in range(lax.axis_size(axis))])]
  transfers between devices with their start and end apart: 25 -> 26, of which waited for: 16 -> 17; matrix products, arithmetic and copies ran while one was open for 0% -> 0% of each run, Pallas kernels for 30% -> 30%
where the time goes in v9:
time: 94.6 us; the launch traced here: 94.1 us
  starting transfers between devices  33 us (35%)
  Pallas kernels  30.6 us (32%)
  waiting for transfers between devices  23.3 us (25%)
  blocking collectives  6.41 us (7%)
    ppermute x26, starting transfers between devices, partner(): lax.ppermute(x, axis, [(i, i ^ bit) for i in range(lax.axis_size(axis))])  33 us
    pallas_call x24, Pallas kernels, local(): pl.pallas_call(body, out_shape=tuple((gives(x.shape, x.dtype) for x in ou...  28.7 us
    ppermute x26, waiting for transfers between devices, partner(): lax.ppermute(x, axis, [(i, i ^ bit) for i in range(lax.axis_size(axis))])  23.3 us
    all_gather x3, blocking collectives, joined(): return [lax.all_gather(x, 'cuts', axis=1, tiled=True) for x in chunks]  6.41 us
  transfers between devices with their start and end apart: 26, of which 17 were waited for; matrix products, arithmetic and copies ran while one was open for 0% of the time, Pallas kernels for 30%

profile of v9, /device:TPU:0, one launch (start us, length us, event | category | flops | bytes accessed | tf_op | source)
XLA Modules:
  0.0 94.1 jit_solution(17793471797400053815)
XLA Ops:
  0.6 1.3 %all_tokens.1 = (bf16[256,512]{1,0:T(8,128)(2,1)S(1)}, bf16[16,256]{1,0:T(8,128)(2,1)S(1)}) custom-call(s32[2,256]{1,0:T(2,128)} %bitcast.19, f32[256,1024]{1,0:T(8,128)} %tokens_ref.3), custom_call_target="tpu_custom_call" | custom-call | bytes 20640 | tf_op jit(solution)/shard_map/all_tokens/pallas_call | solution.py:31
  1.9 4.1 %collective-permute-start.1 = (bf16[256,512]{1,0:T(8,128)(2,1)S(1)}, bf16[256,512]{1,0:T(8,128)(2,1)S(1)}, u32[]{:S(2)}, u32[]{:S(2)}) collective-permute-start(bf16[256,512]{1,0:T(8,128)(2,1)S(1)} %get-tuple-element.87), channel_id=1, source_target_pairs={{0,16},{8,24},{16,0},{24,8},{1,17},{9,25},{17,1},{25,9},{2,18},{10... | collective-permute-start | bytes 786440 | tf_op jit(solution)/shard_map/ppermute | solution.py:304
  6.0 1.7 %route.1 = (bf16[192,1024]{1,0:T(8,128)(2,1)S(1)}, bf16[192,512]{1,0:T(8,128)(2,1)S(1)}) custom-call(s32[2,256]{1,0:T(2,128)} %bitcast.20, f32[256,1024]{1,0:T(8,128)} %tokens_ref.3), custom_call_target="tpu_custom_call" | custom-call | flops 6291456 | bytes 25632 | tf_op jit(solution)/shard_map/route/pallas_call | solution.py:31
  7.8 1.6 %collective-permute-start = (bf16[192,512]{1,0:T(8,128)(2,1)S(1)}, bf16[192,512]{1,0:T(8,128)(2,1)S(1)}, u32[]{:S(2)}, u32[]{:S(2)}) collective-permute-start(bf16[192,512]{1,0:T(8,128)(2,1)S(1)} %get-tuple-element.86), channel_id=1, source_target_pairs={{0,8},{8,0},{16,24},{24,16},{1,9},{9,1},{17,25},{25,17},{2,10},{10... | collective-permute-start | bytes 589832 | tf_op jit(solution)/shard_map/ppermute | solution.py:304
  9.9 3.2 %weigh.1 = (f32[256,128]{1,0:T(8,128)S(1)}, bf16[192,1024]{1,0:T(8,128)(2,1)S(1)}, bf16[192,512]{1,0:T(8,128)(2,1)S(1)}, bf16[192,512]{1,0:T(8,128)(2,1)S(1)}, bf16[192,512]{1,0:T(8,128)(2,1)S(1)}) custom-call(s32[2,256]{1,0:T(2,128)} %bitcast.21, s32[2,256]{1,0:T(2,128)} %bitcast.22, f32[1,256]{1,0:T(1,128)} %bitcast.23, f32[256,1024]{1,0:T(8,128)} %cotangent_ref.1), custom_call_target="tpu_custom_call" | custom-call | flops 12582912 | bytes 33872 | tf_op jit(solution)/shard_map/weigh/pallas_call | solution.py:31
  13.1 5.3 %collective-permute-done.2.lines_ref = bf16[16,256]{1,0:T(8,128)(2,1)S(1)} collective-permute-done((bf16[16,256]{1,0:T(8,128)(2,1)S(1)}, bf16[16,256]{1,0:T(8,128)(2,1)S(1)}, u32[]{:S(2)}, u32[]{:S(2)}) %collective-permute-start.2) | collective-permute-done | bytes 8224 | tf_op jit(solution)/shard_map/ppermute | solution.py:304
  19.5 3.4 %collective-permute-start.4 = (bf16[192,512]{1,0:T(8,128)(2,1)S(1)}, bf16[192,512]{1,0:T(8,128)(2,1)S(1)}, u32[]{:S(2)}, u32[]{:S(2)}) collective-permute-start(bf16[192,512]{1,0:T(8,128)(2,1)S(1)} %get-tuple-element.102), channel_id=1, source_target_pairs={{0,16},{8,24},{16,0},{24,8},{1,17},{9,25},{17,1},{25,9},{2,18},{10... | collective-permute-start | bytes 589832 | tf_op jit(solution)/shard_map/ppermute | solution.py:304
  23.7 2.1 %all_gather.9.refs_1_ = bf16[192,1024]{1,0:T(8,128)(2,1)S(1)} all-gather(bf16[192,512]{1,0:T(8,128)(2,1)S(1)} %collective-permute-done), channel_id=1, replica_groups=mesh['expert'=4,'cuts'=2,'dp'=4] {'cuts'}, dimensions={1}, use_global_device_ids=true | all-gather | bytes 589824 | tf_op jit(solution)/shard_map/all_gather | solution.py:335
  25.8 2.1 %all_gather.10.refs_2_ = bf16[192,1024]{1,0:T(8,128)(2,1)S(1)} all-gather(bf16[192,512]{1,0:T(8,128)(2,1)S(1)} %get-tuple-element.95), channel_id=1, replica_groups=mesh['expert'=4,'cuts'=2,'dp'=4] {'cuts'}, dimensions={1}, use_global_device_ids=true | all-gather | bytes 589824 | tf_op jit(solution)/shard_map/all_gather | solution.py:335
  27.9 2.1 %collective-permute-done.3 = bf16[192,512]{1,0:T(8,128)(2,1)S(1)} collective-permute-done((bf16[192,512]{1,0:T(8,128)(2,1)S(1)}, bf16[192,512]{1,0:T(8,128)(2,1)S(1)}, u32[]{:S(2)}, u32[]{:S(2)}) %collective-permute-start.3) | collective-permute-done | bytes 196640 | tf_op jit(solution)/shard_map/ppermute | solution.py:304
  29.9 2.3 %all_gather.11.refs_3_ = bf16[192,1024]{1,0:T(8,128)(2,1)S(1)} all-gather(bf16[192,512]{1,0:T(8,128)(2,1)S(1)} %collective-permute-done.3), channel_id=1, replica_groups=mesh['expert'=4,'cuts'=2,'dp'=4] {'cuts'}, dimensions={1}, use_global_device_ids=true | all-gather | bytes 589824 | tf_op jit(solution)/shard_map/all_gather | solution.py:335
  32.2 2.3 %hidden.1 = (bf16[768,1024]{1,0:T(8,128)(2,1)S(1)}, bf16[1344,768]{1,0:T(8,128)(2,1)S(1)}, bf16[1344,768]{1,0:T(8,128)(2,1)S(1)}) custom-call(bf16[192,1024]{1,0:T(8,128)(2,1)S(1)} %get-tuple-element.85.refs_0_, bf16[192,1024]{1,0:T(8,128)(2,1)S(1)} %all_gather.9.refs_1_, bf16[192,1024]{1,0:T(8,128)(2,1)S(1)} %all_gather.10.refs_2_, ...), custom_call_target="tpu_custom_call" | custom-call | flops 33030144 | bytes 156672 | tf_op jit(solution)/shard_map/hidden/pallas_call | solution.py:31
  34.6 2.2 %rows_give.1 = (bf16[768,1344]{1,0:T(8,128)(2,1)S(1)}, bf16[768,512]{1,0:T(8,128)(2,1)S(1)}) custom-call(bf16[1344,768]{1,0:T(8,128)(2,1)S(1)} %get-tuple-element.126.units_ref.refs_7_, bf16[1344,1024]{1,0:T(8,128)(2,1)S(1)} %bitcast.11), custom_call_target="tpu_custom_call" | custom-call | flops 16515072 | bytes 119808 | tf_op jit(solution)/shard_map/rows_give/pallas_call | solution.py:31
  39.6 1.4 %outer_leaving.1 = (bf16[768,1024]{1,0:T(8,128)(2,1)S(1)}, bf16[1344,256]{1,0:T(8,128)(2,1)S(1)}, bf16[1344,256]{1,0:T(8,128)(2,1)S(1)}) custom-call(bf16[192,1024]{1,0:T(8,128)(2,1)S(1)} %get-tuple-element.108.refs_0_, bf16[192,512]{1,0:T(8,128)(2,1)S(1)} %collective-permute-done.6.refs_1_, bf16[192,512]{1,0:T(8,128)(2,1)S(1)} %collective-permute-done.4.refs_2_, ...), custom_call_target="tpu_custom_call" | custom-call | flops 16515072 | bytes 102912 | tf_op jit(solution)/shard_map/outer_leaving/pallas_call | solution.py:31
  41.0 1.6 %collective-permute-start.19 = (bf16[1344,256]{1,0:T(8,128)(2,1)S(1)}, bf16[1344,256]{1,0:T(8,128)(2,1)S(1)}, u32[]{:S(2)}, u32[]{:S(2)}) collective-permute-start(bf16[1344,256]{1,0:T(8,128)(2,1)S(1)} %get-tuple-element.144), channel_id=1, source_target_pairs={{0,2},{1,3},{2,0},{3,1},{4,6},{5,7},{6,4},{7,5},{8,10},{9,11},{10,... | collective-permute-start | bytes 2064392 | tf_op jit(solution)/shard_map/ppermute | solution.py:304
  42.6 1.5 %collective-permute-start.18 = (bf16[1344,256]{1,0:T(8,128)(2,1)S(1)}, bf16[1344,256]{1,0:T(8,128)(2,1)S(1)}, u32[]{:S(2)}, u32[]{:S(2)}) collective-permute-start(bf16[1344,256]{1,0:T(8,128)(2,1)S(1)} %get-tuple-element.142), channel_id=1, source_target_pairs={{0,1},{1,0},{2,3},{3,2},{4,5},{5,4},{6,7},{7,6},{8,9},{9,8},{10,11... | collective-permute-start | bytes 2064392 | tf_op jit(solution)/shard_map/ppermute | solution.py:304
  44.1 1.4 %rows_keep.1.keep_ref = bf16[768,512]{1,0:T(8,128)(2,1)S(1)} custom-call(bf16[768,1344]{1,0:T(8,128)(2,1)S(1)} %get-tuple-element.98.turned_ref, bf16[1344,1024]{1,0:T(8,128)(2,1)S(1)} %bitcast.12), custom_call_target="tpu_custom_call" | custom-call | flops 16515072 | bytes 87552 | tf_op jit(solution)/shard_map/rows_keep/pallas_call | solution.py:31
  45.7 3.4 %collective-permute-start.13 = (bf16[192,512]{1,0:T(8,128)(2,1)S(1)}, bf16[192,512]{1,0:T(8,128)(2,1)S(1)}, u32[]{:S(2)}, u32[]{:S(2)}) collective-permute-start(bf16[192,512]{1,0:T(8,128)(2,1)S(1)} %get-tuple-element.118), channel_id=1, source_target_pairs={{0,8},{8,0},{16,24},{24,16},{1,9},{9,1},{17,25},{25,17},{2,10},{10... | collective-permute-start | bytes 589832 | tf_op jit(solution)/shard_map/ppermute | solution.py:304
  49.1 1.4 %collective-permute-start.11 = (bf16[192,512]{1,0:T(8,128)(2,1)S(1)}, bf16[192,512]{1,0:T(8,128)(2,1)S(1)}, u32[]{:S(2)}, u32[]{:S(2)}) collective-permute-start(bf16[192,512]{1,0:T(8,128)(2,1)S(1)} %get-tuple-element.119), channel_id=1, source_target_pairs={{0,16},{8,24},{16,0},{24,8},{1,17},{9,25},{17,1},{25,9},{2,18},{10... | collective-permute-start | bytes 589832 | tf_op jit(solution)/shard_map/ppermute | solution.py:304
  51.6 2.3 %d_act.1.units_ref = bf16[1344,768]{1,0:T(8,128)(2,1)S(1)} custom-call(bf16[768,1024]{1,0:T(8,128)(2,1)S(1)} %get-tuple-element.127.g_ref.rows_ref, bf16[1344,768]{1,0:T(8,128)(2,1)S(1)} %get-tuple-element.122.positive_ref, bf16[1344,1024]{1,0:T(8,128)(2,1)S(1)} %bitcast.13), custom_call_target="tpu_custom_call" | custom-call | flops 33030144 | bytes 132096 | tf_op jit(solution)/shard_map/d_act/pallas_call | solution.py:31
  56.4 2.2 %collective-permute-done.19.came = bf16[1344,256]{1,0:T(8,128)(2,1)S(1)} collective-permute-done((bf16[1344,256]{1,0:T(8,128)(2,1)S(1)}, bf16[1344,256]{1,0:T(8,128)(2,1)S(1)}, u32[]{:S(2)}, u32[]{:S(2)}) %collective-permute-start.19) | collective-permute-done | bytes 688160 | tf_op jit(solution)/shard_map/ppermute | solution.py:304
  58.8 1.6 %collective-permute-start.21 = (bf16[2016,256]{1,0:T(8,128)(2,1)S(1)}, bf16[2016,256]{1,0:T(8,128)(2,1)S(1)}, u32[]{:S(2)}, u32[]{:S(2)}) collective-permute-start(bf16[2016,256]{1,0:T(8,128)(2,1)S(1)} %get-tuple-element.148), channel_id=1, source_target_pairs={{0,1},{1,0},{2,3},{3,2},{4,5},{5,4},{6,7},{7,6},{8,9},{9,8},{10,11... | collective-permute-start | bytes 3096584 | tf_op jit(solution)/shard_map/ppermute | solution.py:304
  60.6 1.6 %collective-permute-start.20 = (bf16[2016,256]{1,0:T(8,128)(2,1)S(1)}, bf16[2016,256]{1,0:T(8,128)(2,1)S(1)}, u32[]{:S(2)}, u32[]{:S(2)}) collective-permute-start(bf16[2016,256]{1,0:T(8,128)(2,1)S(1)} %get-tuple-element.146), channel_id=1, source_target_pairs={{0,2},{1,3},{2,0},{3,1},{4,6},{5,7},{6,4},{7,5},{8,10},{9,11},{10,... | collective-permute-start | bytes 3096584 | tf_op jit(solution)/shard_map/ppermute | solution.py:304
  62.2 2.4 %grad_rows_give.1 = (bf16[768,1344]{1,0:T(8,128)(2,1)S(1)}, bf16[768,512]{1,0:T(8,128)(2,1)S(1)}) custom-call(bf16[1344,768]{1,0:T(8,128)(2,1)S(1)} %d_act.1.units_ref, bf16[1344,1024]{1,0:T(8,128)(2,1)S(1)} %bitcast.15), custom_call_target="tpu_custom_call" | custom-call | flops 16515072 | bytes 119808 | tf_op jit(solution)/shard_map/grad_rows_give/pallas_call | solution.py:31
  64.6 1.7 %collective-permute-done.11.refs_2_ = bf16[192,512]{1,0:T(8,128)(2,1)S(1)} collective-permute-done((bf16[192,512]{1,0:T(8,128)(2,1)S(1)}, bf16[192,512]{1,0:T(8,128)(2,1)S(1)}, u32[]{:S(2)}, u32[]{:S(2)}) %collective-permute-start.11) | collective-permute-done | bytes 196640 | tf_op jit(solution)/shard_map/ppermute | solution.py:304
  66.3 1.4 %grad_rows_keep.1.keep_ref = bf16[768,512]{1,0:T(8,128)(2,1)S(1)} custom-call(bf16[768,1344]{1,0:T(8,128)(2,1)S(1)} %get-tuple-element.136.turned_ref, bf16[1344,1024]{1,0:T(8,128)(2,1)S(1)} %bitcast.16), custom_call_target="tpu_custom_call" | custom-call | flops 16515072 | bytes 87552 | tf_op jit(solution)/shard_map/grad_rows_keep/pallas_call | solution.py:31
  68.7 4.2 %collective-permute-start.15 = (bf16[192,512]{1,0:T(8,128)(2,1)S(1)}, bf16[192,512]{1,0:T(8,128)(2,1)S(1)}, u32[]{:S(2)}, u32[]{:S(2)}) collective-permute-start(bf16[192,512]{1,0:T(8,128)(2,1)S(1)} %get-tuple-element.139), channel_id=1, source_target_pairs={{0,16},{8,24},{16,0},{24,8},{1,17},{9,25},{17,1},{25,9},{2,18},{10... | collective-permute-start | bytes 589832 | tf_op jit(solution)/shard_map/ppermute | solution.py:304
  73.0 1.4 %collective-permute-start.16 = (bf16[192,512]{1,0:T(8,128)(2,1)S(1)}, bf16[192,512]{1,0:T(8,128)(2,1)S(1)}, u32[]{:S(2)}, u32[]{:S(2)}) collective-permute-start(bf16[192,512]{1,0:T(8,128)(2,1)S(1)} %get-tuple-element.140), channel_id=1, source_target_pairs={{0,24},{8,16},{16,8},{24,0},{1,25},{9,17},{17,9},{25,1},{2,26},{10... | collective-permute-start | bytes 589832 | tf_op jit(solution)/shard_map/ppermute | solution.py:304
  76.4 6.6 %collective-permute-done.21.came1.mixed = bf16[2016,256]{1,0:T(8,128)(2,1)S(1)} collective-permute-done((bf16[2016,256]{1,0:T(8,128)(2,1)S(1)}, bf16[2016,256]{1,0:T(8,128)(2,1)S(1)}, u32[]{:S(2)}, u32[]{:S(2)}) %collective-permute-start.21) | collective-permute-done | bytes 1032224 | tf_op jit(solution)/shard_map/ppermute | solution.py:304
  83.2 1.6 %collective-permute-start.25 = (bf16[672,256]{1,0:T(8,128)(2,1)S(1)}, bf16[672,256]{1,0:T(8,128)(2,1)S(1)}, u32[]{:S(2)}, u32[]{:S(2)}) collective-permute-start(bf16[672,256]{1,0:T(8,128)(2,1)S(1)} %get-tuple-element.163), channel_id=1, source_target_pairs={{0,2},{1,3},{2,0},{3,1},{4,6},{5,7},{6,4},{7,5},{8,10},{9,11},{10,... | collective-permute-start | bytes 1032200 | tf_op jit(solution)/shard_map/ppermute | solution.py:304
  85.0 1.6 %collective-permute-start.24 = (bf16[672,256]{1,0:T(8,128)(2,1)S(1)}, bf16[672,256]{1,0:T(8,128)(2,1)S(1)}, u32[]{:S(2)}, u32[]{:S(2)}) collective-permute-start(bf16[672,256]{1,0:T(8,128)(2,1)S(1)} %get-tuple-element.160), channel_id=1, source_target_pairs={{0,1},{1,0},{2,3},{3,2},{4,5},{5,4},{6,7},{7,6},{8,9},{9,8},{10,11... | collective-permute-start | bytes 1032200 | tf_op jit(solution)/shard_map/ppermute | solution.py:304
  90.1 1.5 %join.1 = (f32[256,1024]{1,0:T(8,128)}, f32[256,1024]{1,0:T(8,128)}) custom-call(f32[256,512]{1,0:T(8,128)S(1)} %get-tuple-element.135.refs_0_, f32[256,512]{1,0:T(8,128)S(1)} %get-tuple-element.153.refs_1_, bf16[256,512]{1,0:T(8,128)(2,1)S(1)} %collective-permute-done.22.refs_2_, bf16[256,512]{1,0:T(8,128)(2,1)S(1)} %collective-permute-done.23.refs_3_), custom_call_target="tpu_custom_call" | custom-call | bytes 57344 | tf_op jit(solution)/shard_map/join/pallas_call | solution.py:31
  (53 shorter events, 19.0 us)
Async XLA Ops:
  1.9 30.3 %copy-start.1 = (bf16[1,1024,1344]{1,2,0:T(8,128)(2,1)S(1)}, bf16[1,1024,1344]{1,2,0:T(8,128)(2,1)}, u32[]{:S(2)}) copy-start(bf16[1,1024,1344]{1,2,0:T(8,128)(2,1)} %param.12) | copy-start | bytes 8257540
  1.9 16.9 %collective-permute-start.1 = (bf16[256,512]{1,0:T(8,128)(2,1)S(1)}, bf16[256,512]{1,0:T(8,128)(2,1)S(1)}, u32[]{:S(2)}, u32[]{:S(2)}) collective-permute-start(bf16[256,512]{1,0:T(8,128)(2,1)S(1)} %get-tuple-element.87), channel_id=1, source_target_pairs={{0,16},{8,24},{16,0},{24,8},{1,17},{9,25},{17,1},{25,9},{2,18},{10... | collective-permute-start | bytes 786440 | tf_op jit(solution)/shard_map/ppermute | solution.py:304
  7.8 11.1 %collective-permute-start = (bf16[192,512]{1,0:T(8,128)(2,1)S(1)}, bf16[192,512]{1,0:T(8,128)(2,1)S(1)}, u32[]{:S(2)}, u32[]{:S(2)}) collective-permute-start(bf16[192,512]{1,0:T(8,128)(2,1)S(1)} %get-tuple-element.86), channel_id=1, source_target_pairs={{0,8},{8,0},{16,24},{24,16},{1,9},{9,1},{17,25},{25,17},{2,10},{10... | collective-permute-start | bytes 589832 | tf_op jit(solution)/shard_map/ppermute | solution.py:304
  9.4 9.0 %collective-permute-start.2 = (bf16[16,256]{1,0:T(8,128)(2,1)S(1)}, bf16[16,256]{1,0:T(8,128)(2,1)S(1)}, u32[]{:S(2)}, u32[]{:S(2)}) collective-permute-start(bf16[16,256]{1,0:T(8,128)(2,1)S(1)} %get-tuple-element.88), channel_id=1, source_target_pairs={{0,16},{8,24},{16,0},{24,8},{1,17},{9,25},{17,1},{25,9},{2,18},{10... | collective-permute-start | bytes 24584 | tf_op jit(solution)/shard_map/ppermute | solution.py:304
  19.3 10.7 %collective-permute-start.3 = (bf16[192,512]{1,0:T(8,128)(2,1)S(1)}, bf16[192,512]{1,0:T(8,128)(2,1)S(1)}, u32[]{:S(2)}, u32[]{:S(2)}) collective-permute-start(bf16[192,512]{1,0:T(8,128)(2,1)S(1)} %get-tuple-element.96), channel_id=1, source_target_pairs={{0,8},{8,0},{16,24},{24,16},{1,9},{9,1},{17,25},{25,17},{2,10},{10... | collective-permute-start | bytes 589832 | tf_op jit(solution)/shard_map/ppermute | solution.py:304
  19.5 17.6 %collective-permute-start.4 = (bf16[192,512]{1,0:T(8,128)(2,1)S(1)}, bf16[192,512]{1,0:T(8,128)(2,1)S(1)}, u32[]{:S(2)}, u32[]{:S(2)}) collective-permute-start(bf16[192,512]{1,0:T(8,128)(2,1)S(1)} %get-tuple-element.102), channel_id=1, source_target_pairs={{0,16},{8,24},{16,0},{24,8},{1,17},{9,25},{17,1},{25,9},{2,18},{10... | collective-permute-start | bytes 589832 | tf_op jit(solution)/shard_map/ppermute | solution.py:304
  22.9 14.3 %collective-permute-start.5 = (bf16[192,512]{1,0:T(8,128)(2,1)S(1)}, bf16[192,512]{1,0:T(8,128)(2,1)S(1)}, u32[]{:S(2)}, u32[]{:S(2)}) collective-permute-start(bf16[192,512]{1,0:T(8,128)(2,1)S(1)} %get-tuple-element.103), channel_id=1, source_target_pairs={{0,24},{8,16},{16,8},{24,0},{1,25},{9,17},{17,9},{25,1},{2,26},{10... | collective-permute-start | bytes 589832 | tf_op jit(solution)/shard_map/ppermute | solution.py:304
  23.7 13.9 %collective-permute-start.6 = (bf16[192,512]{1,0:T(8,128)(2,1)S(1)}, bf16[192,512]{1,0:T(8,128)(2,1)S(1)}, u32[]{:S(2)}, u32[]{:S(2)}) collective-permute-start(bf16[192,512]{1,0:T(8,128)(2,1)S(1)} %get-tuple-element.104), channel_id=1, source_target_pairs={{0,8},{8,0},{16,24},{24,16},{1,9},{9,1},{17,25},{25,17},{2,10},{10... | collective-permute-start | bytes 589832 | tf_op jit(solution)/shard_map/ppermute | solution.py:304
  32.2 2.4 %copy-start = (bf16[1,1344,1024]{2,1,0:T(8,128)(2,1)S(1)}, bf16[1,1344,1024]{2,1,0:T(8,128)(2,1)}, u32[]{:S(2)}) copy-start(bf16[1,1344,1024]{2,1,0:T(8,128)(2,1)} %param.13) | copy-start | bytes 8257540
  37.6 1.4 %collective-permute-start.8 = (bf16[192,512]{1,0:T(8,128)(2,1)S(1)}, bf16[192,512]{1,0:T(8,128)(2,1)S(1)}, u32[]{:S(2)}, u32[]{:S(2)}) collective-permute-start(bf16[192,512]{1,0:T(8,128)(2,1)S(1)} %collective-permute-done.6.refs_1_), channel_id=1, source_target_pairs={{0,4},{4,0},{1,5},{5,1},{2,6},{6,2},{3,7},{7,3},{8,12},{12,8},{9,1... | collective-permute-start | bytes 589832 | tf_op jit(solution)/shard_map/ppermute | solution.py:304
  37.6 1.7 %collective-permute-start.9 = (bf16[192,512]{1,0:T(8,128)(2,1)S(1)}, bf16[192,512]{1,0:T(8,128)(2,1)S(1)}, u32[]{:S(2)}, u32[]{:S(2)}) collective-permute-start(bf16[192,512]{1,0:T(8,128)(2,1)S(1)} %collective-permute-done.4.refs_2_), channel_id=1, source_target_pairs={{0,4},{4,0},{1,5},{5,1},{2,6},{6,2},{3,7},{7,3},{8,12},{12,8},{9,1... | collective-permute-start | bytes 589832 | tf_op jit(solution)/shard_map/ppermute | solution.py:304
  38.1 1.5 %collective-permute-start.10 = (bf16[192,512]{1,0:T(8,128)(2,1)S(1)}, bf16[192,512]{1,0:T(8,128)(2,1)S(1)}, u32[]{:S(2)}, u32[]{:S(2)}) collective-permute-start(bf16[192,512]{1,0:T(8,128)(2,1)S(1)} %collective-permute-done.5.refs_3_), channel_id=1, source_target_pairs={{0,4},{4,0},{1,5},{5,1},{2,6},{6,2},{3,7},{7,3},{8,12},{12,8},{9,1... | collective-permute-start | bytes 589832 | tf_op jit(solution)/shard_map/ppermute | solution.py:304
  38.1 7.4 %collective-permute-start.7 = (bf16[768,512]{1,0:T(8,128)(2,1)S(1)}, bf16[768,512]{1,0:T(8,128)(2,1)S(1)}, u32[]{:S(2)}, u32[]{:S(2)}) collective-permute-start(bf16[768,512]{1,0:T(8,128)(2,1)S(1)} %get-tuple-element.107), channel_id=1, source_target_pairs={{0,4},{4,0},{1,5},{5,1},{2,6},{6,2},{3,7},{7,3},{8,12},{12,8},{9,1... | collective-permute-start | bytes 2359304 | tf_op jit(solution)/shard_map/ppermute | solution.py:304
  41.0 17.6 %collective-permute-start.19 = (bf16[1344,256]{1,0:T(8,128)(2,1)S(1)}, bf16[1344,256]{1,0:T(8,128)(2,1)S(1)}, u32[]{:S(2)}, u32[]{:S(2)}) collective-permute-start(bf16[1344,256]{1,0:T(8,128)(2,1)S(1)} %get-tuple-element.144), channel_id=1, source_target_pairs={{0,2},{1,3},{2,0},{3,1},{4,6},{5,7},{6,4},{7,5},{8,10},{9,11},{10,... | collective-permute-start | bytes 2064392 | tf_op jit(solution)/shard_map/ppermute | solution.py:304
  42.6 17.8 %collective-permute-start.18 = (bf16[1344,256]{1,0:T(8,128)(2,1)S(1)}, bf16[1344,256]{1,0:T(8,128)(2,1)S(1)}, u32[]{:S(2)}, u32[]{:S(2)}) collective-permute-start(bf16[1344,256]{1,0:T(8,128)(2,1)S(1)} %get-tuple-element.142), channel_id=1, source_target_pairs={{0,1},{1,0},{2,3},{3,2},{4,5},{5,4},{6,7},{7,6},{8,9},{9,8},{10,11... | collective-permute-start | bytes 2064392 | tf_op jit(solution)/shard_map/ppermute | solution.py:304
  45.7 18.9 %collective-permute-start.13 = (bf16[192,512]{1,0:T(8,128)(2,1)S(1)}, bf16[192,512]{1,0:T(8,128)(2,1)S(1)}, u32[]{:S(2)}, u32[]{:S(2)}) collective-permute-start(bf16[192,512]{1,0:T(8,128)(2,1)S(1)} %get-tuple-element.118), channel_id=1, source_target_pairs={{0,8},{8,0},{16,24},{24,16},{1,9},{9,1},{17,25},{25,17},{2,10},{10... | collective-permute-start | bytes 589832 | tf_op jit(solution)/shard_map/ppermute | solution.py:304
  49.1 17.2 %collective-permute-start.11 = (bf16[192,512]{1,0:T(8,128)(2,1)S(1)}, bf16[192,512]{1,0:T(8,128)(2,1)S(1)}, u32[]{:S(2)}, u32[]{:S(2)}) collective-permute-start(bf16[192,512]{1,0:T(8,128)(2,1)S(1)} %get-tuple-element.119), channel_id=1, source_target_pairs={{0,16},{8,24},{16,0},{24,8},{1,17},{9,25},{17,1},{25,9},{2,18},{10... | collective-permute-start | bytes 589832 | tf_op jit(solution)/shard_map/ppermute | solution.py:304
  50.5 15.8 %collective-permute-start.12 = (bf16[192,512]{1,0:T(8,128)(2,1)S(1)}, bf16[192,512]{1,0:T(8,128)(2,1)S(1)}, u32[]{:S(2)}, u32[]{:S(2)}) collective-permute-start(bf16[192,512]{1,0:T(8,128)(2,1)S(1)} %get-tuple-element.120), channel_id=1, source_target_pairs={{0,24},{8,16},{16,8},{24,0},{1,25},{9,17},{17,9},{25,1},{2,26},{10... | collective-permute-start | bytes 589832 | tf_op jit(solution)/shard_map/ppermute | solution.py:304
  58.8 24.2 %collective-permute-start.21 = (bf16[2016,256]{1,0:T(8,128)(2,1)S(1)}, bf16[2016,256]{1,0:T(8,128)(2,1)S(1)}, u32[]{:S(2)}, u32[]{:S(2)}) collective-permute-start(bf16[2016,256]{1,0:T(8,128)(2,1)S(1)} %get-tuple-element.148), channel_id=1, source_target_pairs={{0,1},{1,0},{2,3},{3,2},{4,5},{5,4},{6,7},{7,6},{8,9},{9,8},{10,11... | collective-permute-start | bytes 3096584 | tf_op jit(solution)/shard_map/ppermute | solution.py:304
  60.6 24.2 %collective-permute-start.20 = (bf16[2016,256]{1,0:T(8,128)(2,1)S(1)}, bf16[2016,256]{1,0:T(8,128)(2,1)S(1)}, u32[]{:S(2)}, u32[]{:S(2)}) collective-permute-start(bf16[2016,256]{1,0:T(8,128)(2,1)S(1)} %get-tuple-element.146), channel_id=1, source_target_pairs={{0,2},{1,3},{2,0},{3,1},{4,6},{5,7},{6,4},{7,5},{8,10},{9,11},{10,... | collective-permute-start | bytes 3096584 | tf_op jit(solution)/shard_map/ppermute | solution.py:304
  66.3 2.3 %collective-permute-start.14 = (bf16[768,512]{1,0:T(8,128)(2,1)S(1)}, bf16[768,512]{1,0:T(8,128)(2,1)S(1)}, u32[]{:S(2)}, u32[]{:S(2)}) collective-permute-start(bf16[768,512]{1,0:T(8,128)(2,1)S(1)} %get-tuple-element.137), channel_id=1, source_target_pairs={{0,4},{4,0},{1,5},{5,1},{2,6},{6,2},{3,7},{7,3},{8,12},{12,8},{9,1... | collective-permute-start | bytes 2359304 | tf_op jit(solution)/shard_map/ppermute | solution.py:304
  68.7 19.0 %collective-permute-start.15 = (bf16[192,512]{1,0:T(8,128)(2,1)S(1)}, bf16[192,512]{1,0:T(8,128)(2,1)S(1)}, u32[]{:S(2)}, u32[]{:S(2)}) collective-permute-start(bf16[192,512]{1,0:T(8,128)(2,1)S(1)} %get-tuple-element.139), channel_id=1, source_target_pairs={{0,16},{8,24},{16,0},{24,8},{1,17},{9,25},{17,1},{25,9},{2,18},{10... | collective-permute-start | bytes 589832 | tf_op jit(solution)/shard_map/ppermute | solution.py:304
  73.0 14.8 %collective-permute-start.16 = (bf16[192,512]{1,0:T(8,128)(2,1)S(1)}, bf16[192,512]{1,0:T(8,128)(2,1)S(1)}, u32[]{:S(2)}, u32[]{:S(2)}) collective-permute-start(bf16[192,512]{1,0:T(8,128)(2,1)S(1)} %get-tuple-element.140), channel_id=1, source_target_pairs={{0,24},{8,16},{16,8},{24,0},{1,25},{9,17},{17,9},{25,1},{2,26},{10... | collective-permute-start | bytes 589832 | tf_op jit(solution)/shard_map/ppermute | solution.py:304
  74.4 13.6 %collective-permute-start.17 = (bf16[192,512]{1,0:T(8,128)(2,1)S(1)}, bf16[192,512]{1,0:T(8,128)(2,1)S(1)}, u32[]{:S(2)}, u32[]{:S(2)}) collective-permute-start(bf16[192,512]{1,0:T(8,128)(2,1)S(1)} %get-tuple-element.141), channel_id=1, source_target_pairs={{0,8},{8,0},{16,24},{24,16},{1,9},{9,1},{17,25},{25,17},{2,10},{10... | collective-permute-start | bytes 589832 | tf_op jit(solution)/shard_map/ppermute | solution.py:304
  83.2 8.7 %collective-permute-start.25 = (bf16[672,256]{1,0:T(8,128)(2,1)S(1)}, bf16[672,256]{1,0:T(8,128)(2,1)S(1)}, u32[]{:S(2)}, u32[]{:S(2)}) collective-permute-start(bf16[672,256]{1,0:T(8,128)(2,1)S(1)} %get-tuple-element.163), channel_id=1, source_target_pairs={{0,2},{1,3},{2,0},{3,1},{4,6},{5,7},{6,4},{7,5},{8,10},{9,11},{10,... | collective-permute-start | bytes 1032200 | tf_op jit(solution)/shard_map/ppermute | solution.py:304
  85.0 8.2 %collective-permute-start.24 = (bf16[672,256]{1,0:T(8,128)(2,1)S(1)}, bf16[672,256]{1,0:T(8,128)(2,1)S(1)}, u32[]{:S(2)}, u32[]{:S(2)}) collective-permute-start(bf16[672,256]{1,0:T(8,128)(2,1)S(1)} %get-tuple-element.160), channel_id=1, source_target_pairs={{0,1},{1,0},{2,3},{3,2},{4,5},{5,4},{6,7},{7,6},{8,9},{9,8},{10,11... | collective-permute-start | bytes 1032200 | tf_op jit(solution)/shard_map/ppermute | solution.py:304
  87.7 1.5 %collective-permute-start.22 = (bf16[256,512]{1,0:T(8,128)(2,1)S(1)}, bf16[256,512]{1,0:T(8,128)(2,1)S(1)}, u32[]{:S(2)}, u32[]{:S(2)}) collective-permute-start(bf16[256,512]{1,0:T(8,128)(2,1)S(1)} %get-tuple-element.154), channel_id=1, source_target_pairs={{0,4},{4,0},{1,5},{5,1},{2,6},{6,2},{3,7},{7,3},{8,12},{12,8},{9,1... | collective-permute-start | bytes 786440 | tf_op jit(solution)/shard_map/ppermute | solution.py:304
  88.5 1.6 %collective-permute-start.23 = (bf16[256,512]{1,0:T(8,128)(2,1)S(1)}, bf16[256,512]{1,0:T(8,128)(2,1)S(1)}, u32[]{:S(2)}, u32[]{:S(2)}) collective-permute-start(bf16[256,512]{1,0:T(8,128)(2,1)S(1)} %get-tuple-element.155), channel_id=1, source_target_pairs={{0,4},{4,0},{1,5},{5,1},{2,6},{6,2},{3,7},{7,3},{8,12},{12,8},{9,1... | collective-permute-start | bytes 786440 | tf_op jit(solution)/shard_map/ppermute | solution.py:304

commit v10 on v9

--- a/solution.py
+++ b/solution.py
@@ -340,6 +340,9 @@
     def far_first(chunks):
         return chunks[1:] + chunks[:1]
 
+    def far_started(chunks):
+        return near_first([partner(x, "expert", s) for s, x in far_first(list(enumerate(chunks, 1)))])
+
     def near_first(chunks):
         return chunks[-1:] + chunks[:-1]
 
@@ -429,7 +432,7 @@
     outer_came = [partner(x, "dp", order[0]) for x, order in zip(outer_sent, orders, strict=True)]
     keep, came = after((keep, came), grad_rows)
     chunks = split(keep, came)
-    returned = [chunks[0]] + over_experts(chunks[1:])
+    returned = [chunks[0]] + far_started(chunks[1:])
     grad_rows, positive = after((grad_rows, positive), chunks)
     (d_act,) = local(
         d_act_body, [shape(units, slots)], [grad_rows, positive, outer], work, "d_act"
@@ -454,7 +457,7 @@
         strict=True,
     )
     mixed = [partner(x, "dp", order[0]) for x, order in zip(sends[::-1], orders, strict=True)]
-    grad_give, back = after((grad_give, far_first(returned[1:])))
+    back, grad_give = after((far_first(returned[1:]), grad_give))
     returned = returned[:1] + near_first(back)
     grad_came = partner(grad_give, "cuts", 1)
     inner_kept = grads(staying, d_act, arrived, "inner_staying")

time: 94.6 us -> 94.6 us (level)
  transfers between devices with their start and end apart: 26 -> 26, of which waited for: 17 -> 15; matrix products, arithmetic and copies ran while one was open for 0% -> 0% of each run, Pallas kernels for 30% -> 30%
where the time goes in v10:
time: 94.6 us; the launch traced here: 94.1 us
  starting transfers between devices  33.4 us (35%)
  Pallas kernels  30.6 us (32%)
  waiting for transfers between devices  22.8 us (24%)
  blocking collectives  6.41 us (7%)
    ppermute x26, starting transfers between devices, partner(): lax.ppermute(x, axis, [(i, i ^ bit) for i in range(lax.axis_size(axis))])  33.4 us
    pallas_call x24, Pallas kernels, local(): pl.pallas_call(body, out_shape=tuple((gives(x.shape, x.dtype) for x in ou...  28.8 us
    ppermute x26, waiting for transfers between devices, partner(): lax.ppermute(x, axis, [(i, i ^ bit) for i in range(lax.axis_size(axis))])  22.8 us
    all_gather x3, blocking collectives, joined(): return [lax.all_gather(x, 'cuts', axis=1, tiled=True) for x in chunks]  6.41 us
  transfers between devices with their start and end apart: 26, of which 15 were waited for; matrix products, arithmetic and copies ran while one was open for 0% of the time, Pallas kernels for 30%

profile of v10, /device:TPU:0, one launch (start us, length us, event | category | flops | bytes accessed | tf_op | source)
XLA Modules:
  0.0 94.1 jit_solution(14177959300330888014)
XLA Ops:
  0.6 1.3 %all_tokens.1 = (bf16[256,512]{1,0:T(8,128)(2,1)S(1)}, bf16[16,256]{1,0:T(8,128)(2,1)S(1)}) custom-call(s32[2,256]{1,0:T(2,128)} %bitcast.19, f32[256,1024]{1,0:T(8,128)} %tokens_ref.3), custom_call_target="tpu_custom_call" | custom-call | bytes 20640 | tf_op jit(solution)/shard_map/all_tokens/pallas_call | solution.py:31
  1.9 4.1 %collective-permute-start.1 = (bf16[256,512]{1,0:T(8,128)(2,1)S(1)}, bf16[256,512]{1,0:T(8,128)(2,1)S(1)}, u32[]{:S(2)}, u32[]{:S(2)}) collective-permute-start(bf16[256,512]{1,0:T(8,128)(2,1)S(1)} %get-tuple-element.87), channel_id=1, source_target_pairs={{0,16},{8,24},{16,0},{24,8},{1,17},{9,25},{17,1},{25,9},{2,18},{10... | collective-permute-start | bytes 786440 | tf_op jit(solution)/shard_map/ppermute | solution.py:304
  6.0 1.7 %route.1 = (bf16[192,1024]{1,0:T(8,128)(2,1)S(1)}, bf16[192,512]{1,0:T(8,128)(2,1)S(1)}) custom-call(s32[2,256]{1,0:T(2,128)} %bitcast.20, f32[256,1024]{1,0:T(8,128)} %tokens_ref.3), custom_call_target="tpu_custom_call" | custom-call | flops 6291456 | bytes 25632 | tf_op jit(solution)/shard_map/route/pallas_call | solution.py:31
  7.8 1.6 %collective-permute-start = (bf16[192,512]{1,0:T(8,128)(2,1)S(1)}, bf16[192,512]{1,0:T(8,128)(2,1)S(1)}, u32[]{:S(2)}, u32[]{:S(2)}) collective-permute-start(bf16[192,512]{1,0:T(8,128)(2,1)S(1)} %get-tuple-element.86), channel_id=1, source_target_pairs={{0,8},{8,0},{16,24},{24,16},{1,9},{9,1},{17,25},{25,17},{2,10},{10... | collective-permute-start | bytes 589832 | tf_op jit(solution)/shard_map/ppermute | solution.py:304
  9.9 3.2 %weigh.1 = (f32[256,128]{1,0:T(8,128)S(1)}, bf16[192,1024]{1,0:T(8,128)(2,1)S(1)}, bf16[192,512]{1,0:T(8,128)(2,1)S(1)}, bf16[192,512]{1,0:T(8,128)(2,1)S(1)}, bf16[192,512]{1,0:T(8,128)(2,1)S(1)}) custom-call(s32[2,256]{1,0:T(2,128)} %bitcast.21, s32[2,256]{1,0:T(2,128)} %bitcast.22, f32[1,256]{1,0:T(1,128)} %bitcast.23, f32[256,1024]{1,0:T(8,128)} %cotangent_ref.1), custom_call_target="tpu_custom_call" | custom-call | flops 12582912 | bytes 33872 | tf_op jit(solution)/shard_map/weigh/pallas_call | solution.py:31
  13.1 5.3 %collective-permute-done.2.lines_ref = bf16[16,256]{1,0:T(8,128)(2,1)S(1)} collective-permute-done((bf16[16,256]{1,0:T(8,128)(2,1)S(1)}, bf16[16,256]{1,0:T(8,128)(2,1)S(1)}, u32[]{:S(2)}, u32[]{:S(2)}) %collective-permute-start.2) | collective-permute-done | bytes 8224 | tf_op jit(solution)/shard_map/ppermute | solution.py:304
  19.5 3.4 %collective-permute-start.4 = (bf16[192,512]{1,0:T(8,128)(2,1)S(1)}, bf16[192,512]{1,0:T(8,128)(2,1)S(1)}, u32[]{:S(2)}, u32[]{:S(2)}) collective-permute-start(bf16[192,512]{1,0:T(8,128)(2,1)S(1)} %get-tuple-element.102), channel_id=1, source_target_pairs={{0,16},{8,24},{16,0},{24,8},{1,17},{9,25},{17,1},{25,9},{2,18},{10... | collective-permute-start | bytes 589832 | tf_op jit(solution)/shard_map/ppermute | solution.py:304
  23.7 2.1 %all_gather.9.refs_1_ = bf16[192,1024]{1,0:T(8,128)(2,1)S(1)} all-gather(bf16[192,512]{1,0:T(8,128)(2,1)S(1)} %collective-permute-done), channel_id=1, replica_groups=mesh['expert'=4,'cuts'=2,'dp'=4] {'cuts'}, dimensions={1}, use_global_device_ids=true | all-gather | bytes 589824 | tf_op jit(solution)/shard_map/all_gather | solution.py:335
  25.8 2.1 %all_gather.10.refs_2_ = bf16[192,1024]{1,0:T(8,128)(2,1)S(1)} all-gather(bf16[192,512]{1,0:T(8,128)(2,1)S(1)} %get-tuple-element.95), channel_id=1, replica_groups=mesh['expert'=4,'cuts'=2,'dp'=4] {'cuts'}, dimensions={1}, use_global_device_ids=true | all-gather | bytes 589824 | tf_op jit(solution)/shard_map/all_gather | solution.py:335
  27.9 2.1 %collective-permute-done.3 = bf16[192,512]{1,0:T(8,128)(2,1)S(1)} collective-permute-done((bf16[192,512]{1,0:T(8,128)(2,1)S(1)}, bf16[192,512]{1,0:T(8,128)(2,1)S(1)}, u32[]{:S(2)}, u32[]{:S(2)}) %collective-permute-start.3) | collective-permute-done | bytes 196640 | tf_op jit(solution)/shard_map/ppermute | solution.py:304
  29.9 2.3 %all_gather.11.refs_3_ = bf16[192,1024]{1,0:T(8,128)(2,1)S(1)} all-gather(bf16[192,512]{1,0:T(8,128)(2,1)S(1)} %collective-permute-done.3), channel_id=1, replica_groups=mesh['expert'=4,'cuts'=2,'dp'=4] {'cuts'}, dimensions={1}, use_global_device_ids=true | all-gather | bytes 589824 | tf_op jit(solution)/shard_map/all_gather | solution.py:335
  32.2 2.3 %hidden.1 = (bf16[768,1024]{1,0:T(8,128)(2,1)S(1)}, bf16[1344,768]{1,0:T(8,128)(2,1)S(1)}, bf16[1344,768]{1,0:T(8,128)(2,1)S(1)}) custom-call(bf16[192,1024]{1,0:T(8,128)(2,1)S(1)} %get-tuple-element.85.refs_0_, bf16[192,1024]{1,0:T(8,128)(2,1)S(1)} %all_gather.9.refs_1_, bf16[192,1024]{1,0:T(8,128)(2,1)S(1)} %all_gather.10.refs_2_, ...), custom_call_target="tpu_custom_call" | custom-call | flops 33030144 | bytes 156672 | tf_op jit(solution)/shard_map/hidden/pallas_call | solution.py:31
  34.6 2.2 %rows_give.1 = (bf16[768,1344]{1,0:T(8,128)(2,1)S(1)}, bf16[768,512]{1,0:T(8,128)(2,1)S(1)}) custom-call(bf16[1344,768]{1,0:T(8,128)(2,1)S(1)} %get-tuple-element.126.units_ref.refs_7_, bf16[1344,1024]{1,0:T(8,128)(2,1)S(1)} %bitcast.11), custom_call_target="tpu_custom_call" | custom-call | flops 16515072 | bytes 119808 | tf_op jit(solution)/shard_map/rows_give/pallas_call | solution.py:31
  39.6 1.4 %outer_leaving.1 = (bf16[768,1024]{1,0:T(8,128)(2,1)S(1)}, bf16[1344,256]{1,0:T(8,128)(2,1)S(1)}, bf16[1344,256]{1,0:T(8,128)(2,1)S(1)}) custom-call(bf16[192,1024]{1,0:T(8,128)(2,1)S(1)} %get-tuple-element.108.refs_0_, bf16[192,512]{1,0:T(8,128)(2,1)S(1)} %collective-permute-done.6.refs_1_, bf16[192,512]{1,0:T(8,128)(2,1)S(1)} %collective-permute-done.4.refs_2_, ...), custom_call_target="tpu_custom_call" | custom-call | flops 16515072 | bytes 102912 | tf_op jit(solution)/shard_map/outer_leaving/pallas_call | solution.py:31
  41.0 1.6 %collective-permute-start.19 = (bf16[1344,256]{1,0:T(8,128)(2,1)S(1)}, bf16[1344,256]{1,0:T(8,128)(2,1)S(1)}, u32[]{:S(2)}, u32[]{:S(2)}) collective-permute-start(bf16[1344,256]{1,0:T(8,128)(2,1)S(1)} %get-tuple-element.144), channel_id=1, source_target_pairs={{0,2},{1,3},{2,0},{3,1},{4,6},{5,7},{6,4},{7,5},{8,10},{9,11},{10,... | collective-permute-start | bytes 2064392 | tf_op jit(solution)/shard_map/ppermute | solution.py:304
  42.6 1.5 %collective-permute-start.18 = (bf16[1344,256]{1,0:T(8,128)(2,1)S(1)}, bf16[1344,256]{1,0:T(8,128)(2,1)S(1)}, u32[]{:S(2)}, u32[]{:S(2)}) collective-permute-start(bf16[1344,256]{1,0:T(8,128)(2,1)S(1)} %get-tuple-element.142), channel_id=1, source_target_pairs={{0,1},{1,0},{2,3},{3,2},{4,5},{5,4},{6,7},{7,6},{8,9},{9,8},{10,11... | collective-permute-start | bytes 2064392 | tf_op jit(solution)/shard_map/ppermute | solution.py:304
  44.1 1.4 %rows_keep.1.keep_ref = bf16[768,512]{1,0:T(8,128)(2,1)S(1)} custom-call(bf16[768,1344]{1,0:T(8,128)(2,1)S(1)} %get-tuple-element.98.turned_ref, bf16[1344,1024]{1,0:T(8,128)(2,1)S(1)} %bitcast.12), custom_call_target="tpu_custom_call" | custom-call | flops 16515072 | bytes 87552 | tf_op jit(solution)/shard_map/rows_keep/pallas_call | solution.py:31
  45.7 4.4 %collective-permute-start.11 = (bf16[192,512]{1,0:T(8,128)(2,1)S(1)}, bf16[192,512]{1,0:T(8,128)(2,1)S(1)}, u32[]{:S(2)}, u32[]{:S(2)}) collective-permute-start(bf16[192,512]{1,0:T(8,128)(2,1)S(1)} %get-tuple-element.117), channel_id=1, source_target_pairs={{0,16},{8,24},{16,0},{24,8},{1,17},{9,25},{17,1},{25,9},{2,18},{10... | collective-permute-start | bytes 589832 | tf_op jit(solution)/shard_map/ppermute | solution.py:304
  50.1 1.4 %collective-permute-start.12 = (bf16[192,512]{1,0:T(8,128)(2,1)S(1)}, bf16[192,512]{1,0:T(8,128)(2,1)S(1)}, u32[]{:S(2)}, u32[]{:S(2)}) collective-permute-start(bf16[192,512]{1,0:T(8,128)(2,1)S(1)} %get-tuple-element.118), channel_id=1, source_target_pairs={{0,24},{8,16},{16,8},{24,0},{1,25},{9,17},{17,9},{25,1},{2,26},{10... | collective-permute-start | bytes 589832 | tf_op jit(solution)/shard_map/ppermute | solution.py:304
  51.5 2.3 %d_act.1.units_ref = bf16[1344,768]{1,0:T(8,128)(2,1)S(1)} custom-call(bf16[768,1024]{1,0:T(8,128)(2,1)S(1)} %get-tuple-element.127.g_ref.rows_ref, bf16[1344,768]{1,0:T(8,128)(2,1)S(1)} %get-tuple-element.122.positive_ref, bf16[1344,1024]{1,0:T(8,128)(2,1)S(1)} %bitcast.13), custom_call_target="tpu_custom_call" | custom-call | flops 33030144 | bytes 132096 | tf_op jit(solution)/shard_map/d_act/pallas_call | solution.py:31
  53.8 1.3 %inner_leaving.1 = (bf16[1344,256]{1,0:T(8,128)(2,1)S(1)}, bf16[1344,256]{1,0:T(8,128)(2,1)S(1)}) custom-call(bf16[1344,768]{1,0:T(8,128)(2,1)S(1)} %d_act.1.units_ref, bf16[768,1024]{1,0:T(8,128)(2,1)S(1)} %get-tuple-element.123.rows_ref), custom_call_target="tpu_custom_call" | custom-call | flops 16515072 | bytes 78336 | tf_op jit(solution)/shard_map/inner_leaving/pallas_call | solution.py:31
  56.4 2.3 %collective-permute-done.19.came = bf16[1344,256]{1,0:T(8,128)(2,1)S(1)} collective-permute-done((bf16[1344,256]{1,0:T(8,128)(2,1)S(1)}, bf16[1344,256]{1,0:T(8,128)(2,1)S(1)}, u32[]{:S(2)}, u32[]{:S(2)}) %collective-permute-start.19) | collective-permute-done | bytes 688160 | tf_op jit(solution)/shard_map/ppermute | solution.py:304
  58.8 1.6 %collective-permute-start.21 = (bf16[2016,256]{1,0:T(8,128)(2,1)S(1)}, bf16[2016,256]{1,0:T(8,128)(2,1)S(1)}, u32[]{:S(2)}, u32[]{:S(2)}) collective-permute-start(bf16[2016,256]{1,0:T(8,128)(2,1)S(1)} %get-tuple-element.148), channel_id=1, source_target_pairs={{0,1},{1,0},{2,3},{3,2},{4,5},{5,4},{6,7},{7,6},{8,9},{9,8},{10,11... | collective-permute-start | bytes 3096584 | tf_op jit(solution)/shard_map/ppermute | solution.py:304
  60.6 1.6 %collective-permute-start.20 = (bf16[2016,256]{1,0:T(8,128)(2,1)S(1)}, bf16[2016,256]{1,0:T(8,128)(2,1)S(1)}, u32[]{:S(2)}, u32[]{:S(2)}) collective-permute-start(bf16[2016,256]{1,0:T(8,128)(2,1)S(1)} %get-tuple-element.146), channel_id=1, source_target_pairs={{0,2},{1,3},{2,0},{3,1},{4,6},{5,7},{6,4},{7,5},{8,10},{9,11},{10,... | collective-permute-start | bytes 3096584 | tf_op jit(solution)/shard_map/ppermute | solution.py:304
  62.2 2.4 %grad_rows_give.1 = (bf16[768,1344]{1,0:T(8,128)(2,1)S(1)}, bf16[768,512]{1,0:T(8,128)(2,1)S(1)}) custom-call(bf16[1344,768]{1,0:T(8,128)(2,1)S(1)} %d_act.1.units_ref, bf16[1344,1024]{1,0:T(8,128)(2,1)S(1)} %bitcast.15), custom_call_target="tpu_custom_call" | custom-call | flops 16515072 | bytes 119808 | tf_op jit(solution)/shard_map/grad_rows_give/pallas_call | solution.py:31
  64.7 1.4 %grad_rows_keep.1.keep_ref = bf16[768,512]{1,0:T(8,128)(2,1)S(1)} custom-call(bf16[768,1344]{1,0:T(8,128)(2,1)S(1)} %get-tuple-element.136.turned_ref, bf16[1344,1024]{1,0:T(8,128)(2,1)S(1)} %bitcast.16), custom_call_target="tpu_custom_call" | custom-call | flops 16515072 | bytes 87552 | tf_op jit(solution)/shard_map/grad_rows_keep/pallas_call | solution.py:31
  67.2 4.5 %collective-permute-start.15 = (bf16[192,512]{1,0:T(8,128)(2,1)S(1)}, bf16[192,512]{1,0:T(8,128)(2,1)S(1)}, u32[]{:S(2)}, u32[]{:S(2)}) collective-permute-start(bf16[192,512]{1,0:T(8,128)(2,1)S(1)} %get-tuple-element.139), channel_id=1, source_target_pairs={{0,16},{8,24},{16,0},{24,8},{1,17},{9,25},{17,1},{25,9},{2,18},{10... | collective-permute-start | bytes 589832 | tf_op jit(solution)/shard_map/ppermute | solution.py:304
  71.6 1.4 %collective-permute-start.16 = (bf16[192,512]{1,0:T(8,128)(2,1)S(1)}, bf16[192,512]{1,0:T(8,128)(2,1)S(1)}, u32[]{:S(2)}, u32[]{:S(2)}) collective-permute-start(bf16[192,512]{1,0:T(8,128)(2,1)S(1)} %get-tuple-element.140), channel_id=1, source_target_pairs={{0,24},{8,16},{16,8},{24,0},{1,25},{9,17},{17,9},{25,1},{2,26},{10... | collective-permute-start | bytes 589832 | tf_op jit(solution)/shard_map/ppermute | solution.py:304
  75.0 8.0 %collective-permute-done.21.came1.mixed = bf16[2016,256]{1,0:T(8,128)(2,1)S(1)} collective-permute-done((bf16[2016,256]{1,0:T(8,128)(2,1)S(1)}, bf16[2016,256]{1,0:T(8,128)(2,1)S(1)}, u32[]{:S(2)}, u32[]{:S(2)}) %collective-permute-start.21) | collective-permute-done | bytes 1032224 | tf_op jit(solution)/shard_map/ppermute | solution.py:304
  83.2 1.6 %collective-permute-start.25 = (bf16[672,256]{1,0:T(8,128)(2,1)S(1)}, bf16[672,256]{1,0:T(8,128)(2,1)S(1)}, u32[]{:S(2)}, u32[]{:S(2)}) collective-permute-start(bf16[672,256]{1,0:T(8,128)(2,1)S(1)} %get-tuple-element.163), channel_id=1, source_target_pairs={{0,2},{1,3},{2,0},{3,1},{4,6},{5,7},{6,4},{7,5},{8,10},{9,11},{10,... | collective-permute-start | bytes 1032200 | tf_op jit(solution)/shard_map/ppermute | solution.py:304
  85.0 1.6 %collective-permute-start.24 = (bf16[672,256]{1,0:T(8,128)(2,1)S(1)}, bf16[672,256]{1,0:T(8,128)(2,1)S(1)}, u32[]{:S(2)}, u32[]{:S(2)}) collective-permute-start(bf16[672,256]{1,0:T(8,128)(2,1)S(1)} %get-tuple-element.160), channel_id=1, source_target_pairs={{0,1},{1,0},{2,3},{3,2},{4,5},{5,4},{6,7},{7,6},{8,9},{9,8},{10,11... | collective-permute-start | bytes 1032200 | tf_op jit(solution)/shard_map/ppermute | solution.py:304
  90.0 1.5 %join.1 = (f32[256,1024]{1,0:T(8,128)}, f32[256,1024]{1,0:T(8,128)}) custom-call(f32[256,512]{1,0:T(8,128)S(1)} %get-tuple-element.135.refs_0_, f32[256,512]{1,0:T(8,128)S(1)} %get-tuple-element.153.refs_1_, bf16[256,512]{1,0:T(8,128)(2,1)S(1)} %collective-permute-done.22.refs_2_, bf16[256,512]{1,0:T(8,128)(2,1)S(1)} %collective-permute-done.23.refs_3_), custom_call_target="tpu_custom_call" | custom-call | bytes 57344 | tf_op jit(solution)/shard_map/join/pallas_call | solution.py:31
  (53 shorter events, 16.7 us)
Async XLA Ops:
  1.9 30.3 %copy-start.1 = (bf16[1,1024,1344]{1,2,0:T(8,128)(2,1)S(1)}, bf16[1,1024,1344]{1,2,0:T(8,128)(2,1)}, u32[]{:S(2)}) copy-start(bf16[1,1024,1344]{1,2,0:T(8,128)(2,1)} %param.12) | copy-start | bytes 8257540
  1.9 16.9 %collective-permute-start.1 = (bf16[256,512]{1,0:T(8,128)(2,1)S(1)}, bf16[256,512]{1,0:T(8,128)(2,1)S(1)}, u32[]{:S(2)}, u32[]{:S(2)}) collective-permute-start(bf16[256,512]{1,0:T(8,128)(2,1)S(1)} %get-tuple-element.87), channel_id=1, source_target_pairs={{0,16},{8,24},{16,0},{24,8},{1,17},{9,25},{17,1},{25,9},{2,18},{10... | collective-permute-start | bytes 786440 | tf_op jit(solution)/shard_map/ppermute | solution.py:304
  7.8 11.1 %collective-permute-start = (bf16[192,512]{1,0:T(8,128)(2,1)S(1)}, bf16[192,512]{1,0:T(8,128)(2,1)S(1)}, u32[]{:S(2)}, u32[]{:S(2)}) collective-permute-start(bf16[192,512]{1,0:T(8,128)(2,1)S(1)} %get-tuple-element.86), channel_id=1, source_target_pairs={{0,8},{8,0},{16,24},{24,16},{1,9},{9,1},{17,25},{25,17},{2,10},{10... | collective-permute-start | bytes 589832 | tf_op jit(solution)/shard_map/ppermute | solution.py:304
  9.4 9.0 %collective-permute-start.2 = (bf16[16,256]{1,0:T(8,128)(2,1)S(1)}, bf16[16,256]{1,0:T(8,128)(2,1)S(1)}, u32[]{:S(2)}, u32[]{:S(2)}) collective-permute-start(bf16[16,256]{1,0:T(8,128)(2,1)S(1)} %get-tuple-element.88), channel_id=1, source_target_pairs={{0,16},{8,24},{16,0},{24,8},{1,17},{9,25},{17,1},{25,9},{2,18},{10... | collective-permute-start | bytes 24584 | tf_op jit(solution)/shard_map/ppermute | solution.py:304
  19.3 10.7 %collective-permute-start.3 = (bf16[192,512]{1,0:T(8,128)(2,1)S(1)}, bf16[192,512]{1,0:T(8,128)(2,1)S(1)}, u32[]{:S(2)}, u32[]{:S(2)}) collective-permute-start(bf16[192,512]{1,0:T(8,128)(2,1)S(1)} %get-tuple-element.96), channel_id=1, source_target_pairs={{0,8},{8,0},{16,24},{24,16},{1,9},{9,1},{17,25},{25,17},{2,10},{10... | collective-permute-start | bytes 589832 | tf_op jit(solution)/shard_map/ppermute | solution.py:304
  19.5 17.6 %collective-permute-start.4 = (bf16[192,512]{1,0:T(8,128)(2,1)S(1)}, bf16[192,512]{1,0:T(8,128)(2,1)S(1)}, u32[]{:S(2)}, u32[]{:S(2)}) collective-permute-start(bf16[192,512]{1,0:T(8,128)(2,1)S(1)} %get-tuple-element.102), channel_id=1, source_target_pairs={{0,16},{8,24},{16,0},{24,8},{1,17},{9,25},{17,1},{25,9},{2,18},{10... | collective-permute-start | bytes 589832 | tf_op jit(solution)/shard_map/ppermute | solution.py:304
  22.9 14.3 %collective-permute-start.5 = (bf16[192,512]{1,0:T(8,128)(2,1)S(1)}, bf16[192,512]{1,0:T(8,128)(2,1)S(1)}, u32[]{:S(2)}, u32[]{:S(2)}) collective-permute-start(bf16[192,512]{1,0:T(8,128)(2,1)S(1)} %get-tuple-element.103), channel_id=1, source_target_pairs={{0,24},{8,16},{16,8},{24,0},{1,25},{9,17},{17,9},{25,1},{2,26},{10... | collective-permute-start | bytes 589832 | tf_op jit(solution)/shard_map/ppermute | solution.py:304
  23.7 13.9 %collective-permute-start.6 = (bf16[192,512]{1,0:T(8,128)(2,1)S(1)}, bf16[192,512]{1,0:T(8,128)(2,1)S(1)}, u32[]{:S(2)}, u32[]{:S(2)}) collective-permute-start(bf16[192,512]{1,0:T(8,128)(2,1)S(1)} %get-tuple-element.104), channel_id=1, source_target_pairs={{0,8},{8,0},{16,24},{24,16},{1,9},{9,1},{17,25},{25,17},{2,10},{10... | collective-permute-start | bytes 589832 | tf_op jit(solution)/shard_map/ppermute | solution.py:304
  32.2 2.4 %copy-start = (bf16[1,1344,1024]{2,1,0:T(8,128)(2,1)S(1)}, bf16[1,1344,1024]{2,1,0:T(8,128)(2,1)}, u32[]{:S(2)}) copy-start(bf16[1,1344,1024]{2,1,0:T(8,128)(2,1)} %param.13) | copy-start | bytes 8257540
  37.6 1.4 %collective-permute-start.8 = (bf16[192,512]{1,0:T(8,128)(2,1)S(1)}, bf16[192,512]{1,0:T(8,128)(2,1)S(1)}, u32[]{:S(2)}, u32[]{:S(2)}) collective-permute-start(bf16[192,512]{1,0:T(8,128)(2,1)S(1)} %collective-permute-done.6.refs_1_), channel_id=1, source_target_pairs={{0,4},{4,0},{1,5},{5,1},{2,6},{6,2},{3,7},{7,3},{8,12},{12,8},{9,1... | collective-permute-start | bytes 589832 | tf_op jit(solution)/shard_map/ppermute | solution.py:304
  37.6 1.7 %collective-permute-start.9 = (bf16[192,512]{1,0:T(8,128)(2,1)S(1)}, bf16[192,512]{1,0:T(8,128)(2,1)S(1)}, u32[]{:S(2)}, u32[]{:S(2)}) collective-permute-start(bf16[192,512]{1,0:T(8,128)(2,1)S(1)} %collective-permute-done.4.refs_2_), channel_id=1, source_target_pairs={{0,4},{4,0},{1,5},{5,1},{2,6},{6,2},{3,7},{7,3},{8,12},{12,8},{9,1... | collective-permute-start | bytes 589832 | tf_op jit(solution)/shard_map/ppermute | solution.py:304
  38.1 1.5 %collective-permute-start.10 = (bf16[192,512]{1,0:T(8,128)(2,1)S(1)}, bf16[192,512]{1,0:T(8,128)(2,1)S(1)}, u32[]{:S(2)}, u32[]{:S(2)}) collective-permute-start(bf16[192,512]{1,0:T(8,128)(2,1)S(1)} %collective-permute-done.5.refs_3_), channel_id=1, source_target_pairs={{0,4},{4,0},{1,5},{5,1},{2,6},{6,2},{3,7},{7,3},{8,12},{12,8},{9,1... | collective-permute-start | bytes 589832 | tf_op jit(solution)/shard_map/ppermute | solution.py:304
  38.1 7.4 %collective-permute-start.7 = (bf16[768,512]{1,0:T(8,128)(2,1)S(1)}, bf16[768,512]{1,0:T(8,128)(2,1)S(1)}, u32[]{:S(2)}, u32[]{:S(2)}) collective-permute-start(bf16[768,512]{1,0:T(8,128)(2,1)S(1)} %get-tuple-element.107), channel_id=1, source_target_pairs={{0,4},{4,0},{1,5},{5,1},{2,6},{6,2},{3,7},{7,3},{8,12},{12,8},{9,1... | collective-permute-start | bytes 2359304 | tf_op jit(solution)/shard_map/ppermute | solution.py:304
  41.0 17.6 %collective-permute-start.19 = (bf16[1344,256]{1,0:T(8,128)(2,1)S(1)}, bf16[1344,256]{1,0:T(8,128)(2,1)S(1)}, u32[]{:S(2)}, u32[]{:S(2)}) collective-permute-start(bf16[1344,256]{1,0:T(8,128)(2,1)S(1)} %get-tuple-element.144), channel_id=1, source_target_pairs={{0,2},{1,3},{2,0},{3,1},{4,6},{5,7},{6,4},{7,5},{8,10},{9,11},{10,... | collective-permute-start | bytes 2064392 | tf_op jit(solution)/shard_map/ppermute | solution.py:304
  42.6 17.8 %collective-permute-start.18 = (bf16[1344,256]{1,0:T(8,128)(2,1)S(1)}, bf16[1344,256]{1,0:T(8,128)(2,1)S(1)}, u32[]{:S(2)}, u32[]{:S(2)}) collective-permute-start(bf16[1344,256]{1,0:T(8,128)(2,1)S(1)} %get-tuple-element.142), channel_id=1, source_target_pairs={{0,1},{1,0},{2,3},{3,2},{4,5},{5,4},{6,7},{7,6},{8,9},{9,8},{10,11... | collective-permute-start | bytes 2064392 | tf_op jit(solution)/shard_map/ppermute | solution.py:304
  45.7 18.9 %collective-permute-start.11 = (bf16[192,512]{1,0:T(8,128)(2,1)S(1)}, bf16[192,512]{1,0:T(8,128)(2,1)S(1)}, u32[]{:S(2)}, u32[]{:S(2)}) collective-permute-start(bf16[192,512]{1,0:T(8,128)(2,1)S(1)} %get-tuple-element.117), channel_id=1, source_target_pairs={{0,16},{8,24},{16,0},{24,8},{1,17},{9,25},{17,1},{25,9},{2,18},{10... | collective-permute-start | bytes 589832 | tf_op jit(solution)/shard_map/ppermute | solution.py:304
  50.1 14.5 %collective-permute-start.12 = (bf16[192,512]{1,0:T(8,128)(2,1)S(1)}, bf16[192,512]{1,0:T(8,128)(2,1)S(1)}, u32[]{:S(2)}, u32[]{:S(2)}) collective-permute-start(bf16[192,512]{1,0:T(8,128)(2,1)S(1)} %get-tuple-element.118), channel_id=1, source_target_pairs={{0,24},{8,16},{16,8},{24,0},{1,25},{9,17},{17,9},{25,1},{2,26},{10... | collective-permute-start | bytes 589832 | tf_op jit(solution)/shard_map/ppermute | solution.py:304
  51.5 13.1 %collective-permute-start.13 = (bf16[192,512]{1,0:T(8,128)(2,1)S(1)}, bf16[192,512]{1,0:T(8,128)(2,1)S(1)}, u32[]{:S(2)}, u32[]{:S(2)}) collective-permute-start(bf16[192,512]{1,0:T(8,128)(2,1)S(1)} %get-tuple-element.119), channel_id=1, source_target_pairs={{0,8},{8,0},{16,24},{24,16},{1,9},{9,1},{17,25},{25,17},{2,10},{10... | collective-permute-start | bytes 589832 | tf_op jit(solution)/shard_map/ppermute | solution.py:304
  58.8 24.2 %collective-permute-start.21 = (bf16[2016,256]{1,0:T(8,128)(2,1)S(1)}, bf16[2016,256]{1,0:T(8,128)(2,1)S(1)}, u32[]{:S(2)}, u32[]{:S(2)}) collective-permute-start(bf16[2016,256]{1,0:T(8,128)(2,1)S(1)} %get-tuple-element.148), channel_id=1, source_target_pairs={{0,1},{1,0},{2,3},{3,2},{4,5},{5,4},{6,7},{7,6},{8,9},{9,8},{10,11... | collective-permute-start | bytes 3096584 | tf_op jit(solution)/shard_map/ppermute | solution.py:304
  60.6 24.2 %collective-permute-start.20 = (bf16[2016,256]{1,0:T(8,128)(2,1)S(1)}, bf16[2016,256]{1,0:T(8,128)(2,1)S(1)}, u32[]{:S(2)}, u32[]{:S(2)}) collective-permute-start(bf16[2016,256]{1,0:T(8,128)(2,1)S(1)} %get-tuple-element.146), channel_id=1, source_target_pairs={{0,2},{1,3},{2,0},{3,1},{4,6},{5,7},{6,4},{7,5},{8,10},{9,11},{10,... | collective-permute-start | bytes 3096584 | tf_op jit(solution)/shard_map/ppermute | solution.py:304
  64.6 2.4 %collective-permute-start.14 = (bf16[768,512]{1,0:T(8,128)(2,1)S(1)}, bf16[768,512]{1,0:T(8,128)(2,1)S(1)}, u32[]{:S(2)}, u32[]{:S(2)}) collective-permute-start(bf16[768,512]{1,0:T(8,128)(2,1)S(1)} %get-tuple-element.137), channel_id=1, source_target_pairs={{0,4},{4,0},{1,5},{5,1},{2,6},{6,2},{3,7},{7,3},{8,12},{12,8},{9,1... | collective-permute-start | bytes 2359304 | tf_op jit(solution)/shard_map/ppermute | solution.py:304
  67.2 20.6 %collective-permute-start.15 = (bf16[192,512]{1,0:T(8,128)(2,1)S(1)}, bf16[192,512]{1,0:T(8,128)(2,1)S(1)}, u32[]{:S(2)}, u32[]{:S(2)}) collective-permute-start(bf16[192,512]{1,0:T(8,128)(2,1)S(1)} %get-tuple-element.139), channel_id=1, source_target_pairs={{0,16},{8,24},{16,0},{24,8},{1,17},{9,25},{17,1},{25,9},{2,18},{10... | collective-permute-start | bytes 589832 | tf_op jit(solution)/shard_map/ppermute | solution.py:304
  71.6 16.1 %collective-permute-start.16 = (bf16[192,512]{1,0:T(8,128)(2,1)S(1)}, bf16[192,512]{1,0:T(8,128)(2,1)S(1)}, u32[]{:S(2)}, u32[]{:S(2)}) collective-permute-start(bf16[192,512]{1,0:T(8,128)(2,1)S(1)} %get-tuple-element.140), channel_id=1, source_target_pairs={{0,24},{8,16},{16,8},{24,0},{1,25},{9,17},{17,9},{25,1},{2,26},{10... | collective-permute-start | bytes 589832 | tf_op jit(solution)/shard_map/ppermute | solution.py:304
  73.0 14.8 %collective-permute-start.17 = (bf16[192,512]{1,0:T(8,128)(2,1)S(1)}, bf16[192,512]{1,0:T(8,128)(2,1)S(1)}, u32[]{:S(2)}, u32[]{:S(2)}) collective-permute-start(bf16[192,512]{1,0:T(8,128)(2,1)S(1)} %get-tuple-element.141), channel_id=1, source_target_pairs={{0,8},{8,0},{16,24},{24,16},{1,9},{9,1},{17,25},{25,17},{2,10},{10... | collective-permute-start | bytes 589832 | tf_op jit(solution)/shard_map/ppermute | solution.py:304
  83.2 8.7 %collective-permute-start.25 = (bf16[672,256]{1,0:T(8,128)(2,1)S(1)}, bf16[672,256]{1,0:T(8,128)(2,1)S(1)}, u32[]{:S(2)}, u32[]{:S(2)}) collective-permute-start(bf16[672,256]{1,0:T(8,128)(2,1)S(1)} %get-tuple-element.163), channel_id=1, source_target_pairs={{0,2},{1,3},{2,0},{3,1},{4,6},{5,7},{6,4},{7,5},{8,10},{9,11},{10,... | collective-permute-start | bytes 1032200 | tf_op jit(solution)/shard_map/ppermute | solution.py:304
  85.0 8.2 %collective-permute-start.24 = (bf16[672,256]{1,0:T(8,128)(2,1)S(1)}, bf16[672,256]{1,0:T(8,128)(2,1)S(1)}, u32[]{:S(2)}, u32[]{:S(2)}) collective-permute-start(bf16[672,256]{1,0:T(8,128)(2,1)S(1)} %get-tuple-element.160), channel_id=1, source_target_pairs={{0,1},{1,0},{2,3},{3,2},{4,5},{5,4},{6,7},{7,6},{8,9},{9,8},{10,11... | collective-permute-start | bytes 1032200 | tf_op jit(solution)/shard_map/ppermute | solution.py:304
  87.7 1.5 %collective-permute-start.22 = (bf16[256,512]{1,0:T(8,128)(2,1)S(1)}, bf16[256,512]{1,0:T(8,128)(2,1)S(1)}, u32[]{:S(2)}, u32[]{:S(2)}) collective-permute-start(bf16[256,512]{1,0:T(8,128)(2,1)S(1)} %get-tuple-element.154), channel_id=1, source_target_pairs={{0,4},{4,0},{1,5},{5,1},{2,6},{6,2},{3,7},{7,3},{8,12},{12,8},{9,1... | collective-permute-start | bytes 786440 | tf_op jit(solution)/shard_map/ppermute | solution.py:304
  88.3 1.7 %collective-permute-start.23 = (bf16[256,512]{1,0:T(8,128)(2,1)S(1)}, bf16[256,512]{1,0:T(8,128)(2,1)S(1)}, u32[]{:S(2)}, u32[]{:S(2)}) collective-permute-start(bf16[256,512]{1,0:T(8,128)(2,1)S(1)} %get-tuple-element.155), channel_id=1, source_target_pairs={{0,4},{4,0},{1,5},{5,1},{2,6},{6,2},{3,7},{7,3},{8,12},{12,8},{9,1... | collective-permute-start | bytes 786440 | tf_op jit(solution)/shard_map/ppermute | solution.py:304
